TPU v7x, 32 devices: a whole 2x2x4 slice. The times are simulated.
32 devices in a mesh: groups: 2 (over x), seq: 8 (over z, y), exp: 2 (over core).
Axes of the slice: x: 2, y: 2, z: 4, core: 2. Of those that a mesh axis runs over, the one named last changes fastest.
Arguments:
- queries: bfloat16 [4096, 2048], P(('groups', 'seq'), 'exp'), parts along dimension 0, may hold values from -6 to 6
- key_rows: bfloat16 [4096, 256], P(('groups', 'seq'), 'exp'), parts along dimension 0, may hold values from -6 to 6
- values: bfloat16 [4096, 256], P(('groups', 'seq'), 'exp'), parts along dimension 0, may hold values from -6 to 6
- sink_logit: float32 [32], P('exp'), may hold values from 0 to 5
- o_weight: bfloat16 [2048, 1440], P('exp'), may hold values from -0.5 to 0.5
- residual: bfloat16 [4096, 1440], P(('groups', 'seq')), parts along dimension 0, may hold values from -30 to 30
- norm_gain: float32 [1440], replicated, may hold values from 0.1 to 1.9
- routes: int32 [4096, 4], P(('groups', 'seq')), parts along dimension 0, may hold values from 0 to 7, all different within a row; in each aligned block of 128 rows (0 to 127, 128 to 255, ...) at most 128 rows name the same one
- gate_codes: int32 [4096, 4], P(('groups', 'seq')), parts along dimension 0, may hold values from 1 to 256
- w_gate: bfloat16 [8, 1440, 1440], P('seq', None, 'exp'), may hold values from -0.15625 to 0.15625
- w_up: bfloat16 [8, 1440, 1440], P('seq', None, 'exp'), may hold values from -0.15625 to 0.15625
- w_down: bfloat16 [8, 1440, 1440], P('seq', 'exp'), may hold values from -0.15625 to 0.15625
Outputs:
- attended: bfloat16 [4096, 1440], P(('groups', 'seq', 'exp')), parts along dimension 0
- expert_mix: bfloat16 [4096, 1440], P(('groups', 'seq', 'exp')), parts along dimension 0
There are 2 independent parts, one for each index of `groups`. A program takes and returns all parts, laid end to end along the dimension named above; an argument that names none is the same for every part. Nothing has to cross between parts.
Inputs may be any that keep to these rules, and one draw needn't show every extreme that they name: `routes`: each row names 4 different experts; in each aligned block of 128 rows no expert is named by more than 128 rows, and in some block one expert is named by exactly 128 rows.
All inputs are finite; a program needn't handle non-finite values.
Results may differ from a plain program's by a relative error of at most 0.013.
Values may be sent and summed in bfloat16 or wider, within the bound.
No kernel may reach another device: no remote copies, remote signals or barrier semaphores. Data moves between devices by JAX's collectives and lax.ppermute only.
A program may use at most 128 MiB of HBM per device.

v0:
```python
import jax
import jax.numpy as jnp
from jax import lax
from jax.sharding import PartitionSpec as P

HEAD_DIM = 64
WINDOW = 128
TOP = 4


def shifted(value, axis, steps):
    count = lax.axis_size(axis)
    first, last = (max(0, -steps), min(count, count - steps))
    return lax.ppermute(value, axis, [(source, source + steps) for source in range(first, last)])


def swiglu(gate_val, up_val):
    return (up_val + 1.0) * gate_val * jax.nn.sigmoid(1.702 * gate_val)


def rms_norm(stream, norm_gain):
    widened = stream.astype(jnp.float32)
    spread = jnp.mean(widened * widened, axis=-1, keepdims=True)
    return (widened * lax.rsqrt(spread + 1e-05) * norm_gain).astype(jnp.bfloat16)


def window_attention(queries, key_rows, values, sink_logit):
    row_count = queries.shape[0]
    kv_local = key_rows.shape[1] // HEAD_DIM
    group_size = queries.shape[1] // HEAD_DIM // kv_local
    rim_keys, rim_values = shifted(
        (key_rows[row_count - WINDOW :], values[row_count - WINDOW :]), "seq", 1
    )
    full_keys = jnp.concatenate([rim_keys, key_rows], axis=0).reshape(
        WINDOW + row_count, kv_local, HEAD_DIM
    )
    full_values = jnp.concatenate([rim_values, values], axis=0).reshape(
        WINDOW + row_count, kv_local, HEAD_DIM
    )
    grouped = queries.reshape(row_count, kv_local, group_size, HEAD_DIM)
    scores = jnp.einsum(
        "tgjd,ugd->gjtu", grouped, full_keys, preferred_element_type=jnp.float32
    ) * HEAD_DIM ** (-0.5)
    query_pos = jnp.arange(row_count, dtype=jnp.int32)[:, None] + WINDOW
    key_pos = jnp.arange(WINDOW + row_count, dtype=jnp.int32)[None, :]
    first_key = jnp.where(lax.axis_index("seq") == 0, WINDOW, 0)
    allowed = (key_pos <= query_pos) & (key_pos > query_pos - WINDOW) & (key_pos >= first_key)
    scores = jnp.where(allowed, scores, -1e30)
    sink_vals = sink_logit.reshape(kv_local, group_size)[:, :, None, None]
    ceiling = jnp.maximum(jnp.max(scores, axis=-1, keepdims=True), sink_vals)
    raised = jnp.exp(scores - ceiling)
    denominator = jnp.sum(raised, axis=-1, keepdims=True) + jnp.exp(sink_vals - ceiling)
    weights = (raised / denominator).astype(jnp.bfloat16)
    mixed = jnp.einsum("gjtu,ugd->tgjd", weights, full_values, preferred_element_type=jnp.float32)
    return mixed.astype(jnp.bfloat16).reshape(row_count, kv_local * group_size * HEAD_DIM)


def pack_rows(normed, expert_ids, gate_codes, expert_count, capacity):
    pair_ids = expert_ids.reshape(-1)
    matches = (pair_ids[:, None] == jnp.arange(expert_count, dtype=jnp.int32)[None, :]).astype(
        jnp.int32
    )
    within = jnp.sum((jnp.cumsum(matches, axis=0) - 1) * matches, axis=1)
    sources = normed[jnp.arange(pair_ids.shape[0], dtype=jnp.int32) // expert_ids.shape[1]]
    outbox = jnp.zeros((expert_count * capacity, normed.shape[1]), normed.dtype)
    outbox = outbox.at[pair_ids * capacity + within].set(sources)
    code_vals = gate_codes.astype(jnp.float32)
    shares = (code_vals / jnp.sum(code_vals, axis=1, keepdims=True)).reshape(-1)
    return (outbox, pair_ids, within, shares)


def expert_apply(arrived, w_gate, w_up, w_down):
    flat_rows = arrived.reshape(-1, arrived.shape[-1])
    gate_val = jnp.dot(flat_rows, w_gate[0], preferred_element_type=jnp.float32)
    up_val = jnp.dot(flat_rows, w_up[0], preferred_element_type=jnp.float32)
    hidden = swiglu(gate_val, up_val).astype(jnp.bfloat16)
    result = jnp.dot(hidden, w_down[0], preferred_element_type=jnp.float32)
    return result.reshape(arrived.shape)


def local(
    queries,
    key_rows,
    values,
    sink_logit,
    o_weight,
    residual,
    norm_gain,
    routes,
    gate_codes,
    w_gate,
    w_up,
    w_down,
):
    heads_out = window_attention(queries, key_rows, values, sink_logit)
    proj_terms = jnp.dot(heads_out, o_weight, preferred_element_type=jnp.float32)
    owners = lax.axis_size("exp")
    owner_pos = lax.axis_index("exp")
    block_rows = residual.shape[0] // owners
    expert_count = w_gate.shape[0] * lax.axis_size("seq")
    capacity = max(2, 2 * block_rows * TOP // expert_count)
    feature_dim = residual.shape[1]
    own_stream = lax.dynamic_slice_in_dim(residual, owner_pos * block_rows, block_rows, 0)
    own_routes = lax.dynamic_slice_in_dim(routes, owner_pos * block_rows, block_rows, 0)
    own_codes = lax.dynamic_slice_in_dim(gate_codes, owner_pos * block_rows, block_rows, 0)
    own_terms = lax.psum_scatter(proj_terms, "exp", scatter_dimension=0, tiled=True)
    attended = (own_stream.astype(jnp.float32) + own_terms).astype(jnp.bfloat16)
    normed = rms_norm(attended, norm_gain)
    outbox, pair_ids, within, shares = pack_rows(
        normed, own_routes, own_codes, expert_count, capacity
    )
    partial_value = expert_apply(
        lax.all_gather(
            lax.all_to_all(
                outbox.reshape(expert_count, capacity, feature_dim),
                "seq",
                split_axis=0,
                concat_axis=0,
                tiled=True,
            ),
            "exp",
            axis=0,
            tiled=True,
        ),
        w_gate,
        w_up,
        w_down,
    )
    whole = lax.psum_scatter(
        partial_value.astype(jnp.bfloat16), "exp", scatter_dimension=0, tiled=True
    ).astype(jnp.float32)
    returned = lax.all_to_all(
        whole.astype(jnp.bfloat16), "seq", split_axis=0, concat_axis=0, tiled=True
    ).astype(whole.dtype)
    picked = returned[pair_ids, within]
    mixture = jnp.sum((picked * shares[:, None]).reshape(-1, TOP, feature_dim), axis=1)
    return (attended, mixture.astype(jnp.bfloat16))


def solution(mesh):
    placed = (
        P(("groups", "seq"), "exp"),
        P(("groups", "seq"), "exp"),
        P(("groups", "seq"), "exp"),
        P("exp"),
        P("exp", None),
        P(("groups", "seq"), None),
        P(),
        P(("groups", "seq"), None),
        P(("groups", "seq"), None),
        P("seq", None, "exp"),
        P("seq", None, "exp"),
        P("seq", "exp", None),
    )
    return jax.shard_map(
        local,
        mesh=mesh,
        in_specs=placed,
        out_specs=(P(("groups", "seq", "exp"), None), P(("groups", "seq", "exp"), None)),
        check_vma=False,
    )
```

profile of v0, /device:TPU:0, one launch (start us, length us, event | category | flops | bytes accessed | tf_op | source)
XLA Modules:
  0.0 291.0 jit_solution(6697658859597464996)
XLA Ops:
  7.2 0.0 reduce-scatter.3.cloned.1.call-start
  7.2 0.9 slice.13
  8.1 5.5 %collective-permute-start.1 = (bf16[128,128]{1,0:T(8,128)(2,1)S(1)}, bf16[128,128]{1,0:T(8,128)(2,1)}, u32[]{:S(2)}, u32[]{:S(2)}) collective-permute-start(bf16[128,128]{1,0:T(8,128)(2,1)S(1)} %slice.13), channel_id=1, source_target_pairs={{0,2},{2,4},{4,6},{6,8},{8,10},{10,12},{12,14},{1,3},{3,5},{5,7},{... | collective-permute-start | bytes 98312 | tf_op jit(solution)/shard_map/ppermute | solution.py:14
  13.6 0.8 slice.12
  14.4 3.4 %collective-permute-start = (bf16[128,128]{1,0:T(8,128)(2,1)S(1)}, bf16[128,128]{1,0:T(8,128)(2,1)}, u32[]{:S(2)}, u32[]{:S(2)}) collective-permute-start(bf16[128,128]{1,0:T(8,128)(2,1)S(1)} %slice.12), channel_id=1, source_target_pairs={{0,2},{2,4},{4,6},{6,8},{8,10},{10,12},{12,14},{1,3},{3,5},{5,7},{... | collective-permute-start | bytes 98312 | tf_op jit(solution)/shard_map/ppermute | solution.py:14
  17.8 0.8 fusion.27
  18.6 1.2 copy.65
  19.8 0.7 max.18
  20.6 1.5 pad_maximum_fusion.1
  22.1 1.6 copy.64
  23.7 2.0 fusion.7
  25.8 0.1 broadcast_maximum_fusion
  25.8 2.6 copy-done.2
  28.4 1.3 fusion.4
  29.7 0.1 exponential_add_fusion
  29.8 0.8 pad_maximum_fusion
  30.5 0.1 copy.63
  30.7 4.6 %fusion.22 = bf16[2,64,8,256]{3,1,2,0:T(8,128)(2,1)S(1)} fusion(bf16[384,2,64,1]{0,2,3,1:T(8,128)(2,1)S(1)} %bitcast.77, f32[2,384,256,8]{2,1,3,0:T(8,128)} %copy-done.2, f32[2,8,256]{2,1,0:T(8,128)S(1)} %exponential_add_fusion, f32[2,8,256]{2,1,0:T(8,128)S(1)} %broadcast_maximum_fusion, pred[256,384]{0,1:T(8,128)(4,1)S(1)} %copy-done.4), kind=kOutput, calls=%fused_computation.27 | convolution fusion | flops 209453056 | bytes 7045120 | tf_op jit(solution)/shard_map/gjtu,ugd->tgjd/dot_general | solution.py:54
  35.3 2.1 fusion.37
  37.4 0.2 all-gather.2.cloned.1.call-start
  37.6 0.1 copy.67
  37.8 0.1 eq.33
  37.9 0.1 eq.29
  38.0 0.1 reshape.209
  38.1 1.1 reduce-window.6
  39.2 0.2 slice_reduce_fusion
  39.5 0.1 fusion.28
  39.6 6.5 %reduce-scatter.3.cloned.1.call-done = f32[128,1440]{0,1:T(8,128)} async-done(((f32[256,1440]{0,1:T(8,128)}), f32[128,1440]{0,1:T(8,128)}) %reduce-scatter.3.cloned.1.call-update) | async-done | bytes 737296 | tf_op jit(solution)/shard_map/reduce_scatter | solution.py:106
  46.2 1.4 fusion.23
  47.6 0.3 fusion.25
  47.9 0.2 copy.70
  48.1 10.2 %scatter_custom_fusion = bf16[1024,1440]{1,0:T(8,128)(2,1)} fusion(s32[512]{0:T(512)S(1)} %bitcast.80, bf16[128,1440]{1,0:T(8,128)(2,1)S(1)} %copy.70, s32[1024]{0:T(1024)S(1)} %pad_clamp_fusion, bf16[]{:T(256)} %constant.54.clone.1), kind=kCustom, calls=%fused_computation.24 | custom fusion | bytes 2949122 | tf_op jit(solution)/shard_map/scatter | solution.py:66
  58.3 3.5 %copy.72 = bf16[8,128,1440]{1,2,0:T(8,128)(2,1)S(1)} copy(bf16[8,128,1440]{2,1,0:T(8,128)(2,1)} %bitcast.74) | data formatting | bytes 5898240 | tf_op jit(solution)/shard_map/reshape | solution.py:115
  61.8 73.2 %all_to_all.10 = bf16[8,128,1440]{1,2,0:T(8,128)(2,1)} all-to-all(bf16[8,128,1440]{1,2,0:T(8,128)(2,1)S(1)} %copy.72), channel_id=1, replica_groups=mesh['groups'=2,'seq'=8,'exp'=2] {'seq'}, dimensions={0} | all-to-all | bytes 5898240 | tf_op jit(solution)/shard_map/all_to_all | solution.py:114
  135.0 0.3 reduce-scatter.5.cloned.1.call-start
  135.3 14.5 %all-gather.2.cloned.1.call-done = bf16[16,128,1440]{1,2,0:T(8,128)(2,1)} async-done(((bf16[8,128,1440]{1,2,0:T(8,128)(2,1)}), bf16[16,128,1440]{1,2,0:T(8,128)(2,1)}) %all-gather.2.cloned.1.call-update) | async-done | bytes 5898256 | tf_op jit(solution)/shard_map/all_gather | solution.py:113
  149.7 7.8 %fusion.2 = f32[2048,720]{0,1:T(8,128)S(1)} fusion(bf16[1,1440,720]{2,1,0:T(8,128)(2,1)} %param.22, bf16[16,128,1440]{1,2,0:T(8,128)(2,1)} %all-gather.2.cloned.1.call-done), kind=kOutput, calls=%fused_computation.8 | convolution fusion | flops 4246732800 | bytes 13870080 | tf_op jit(solution)/shard_map/dot_general | solution.py:75
  157.6 6.5 %fusion.11 = bf16[90,16,8,128]{3,2,1,0:T(8,128)(2,1)S(1)} fusion(f32[2048,720]{0,1:T(8,128)S(1)} %fusion.2, bf16[1,1440,720]{2,1,0:T(8,128)(2,1)S(1)} %copy-done.11, bf16[16,128,1440]{1,2,0:T(8,128)(2,1)S(1)} %copy-done.10), kind=kOutput, calls=%fused_computation.20 | convolution fusion | flops 4258529280 | bytes 16819200 | tf_op jit(solution)/shard_map/dot_general | solution.py:74
  164.1 6.8 %convolution_convert_fusion = bf16[16,128,1440]{1,2,0:T(8,128)(2,1)} fusion(bf16[90,16,8,128]{3,2,1,0:T(8,128)(2,1)S(1)} %fusion.11, bf16[1,720,1440]{2,1,0:T(8,128)(2,1)S(1)} %copy-done.12), kind=kOutput, calls=%fused_computation.12 | convolution fusion | flops 4249681920 | bytes 10920960 | tf_op jit(solution)/shard_map/dot_general | solution.py:77
  170.9 15.2 %reduce-scatter.5.cloned.1.call-done = bf16[8,128,1440]{1,2,0:T(8,128)(2,1)} async-done(((bf16[16,128,1440]{1,2,0:T(8,128)(2,1)}), bf16[8,128,1440]{1,2,0:T(8,128)(2,1)}) %reduce-scatter.5.cloned.1.call-update) | async-done | bytes 2949136 | tf_op jit(solution)/shard_map/reduce_scatter | solution.py:129
  186.1 5.9 %all-to-all-start.1 = ((bf16[8,128,1440]{1,2,0:T(8,128)(2,1)}), bf16[8,128,1440]{1,2,0:T(8,128)(2,1)S(1)}, u32[]{:S(2)}, u32[]{:S(2)}) async-start(bf16[8,128,1440]{1,2,0:T(8,128)(2,1)} %reduce-scatter.5.cloned.1.call-done), calls=%async_computation.3 | async-start | bytes 5898240 | tf_op jit(solution)/shard_map/all_to_all | solution.py:132
  192.0 0.1 copy.77
  192.1 66.7 %all-to-all-done.1 = bf16[8,128,1440]{1,2,0:T(8,128)(2,1)S(1)} async-done(((bf16[8,128,1440]{1,2,0:T(8,128)(2,1)}), bf16[8,128,1440]{1,2,0:T(8,128)(2,1)S(1)}, u32[]{:S(2)}, u32[]{:S(2)}) %all-to-all-start.1) | async-done | bytes 2949152 | tf_op jit(solution)/shard_map/all_to_all | solution.py:132
  258.9 3.6 %copy.76 = f32[8,128,1440]{2,1,0:T(8,128)} copy(bf16[8,128,1440]{1,2,0:T(8,128)(2,1)S(1)} %all-to-all-done.1) | data formatting | bytes 8847360 | tf_op jit(solution)/shard_map/convert_element_type | solution.py:134
  262.4 12.1 %gather_fusion = f32[512,1440]{1,0:T(8,128)} fusion(f32[8,128,1440]{2,1,0:T(8,128)} %copy.76, s32[512]{0:T(512)S(1)} %bitcast.73), kind=kCustom, calls=%fused_computation.1 | custom fusion | bytes 5902336 | tf_op jit(solution)/shard_map/gather | solution.py:135
  274.5 4.8 %gather.10 = f32[128,4,1440]{2,1,0:T(4,128)} reshape(f32[512,1440]{1,0:T(8,128)} %gather_fusion) | data formatting | bytes 5898240 | tf_op jit(solution)/shard_map/gather | solution.py:135
  279.3 4.2 %multiply_reduce_fusion = bf16[128,1440]{1,0:T(8,128)(2,1)S(1)} fusion(f32[128,4,1440]{2,1,0:T(4,128)} %gather.10, f32[128,4]{1,0:T(8,128)S(1)} %copy.77), kind=kLoop, calls=%fused_computation.16 | loop fusion | flops 1290240 | bytes 3319808 | tf_op jit(solution)/shard_map/reduce_sum | solution.py:136
  283.5 0.9 copy.78
  (42 shorter events, 0.3 us)
Async XLA Ops:
  7.2 28.1 %copy-start = (bf16[1024,1440]{0,1:T(8,128)(2,1)S(1)}, bf16[1024,1440]{0,1:T(8,128)(2,1)}, u32[]{:S(2)}) copy-start(bf16[1024,1440]{0,1:T(8,128)(2,1)} %param.16) | copy-start | bytes 8847364
  7.2 39.0 %reduce-scatter.3.cloned.1.call-start = ((), (), s32[]{:S(2)}) async-start(), calls=%async_computation.4 | async-start | bytes 2211840 | tf_op jit(solution)/shard_map/reduce_scatter | solution.py:106
  8.1 12.4 %collective-permute-start.1 = (bf16[128,128]{1,0:T(8,128)(2,1)S(1)}, bf16[128,128]{1,0:T(8,128)(2,1)}, u32[]{:S(2)}, u32[]{:S(2)}) collective-permute-start(bf16[128,128]{1,0:T(8,128)(2,1)S(1)} %slice.13), channel_id=1, source_target_pairs={{0,2},{2,4},{4,6},{6,8},{8,10},{10,12},{12,14},{1,3},{3,5},{5,7},{... | collective-permute-start | bytes 98312 | tf_op jit(solution)/shard_map/ppermute | solution.py:14
  14.4 15.4 %collective-permute-start = (bf16[128,128]{1,0:T(8,128)(2,1)S(1)}, bf16[128,128]{1,0:T(8,128)(2,1)}, u32[]{:S(2)}, u32[]{:S(2)}) collective-permute-start(bf16[128,128]{1,0:T(8,128)(2,1)S(1)} %slice.12), channel_id=1, source_target_pairs={{0,2},{2,4},{4,6},{6,8},{8,10},{10,12},{12,14},{1,3},{3,5},{5,7},{... | collective-permute-start | bytes 98312 | tf_op jit(solution)/shard_map/ppermute | solution.py:14
  23.7 4.7 %copy-start.3 = (pred[256,384]{0,1:T(8,128)(4,1)S(1)}, pred[256,384]{0,1:T(8,128)(4,1)}, u32[]{:S(2)}) copy-start(pred[256,384]{0,1:T(8,128)(4,1)} %fusion.27) | copy-start | bytes 294916
  23.7 6.1 %copy-start.6 = (bf16[256,128]{1,0:T(8,128)(2,1)S(1)}, bf16[256,128]{1,0:T(8,128)(2,1)}, u32[]{:S(2)}) copy-start(bf16[256,128]{1,0:T(8,128)(2,1)} %param.14) | copy-start | bytes 196612
  25.7 2.7 copy-start.2
  25.7 4.9 %copy-start.4 = (pred[256,384]{0,1:T(8,128)(4,1)S(1)}, pred[256,384]{0,1:T(8,128)(4,1)}, u32[]{:S(2)}) copy-start(pred[256,384]{0,1:T(8,128)(4,1)} %fusion.27) | copy-start | bytes 294916
  35.2 2.4 copy-start.9
  35.3 12.4 %copy-start.7 = (f32[1440]{0:T(1024)S(1)}, f32[1440]{0:T(1024)}, u32[]{:S(2)}) copy-start(f32[1440]{0:T(1024)} %param.18) | copy-start | bytes 17284
  37.4 112.4 %all-gather.2.cloned.1.call-start = ((), (), s32[]{:S(2)}) async-start(), calls=%async_computation.5 | async-start | bytes 8847360 | tf_op jit(solution)/shard_map/all_gather | solution.py:113
  47.6 10.7 %copy-start.5 = (bf16[128,1440]{0,1:T(8,128)(2,1)}, bf16[128,1440]{0,1:T(8,128)(2,1)S(1)}, u32[]{:S(2)}) copy-start(bf16[128,1440]{0,1:T(8,128)(2,1)S(1)} %get-tuple-element.9) | copy-start | bytes 1105924
  135.0 22.6 %copy-start.11 = (bf16[1,1440,720]{2,1,0:T(8,128)(2,1)S(1)}, bf16[1,1440,720]{2,1,0:T(8,128)(2,1)}, u32[]{:S(2)}) copy-start(bf16[1,1440,720]{2,1,0:T(8,128)(2,1)} %param.21) | copy-start | bytes 6220804
  135.0 51.1 %reduce-scatter.5.cloned.1.call-start = ((), (), s32[]{:S(2)}) async-start(), calls=%async_computation.6 | async-start | bytes 8847360 | tf_op jit(solution)/shard_map/reduce_scatter | solution.py:129
  149.7 7.8 %copy-start.10 = (bf16[16,128,1440]{1,2,0:T(8,128)(2,1)S(1)}, bf16[16,128,1440]{1,2,0:T(8,128)(2,1)}, u32[]{:S(2)}) copy-start(bf16[16,128,1440]{1,2,0:T(8,128)(2,1)} %all-gather.2.cloned.1.call-done) | copy-start | bytes 17694724
  157.6 6.5 %copy-start.12 = (bf16[1,720,1440]{2,1,0:T(8,128)(2,1)S(1)}, bf16[1,720,1440]{2,1,0:T(8,128)(2,1)}, u32[]{:S(2)}) copy-start(bf16[1,720,1440]{2,1,0:T(8,128)(2,1)} %param.23) | copy-start | bytes 6220804
  170.8 21.1 %copy-start.8 = (s32[256,4]{0,1:T(4,128)S(1)}, s32[256,4]{0,1:T(4,128)}, u32[]{:S(2)}) copy-start(s32[256,4]{0,1:T(4,128)} %param.20) | copy-start | bytes 12292
  186.1 72.8 %all-to-all-start.1 = ((bf16[8,128,1440]{1,2,0:T(8,128)(2,1)}), bf16[8,128,1440]{1,2,0:T(8,128)(2,1)S(1)}, u32[]{:S(2)}, u32[]{:S(2)}) async-start(bf16[8,128,1440]{1,2,0:T(8,128)(2,1)} %reduce-scatter.5.cloned.1.call-done), calls=%async_computation.3 | async-start | bytes 5898240 | tf_op jit(solution)/shard_map/all_to_all | solution.py:132
  262.4 22.0 %copy-start.1 = (bf16[1024,1440]{0,1:T(8,128)(2,1)S(1)}, bf16[1024,1440]{0,1:T(8,128)(2,1)}, u32[]{:S(2)}) copy-start(bf16[1024,1440]{0,1:T(8,128)(2,1)} %param.16) | copy-start | bytes 8847364
Sparse Core Ops, SparseCore 0:
  37.5 8.6 reduce-scatter.2
  135.1 14.5 all-gather.1
  171.0 15.0 reduce-scatter.4
where the time goes:
time: 292 us; the launch traced here: 291 us
  waiting for transfers between devices  103 us (35%)
  blocking collectives  73.2 us (25%)
  local copies, waits for them, and re-layouts  44 us (15%)
  matrix products  29.7 us (10%)
  starting transfers between devices  15.3 us (5%)
  between operations  14 us (5%)
  other arithmetic  11.7 us (4%)
    all_to_all x1, blocking collectives, local(): lax.all_to_all(outbox.reshape(expert_count, capacity, feature_dim), 'seq'...  73.2 us
    all_to_all x1, waiting for transfers between devices, local(): lax.all_to_all(whole.astype(jnp.bfloat16), 'seq', split_axis=0, concat_ax...  66.7 us
    gather x2, local copies, waits for them, and re-layouts, local(): picked = returned[pair_ids, within]  16.9 us
    reduce_scatter x1, waiting for transfers between devices, local(): lax.psum_scatter(partial_value.astype(jnp.bfloat16), 'exp', scatter_dimen...  15.2 us
    all_gather x1, waiting for transfers between devices, local(): lax.all_gather(lax.all_to_all(outbox.reshape(expert_count, capacity, feat...  14.5 us
    scatter x1, local copies, waits for them, and re-layouts, pack_rows(): outbox = outbox.at[pair_ids * capacity + within].set(sources)  10.2 us
    ppermute x2, starting transfers between devices, shifted(): lax.ppermute(value, axis, [(source, source + steps) for source in range(f...  8.89 us
    dot_general x1, matrix products, expert_apply(): up_val = jnp.dot(flat_rows, w_up[0], preferred_element_type=jnp.float32)  7.8 us
  transfers between devices with their start and end apart: 6, of which 4 were waited for; matrix products, arithmetic and copies ran while one was open for 4% of the time, Pallas kernels for 0%

commit v1 on v0

v1 whole, which is shorter than its diff:
```python
import functools

import jax
import jax.numpy as jnp
from jax import lax
from jax.experimental import pallas as pl
from jax.experimental.pallas import tpu as pltpu
from jax.sharding import PartitionSpec as P

HEAD_DIM = 64
WINDOW = 128
TOP = 4
BF16_ROWS = 16
F32 = jnp.float32
BF16 = jnp.bfloat16
VMEM = pl.BlockSpec(memory_space=pltpu.VMEM)
SMEM = pl.BlockSpec(memory_space=pltpu.SMEM)


def swiglu(gate_val, up_val):
    return (up_val + 1.0) * gate_val * jax.nn.sigmoid(1.702 * gate_val)


def heads_of(q_rows, past, present, sink_ref, earlier, first):
    kv_width = past.shape[1] // 2
    kv_heads = kv_width // HEAD_DIM
    group = q_rows.shape[1] // kv_width
    q_cols = (q_rows * HEAD_DIM ** (-0.5)).T
    both = jnp.concatenate([past, present], axis=0)
    outs = []
    for g in range(kv_heads):
        keys = both[:, g * HEAD_DIM : (g + 1) * HEAD_DIM]
        vals = both[:, kv_width + g * HEAD_DIM : kv_width + (g + 1) * HEAD_DIM].T
        for j in range(0, group, 2):
            pair = [g * group + j, g * group + j + 1]
            q_pair = jnp.concatenate([q_cols[h * HEAD_DIM : (h + 1) * HEAD_DIM] for h in pair], axis=1)
            scores = jnp.dot(keys, q_pair, preferred_element_type=F32)
            seen = jnp.where(earlier, jnp.where(first, -1e30, scores[:WINDOW]), scores[WINDOW:])
            sink = jnp.concatenate([jnp.full((1, WINDOW), sink_ref[h], F32) for h in pair], axis=1)
            ceiling = jnp.maximum(jnp.max(seen, axis=0, keepdims=True), sink)
            raised = jnp.exp(seen - ceiling)
            total = jnp.sum(raised, axis=0, keepdims=True) + jnp.exp(sink - ceiling)
            spread = jnp.concatenate([jnp.where(earlier, raised, 0.0), jnp.where(earlier, 0.0, raised)], axis=0)
            mixed = jnp.dot(vals, spread.astype(BF16), preferred_element_type=F32) / total
            mixed = mixed.astype(BF16)
            outs += [mixed[:, :WINDOW], mixed[:, WINDOW:]]
    return jnp.concatenate(outs, axis=0)


def front_kernel(
    code_rows, place, sink_a, sink_b, q_a, q_b, kv_a, kv_b, rim_a, rim_b, ow_a, ow_b,
    resid, gain, routes, codes, attended_ref, parcel_ref,
):
    core, first = place[0], place[1] == 1
    start = pl.multiple_of(core * WINDOW, WINDOW)
    rows = pl.ds(start, WINDOW)
    shape = (WINDOW, 2 * WINDOW)
    key_at = lax.broadcasted_iota(jnp.int32, shape, 0)
    query_at = lax.rem(lax.broadcasted_iota(jnp.int32, shape, 1), WINDOW)
    earlier = key_at > query_at
    lead = core == 0
    projected = None
    for q, kv, rim, sink, ow in ((q_a, kv_a, rim_a, sink_a, ow_a), (q_b, kv_b, rim_b, sink_b, ow_b)):
        past = jnp.where(lead, rim[...], kv[:WINDOW, :])
        heads = heads_of(q[rows, :], past, kv[rows, :], sink, earlier, first)
        term = jnp.dot(ow[...], heads, preferred_element_type=F32)
        projected = term if projected is None else projected + term
    attended = (resid[:, rows].astype(F32) + projected).astype(BF16)
    attended_ref[...] = attended
    widened = attended.astype(F32)
    spread = jnp.mean(widened * widened, axis=0, keepdims=True)
    gains = jnp.broadcast_to(gain[...], (WINDOW, gain.shape[1])).T
    parcel_ref[code_rows:, :] = (widened * lax.rsqrt(spread + 1e-05) * gains).astype(BF16)
    if code_rows:
        expert = lax.broadcasted_iota(jnp.int32, (code_rows, WINDOW), 0)
        table = jnp.zeros((code_rows, WINDOW), F32)
        for k in range(TOP):
            named = jnp.broadcast_to(routes[k : k + 1, rows], expert.shape) == expert
            table += jnp.where(named, jnp.broadcast_to(codes[k : k + 1, rows], expert.shape).astype(F32), 0.0)
        parcel_ref[:code_rows, :] = table.astype(BF16)


def front(code_rows, queries, key_rows, values, sink_logit, o_weight, residual, norm_gain, routes, gate_codes):
    seq, core = lax.axis_index("seq"), lax.axis_index("exp")
    count, cores = lax.axis_size("seq"), lax.axis_size("exp")
    place = jnp.stack([core, jnp.where((seq == 0) & (core == 0), 1, 0)]).astype(jnp.int32)
    kv = jnp.concatenate([key_rows, values], axis=1)
    rim = kv[kv.shape[0] - WINDOW :]

    def to_next(source_core):
        steps = [(s * cores + source_core, (s + 1) * cores) for s in range(count - 1)]
        return lax.ppermute(rim, ("seq", "exp"), steps)

    rim_a, rim_b = to_next(0), to_next(1)
    ow = o_weight.T
    kv_b, q_b, sink_b, ow_b = [swapped(value) for value in (kv, queries, sink_logit, ow)]
    features = residual.shape[1]
    block = residual.shape[0] // cores
    return pl.pallas_call(
        functools.partial(front_kernel, code_rows),
        out_shape=(
            jax.ShapeDtypeStruct((features, block), BF16),
            jax.ShapeDtypeStruct((code_rows + features, block), BF16),
        ),
        in_specs=[SMEM] * 3 + [VMEM] * 12,
        out_specs=(VMEM, VMEM),
        cost_estimate=pl.CostEstimate(flops=2 * 10**9, bytes_accessed=10**7, transcendentals=10**6),
        compiler_params=pltpu.CompilerParams(vmem_limit_bytes=40 * 2**20),
        name="front",
    )(
        place, sink_logit, sink_b, queries, q_b, kv, kv_b, rim_a, rim_b, ow, ow_b,
        residual.T, norm_gain[None, :], routes.T, gate_codes.T,
    )


def swapped(value):
    return lax.ppermute(value, "exp", [(0, 1), (1, 0)])


def expert_kernel(code_rows, count, place, *refs):
    parcels, weights, outs = refs[:count], refs[count : count + 6], refs[count + 6 :]
    rows = jnp.concatenate([ref[code_rows:, :] for ref in parcels], axis=1).T
    total = None
    for w_gate, w_up, w_down in (weights[:3], weights[3:]):
        gate_val = jnp.dot(rows, w_gate[...], preferred_element_type=F32)
        up_val = jnp.dot(rows, w_up[...], preferred_element_type=F32)
        hidden = swiglu(gate_val, up_val).astype(BF16)
        term = jnp.dot(hidden, w_down[...], preferred_element_type=F32)
        total = term if total is None else total + term
    total = total.T
    for i in range(count):
        codes = parcels[i][:code_rows, :].astype(F32)
        mine = lax.broadcasted_iota(jnp.int32, codes.shape, 0) == place[0]
        code = jnp.sum(jnp.where(mine, codes, 0.0), axis=0, keepdims=True)
        share = code / jnp.sum(codes, axis=0, keepdims=True)
        outs[i][...] = (total[:, i * WINDOW : (i + 1) * WINDOW] * share).astype(BF16)


def expert_terms(code_rows, expert, parcels, weights):
    count = len(parcels)
    features = parcels[0].shape[0] - code_rows
    flops = 2 * count * WINDOW * features * 3 * 2 * weights[0].shape[1]
    return pl.pallas_call(
        functools.partial(expert_kernel, code_rows, count),
        out_shape=[jax.ShapeDtypeStruct((features, WINDOW), BF16)] * count,
        in_specs=[SMEM] + [VMEM] * (count + 6),
        out_specs=[VMEM] * count,
        cost_estimate=pl.CostEstimate(flops=flops, bytes_accessed=14 * 10**6, transcendentals=10**5),
        compiler_params=pltpu.CompilerParams(vmem_limit_bytes=48 * 2**20),
        name="experts",
    )(expert, *parcels, *weights)


def ring_of(count):
    order = list(range(0, count, 2)) + list(range(count - 1, 0, -2))
    right = [(order[i], order[(i + 1) % count]) for i in range(count)]
    return right, [(target, source) for source, target in right]


def mixed_by_ring(parcel, code_rows, weights):
    count = lax.axis_size("seq")
    right, left = ring_of(count)
    far = count // 2
    expert = lax.axis_index("seq").astype(jnp.int32)[None]
    to_right = functools.partial(lax.ppermute, axis_name="seq", perm=right)
    to_left = functools.partial(lax.ppermute, axis_name="seq", perm=left)
    apply = functools.partial(expert_terms, code_rows, expert, weights=weights)
    features = parcel.shape[0] - code_rows
    half = features // 2
    cut = code_rows + half
    from_left, from_right = parcel, parcel
    terms = {}
    for k in range(1, far):
        from_left, from_right = to_right(from_left), to_left(from_right)
        terms[-k], terms[k] = apply([from_left, from_right])
        if k == 1:
            terms[0] = apply([parcel])[0]
    upper, lower = to_right(from_left[:cut]), to_left(from_right[cut:])
    farthest = apply([jnp.concatenate([upper, lower], axis=0)])[0]
    add = lambda a, b: (a.astype(F32) + b.astype(F32)).astype(BF16)
    going_right, going_left = to_right(farthest[:half]), to_left(farthest[half:])
    for k in range(far - 1, 0, -1):
        if k == far - 1:
            going_right = jnp.concatenate([add(terms[k][:half], going_right), terms[k][half:]], axis=0)
            going_left = jnp.concatenate([terms[-k][:half], add(terms[-k][half:], going_left)], axis=0)
        else:
            going_right, going_left = add(terms[k], going_right), add(terms[-k], going_left)
        going_right, going_left = to_right(going_right), to_left(going_left)
    return (terms[0].astype(F32) + going_right.astype(F32) + going_left.astype(F32)).astype(BF16)


def pack_rows(normed, expert_ids, gate_codes, expert_count, capacity):
    pair_ids = expert_ids.reshape(-1)
    matches = (pair_ids[:, None] == jnp.arange(expert_count, dtype=jnp.int32)[None, :]).astype(
        jnp.int32
    )
    within = jnp.sum((jnp.cumsum(matches, axis=0) - 1) * matches, axis=1)
    sources = normed[jnp.arange(pair_ids.shape[0], dtype=jnp.int32) // expert_ids.shape[1]]
    outbox = jnp.zeros((expert_count * capacity, normed.shape[1]), normed.dtype)
    outbox = outbox.at[pair_ids * capacity + within].set(sources)
    code_vals = gate_codes.astype(F32)
    shares = (code_vals / jnp.sum(code_vals, axis=1, keepdims=True)).reshape(-1)
    return (outbox, pair_ids, within, shares)


def mixed_by_packing(normed, routes, gate_codes, weights, expert_count, capacity):
    w_gate, w_up, w_down = weights
    owners, block = lax.axis_size("exp"), normed.shape[0]
    owner_pos = lax.axis_index("exp")
    own = lambda value: lax.dynamic_slice_in_dim(value, owner_pos * block, block, 0)
    outbox, pair_ids, within, shares = pack_rows(
        normed, own(routes), own(gate_codes), expert_count, capacity
    )
    outbox = outbox.reshape(expert_count, capacity, normed.shape[1])
    exchange = functools.partial(lax.all_to_all, axis_name="seq", split_axis=0, concat_axis=0, tiled=True)
    arrived = lax.all_gather(exchange(outbox), "exp", axis=0, tiled=True)
    flat_rows = arrived.reshape(-1, arrived.shape[-1])
    gate_val = jnp.dot(flat_rows, w_gate, preferred_element_type=F32)
    up_val = jnp.dot(flat_rows, w_up, preferred_element_type=F32)
    hidden = swiglu(gate_val, up_val).astype(BF16)
    partial_value = jnp.dot(hidden, w_down, preferred_element_type=F32).reshape(arrived.shape)
    whole = lax.psum_scatter(partial_value.astype(BF16), "exp", scatter_dimension=0, tiled=True)
    picked = exchange(whole)[pair_ids, within].astype(F32)
    mixture = jnp.sum((picked * shares[:, None]).reshape(-1, TOP, normed.shape[1]), axis=1)
    return mixture.astype(BF16)


def local(
    queries,
    key_rows,
    values,
    sink_logit,
    o_weight,
    residual,
    norm_gain,
    routes,
    gate_codes,
    w_gate,
    w_up,
    w_down,
):
    block_rows = residual.shape[0] // lax.axis_size("exp")
    expert_count = w_gate.shape[0] * lax.axis_size("seq")
    capacity = max(2, 2 * block_rows * TOP // expert_count)
    weights = (w_gate[0], w_up[0], w_down[0])
    attention = (queries, key_rows, values, sink_logit, o_weight, residual, norm_gain, routes, gate_codes)
    if capacity < block_rows:
        attended, normed = front(0, *attention)
        mixture = mixed_by_packing(normed.T, routes, gate_codes, weights, expert_count, capacity)
        return (attended.T, mixture)
    code_rows = -(-expert_count // BF16_ROWS) * BF16_ROWS
    attended, parcel = front(code_rows, *attention)
    weights = weights + tuple(swapped(weight) for weight in weights)
    return (attended.T, mixed_by_ring(parcel, code_rows, weights).T)


def solution(mesh):
    placed = (
        P(("groups", "seq"), "exp"),
        P(("groups", "seq"), "exp"),
        P(("groups", "seq"), "exp"),
        P("exp"),
        P("exp", None),
        P(("groups", "seq"), None),
        P(),
        P(("groups", "seq"), None),
        P(("groups", "seq"), None),
        P("seq", None, "exp"),
        P("seq", None, "exp"),
        P("seq", "exp", None),
    )
    return jax.shard_map(
        local,
        mesh=mesh,
        in_specs=placed,
        out_specs=(P(("groups", "seq", "exp"), None), P(("groups", "seq", "exp"), None)),
        check_vma=False,
    )
```

time: 292 us -> 135 us (0.46)
  blocking collectives: 73.2 us -> 0 us
  waiting for transfers between devices: 103 us -> 48 us
  Pallas kernels: 0 us -> 42.6 us
  local copies, waits for them, and re-layouts: 44 us -> 8.52 us
  matrix products: 29.7 us -> 0 us
  starting transfers between devices: 15.3 us -> 33.3 us
  between operations: 14 us -> 0.89 us
  other arithmetic: 11.7 us -> 1.53 us
    all_to_all x1 -> x0, blocking collectives: 73.2 us -> none  [local(): lax.all_to_all(outbox.reshape(expert_count, capacity, feature_dim), 'seq'...]
    all_to_all x1 -> x0, waiting for transfers between devices: 66.7 us -> none  [local(): lax.all_to_all(whole.astype(jnp.bfloat16), 'seq', split_axis=0, concat_ax...]
    ppermute x2 -> x25, waiting for transfers between devices: 0.01 us -> 48 us  [the longest x6 17.6 us: mixed_by_ring(): going_right, going_left = (to_right(going_right), to_left(going_left))]
    pallas_call x0 -> x6, Pallas kernels: none -> 42.6 us  [the longest x5 34.6 us: expert_terms(): pl.pallas_call(functools.partial(expert_kernel, code_rows, count), out_sh...]
    dot_general x6 -> x0, matrix products: 29.7 us -> none  [the longest x1 7.8 us: expert_apply(): up_val = jnp.dot(flat_rows, w_up[0], preferred_element_type=jnp.float32)]
    ppermute x2 -> x25, starting transfers between devices: 8.89 us -> 33.3 us  [the longest x6 9.43 us: mixed_by_ring(): from_left, from_right = (to_right(from_left), to_left(from_right))]
    reduce_scatter x2 -> x0, waiting for transfers between devices: 21.8 us -> none  [the longest x1 15.2 us: local(): lax.psum_scatter(partial_value.astype(jnp.bfloat16), 'exp', scatter_dimen...]
    gather x2 -> x0, local copies, waits for them, and re-layouts: 16.9 us -> none  [local(): picked = returned[pair_ids, within]]
  transfers between devices with their start and end apart: 6 -> 25, of which waited for: 4 -> 12; matrix products, arithmetic and copies ran while one was open for 4% -> 2% of each run, Pallas kernels for 0% -> 27%
where the time goes in v1:
time: 135 us
  waiting for transfers between devices  48 us (36%)
  Pallas kernels  42.6 us (32%)
  starting transfers between devices  33.3 us (25%)
  local copies, waits for them, and re-layouts  8.52 us (6%)
  other arithmetic  1.53 us (1%)
    pallas_call x5, Pallas kernels, expert_terms(): pl.pallas_call(functools.partial(expert_kernel, code_rows, count), out_sh...  34.6 us
    ppermute x6, waiting for transfers between devices, mixed_by_ring(): going_right, going_left = (to_right(going_right), to_left(going_left))  17.6 us
    ppermute x6, waiting for transfers between devices, mixed_by_ring(): from_left, from_right = (to_right(from_left), to_left(from_right))  15.7 us
    ppermute x6, starting transfers between devices, mixed_by_ring(): from_left, from_right = (to_right(from_left), to_left(from_right))  9.43 us
    pallas_call x1, Pallas kernels, front(): pl.pallas_call(functools.partial(front_kernel, code_rows), out_shape=(jax...  8 us
    ppermute x7, waiting for transfers between devices, swapped(): return lax.ppermute(value, 'exp', [(0, 1), (1, 0)])  7.98 us
    ppermute x6, starting transfers between devices, mixed_by_ring(): going_right, going_left = (to_right(going_right), to_left(going_left))  7.09 us
    ppermute x7, starting transfers between devices, swapped(): return lax.ppermute(value, 'exp', [(0, 1), (1, 0)])  6.92 us
  transfers between devices with their start and end apart: 25, of which 12 were waited for; matrix products, arithmetic and copies ran while one was open for 2% of the time, Pallas kernels for 27%

profile of v1, /device:TPU:0, one launch (start us, length us, event | category | flops | bytes accessed | tf_op | source)
XLA Modules:
  0.0 134.8 jit_solution(8226455322733929014)
XLA Ops:
  0.6 0.5 collective-permute-start.5
  1.2 0.4 collective-permute-start.7
  1.7 0.4 collective-permute-start
  2.2 0.9 constant_dynamic-update-slice_fusion.1
  3.0 0.9 constant_dynamic-update-slice_fusion.kv_a
  3.9 5.9 %collective-permute-done.sink_b = f32[16]{0:T(128)S(1)} collective-permute-done((f32[16]{0:T(128)}, f32[16]{0:T(128)S(1)}, u32[]{:S(2)}, u32[]{:S(2)}) %collective-permute-start) | collective-permute-done | bytes 96 | tf_op jit(solution)/shard_map/ppermute | solution.py:117
  9.8 4.8 %collective-permute-start.3 = (bf16[128,256]{1,0:T(8,128)(2,1)S(1)}, bf16[128,256]{1,0:T(8,128)(2,1)S(1)}, u32[]{:S(2)}, u32[]{:S(2)}) collective-permute-start(bf16[128,256]{1,0:T(8,128)(2,1)S(1)} %slice.36), channel_id=1, source_target_pairs={{0,2},{2,4},{4,6},{6,8},{8,10},{10,12},{12,14},{16,18},{18,20},{20... | collective-permute-start | bytes 196616 | tf_op jit(solution)/shard_map/ppermute | solution.py:92
  14.6 1.9 %collective-permute-done.3.rim_a = bf16[128,256]{1,0:T(8,128)(2,1)S(1)} collective-permute-done((bf16[128,256]{1,0:T(8,128)(2,1)S(1)}, bf16[128,256]{1,0:T(8,128)(2,1)S(1)}, u32[]{:S(2)}, u32[]{:S(2)}) %collective-permute-start.3) | collective-permute-done | bytes 65568 | tf_op jit(solution)/shard_map/ppermute | solution.py:92
  16.4 0.7 collective-permute-start.4
  17.1 5.0 %collective-permute-start.2 = (bf16[256,256]{1,0:T(8,128)(2,1)S(1)}, bf16[256,256]{1,0:T(8,128)(2,1)S(1)}, u32[]{:S(2)}, u32[]{:S(2)}) collective-permute-start(bf16[256,256]{1,0:T(8,128)(2,1)S(1)} %constant_dynamic-update-slice_fusion.kv_a), channel_id=1, source_target_pairs={{0,1},{1,0},{2,3},{3,2},{4,5},{5,4},{6,7},{7,6},{8,9},{9,8},{10,11... | collective-permute-start | bytes 393224 | tf_op jit(solution)/shard_map/ppermute | solution.py:117
  22.1 1.0 collective-permute-done.2.kv_b
  23.1 0.4 collective-permute-start.1
  23.5 0.7 broadcast_in_dim.6.gain
  24.3 1.1 collective-permute-done.1.q_b
  25.4 1.8 %copy-done.2 = bf16[1024,1440]{0,1:T(8,128)(2,1)S(1)} copy-done((bf16[1024,1440]{0,1:T(8,128)(2,1)S(1)}, bf16[1024,1440]{0,1:T(8,128)(2,1)}, u32[]{:S(2)}) %copy-start.2) | copy-done | bytes 2949144
  27.2 1.1 copy-done.3
  28.3 1.0 copy-done.4
  29.4 0.7 copy-done.5
  30.1 0.7 copy-done.6
  30.8 0.7 copy-done.7
  31.4 8.0 %front.1 = (bf16[1440,128]{1,0:T(8,128)(2,1)}, bf16[1456,128]{1,0:T(8,128)(2,1)S(1)}) custom-call(s32[2]{0:T(128)S(1)} %pad_add_fusion.place, f32[16]{0:T(128)S(1)} %copy-done.7, f32[16]{0:T(128)S(1)} %collective-permute-done.sink_b, bf16[256,1024]{1,0:T(8,128)(2,1)S(1)} %copy-done.4, bf16[256,1024]{1,0:T(8,128)(2,1)} %collective-permute-done.1.q_b, ...), custom_call_target="tpu_custom_call" | custom-call | flops 2000000000 | bytes 10000000 | tf_op jit(solution)/shard_map/front/pallas_call | solution.py:99
  39.4 4.5 %collective-permute-start.9 = (bf16[1456,128]{1,0:T(8,128)(2,1)S(1)}, bf16[1456,128]{1,0:T(8,128)(2,1)S(1)}, u32[]{:S(2)}, u32[]{:S(2)}) collective-permute-start(bf16[1456,128]{1,0:T(8,128)(2,1)S(1)} %get-tuple-element.11.refs_0_), channel_id=1, source_target_pairs={{0,4},{4,8},{8,12},{12,14},{14,10},{10,6},{6,2},{2,0},{1,5},{5,9},... | collective-permute-start | bytes 1118216 | tf_op jit(solution)/shard_map/ppermute | solution.py:174
  43.9 8.2 %collective-permute-done.9.refs_0_ = bf16[1456,128]{1,0:T(8,128)(2,1)S(1)} collective-permute-done((bf16[1456,128]{1,0:T(8,128)(2,1)S(1)}, bf16[1456,128]{1,0:T(8,128)(2,1)S(1)}, u32[]{:S(2)}, u32[]{:S(2)}) %collective-permute-start.9) | collective-permute-done | bytes 372768 | tf_op jit(solution)/shard_map/ppermute | solution.py:174
  52.1 2.5 %collective-permute-start.11 = (bf16[1456,128]{1,0:T(8,128)(2,1)S(1)}, bf16[1456,128]{1,0:T(8,128)(2,1)S(1)}, u32[]{:S(2)}, u32[]{:S(2)}) collective-permute-start(bf16[1456,128]{1,0:T(8,128)(2,1)S(1)} %collective-permute-done.9.refs_0_), channel_id=1, source_target_pairs={{0,4},{4,8},{8,12},{12,14},{14,10},{10,6},{6,2},{2,0},{1,5},{5,9},... | collective-permute-start | bytes 1118216 | tf_op jit(solution)/shard_map/ppermute | solution.py:174
  54.6 7.4 %collective-permute-done.11.refs_0_ = bf16[1456,128]{1,0:T(8,128)(2,1)S(1)} collective-permute-done((bf16[1456,128]{1,0:T(8,128)(2,1)S(1)}, bf16[1456,128]{1,0:T(8,128)(2,1)S(1)}, u32[]{:S(2)}, u32[]{:S(2)}) %collective-permute-start.11) | collective-permute-done | bytes 372768 | tf_op jit(solution)/shard_map/ppermute | solution.py:174
  62.0 2.5 %collective-permute-start.13 = (bf16[1456,128]{1,0:T(8,128)(2,1)S(1)}, bf16[1456,128]{1,0:T(8,128)(2,1)S(1)}, u32[]{:S(2)}, u32[]{:S(2)}) collective-permute-start(bf16[1456,128]{1,0:T(8,128)(2,1)S(1)} %collective-permute-done.11.refs_0_), channel_id=1, source_target_pairs={{0,4},{4,8},{8,12},{12,14},{14,10},{10,6},{6,2},{2,0},{1,5},{5,9},... | collective-permute-start | bytes 1118216 | tf_op jit(solution)/shard_map/ppermute | solution.py:174
  64.5 7.6 %experts.6 = (bf16[1440,128]{1,0:T(8,128)(2,1)S(1)}, bf16[1440,128]{1,0:T(8,128)(2,1)S(1)}) custom-call(s32[1]{0:T(128)} %bitcast.7.place, bf16[1456,128]{1,0:T(8,128)(2,1)S(1)} %collective-permute-done.9.refs_0_, bf16[1456,128]{1,0:T(8,128)(2,1)S(1)} %collective-permute-done.10.refs_1_, bf16[1440,720]{1,0:T(8,128)(2,1)S(1)} %bitcast.14, ...), custom_call_target="tpu_custom_call" | custom-call | flops 3185049600 | bytes 14000000 | tf_op jit(solution)/shard_map/experts/pallas_call | solution.py:143
  72.2 2.1 %collective-permute-start.15 = (bf16[736,128]{1,0:T(8,128)(2,1)S(1)}, bf16[736,128]{1,0:T(8,128)(2,1)S(1)}, u32[]{:S(2)}, u32[]{:S(2)}) collective-permute-start(bf16[736,128]{1,0:T(8,128)(2,1)S(1)} %slice.37), channel_id=1, source_target_pairs={{0,4},{4,8},{8,12},{12,14},{14,10},{10,6},{6,2},{2,0},{1,5},{5,9},... | collective-permute-start | bytes 565256 | tf_op jit(solution)/shard_map/ppermute | solution.py:178
  74.3 0.2 collective-permute-start.16
  74.5 7.6 %experts.7 = (bf16[1440,128]{1,0:T(8,128)(2,1)S(1)}, bf16[1440,128]{1,0:T(8,128)(2,1)S(1)}) custom-call(s32[1]{0:T(128)} %bitcast.7.place, bf16[1456,128]{1,0:T(8,128)(2,1)S(1)} %collective-permute-done.11.refs_0_, bf16[1456,128]{1,0:T(8,128)(2,1)S(1)} %collective-permute-done.12.refs_1_, bf16[1440,720]{1,0:T(8,128)(2,1)S(1)} %bitcast.15, ...), custom_call_target="tpu_custom_call" | custom-call | flops 3185049600 | bytes 14000000 | tf_op jit(solution)/shard_map/experts/pallas_call | solution.py:143
  82.2 5.9 %experts.9 = bf16[1440,128]{1,0:T(8,128)(2,1)S(1)} custom-call(s32[1]{0:T(128)} %bitcast.7.place, bf16[1456,128]{1,0:T(8,128)(2,1)S(1)} %pad_maximum_fusion.refs_0_, bf16[1440,720]{1,0:T(8,128)(2,1)S(1)} %bitcast.16, bf16[1440,720]{1,0:T(8,128)(2,1)S(1)} %bitcast.22, bf16[720,1440]{1,0:T(8,128)(2,1)} %bitcast.33, ...), custom_call_target="tpu_custom_call" | custom-call | flops 1592524800 | bytes 14000000 | tf_op jit(solution)/shard_map/experts/pallas_call | solution.py:143
  88.1 2.1 %collective-permute-start.17 = (bf16[720,128]{1,0:T(8,128)(2,1)S(1)}, bf16[720,128]{1,0:T(8,128)(2,1)S(1)}, u32[]{:S(2)}, u32[]{:S(2)}) collective-permute-start(bf16[720,128]{1,0:T(8,128)(2,1)S(1)} %get-tuple-element.18), channel_id=1, source_target_pairs={{0,4},{4,8},{8,12},{12,14},{14,10},{10,6},{6,2},{2,0},{1,5},{5,9},... | collective-permute-start | bytes 552968 | tf_op jit(solution)/shard_map/ppermute | solution.py:181
  90.2 7.6 %experts.8 = (bf16[1440,128]{1,0:T(8,128)(2,1)S(1)}, bf16[1440,128]{1,0:T(8,128)(2,1)S(1)}) custom-call(s32[1]{0:T(128)} %bitcast.7.place, bf16[1456,128]{1,0:T(8,128)(2,1)S(1)} %collective-permute-done.13.refs_0_, bf16[1456,128]{1,0:T(8,128)(2,1)S(1)} %collective-permute-done.14.refs_1_, bf16[1440,720]{1,0:T(8,128)(2,1)S(1)} %bitcast.17, ...), custom_call_target="tpu_custom_call" | custom-call | flops 3185049600 | bytes 14000000 | tf_op jit(solution)/shard_map/experts/pallas_call | solution.py:143
  98.0 2.0 %collective-permute-start.18 = (bf16[1440,128]{1,0:T(8,128)(2,1)S(1)}, bf16[1440,128]{1,0:T(8,128)(2,1)S(1)}, u32[]{:S(2)}, u32[]{:S(2)}) collective-permute-start(bf16[1440,128]{1,0:T(8,128)(2,1)S(1)} %pad_maximum_fusion.1), channel_id=1, source_target_pairs={{0,4},{4,8},{8,12},{12,14},{14,10},{10,6},{6,2},{2,0},{1,5},{5,9},... | collective-permute-start | bytes 1105928 | tf_op jit(solution)/shard_map/ppermute | solution.py:188
  100.0 4.8 %collective-permute-done.21 = bf16[720,128]{1,0:T(8,128)(2,1)S(1)} collective-permute-done((bf16[720,128]{1,0:T(8,128)(2,1)S(1)}, bf16[720,128]{1,0:T(8,128)(2,1)S(1)}, u32[]{:S(2)}, u32[]{:S(2)}) %collective-permute-start.21) | collective-permute-done | bytes 184352 | tf_op jit(solution)/shard_map/ppermute | solution.py:181
  105.0 1.6 %collective-permute-done.18 = bf16[1440,128]{1,0:T(8,128)(2,1)S(1)} collective-permute-done((bf16[1440,128]{1,0:T(8,128)(2,1)S(1)}, bf16[1440,128]{1,0:T(8,128)(2,1)S(1)}, u32[]{:S(2)}, u32[]{:S(2)}) %collective-permute-start.18) | collective-permute-done | bytes 368672 | tf_op jit(solution)/shard_map/ppermute | solution.py:188
  106.6 0.1 add_convert_fusion.4
  106.7 2.3 %collective-permute-start.19 = (bf16[1440,128]{1,0:T(8,128)(2,1)S(1)}, bf16[1440,128]{1,0:T(8,128)(2,1)S(1)}, u32[]{:S(2)}, u32[]{:S(2)}) collective-permute-start(bf16[1440,128]{1,0:T(8,128)(2,1)S(1)} %add_convert_fusion.4), channel_id=1, source_target_pairs={{0,4},{4,8},{8,12},{12,14},{14,10},{10,6},{6,2},{2,0},{1,5},{5,9},... | collective-permute-start | bytes 1105928 | tf_op jit(solution)/shard_map/ppermute | solution.py:188
  109.0 6.0 %collective-permute-done.22 = bf16[1440,128]{1,0:T(8,128)(2,1)S(1)} collective-permute-done((bf16[1440,128]{1,0:T(8,128)(2,1)S(1)}, bf16[1440,128]{1,0:T(8,128)(2,1)S(1)}, u32[]{:S(2)}, u32[]{:S(2)}) %collective-permute-start.22) | collective-permute-done | bytes 368672 | tf_op jit(solution)/shard_map/ppermute | solution.py:188
  115.0 0.1 add_convert_fusion.2
  115.2 1.0 collective-permute-done.19
  116.2 0.1 add_convert_fusion.3
  116.3 2.5 %collective-permute-start.20 = (bf16[1440,128]{1,0:T(8,128)(2,1)S(1)}, bf16[1440,128]{1,0:T(8,128)(2,1)S(1)}, u32[]{:S(2)}, u32[]{:S(2)}) collective-permute-start(bf16[1440,128]{1,0:T(8,128)(2,1)S(1)} %add_convert_fusion.3), channel_id=1, source_target_pairs={{0,4},{4,8},{8,12},{12,14},{14,10},{10,6},{6,2},{2,0},{1,5},{5,9},... | collective-permute-start | bytes 1105928 | tf_op jit(solution)/shard_map/ppermute | solution.py:188
  118.8 7.5 %collective-permute-done.23 = bf16[1440,128]{1,0:T(8,128)(2,1)S(1)} collective-permute-done((bf16[1440,128]{1,0:T(8,128)(2,1)S(1)}, bf16[1440,128]{1,0:T(8,128)(2,1)S(1)}, u32[]{:S(2)}, u32[]{:S(2)}) %collective-permute-start.23) | collective-permute-done | bytes 368672 | tf_op jit(solution)/shard_map/ppermute | solution.py:188
  126.3 0.1 add_convert_fusion.1
  126.4 5.9 %experts.5 = bf16[1440,128]{1,0:T(8,128)(2,1)S(1)} custom-call(s32[1]{0:T(128)} %bitcast.7.place, bf16[1456,128]{1,0:T(8,128)(2,1)S(1)} %get-tuple-element.11.refs_0_, bf16[1440,720]{1,0:T(8,128)(2,1)S(1)} %bitcast.18, bf16[1440,720]{1,0:T(8,128)(2,1)S(1)} %bitcast.24, bf16[720,1440]{1,0:T(8,128)(2,1)} %bitcast.35, ...), custom_call_target="tpu_custom_call" | custom-call | flops 1592524800 | bytes 14000000 | tf_op jit(solution)/shard_map/experts/pallas_call | solution.py:143
  132.3 1.6 %collective-permute-done.24 = bf16[1440,128]{1,0:T(8,128)(2,1)S(1)} collective-permute-done((bf16[1440,128]{1,0:T(8,128)(2,1)S(1)}, bf16[1440,128]{1,0:T(8,128)(2,1)S(1)}, u32[]{:S(2)}, u32[]{:S(2)}) %collective-permute-start.24) | collective-permute-done | bytes 368672 | tf_op jit(solution)/shard_map/ppermute | solution.py:188
  133.9 0.9 fusion
  (44 shorter events, 0.8 us)
Async XLA Ops:
  0.6 24.8 %collective-permute-start.5 = (bf16[1440,1024]{1,0:T(8,128)(2,1)}, bf16[1440,1024]{1,0:T(8,128)(2,1)S(1)}, u32[]{:S(2)}, u32[]{:S(2)}) collective-permute-start(bf16[1440,1024]{1,0:T(8,128)(2,1)} %bitcast.25), channel_id=1, source_target_pairs={{0,1},{1,0},{2,3},{3,2},{4,5},{5,4},{6,7},{7,6},{8,9},{9,8},{10,11... | collective-permute-start | bytes 8847368 | tf_op jit(solution)/shard_map/ppermute | solution.py:117
  1.1 63.4 %collective-permute-start.6 = (bf16[1440,720]{1,0:T(8,128)(2,1)}, bf16[1440,720]{1,0:T(8,128)(2,1)}, u32[]{:S(2)}, u32[]{:S(2)}) collective-permute-start(bf16[1440,720]{1,0:T(8,128)(2,1)} %bitcast.13), channel_id=1, source_target_pairs={{0,1},{1,0},{2,3},{3,2},{4,5},{5,4},{6,7},{7,6},{8,9},{9,8},{10,11... | collective-permute-start | bytes 6220808 | tf_op jit(solution)/shard_map/ppermute | solution.py:117
  1.2 63.3 %collective-permute-start.7 = (bf16[1440,720]{1,0:T(8,128)(2,1)}, bf16[1440,720]{1,0:T(8,128)(2,1)}, u32[]{:S(2)}, u32[]{:S(2)}) collective-permute-start(bf16[1440,720]{1,0:T(8,128)(2,1)} %bitcast.19), channel_id=1, source_target_pairs={{0,1},{1,0},{2,3},{3,2},{4,5},{5,4},{6,7},{7,6},{8,9},{9,8},{10,11... | collective-permute-start | bytes 6220808 | tf_op jit(solution)/shard_map/ppermute | solution.py:117
  1.7 62.9 %collective-permute-start.8 = (bf16[720,1440]{1,0:T(8,128)(2,1)}, bf16[720,1440]{1,0:T(8,128)(2,1)}, u32[]{:S(2)}, u32[]{:S(2)}) collective-permute-start(bf16[720,1440]{1,0:T(8,128)(2,1)} %bitcast.30), channel_id=1, source_target_pairs={{0,1},{1,0},{2,3},{3,2},{4,5},{5,4},{6,7},{7,6},{8,9},{9,8},{10,11... | collective-permute-start | bytes 6220808 | tf_op jit(solution)/shard_map/ppermute | solution.py:117
  1.7 8.0 %collective-permute-start = (f32[16]{0:T(128)}, f32[16]{0:T(128)S(1)}, u32[]{:S(2)}, u32[]{:S(2)}) collective-permute-start(f32[16]{0:T(128)} %sink_a.1), channel_id=1, source_target_pairs={{0,1},{1,0},{2,3},{3,2},{4,5},{5,4},{6,7},{7,6},{8,9},{9,8},{10,11... | collective-permute-start | bytes 200 | tf_op jit(solution)/shard_map/ppermute | solution.py:117
  9.8 6.7 %collective-permute-start.3 = (bf16[128,256]{1,0:T(8,128)(2,1)S(1)}, bf16[128,256]{1,0:T(8,128)(2,1)S(1)}, u32[]{:S(2)}, u32[]{:S(2)}) collective-permute-start(bf16[128,256]{1,0:T(8,128)(2,1)S(1)} %slice.36), channel_id=1, source_target_pairs={{0,2},{2,4},{4,6},{6,8},{8,10},{10,12},{12,14},{16,18},{18,20},{20... | collective-permute-start | bytes 196616 | tf_op jit(solution)/shard_map/ppermute | solution.py:92
  16.4 0.7 collective-permute-start.4
  17.1 6.0 %collective-permute-start.2 = (bf16[256,256]{1,0:T(8,128)(2,1)S(1)}, bf16[256,256]{1,0:T(8,128)(2,1)S(1)}, u32[]{:S(2)}, u32[]{:S(2)}) collective-permute-start(bf16[256,256]{1,0:T(8,128)(2,1)S(1)} %constant_dynamic-update-slice_fusion.kv_a), channel_id=1, source_target_pairs={{0,1},{1,0},{2,3},{3,2},{4,5},{5,4},{6,7},{7,6},{8,9},{9,8},{10,11... | collective-permute-start | bytes 393224 | tf_op jit(solution)/shard_map/ppermute | solution.py:117
  23.1 2.3 %collective-permute-start.1 = (bf16[256,1024]{1,0:T(8,128)(2,1)}, bf16[256,1024]{1,0:T(8,128)(2,1)}, u32[]{:S(2)}, u32[]{:S(2)}) collective-permute-start(bf16[256,1024]{1,0:T(8,128)(2,1)} %q_a.1), channel_id=1, source_target_pairs={{0,1},{1,0},{2,3},{3,2},{4,5},{5,4},{6,7},{7,6},{8,9},{9,8},{10,11... | collective-permute-start | bytes 1572872 | tf_op jit(solution)/shard_map/ppermute | solution.py:117
  25.4 1.8 %copy-start.2 = (bf16[1024,1440]{0,1:T(8,128)(2,1)S(1)}, bf16[1024,1440]{0,1:T(8,128)(2,1)}, u32[]{:S(2)}) copy-start(bf16[1024,1440]{0,1:T(8,128)(2,1)} %param.16) | copy-start | bytes 8847364
  27.2 1.1 copy-start.3
  28.3 1.0 copy-start.4
  29.4 0.7 copy-start.5
  30.1 0.7 copy-start.6
  30.7 0.7 copy-start.7
  31.4 33.1 %copy-start = (bf16[1,1440,720]{2,1,0:T(8,128)(2,1)S(1)}, bf16[1,1440,720]{2,1,0:T(8,128)(2,1)}, u32[]{:S(2)}) copy-start(bf16[1,1440,720]{2,1,0:T(8,128)(2,1)} %param.21) | copy-start | bytes 6220804
  31.4 33.1 %copy-start.1 = (bf16[1,1440,720]{2,1,0:T(8,128)(2,1)S(1)}, bf16[1,1440,720]{2,1,0:T(8,128)(2,1)}, u32[]{:S(2)}) copy-start(bf16[1,1440,720]{2,1,0:T(8,128)(2,1)} %param.22) | copy-start | bytes 6220804
  39.4 12.7 %collective-permute-start.9 = (bf16[1456,128]{1,0:T(8,128)(2,1)S(1)}, bf16[1456,128]{1,0:T(8,128)(2,1)S(1)}, u32[]{:S(2)}, u32[]{:S(2)}) collective-permute-start(bf16[1456,128]{1,0:T(8,128)(2,1)S(1)} %get-tuple-element.11.refs_0_), channel_id=1, source_target_pairs={{0,4},{4,8},{8,12},{12,14},{14,10},{10,6},{6,2},{2,0},{1,5},{5,9},... | collective-permute-start | bytes 1118216 | tf_op jit(solution)/shard_map/ppermute | solution.py:174
  43.9 10.7 %collective-permute-start.10 = (bf16[1456,128]{1,0:T(8,128)(2,1)S(1)}, bf16[1456,128]{1,0:T(8,128)(2,1)S(1)}, u32[]{:S(2)}, u32[]{:S(2)}) collective-permute-start(bf16[1456,128]{1,0:T(8,128)(2,1)S(1)} %get-tuple-element.11.refs_0_), channel_id=1, source_target_pairs={{4,0},{8,4},{12,8},{14,12},{10,14},{6,10},{2,6},{0,2},{5,1},{9,5},... | collective-permute-start | bytes 1118216 | tf_op jit(solution)/shard_map/ppermute | solution.py:174
  52.1 9.9 %collective-permute-start.11 = (bf16[1456,128]{1,0:T(8,128)(2,1)S(1)}, bf16[1456,128]{1,0:T(8,128)(2,1)S(1)}, u32[]{:S(2)}, u32[]{:S(2)}) collective-permute-start(bf16[1456,128]{1,0:T(8,128)(2,1)S(1)} %collective-permute-done.9.refs_0_), channel_id=1, source_target_pairs={{0,4},{4,8},{8,12},{12,14},{14,10},{10,6},{6,2},{2,0},{1,5},{5,9},... | collective-permute-start | bytes 1118216 | tf_op jit(solution)/shard_map/ppermute | solution.py:174
  54.6 9.9 %collective-permute-start.12 = (bf16[1456,128]{1,0:T(8,128)(2,1)S(1)}, bf16[1456,128]{1,0:T(8,128)(2,1)S(1)}, u32[]{:S(2)}, u32[]{:S(2)}) collective-permute-start(bf16[1456,128]{1,0:T(8,128)(2,1)S(1)} %collective-permute-done.10.refs_1_), channel_id=1, source_target_pairs={{4,0},{8,4},{12,8},{14,12},{10,14},{6,10},{2,6},{0,2},{5,1},{9,5},... | collective-permute-start | bytes 1118216 | tf_op jit(solution)/shard_map/ppermute | solution.py:174
  62.0 10.2 %collective-permute-start.13 = (bf16[1456,128]{1,0:T(8,128)(2,1)S(1)}, bf16[1456,128]{1,0:T(8,128)(2,1)S(1)}, u32[]{:S(2)}, u32[]{:S(2)}) collective-permute-start(bf16[1456,128]{1,0:T(8,128)(2,1)S(1)} %collective-permute-done.11.refs_0_), channel_id=1, source_target_pairs={{0,4},{4,8},{8,12},{12,14},{14,10},{10,6},{6,2},{2,0},{1,5},{5,9},... | collective-permute-start | bytes 1118216 | tf_op jit(solution)/shard_map/ppermute | solution.py:174
  64.5 9.8 %collective-permute-start.14 = (bf16[1456,128]{1,0:T(8,128)(2,1)S(1)}, bf16[1456,128]{1,0:T(8,128)(2,1)S(1)}, u32[]{:S(2)}, u32[]{:S(2)}) collective-permute-start(bf16[1456,128]{1,0:T(8,128)(2,1)S(1)} %collective-permute-done.12.refs_1_), channel_id=1, source_target_pairs={{4,0},{8,4},{12,8},{14,12},{10,14},{6,10},{2,6},{0,2},{5,1},{9,5},... | collective-permute-start | bytes 1118216 | tf_op jit(solution)/shard_map/ppermute | solution.py:174
  72.2 10.0 %collective-permute-start.15 = (bf16[736,128]{1,0:T(8,128)(2,1)S(1)}, bf16[736,128]{1,0:T(8,128)(2,1)S(1)}, u32[]{:S(2)}, u32[]{:S(2)}) collective-permute-start(bf16[736,128]{1,0:T(8,128)(2,1)S(1)} %slice.37), channel_id=1, source_target_pairs={{0,4},{4,8},{8,12},{12,14},{14,10},{10,6},{6,2},{2,0},{1,5},{5,9},... | collective-permute-start | bytes 565256 | tf_op jit(solution)/shard_map/ppermute | solution.py:178
  74.3 7.9 %collective-permute-start.16 = (bf16[720,128]{1,0:T(8,128)(2,1)S(1)}, bf16[720,128]{1,0:T(8,128)(2,1)S(1)}, u32[]{:S(2)}, u32[]{:S(2)}) collective-permute-start(bf16[720,128]{1,0:T(8,128)(2,1)S(1)} %slice.38), channel_id=1, source_target_pairs={{4,0},{8,4},{12,8},{14,12},{10,14},{6,10},{2,6},{0,2},{5,1},{9,5},... | collective-permute-start | bytes 552968 | tf_op jit(solution)/shard_map/ppermute | solution.py:178
  88.1 9.8 %collective-permute-start.17 = (bf16[720,128]{1,0:T(8,128)(2,1)S(1)}, bf16[720,128]{1,0:T(8,128)(2,1)S(1)}, u32[]{:S(2)}, u32[]{:S(2)}) collective-permute-start(bf16[720,128]{1,0:T(8,128)(2,1)S(1)} %get-tuple-element.18), channel_id=1, source_target_pairs={{0,4},{4,8},{8,12},{12,14},{14,10},{10,6},{6,2},{2,0},{1,5},{5,9},... | collective-permute-start | bytes 552968 | tf_op jit(solution)/shard_map/ppermute | solution.py:181
  97.8 7.1 %collective-permute-start.21 = (bf16[720,128]{1,0:T(8,128)(2,1)S(1)}, bf16[720,128]{1,0:T(8,128)(2,1)S(1)}, u32[]{:S(2)}, u32[]{:S(2)}) collective-permute-start(bf16[720,128]{1,0:T(8,128)(2,1)S(1)} %get-tuple-element.19), channel_id=1, source_target_pairs={{4,0},{8,4},{12,8},{14,12},{10,14},{6,10},{2,6},{0,2},{5,1},{9,5},... | collective-permute-start | bytes 552968 | tf_op jit(solution)/shard_map/ppermute | solution.py:181
  98.0 8.6 %collective-permute-start.18 = (bf16[1440,128]{1,0:T(8,128)(2,1)S(1)}, bf16[1440,128]{1,0:T(8,128)(2,1)S(1)}, u32[]{:S(2)}, u32[]{:S(2)}) collective-permute-start(bf16[1440,128]{1,0:T(8,128)(2,1)S(1)} %pad_maximum_fusion.1), channel_id=1, source_target_pairs={{0,4},{4,8},{8,12},{12,14},{14,10},{10,6},{6,2},{2,0},{1,5},{5,9},... | collective-permute-start | bytes 1105928 | tf_op jit(solution)/shard_map/ppermute | solution.py:188
  105.0 10.1 %collective-permute-start.22 = (bf16[1440,128]{1,0:T(8,128)(2,1)S(1)}, bf16[1440,128]{1,0:T(8,128)(2,1)S(1)}, u32[]{:S(2)}, u32[]{:S(2)}) collective-permute-start(bf16[1440,128]{1,0:T(8,128)(2,1)S(1)} %pad_maximum_fusion.2), channel_id=1, source_target_pairs={{4,0},{8,4},{12,8},{14,12},{10,14},{6,10},{2,6},{0,2},{5,1},{9,5},... | collective-permute-start | bytes 1105928 | tf_op jit(solution)/shard_map/ppermute | solution.py:188
  106.7 9.5 %collective-permute-start.19 = (bf16[1440,128]{1,0:T(8,128)(2,1)S(1)}, bf16[1440,128]{1,0:T(8,128)(2,1)S(1)}, u32[]{:S(2)}, u32[]{:S(2)}) collective-permute-start(bf16[1440,128]{1,0:T(8,128)(2,1)S(1)} %add_convert_fusion.4), channel_id=1, source_target_pairs={{0,4},{4,8},{8,12},{12,14},{14,10},{10,6},{6,2},{2,0},{1,5},{5,9},... | collective-permute-start | bytes 1105928 | tf_op jit(solution)/shard_map/ppermute | solution.py:188
  115.1 11.1 %collective-permute-start.23 = (bf16[1440,128]{1,0:T(8,128)(2,1)S(1)}, bf16[1440,128]{1,0:T(8,128)(2,1)S(1)}, u32[]{:S(2)}, u32[]{:S(2)}) collective-permute-start(bf16[1440,128]{1,0:T(8,128)(2,1)S(1)} %add_convert_fusion.2), channel_id=1, source_target_pairs={{4,0},{8,4},{12,8},{14,12},{10,14},{6,10},{2,6},{0,2},{5,1},{9,5},... | collective-permute-start | bytes 1105928 | tf_op jit(solution)/shard_map/ppermute | solution.py:188
  116.3 16.0 %collective-permute-start.20 = (bf16[1440,128]{1,0:T(8,128)(2,1)S(1)}, bf16[1440,128]{1,0:T(8,128)(2,1)S(1)}, u32[]{:S(2)}, u32[]{:S(2)}) collective-permute-start(bf16[1440,128]{1,0:T(8,128)(2,1)S(1)} %add_convert_fusion.3), channel_id=1, source_target_pairs={{0,4},{4,8},{8,12},{12,14},{14,10},{10,6},{6,2},{2,0},{1,5},{5,9},... | collective-permute-start | bytes 1105928 | tf_op jit(solution)/shard_map/ppermute | solution.py:188
  126.4 7.6 %collective-permute-start.24 = (bf16[1440,128]{1,0:T(8,128)(2,1)S(1)}, bf16[1440,128]{1,0:T(8,128)(2,1)S(1)}, u32[]{:S(2)}, u32[]{:S(2)}) collective-permute-start(bf16[1440,128]{1,0:T(8,128)(2,1)S(1)} %add_convert_fusion.1), channel_id=1, source_target_pairs={{4,0},{8,4},{12,8},{14,12},{10,14},{6,10},{2,6},{0,2},{5,1},{9,5},... | collective-permute-start | bytes 1105928 | tf_op jit(solution)/shard_map/ppermute | solution.py:188

commit v2 on v1

v2 whole, which is shorter than its diff:
```python
import functools

import jax
import jax.numpy as jnp
from jax import lax
from jax.experimental import pallas as pl
from jax.experimental.pallas import tpu as pltpu
from jax.sharding import PartitionSpec as P

HEAD_DIM = 64
WINDOW = 128
TOP = 4
BF16_ROWS = 16
F32 = jnp.float32
BF16 = jnp.bfloat16
VMEM = pl.BlockSpec(memory_space=pltpu.VMEM)
SMEM = pl.BlockSpec(memory_space=pltpu.SMEM)
ANY = pl.BlockSpec(memory_space=pl.ANY)
in_hbm = functools.partial(pltpu.with_memory_space_constraint, memory_space=pltpu.HBM)
in_vmem = functools.partial(pltpu.with_memory_space_constraint, memory_space=pltpu.VMEM)


def swiglu(gate_val, up_val):
    return (up_val + 1.0) * gate_val * jax.nn.sigmoid(1.702 * gate_val)


def heads_of(q_cols, past, present, sinks, first):
    kv_width = past.shape[1] // 2
    group = q_cols.shape[0] // kv_width
    shape = (WINDOW, group * WINDOW)
    query_at = lax.rem(lax.broadcasted_iota(jnp.int32, shape, 1), WINDOW)
    earlier = lax.broadcasted_iota(jnp.int32, shape, 0) > query_at
    both = jnp.concatenate([past, present], axis=0)
    outs = []
    for g in range(kv_width // HEAD_DIM):
        keys = both[:, g * HEAD_DIM : (g + 1) * HEAD_DIM]
        vals = both[:, kv_width + g * HEAD_DIM : kv_width + (g + 1) * HEAD_DIM].T
        heads = range(g * group, (g + 1) * group)
        q_group = jnp.concatenate([q_cols[h * HEAD_DIM : (h + 1) * HEAD_DIM] for h in heads], axis=1)
        scores = jnp.dot(keys, q_group, preferred_element_type=F32)
        seen = jnp.where(earlier, jnp.where(first, -1e30, scores[:WINDOW]), scores[WINDOW:])
        sink = jnp.concatenate([jnp.broadcast_to(sinks[:, h : h + 1], (1, WINDOW)) for h in heads], axis=1)
        ceiling = jnp.maximum(jnp.max(seen, axis=0, keepdims=True), sink)
        raised = jnp.exp(seen - ceiling)
        total = jnp.sum(raised, axis=0, keepdims=True) + jnp.exp(sink - ceiling)
        spread = jnp.concatenate([jnp.where(earlier, raised, 0.0), jnp.where(earlier, 0.0, raised)], axis=0)
        mixed = jnp.dot(vals, spread.astype(BF16), preferred_element_type=F32) * (1.0 / total)
        mixed = mixed.astype(BF16)
        outs += [mixed[:, i * WINDOW : (i + 1) * WINDOW] for i in range(group)]
    return jnp.concatenate(outs, axis=0)


def pack_kernel(place, sink, k, v, q, packed, rim, sems):
    count, last, width = k.shape[0], k.shape[0] - WINDOW, k.shape[1]
    base = 2 * count + BF16_ROWS
    rows = pl.ds(pl.multiple_of((1 - place[0]) * WINDOW, WINDOW), WINDOW)
    moves = [
        (k.at[last:, :], rim.at[:WINDOW, :]),
        (v.at[last:, :], rim.at[WINDOW:, :]),
        (k, packed.at[:count, :]),
        (v, packed.at[count : 2 * count, :]),
    ]
    for j in range(q.shape[1] // width):
        to = base + j * WINDOW
        moves.append((q.at[rows, j * width : (j + 1) * width], packed.at[to : to + WINDOW, :]))
    copies = [pltpu.make_async_copy(source, target, sems.at[i]) for i, (source, target) in enumerate(moves)]
    for copy in copies:
        copy.start()
    shape = (BF16_ROWS, width)
    lane, row = (lax.broadcasted_iota(jnp.int32, shape, i) for i in (1, 0))
    left = jnp.zeros(shape, F32)
    for h in range(sink.shape[0]):
        left = jnp.where(lane == h, sink[h], left)
    terms = jnp.zeros(shape, F32)
    for i in range(3):
        term = left.astype(BF16).astype(F32)
        terms = jnp.where(row == i, term, terms)
        left = left - term
    packed[2 * count : base, :] = terms.astype(BF16)
    for copy in copies:
        copy.wait()


def pack(place, sink_logit, key_rows, values, queries):
    rows, width = key_rows.shape
    blocks = queries.shape[1] // width
    return pl.pallas_call(
        pack_kernel,
        out_shape=[
            jax.ShapeDtypeStruct((n, width), BF16) for n in (2 * rows + BF16_ROWS + blocks * WINDOW, 2 * WINDOW)
        ],
        in_specs=[SMEM, SMEM, ANY, ANY, ANY],
        out_specs=[VMEM, VMEM],
        scratch_shapes=[pltpu.SemaphoreType.DMA((4 + blocks,))],
        cost_estimate=pl.CostEstimate(flops=0, bytes_accessed=4 * key_rows.size, transcendentals=0),
        compiler_params=pltpu.CompilerParams(vmem_limit_bytes=4 * 2**20),
        name="pack",
    )(place, sink_logit, in_hbm(key_rows), in_hbm(values), in_hbm(queries))


def front_kernel(code_rows, place, packed_a, rim_a, packed_b, *refs):
    hbm, outs, scratch = refs[:6], refs[6 : 9 if code_rows else 7], refs[9 if code_rows else 7 :]
    q_a, ow_a, ow_b, resid, routes, codes = hbm
    core, first = place[0], place[1] == 1
    start = pl.multiple_of(core * WINDOW, WINDOW)
    rows = pl.ds(start, WINDOW)
    held, sems = scratch[:-1], scratch[-1]
    sources = (q_a.at[rows, :], ow_a, ow_b, resid.at[:, rows], routes.at[:, rows], codes.at[:, rows])
    copies = [pltpu.make_async_copy(source, held[i], sems.at[i]) for i, source in enumerate(sources)]
    for copy in copies:
        copy.start()
    lead = core == 0
    width = rim_a.shape[1]
    blocks = held[0].shape[1] // width
    base = packed_a.shape[0] - blocks * WINDOW
    count = (base - BF16_ROWS) // 2
    tail = packed_b.at[packed_a.shape[0] :, :]
    later = pl.ds(pl.multiple_of(count + start, WINDOW), WINDOW)

    def attend(packed, rim, q_blocks):
        past = jnp.concatenate(
            [
                jnp.where(lead, rim[:WINDOW, :], packed[:WINDOW, :]),
                jnp.where(lead, rim[WINDOW:, :], packed[count : count + WINDOW, :]),
            ],
            axis=1,
        )
        present = jnp.concatenate([packed[rows, :], packed[later, :]], axis=1)
        terms = packed[2 * count : base, :].astype(F32)
        sinks = terms[0:1] + terms[1:2] + terms[2:3]
        q_cols = jnp.concatenate([(block * HEAD_DIM ** (-0.5)).T for block in q_blocks], axis=0)
        return heads_of(q_cols, past, present, sinks, first)

    theirs = attend(
        packed_b, tail, [packed_b[base + j * WINDOW : base + (j + 1) * WINDOW, :] for j in range(blocks)]
    )
    copies[0].wait()
    ours = attend(packed_a, rim_a, [held[0][:, j * width : (j + 1) * width] for j in range(blocks)])
    copies[2].wait()
    projected = jnp.dot(held[2][...], theirs, preferred_element_type=F32)
    copies[1].wait()
    projected += jnp.dot(held[1][...], ours, preferred_element_type=F32)
    for copy in copies[3:]:
        copy.wait()
    attended = (held[3][...].astype(F32) + projected).astype(BF16)
    outs[0][...] = attended
    if code_rows:
        expert = lax.broadcasted_iota(jnp.int32, (code_rows, WINDOW), 0)
        table = jnp.zeros((code_rows, WINDOW), F32)
        for k in range(TOP):
            named = jnp.broadcast_to(held[4][k : k + 1, :], expert.shape) == expert
            table += jnp.where(named, jnp.broadcast_to(held[5][k : k + 1, :], expert.shape).astype(F32), 0.0)
        outs[1][:code_rows, :] = table.astype(BF16)
        half = half_of(attended.shape[0])
        outs[1][code_rows:, :] = attended[:half]
        outs[2][...] = attended[half:]


def front(code_rows, queries, key_rows, values, sink_logit, o_weight, residual, routes, gate_codes):
    seq, core = lax.axis_index("seq"), lax.axis_index("exp")
    place = jnp.stack([core, jnp.where((seq == 0) & (core == 0), 1, 0)]).astype(jnp.int32)
    ow_b = swapped(o_weight.T)
    packed, rim = pack(place, sink_logit, key_rows, values, queries)
    rim_a = lax.ppermute(rim, "seq", [(s, s + 1) for s in range(lax.axis_size("seq") - 1)])
    packed_b = swapped(jnp.concatenate([packed, rim_a], axis=0))
    features, block = residual.shape[1], residual.shape[0] // lax.axis_size("exp")
    half = half_of(features)
    shapes = [(features, block)] + ([(code_rows + half, block), (features - half, block)] if code_rows else [])
    held = [queries[:WINDOW], o_weight.T, o_weight.T]
    held += [residual.T[:, :WINDOW], routes.T[:, :WINDOW], gate_codes.T[:, :WINDOW]]
    outs = pl.pallas_call(
        functools.partial(front_kernel, code_rows),
        out_shape=[jax.ShapeDtypeStruct(shape, BF16) for shape in shapes],
        in_specs=[SMEM] + [VMEM] * 3 + [ANY] * 6,
        out_specs=[VMEM] * len(shapes),
        scratch_shapes=[pltpu.VMEM(h.shape, h.dtype) for h in held] + [pltpu.SemaphoreType.DMA((len(held),))],
        cost_estimate=pl.CostEstimate(flops=2 * 10**9, bytes_accessed=10**7, transcendentals=10**6),
        compiler_params=pltpu.CompilerParams(vmem_limit_bytes=20 * 2**20),
        name="front",
    )(
        place, packed, rim_a, packed_b, in_hbm(queries), in_hbm(o_weight.T), in_hbm(ow_b),
        in_hbm(residual.T), in_hbm(routes.T), in_hbm(gate_codes.T),
    )
    return outs, packed_b[:BF16_ROWS]


def swapped(value):
    return lax.ppermute(value, "exp", [(0, 1), (1, 0)])


def after(value, *earlier):
    return lax.optimization_barrier((value, *earlier))[0]


def rms_norm(stream, norm_gain):
    widened = stream.astype(F32)
    spread = jnp.mean(widened * widened, axis=-1, keepdims=True)
    return (widened * lax.rsqrt(spread + 1e-05) * norm_gain).astype(BF16)


def expert_kernel(code_rows, place, gain, upper, lower, *refs):
    weights, (out_upper, out_lower) = refs[:6], refs[6:]
    rows = rms_norm(jnp.concatenate([upper[code_rows:, :], lower[...]], axis=0).T, gain[...])
    total = None
    for w_gate, w_up, w_down in (weights[:3], weights[3:]):
        gate_val = jnp.dot(rows, w_gate[...], preferred_element_type=F32)
        up_val = jnp.dot(rows, w_up[...], preferred_element_type=F32)
        hidden = swiglu(gate_val, up_val).astype(BF16)
        term = jnp.dot(hidden, w_down[...], preferred_element_type=F32)
        total = term if total is None else total + term
    codes = upper[:code_rows, :].astype(F32)
    mine = lax.broadcasted_iota(jnp.int32, codes.shape, 0) == place[0]
    code = jnp.sum(jnp.where(mine, codes, 0.0), axis=0, keepdims=True)
    term = (total.T * (code / jnp.sum(codes, axis=0, keepdims=True))).astype(BF16)
    half = out_upper.shape[0]
    out_upper[...] = term[:half]
    out_lower[...] = term[half:]


def expert_terms(code_rows, expert, gain, weights, parcel):
    features = gain.shape[1]
    half = half_of(features)
    flops = 2 * WINDOW * features * 3 * 2 * weights[0].shape[1]
    return pl.pallas_call(
        functools.partial(expert_kernel, code_rows),
        out_shape=[jax.ShapeDtypeStruct((n, WINDOW), BF16) for n in (half, features - half)],
        in_specs=[SMEM] + [VMEM] * 9,
        out_specs=[VMEM] * 2,
        cost_estimate=pl.CostEstimate(flops=flops, bytes_accessed=10**6, transcendentals=10**5),
        compiler_params=pltpu.CompilerParams(vmem_limit_bytes=24 * 2**20),
        name="experts",
    )(expert, gain, *parcel, *weights)


def half_of(features):
    return features // 2 // BF16_ROWS * BF16_ROWS


def ring_of(count):
    order = list(range(0, count, 2)) + list(range(count - 1, 0, -2))
    right = [(order[i], order[(i + 1) % count]) for i in range(count)]
    return right, [(target, source) for source, target in right]


def add(a, b):
    return (a.astype(F32) + b.astype(F32)).astype(BF16)


def mixed_by_ring(parcel, code_rows, gain, weights):
    count = lax.axis_size("seq")
    right, left = ring_of(count)
    far = count // 2
    expert = lax.axis_index("seq").astype(jnp.int32)[None]
    to_right = functools.partial(lax.ppermute, axis_name="seq", perm=right)
    to_left = functools.partial(lax.ppermute, axis_name="seq", perm=left)
    apply = functools.partial(expert_terms, code_rows, expert, gain, weights)
    at = {0: parcel}
    at[-1], at[1] = [to_right(half) for half in parcel], [to_left(half) for half in parcel]
    terms, waited = {}, ()
    for k in range(2, far + 1):
        upper_left = to_right(after(at[1 - k][0], *waited))
        upper_right = to_left(after(at[k - 1][0], *waited)) if k < far else None
        if k > 2:
            terms[k - 2] = apply(after(at[k - 2], *at[1 - k][:1], *at[k - 1][:1]))
            waited = terms[k - 2]
        lower_left = to_right(after(at[1 - k][1], *waited)) if k < far else None
        lower_right = to_left(after(at[k - 1][1], *waited))
        terms[1 - k] = apply(after(at[1 - k], *waited))
        waited = terms[1 - k]
        at[-k], at[k] = [upper_left, lower_left], [upper_right, lower_right]
    opposite = [at[-far][0], at[far][1]]
    left_up = to_left(terms[1 - far][0])
    terms[far - 1] = apply(after(at[far - 1], *waited))
    right_low = to_right(terms[far - 1][1])
    farthest = apply(after(opposite, *terms[far - 1]))
    right_up, left_low = to_right(farthest[0]), to_left(farthest[1])
    terms[0] = apply(after(parcel, left_up, right_low))
    for k in range(far - 1, 0, -1):
        if k > 1:
            going = add(terms[1 - k][0], left_up), add(terms[k - 1][1], right_low)
            left_up, right_low = to_left(going[0]), to_right(going[1])
        going = add(terms[-k][1], left_low), add(terms[k][0], right_up)
        if k == far - 1:
            going = after(going, *terms[0])
        left_low, right_up = to_left(going[0]), to_right(going[1])
    near, left_up, right_low = after((terms[0], left_up, right_low), left_low, right_up)
    upper = near[0].astype(F32) + left_up.astype(F32) + right_up.astype(F32)
    lower = near[1].astype(F32) + left_low.astype(F32) + right_low.astype(F32)
    return jnp.concatenate([upper, lower], axis=0).astype(BF16)


def pack_rows(normed, expert_ids, gate_codes, expert_count, capacity):
    pair_ids = expert_ids.reshape(-1)
    matches = (pair_ids[:, None] == jnp.arange(expert_count, dtype=jnp.int32)[None, :]).astype(
        jnp.int32
    )
    within = jnp.sum((jnp.cumsum(matches, axis=0) - 1) * matches, axis=1)
    sources = normed[jnp.arange(pair_ids.shape[0], dtype=jnp.int32) // expert_ids.shape[1]]
    outbox = jnp.zeros((expert_count * capacity, normed.shape[1]), normed.dtype)
    outbox = outbox.at[pair_ids * capacity + within].set(sources)
    code_vals = gate_codes.astype(F32)
    shares = (code_vals / jnp.sum(code_vals, axis=1, keepdims=True)).reshape(-1)
    return (outbox, pair_ids, within, shares)


def mixed_by_packing(normed, routes, gate_codes, weights, expert_count, capacity):
    w_gate, w_up, w_down = weights
    owners, block = lax.axis_size("exp"), normed.shape[0]
    owner_pos = lax.axis_index("exp")
    own = lambda value: lax.dynamic_slice_in_dim(value, owner_pos * block, block, 0)
    outbox, pair_ids, within, shares = pack_rows(
        normed, own(routes), own(gate_codes), expert_count, capacity
    )
    outbox = outbox.reshape(expert_count, capacity, normed.shape[1])
    exchange = functools.partial(lax.all_to_all, axis_name="seq", split_axis=0, concat_axis=0, tiled=True)
    arrived = lax.all_gather(exchange(outbox), "exp", axis=0, tiled=True)
    flat_rows = arrived.reshape(-1, arrived.shape[-1])
    gate_val = jnp.dot(flat_rows, w_gate, preferred_element_type=F32)
    up_val = jnp.dot(flat_rows, w_up, preferred_element_type=F32)
    hidden = swiglu(gate_val, up_val).astype(BF16)
    partial_value = jnp.dot(hidden, w_down, preferred_element_type=F32).reshape(arrived.shape)
    whole = lax.psum_scatter(partial_value.astype(BF16), "exp", scatter_dimension=0, tiled=True)
    picked = exchange(whole)[pair_ids, within].astype(F32)
    mixture = jnp.sum((picked * shares[:, None]).reshape(-1, TOP, normed.shape[1]), axis=1)
    return mixture.astype(BF16)


def local(
    queries,
    key_rows,
    values,
    sink_logit,
    o_weight,
    residual,
    norm_gain,
    routes,
    gate_codes,
    w_gate,
    w_up,
    w_down,
):
    block_rows = residual.shape[0] // lax.axis_size("exp")
    expert_count = w_gate.shape[0] * lax.axis_size("seq")
    capacity = max(2, 2 * block_rows * TOP // expert_count)
    weights = (w_gate[0], w_up[0], w_down[0])
    attention = (queries, key_rows, values, sink_logit, o_weight, residual, routes, gate_codes)
    if capacity < block_rows:
        (attended,), _ = front(0, *attention)
        attended = attended.T
        normed = rms_norm(attended, norm_gain)
        return (attended, mixed_by_packing(normed, routes, gate_codes, weights, expert_count, capacity))
    code_rows = -(-expert_count // BF16_ROWS) * BF16_ROWS
    (attended, *parcel), arrived = front(code_rows, *attention)
    gate_b, up_b = (swapped(after(weight, arrived)) for weight in weights[:2])
    down_b = swapped(after(weights[2], gate_b, up_b, attended))
    weights = [in_vmem(weight) for weight in (*weights, gate_b, up_b, down_b)]
    return (attended.T, mixed_by_ring(parcel, code_rows, norm_gain[None, :], weights).T)


def solution(mesh):
    placed = (
        P(("groups", "seq"), "exp"),
        P(("groups", "seq"), "exp"),
        P(("groups", "seq"), "exp"),
        P("exp"),
        P("exp", None),
        P(("groups", "seq"), None),
        P(),
        P(("groups", "seq"), None),
        P(("groups", "seq"), None),
        P("seq", None, "exp"),
        P("seq", None, "exp"),
        P("seq", "exp", None),
    )
    return jax.shard_map(
        local,
        mesh=mesh,
        in_specs=placed,
        out_specs=(P(("groups", "seq", "exp"), None), P(("groups", "seq", "exp"), None)),
        check_vma=False,
    )
```

time: 135 us -> 105 us (0.78)
  waiting for transfers between devices: 48 us -> 33.4 us
  Pallas kernels: 42.6 us -> 28.8 us
  local copies, waits for them, and re-layouts: 8.52 us -> 2.25 us
  starting transfers between devices: 33.3 us -> 37.7 us
    pallas_call x6 -> x10, Pallas kernels: 42.6 us -> 28.8 us  [the longest x8 20 us: expert_terms(): pl.pallas_call(functools.partial(expert_kernel, code_rows), out_shape=[ja...]
    ppermute x18 -> x29, starting transfers between devices: 26.4 us -> 36.4 us  [the longest x4 6.35 us: mixed_by_ring(): left_up, right_low = (to_left(going[0]), to_right(going[1]))]
    ppermute x18 -> x29, waiting for transfers between devices: 40 us -> 31.6 us  [the longest x6 14.2 us: mixed_by_ring(): left_low, right_up = (to_left(going[0]), to_right(going[1]))]
    ppermute x7 -> x5, waiting for transfers between devices: 7.98 us -> 1.82 us  [swapped(): return lax.ppermute(value, 'exp', [(0, 1), (1, 0)])]
    ppermute x7 -> x5, starting transfers between devices: 6.92 us -> 1.3 us  [swapped(): return lax.ppermute(value, 'exp', [(0, 1), (1, 0)])]
    unnamed x17 -> x12, local copies, waits for them, and re-layouts: 6.88 us -> 2.24 us
  transfers between devices with their start and end apart: 25 -> 34, of which waited for: 12 -> 15; matrix products, arithmetic and copies ran while one was open for 2% -> 1% of each run, Pallas kernels for 27% -> 25%
where the time goes in v2:
time: 105 us
  starting transfers between devices  37.7 us (36%)
  waiting for transfers between devices  33.4 us (32%)
  Pallas kernels  28.8 us (27%)
  local copies, waits for them, and re-layouts  2.25 us (2%)
  other arithmetic  1.53 us (1%)
    pallas_call x8, Pallas kernels, expert_terms(): pl.pallas_call(functools.partial(expert_kernel, code_rows), out_shape=[ja...  20 us
    ppermute x6, waiting for transfers between devices, mixed_by_ring(): left_low, right_up = (to_left(going[0]), to_right(going[1]))  14.2 us
    pallas_call x1, Pallas kernels, front(): pl.pallas_call(functools.partial(front_kernel, code_rows), out_shape=[jax...  7.17 us
    ppermute x4, starting transfers between devices, mixed_by_ring(): left_up, right_low = (to_left(going[0]), to_right(going[1]))  6.35 us
    ppermute x6, starting transfers between devices, mixed_by_ring(): left_low, right_up = (to_left(going[0]), to_right(going[1]))  5.33 us
    ppermute x2, waiting for transfers between devices, mixed_by_ring(): right_up, left_low = (to_right(farthest[0]), to_left(farthest[1]))  4.98 us
    ppermute x1, starting transfers between devices, front(): lax.ppermute(rim, 'seq', [(s, s + 1) for s in range(lax.axis_size('seq')...  4.45 us
    ppermute x2, starting transfers between devices, mixed_by_ring(): to_left(half)  3.6 us
  transfers between devices with their start and end apart: 34, of which 15 were waited for; matrix products, arithmetic and copies ran while one was open for 1% of the time, Pallas kernels for 25%

profile of v2, /device:TPU:0, one launch (start us, length us, event | category | flops | bytes accessed | tf_op | source)
XLA Modules:
  0.0 104.5 jit_solution(18347858965782356648)
XLA Ops:
  1.2 0.7 copy-done.3
  1.9 1.6 %pack.1 = (bf16[1552,128]{1,0:T(8,128)(2,1)S(1)}, bf16[256,128]{1,0:T(8,128)(2,1)S(1)}) custom-call(s32[2]{0:T(128)S(1)} %pad_add_fusion.place, f32[16]{0:T(128)S(1)} %copy-done.3, bf16[256,128]{1,0:T(8,128)(2,1)} %k.1, bf16[256,128]{1,0:T(8,128)(2,1)} %v.1, bf16[256,1024]{1,0:T(8,128)(2,1)} %refs_0_.1), custom_call_target="tpu_custom_call" | custom-call | bytes 131072 | tf_op jit(solution)/shard_map/pack/pallas_call | solution.py:87
  3.5 4.5 %collective-permute-start = (bf16[256,128]{1,0:T(8,128)(2,1)S(1)}, bf16[256,128]{1,0:T(8,128)(2,1)S(1)}, u32[]{:S(2)}, u32[]{:S(2)}) collective-permute-start(bf16[256,128]{1,0:T(8,128)(2,1)S(1)} %get-tuple-element.55), channel_id=1, source_target_pairs={{0,2},{2,4},{4,6},{6,8},{8,10},{10,12},{12,14},{1,3},{3,5},{5,7},{... | collective-permute-start | bytes 196616 | tf_op jit(solution)/shard_map/ppermute | solution.py:164
  8.0 2.0 %collective-permute-done.rim_a = bf16[256,128]{1,0:T(8,128)(2,1)S(1)} collective-permute-done((bf16[256,128]{1,0:T(8,128)(2,1)S(1)}, bf16[256,128]{1,0:T(8,128)(2,1)S(1)}, u32[]{:S(2)}, u32[]{:S(2)}) %collective-permute-start) | collective-permute-done | bytes 65568 | tf_op jit(solution)/shard_map/ppermute | solution.py:164
  10.1 1.8 %collective-permute-done.1.packed_b = bf16[1808,128]{1,0:T(8,128)(2,1)S(1)} collective-permute-done((bf16[1808,128]{1,0:T(8,128)(2,1)S(1)}, bf16[1808,128]{1,0:T(8,128)(2,1)S(1)}, u32[]{:S(2)}, u32[]{:S(2)}) %collective-permute-start.1) | collective-permute-done | bytes 462880 | tf_op jit(solution)/shard_map/ppermute | solution.py:188
  12.4 1.6 %copy-done.4 = bf16[1440,1024]{1,0:T(8,128)(2,1)} copy-done((bf16[1440,1024]{1,0:T(8,128)(2,1)}, bf16[1440,1024]{1,0:T(8,128)(2,1)S(1)}, u32[]{:S(2)}) %copy-start.4) | copy-done | bytes 2949144
  14.0 7.2 %front.1 = (bf16[1440,128]{1,0:T(8,128)(2,1)}, bf16[736,128]{1,0:T(8,128)(2,1)S(1)}, bf16[720,128]{1,0:T(8,128)(2,1)S(1)}) custom-call(s32[2]{0:T(128)S(1)} %pad_add_fusion.place, bf16[1552,128]{1,0:T(8,128)(2,1)S(1)} %get-tuple-element.54.packed_a, bf16[256,128]{1,0:T(8,128)(2,1)S(1)} %collective-permute-done.rim_a, ...), custom_call_target="tpu_custom_call" | custom-call | flops 2000000000 | bytes 10000000 | tf_op jit(solution)/shard_map/front/pallas_call | solution.py:171
  21.4 2.5 %collective-permute-start.11 = (bf16[736,128]{1,0:T(8,128)(2,1)S(1)}, bf16[736,128]{1,0:T(8,128)(2,1)S(1)}, u32[]{:S(2)}, u32[]{:S(2)}) collective-permute-start(bf16[736,128]{1,0:T(8,128)(2,1)S(1)} %get-tuple-element.85.upper), channel_id=1, source_target_pairs={{4,0},{8,4},{12,8},{14,12},{10,14},{6,10},{2,6},{0,2},{5,1},{9,5},... | collective-permute-start | bytes 565256 | tf_op jit(solution)/shard_map/ppermute | solution.py:258
  23.9 1.0 collective-permute-start.3
  24.8 2.0 %collective-permute-start.5 = (bf16[720,128]{1,0:T(8,128)(2,1)S(1)}, bf16[720,128]{1,0:T(8,128)(2,1)S(1)}, u32[]{:S(2)}, u32[]{:S(2)}) collective-permute-start(bf16[720,128]{1,0:T(8,128)(2,1)S(1)} %get-tuple-element.86.lower), channel_id=1, source_target_pairs={{0,4},{4,8},{8,12},{12,14},{14,10},{10,6},{6,2},{2,0},{1,5},{5,9},... | collective-permute-start | bytes 552968 | tf_op jit(solution)/shard_map/ppermute | solution.py:258
  26.8 3.2 %collective-permute-done.11.upper = bf16[736,128]{1,0:T(8,128)(2,1)S(1)} collective-permute-done((bf16[736,128]{1,0:T(8,128)(2,1)S(1)}, bf16[736,128]{1,0:T(8,128)(2,1)S(1)}, u32[]{:S(2)}, u32[]{:S(2)}) %collective-permute-start.11) | collective-permute-done | bytes 188448 | tf_op jit(solution)/shard_map/ppermute | solution.py:258
  30.1 0.8 collective-permute-start.13
  30.9 0.6 collective-permute-done.3.upper
  31.4 0.9 collective-permute-start.4
  32.4 1.1 %collective-permute-start.12 = (bf16[720,128]{1,0:T(8,128)(2,1)S(1)}, bf16[720,128]{1,0:T(8,128)(2,1)S(1)}, u32[]{:S(2)}, u32[]{:S(2)}) collective-permute-start(bf16[720,128]{1,0:T(8,128)(2,1)S(1)} %get-tuple-element.86.lower), channel_id=1, source_target_pairs={{4,0},{8,4},{12,8},{14,12},{10,14},{6,10},{2,6},{0,2},{5,1},{9,5},... | collective-permute-start | bytes 552968 | tf_op jit(solution)/shard_map/ppermute | solution.py:258
  33.5 1.9 %collective-permute-done.5.lower = bf16[720,128]{1,0:T(8,128)(2,1)S(1)} collective-permute-done((bf16[720,128]{1,0:T(8,128)(2,1)S(1)}, bf16[720,128]{1,0:T(8,128)(2,1)S(1)}, u32[]{:S(2)}, u32[]{:S(2)}) %collective-permute-start.5) | collective-permute-done | bytes 184352 | tf_op jit(solution)/shard_map/ppermute | solution.py:258
  35.4 0.9 collective-permute-start.10
  36.3 2.5 %experts.8 = (bf16[720,128]{1,0:T(8,128)(2,1)S(1)}, bf16[720,128]{1,0:T(8,128)(2,1)S(1)}) custom-call(s32[1]{0:T(128)} %bitcast.7.place, f32[1,1440]{1,0:T(1,128)S(1)} %broadcast_in_dim.7.gain, bf16[736,128]{1,0:T(8,128)(2,1)S(1)} %collective-permute-done.3.upper, bf16[720,128]{1,0:T(8,128)(2,1)S(1)} %collective-permute-done.5.lower, ...), custom_call_target="tpu_custom_call" | custom-call | flops 1592524800 | bytes 1000000 | tf_op jit(solution)/shard_map/experts/pallas_call | solution.py:224
  38.8 1.2 %collective-permute-start.16 = (bf16[736,128]{1,0:T(8,128)(2,1)S(1)}, bf16[736,128]{1,0:T(8,128)(2,1)S(1)}, u32[]{:S(2)}, u32[]{:S(2)}) collective-permute-start(bf16[736,128]{1,0:T(8,128)(2,1)S(1)} %collective-permute-done.13.upper), channel_id=1, source_target_pairs={{4,0},{8,4},{12,8},{14,12},{10,14},{6,10},{2,6},{0,2},{5,1},{9,5},... | collective-permute-start | bytes 565256 | tf_op jit(solution)/shard_map/ppermute | solution.py:262
  40.0 1.0 %collective-permute-start.9 = (bf16[736,128]{1,0:T(8,128)(2,1)S(1)}, bf16[736,128]{1,0:T(8,128)(2,1)S(1)}, u32[]{:S(2)}, u32[]{:S(2)}) collective-permute-start(bf16[736,128]{1,0:T(8,128)(2,1)S(1)} %collective-permute-done.4.upper), channel_id=1, source_target_pairs={{0,4},{4,8},{8,12},{12,14},{14,10},{10,6},{6,2},{2,0},{1,5},{5,9},... | collective-permute-start | bytes 565256 | tf_op jit(solution)/shard_map/ppermute | solution.py:261
  41.1 1.0 collective-permute-start.15
  42.0 2.5 %experts.9 = (bf16[720,128]{1,0:T(8,128)(2,1)S(1)}, bf16[720,128]{1,0:T(8,128)(2,1)S(1)}) custom-call(s32[1]{0:T(128)} %bitcast.7.place, f32[1,1440]{1,0:T(1,128)S(1)} %broadcast_in_dim.7.gain, bf16[736,128]{1,0:T(8,128)(2,1)S(1)} %collective-permute-done.11.upper, bf16[720,128]{1,0:T(8,128)(2,1)S(1)} %collective-permute-done.12.lower, ...), custom_call_target="tpu_custom_call" | custom-call | flops 1592524800 | bytes 1000000 | tf_op jit(solution)/shard_map/experts/pallas_call | solution.py:224
  44.5 1.1 %collective-permute-start.14 = (bf16[720,128]{1,0:T(8,128)(2,1)S(1)}, bf16[720,128]{1,0:T(8,128)(2,1)S(1)}, u32[]{:S(2)}, u32[]{:S(2)}) collective-permute-start(bf16[720,128]{1,0:T(8,128)(2,1)S(1)} %collective-permute-done.10.lower), channel_id=1, source_target_pairs={{0,4},{4,8},{8,12},{12,14},{14,10},{10,6},{6,2},{2,0},{1,5},{5,9},... | collective-permute-start | bytes 552968 | tf_op jit(solution)/shard_map/ppermute | solution.py:266
  45.7 2.8 %collective-permute-done.15.lower = bf16[720,128]{1,0:T(8,128)(2,1)S(1)} collective-permute-done((bf16[720,128]{1,0:T(8,128)(2,1)S(1)}, bf16[720,128]{1,0:T(8,128)(2,1)S(1)}, u32[]{:S(2)}, u32[]{:S(2)}) %collective-permute-start.15) | collective-permute-done | bytes 184352 | tf_op jit(solution)/shard_map/ppermute | solution.py:267
  49.0 2.5 %experts.10 = (bf16[720,128]{1,0:T(8,128)(2,1)S(1)}, bf16[720,128]{1,0:T(8,128)(2,1)S(1)}) custom-call(s32[1]{0:T(128)} %bitcast.7.place, f32[1,1440]{1,0:T(1,128)S(1)} %broadcast_in_dim.7.gain, bf16[736,128]{1,0:T(8,128)(2,1)S(1)} %collective-permute-done.13.upper, bf16[720,128]{1,0:T(8,128)(2,1)S(1)} %collective-permute-done.15.lower, ...), custom_call_target="tpu_custom_call" | custom-call | flops 1592524800 | bytes 1000000 | tf_op jit(solution)/shard_map/experts/pallas_call | solution.py:224
  51.5 2.5 %experts.11 = (bf16[720,128]{1,0:T(8,128)(2,1)S(1)}, bf16[720,128]{1,0:T(8,128)(2,1)S(1)}) custom-call(s32[1]{0:T(128)} %bitcast.7.place, f32[1,1440]{1,0:T(1,128)S(1)} %broadcast_in_dim.7.gain, bf16[736,128]{1,0:T(8,128)(2,1)S(1)} %collective-permute-done.9.upper, bf16[720,128]{1,0:T(8,128)(2,1)S(1)} %collective-permute-done.14.lower, ...), custom_call_target="tpu_custom_call" | custom-call | flops 1592524800 | bytes 1000000 | tf_op jit(solution)/shard_map/experts/pallas_call | solution.py:224
  54.0 2.5 %experts.12 = (bf16[720,128]{1,0:T(8,128)(2,1)S(1)}, bf16[720,128]{1,0:T(8,128)(2,1)S(1)}) custom-call(s32[1]{0:T(128)} %bitcast.7.place, f32[1,1440]{1,0:T(1,128)S(1)} %broadcast_in_dim.7.gain, bf16[736,128]{1,0:T(8,128)(2,1)S(1)} %collective-permute-done.16.upper, bf16[720,128]{1,0:T(8,128)(2,1)S(1)} %collective-permute-done.18.lower, ...), custom_call_target="tpu_custom_call" | custom-call | flops 1592524800 | bytes 1000000 | tf_op jit(solution)/shard_map/experts/pallas_call | solution.py:224
  56.5 1.6 %collective-permute-start.19 = (bf16[720,128]{1,0:T(8,128)(2,1)S(1)}, bf16[720,128]{1,0:T(8,128)(2,1)S(1)}, u32[]{:S(2)}, u32[]{:S(2)}) collective-permute-start(bf16[720,128]{1,0:T(8,128)(2,1)S(1)} %get-tuple-element.84), channel_id=1, source_target_pairs={{0,4},{4,8},{8,12},{12,14},{14,10},{10,6},{6,2},{2,0},{1,5},{5,9},... | collective-permute-start | bytes 552968 | tf_op jit(solution)/shard_map/ppermute | solution.py:274
  58.6 2.5 %experts.14 = (bf16[720,128]{1,0:T(8,128)(2,1)S(1)}, bf16[720,128]{1,0:T(8,128)(2,1)S(1)}) custom-call(s32[1]{0:T(128)} %bitcast.7.place, f32[1,1440]{1,0:T(1,128)S(1)} %broadcast_in_dim.7.gain, bf16[736,128]{1,0:T(8,128)(2,1)S(1)} %collective-permute-done.4.upper, bf16[720,128]{1,0:T(8,128)(2,1)S(1)} %collective-permute-done.10.lower, ...), custom_call_target="tpu_custom_call" | custom-call | flops 1592524800 | bytes 1000000 | tf_op jit(solution)/shard_map/experts/pallas_call | solution.py:224
  61.1 1.6 %collective-permute-start.25 = (bf16[720,128]{1,0:T(8,128)(2,1)S(1)}, bf16[720,128]{1,0:T(8,128)(2,1)S(1)}, u32[]{:S(2)}, u32[]{:S(2)}) collective-permute-start(bf16[720,128]{1,0:T(8,128)(2,1)S(1)} %collective-permute-done.18.lower), channel_id=1, source_target_pairs={{4,0},{8,4},{12,8},{14,12},{10,14},{6,10},{2,6},{0,2},{5,1},{9,5},... | collective-permute-start | bytes 552968 | tf_op jit(solution)/shard_map/ppermute | solution.py:267
  63.2 1.9 %collective-permute-done.17 = bf16[720,128]{1,0:T(8,128)(2,1)S(1)} collective-permute-done((bf16[720,128]{1,0:T(8,128)(2,1)S(1)}, bf16[720,128]{1,0:T(8,128)(2,1)S(1)}, u32[]{:S(2)}, u32[]{:S(2)}) %collective-permute-start.17) | collective-permute-done | bytes 184352 | tf_op jit(solution)/shard_map/ppermute | solution.py:272
  65.2 2.1 %collective-permute-start.22 = (bf16[720,128]{1,0:T(8,128)(2,1)S(1)}, bf16[720,128]{1,0:T(8,128)(2,1)S(1)}, u32[]{:S(2)}, u32[]{:S(2)}) collective-permute-start(bf16[720,128]{1,0:T(8,128)(2,1)S(1)} %add_convert_fusion.9), channel_id=1, source_target_pairs={{0,4},{4,8},{8,12},{12,14},{14,10},{10,6},{6,2},{2,0},{1,5},{5,9},... | collective-permute-start | bytes 552968 | tf_op jit(solution)/shard_map/ppermute | solution.py:281
  67.6 2.5 %experts.13 = (bf16[720,128]{1,0:T(8,128)(2,1)S(1)}, bf16[720,128]{1,0:T(8,128)(2,1)S(1)}) custom-call(s32[1]{0:T(128)} %bitcast.7.place, f32[1,1440]{1,0:T(1,128)S(1)} %broadcast_in_dim.7.gain, bf16[736,128]{1,0:T(8,128)(2,1)S(1)} %get-tuple-element.85.upper, bf16[720,128]{1,0:T(8,128)(2,1)S(1)} %get-tuple-element.86.lower, bf16[1440,720]{1,0:T(8,128)(2,1)S(1)} %bitcast.20, ...), custom_call_target="tpu_custom_call" | custom-call | flops 1592524800 | bytes 1000000 | tf_op jit(solution)/shard_map/experts/pallas_call | solution.py:224
  70.1 2.5 %experts.15 = (bf16[720,128]{1,0:T(8,128)(2,1)S(1)}, bf16[720,128]{1,0:T(8,128)(2,1)S(1)}) custom-call(s32[1]{0:T(128)} %bitcast.7.place, f32[1,1440]{1,0:T(1,128)S(1)} %broadcast_in_dim.7.gain, bf16[736,128]{1,0:T(8,128)(2,1)S(1)} %collective-permute-done.24.upper, bf16[720,128]{1,0:T(8,128)(2,1)S(1)} %collective-permute-done.25.lower, ...), custom_call_target="tpu_custom_call" | custom-call | flops 1592524800 | bytes 1000000 | tf_op jit(solution)/shard_map/experts/pallas_call | solution.py:224
  72.6 2.1 %collective-permute-start.27 = (bf16[720,128]{1,0:T(8,128)(2,1)S(1)}, bf16[720,128]{1,0:T(8,128)(2,1)S(1)}, u32[]{:S(2)}, u32[]{:S(2)}) collective-permute-start(bf16[720,128]{1,0:T(8,128)(2,1)S(1)} %get-tuple-element.99), channel_id=1, source_target_pairs={{0,4},{4,8},{8,12},{12,14},{14,10},{10,6},{6,2},{2,0},{1,5},{5,9},... | collective-permute-start | bytes 552968 | tf_op jit(solution)/shard_map/ppermute | solution.py:276
  74.7 2.1 %collective-permute-start.23 = (bf16[720,128]{1,0:T(8,128)(2,1)S(1)}, bf16[720,128]{1,0:T(8,128)(2,1)S(1)}, u32[]{:S(2)}, u32[]{:S(2)}) collective-permute-start(bf16[720,128]{1,0:T(8,128)(2,1)S(1)} %add_convert_fusion.8), channel_id=1, source_target_pairs={{0,4},{4,8},{8,12},{12,14},{14,10},{10,6},{6,2},{2,0},{1,5},{5,9},... | collective-permute-start | bytes 552968 | tf_op jit(solution)/shard_map/ppermute | solution.py:281
  76.8 2.6 %collective-permute-done.27 = bf16[720,128]{1,0:T(8,128)(2,1)S(1)} collective-permute-done((bf16[720,128]{1,0:T(8,128)(2,1)S(1)}, bf16[720,128]{1,0:T(8,128)(2,1)S(1)}, u32[]{:S(2)}, u32[]{:S(2)}) %collective-permute-start.27) | collective-permute-done | bytes 184352 | tf_op jit(solution)/shard_map/ppermute | solution.py:276
  79.5 2.4 %collective-permute-done.26 = bf16[720,128]{1,0:T(8,128)(2,1)S(1)} collective-permute-done((bf16[720,128]{1,0:T(8,128)(2,1)S(1)}, bf16[720,128]{1,0:T(8,128)(2,1)S(1)}, u32[]{:S(2)}, u32[]{:S(2)}) %collective-permute-start.26) | collective-permute-done | bytes 184352 | tf_op jit(solution)/shard_map/ppermute | solution.py:276
  82.1 1.9 %collective-permute-start.21 = (bf16[720,128]{1,0:T(8,128)(2,1)S(1)}, bf16[720,128]{1,0:T(8,128)(2,1)S(1)}, u32[]{:S(2)}, u32[]{:S(2)}) collective-permute-start(bf16[720,128]{1,0:T(8,128)(2,1)S(1)} %add_convert_fusion.10), channel_id=1, source_target_pairs={{4,0},{8,4},{12,8},{14,12},{10,14},{6,10},{2,6},{0,2},{5,1},{9,5},... | collective-permute-start | bytes 552968 | tf_op jit(solution)/shard_map/ppermute | solution.py:281
  84.1 3.6 %collective-permute-done.31 = bf16[720,128]{1,0:T(8,128)(2,1)S(1)} collective-permute-done((bf16[720,128]{1,0:T(8,128)(2,1)S(1)}, bf16[720,128]{1,0:T(8,128)(2,1)S(1)}, u32[]{:S(2)}, u32[]{:S(2)}) %collective-permute-start.31) | collective-permute-done | bytes 184352 | tf_op jit(solution)/shard_map/ppermute | solution.py:285
  87.8 1.5 %collective-permute-start.32 = (bf16[720,128]{1,0:T(8,128)(2,1)S(1)}, bf16[720,128]{1,0:T(8,128)(2,1)S(1)}, u32[]{:S(2)}, u32[]{:S(2)}) collective-permute-start(bf16[720,128]{1,0:T(8,128)(2,1)S(1)} %add_convert_fusion.3), channel_id=1, source_target_pairs={{0,4},{4,8},{8,12},{12,14},{14,10},{10,6},{6,2},{2,0},{1,5},{5,9},... | collective-permute-start | bytes 552968 | tf_op jit(solution)/shard_map/ppermute | solution.py:285
  89.3 3.0 %collective-permute-done.28 = bf16[720,128]{1,0:T(8,128)(2,1)S(1)} collective-permute-done((bf16[720,128]{1,0:T(8,128)(2,1)S(1)}, bf16[720,128]{1,0:T(8,128)(2,1)S(1)}, u32[]{:S(2)}, u32[]{:S(2)}) %collective-permute-start.28) | collective-permute-done | bytes 184352 | tf_op jit(solution)/shard_map/ppermute | solution.py:285
  92.4 0.6 collective-permute-start.29
  93.4 2.4 %collective-permute-start.33 = (bf16[720,128]{1,0:T(8,128)(2,1)S(1)}, bf16[720,128]{1,0:T(8,128)(2,1)S(1)}, u32[]{:S(2)}, u32[]{:S(2)}) collective-permute-start(bf16[720,128]{1,0:T(8,128)(2,1)S(1)} %add_convert_fusion.2), channel_id=1, source_target_pairs={{0,4},{4,8},{8,12},{12,14},{14,10},{10,6},{6,2},{2,0},{1,5},{5,9},... | collective-permute-start | bytes 552968 | tf_op jit(solution)/shard_map/ppermute | solution.py:285
  95.8 2.2 %collective-permute-done.29 = bf16[720,128]{1,0:T(8,128)(2,1)S(1)} collective-permute-done((bf16[720,128]{1,0:T(8,128)(2,1)S(1)}, bf16[720,128]{1,0:T(8,128)(2,1)S(1)}, u32[]{:S(2)}, u32[]{:S(2)}) %collective-permute-start.29) | collective-permute-done | bytes 184352 | tf_op jit(solution)/shard_map/ppermute | solution.py:285
  98.0 0.6 collective-permute-start.30
  99.0 4.6 %collective-permute-done.30 = bf16[720,128]{1,0:T(8,128)(2,1)S(1)} collective-permute-done((bf16[720,128]{1,0:T(8,128)(2,1)S(1)}, bf16[720,128]{1,0:T(8,128)(2,1)S(1)}, u32[]{:S(2)}, u32[]{:S(2)}) %collective-permute-start.30) | collective-permute-done | bytes 184352 | tf_op jit(solution)/shard_map/ppermute | solution.py:285
  103.8 0.8 maximum_bitcast_fusion
  (57 shorter events, 5.0 us)
Async XLA Ops:
  0.6 11.7 %collective-permute-start.2 = (bf16[1440,1024]{1,0:T(8,128)(2,1)}, bf16[1440,1024]{1,0:T(8,128)(2,1)S(1)}, u32[]{:S(2)}, u32[]{:S(2)}) collective-permute-start(bf16[1440,1024]{1,0:T(8,128)(2,1)} %bitcast.40), channel_id=1, source_target_pairs={{0,1},{1,0},{2,3},{3,2},{4,5},{5,4},{6,7},{7,6},{8,9},{9,8},{10,11... | collective-permute-start | bytes 8847368 | tf_op jit(solution)/shard_map/ppermute | solution.py:188
  1.2 0.7 copy-start.3
  3.5 6.4 %collective-permute-start = (bf16[256,128]{1,0:T(8,128)(2,1)S(1)}, bf16[256,128]{1,0:T(8,128)(2,1)S(1)}, u32[]{:S(2)}, u32[]{:S(2)}) collective-permute-start(bf16[256,128]{1,0:T(8,128)(2,1)S(1)} %get-tuple-element.55), channel_id=1, source_target_pairs={{0,2},{2,4},{4,6},{6,8},{8,10},{10,12},{12,14},{1,3},{3,5},{5,7},{... | collective-permute-start | bytes 196616 | tf_op jit(solution)/shard_map/ppermute | solution.py:164
  10.0 1.9 %collective-permute-start.1 = (bf16[1808,128]{1,0:T(8,128)(2,1)S(1)}, bf16[1808,128]{1,0:T(8,128)(2,1)S(1)}, u32[]{:S(2)}, u32[]{:S(2)}) collective-permute-start(bf16[1808,128]{1,0:T(8,128)(2,1)S(1)} %pad_maximum_fusion), channel_id=1, source_target_pairs={{0,1},{1,0},{2,3},{3,2},{4,5},{5,4},{6,7},{7,6},{8,9},{9,8},{10,11... | collective-permute-start | bytes 1388552 | tf_op jit(solution)/shard_map/ppermute | solution.py:188
  11.9 9.3 %collective-permute-start.6 = (bf16[1440,720]{1,0:T(8,128)(2,1)}, bf16[1440,720]{1,0:T(8,128)(2,1)S(1)}, u32[]{:S(2)}, u32[]{:S(2)}) collective-permute-start(bf16[1440,720]{1,0:T(8,128)(2,1)} %bitcast.13), channel_id=1, source_target_pairs={{0,1},{1,0},{2,3},{3,2},{4,5},{5,4},{6,7},{7,6},{8,9},{9,8},{10,11... | collective-permute-start | bytes 6220808 | tf_op jit(solution)/shard_map/ppermute | solution.py:188
  12.0 9.2 %collective-permute-start.7 = (bf16[1440,720]{1,0:T(8,128)(2,1)}, bf16[1440,720]{1,0:T(8,128)(2,1)S(1)}, u32[]{:S(2)}, u32[]{:S(2)}) collective-permute-start(bf16[1440,720]{1,0:T(8,128)(2,1)} %bitcast.22), channel_id=1, source_target_pairs={{0,1},{1,0},{2,3},{3,2},{4,5},{5,4},{6,7},{7,6},{8,9},{9,8},{10,11... | collective-permute-start | bytes 6220808 | tf_op jit(solution)/shard_map/ppermute | solution.py:188
  12.4 1.6 %copy-start.4 = (bf16[1440,1024]{1,0:T(8,128)(2,1)}, bf16[1440,1024]{1,0:T(8,128)(2,1)S(1)}, u32[]{:S(2)}) copy-start(bf16[1440,1024]{1,0:T(8,128)(2,1)S(1)} %collective-permute-done.2.refs_2_) | copy-start | bytes 8847364
  14.0 7.2 %copy-start.2 = (bf16[1,720,1440]{2,1,0:T(8,128)(2,1)S(1)}, bf16[1,720,1440]{2,1,0:T(8,128)(2,1)}, u32[]{:S(2)}) copy-start(bf16[1,720,1440]{2,1,0:T(8,128)(2,1)} %param.23) | copy-start | bytes 6220804
  14.0 19.5 %copy-start.5 = (f32[1440]{0:T(1024)S(1)}, f32[1440]{0:T(1024)}, u32[]{:S(2)}) copy-start(f32[1440]{0:T(1024)} %param.18) | copy-start | bytes 17284
  14.0 22.4 %copy-start = (bf16[1,1440,720]{2,1,0:T(8,128)(2,1)S(1)}, bf16[1,1440,720]{2,1,0:T(8,128)(2,1)}, u32[]{:S(2)}) copy-start(bf16[1,1440,720]{2,1,0:T(8,128)(2,1)} %param.21) | copy-start | bytes 6220804
  14.0 22.4 %copy-start.1 = (bf16[1,1440,720]{2,1,0:T(8,128)(2,1)S(1)}, bf16[1,1440,720]{2,1,0:T(8,128)(2,1)}, u32[]{:S(2)}) copy-start(bf16[1,1440,720]{2,1,0:T(8,128)(2,1)} %param.22) | copy-start | bytes 6220804
  21.2 15.2 %collective-permute-start.8 = (bf16[720,1440]{1,0:T(8,128)(2,1)S(1)}, bf16[720,1440]{1,0:T(8,128)(2,1)S(1)}, u32[]{:S(2)}, u32[]{:S(2)}) collective-permute-start(bf16[720,1440]{1,0:T(8,128)(2,1)S(1)} %bitcast.31), channel_id=1, source_target_pairs={{0,1},{1,0},{2,3},{3,2},{4,5},{5,4},{6,7},{7,6},{8,9},{9,8},{10,11... | collective-permute-start | bytes 6220808 | tf_op jit(solution)/shard_map/ppermute | solution.py:188
  21.4 8.7 %collective-permute-start.11 = (bf16[736,128]{1,0:T(8,128)(2,1)S(1)}, bf16[736,128]{1,0:T(8,128)(2,1)S(1)}, u32[]{:S(2)}, u32[]{:S(2)}) collective-permute-start(bf16[736,128]{1,0:T(8,128)(2,1)S(1)} %get-tuple-element.85.upper), channel_id=1, source_target_pairs={{4,0},{8,4},{12,8},{14,12},{10,14},{6,10},{2,6},{0,2},{5,1},{9,5},... | collective-permute-start | bytes 565256 | tf_op jit(solution)/shard_map/ppermute | solution.py:258
  23.9 7.6 %collective-permute-start.3 = (bf16[736,128]{1,0:T(8,128)(2,1)S(1)}, bf16[736,128]{1,0:T(8,128)(2,1)S(1)}, u32[]{:S(2)}, u32[]{:S(2)}) collective-permute-start(bf16[736,128]{1,0:T(8,128)(2,1)S(1)} %get-tuple-element.85.upper), channel_id=1, source_target_pairs={{0,4},{4,8},{8,12},{12,14},{14,10},{10,6},{6,2},{2,0},{1,5},{5,9},... | collective-permute-start | bytes 565256 | tf_op jit(solution)/shard_map/ppermute | solution.py:258
  24.8 10.6 %collective-permute-start.5 = (bf16[720,128]{1,0:T(8,128)(2,1)S(1)}, bf16[720,128]{1,0:T(8,128)(2,1)S(1)}, u32[]{:S(2)}, u32[]{:S(2)}) collective-permute-start(bf16[720,128]{1,0:T(8,128)(2,1)S(1)} %get-tuple-element.86.lower), channel_id=1, source_target_pairs={{0,4},{4,8},{8,12},{12,14},{14,10},{10,6},{6,2},{2,0},{1,5},{5,9},... | collective-permute-start | bytes 552968 | tf_op jit(solution)/shard_map/ppermute | solution.py:258
  30.1 8.8 %collective-permute-start.13 = (bf16[736,128]{1,0:T(8,128)(2,1)S(1)}, bf16[736,128]{1,0:T(8,128)(2,1)S(1)}, u32[]{:S(2)}, u32[]{:S(2)}) collective-permute-start(bf16[736,128]{1,0:T(8,128)(2,1)S(1)} %collective-permute-done.11.upper), channel_id=1, source_target_pairs={{4,0},{8,4},{12,8},{14,12},{10,14},{6,10},{2,6},{0,2},{5,1},{9,5},... | collective-permute-start | bytes 565256 | tf_op jit(solution)/shard_map/ppermute | solution.py:262
  31.4 8.5 %collective-permute-start.4 = (bf16[736,128]{1,0:T(8,128)(2,1)S(1)}, bf16[736,128]{1,0:T(8,128)(2,1)S(1)}, u32[]{:S(2)}, u32[]{:S(2)}) collective-permute-start(bf16[736,128]{1,0:T(8,128)(2,1)S(1)} %collective-permute-done.3.upper), channel_id=1, source_target_pairs={{0,4},{4,8},{8,12},{12,14},{14,10},{10,6},{6,2},{2,0},{1,5},{5,9},... | collective-permute-start | bytes 565256 | tf_op jit(solution)/shard_map/ppermute | solution.py:261
  32.4 8.7 %collective-permute-start.12 = (bf16[720,128]{1,0:T(8,128)(2,1)S(1)}, bf16[720,128]{1,0:T(8,128)(2,1)S(1)}, u32[]{:S(2)}, u32[]{:S(2)}) collective-permute-start(bf16[720,128]{1,0:T(8,128)(2,1)S(1)} %get-tuple-element.86.lower), channel_id=1, source_target_pairs={{4,0},{8,4},{12,8},{14,12},{10,14},{6,10},{2,6},{0,2},{5,1},{9,5},... | collective-permute-start | bytes 552968 | tf_op jit(solution)/shard_map/ppermute | solution.py:258
  35.4 9.1 %collective-permute-start.10 = (bf16[720,128]{1,0:T(8,128)(2,1)S(1)}, bf16[720,128]{1,0:T(8,128)(2,1)S(1)}, u32[]{:S(2)}, u32[]{:S(2)}) collective-permute-start(bf16[720,128]{1,0:T(8,128)(2,1)S(1)} %collective-permute-done.5.lower), channel_id=1, source_target_pairs={{0,4},{4,8},{8,12},{12,14},{14,10},{10,6},{6,2},{2,0},{1,5},{5,9},... | collective-permute-start | bytes 552968 | tf_op jit(solution)/shard_map/ppermute | solution.py:266
  38.8 10.2 %collective-permute-start.16 = (bf16[736,128]{1,0:T(8,128)(2,1)S(1)}, bf16[736,128]{1,0:T(8,128)(2,1)S(1)}, u32[]{:S(2)}, u32[]{:S(2)}) collective-permute-start(bf16[736,128]{1,0:T(8,128)(2,1)S(1)} %collective-permute-done.13.upper), channel_id=1, source_target_pairs={{4,0},{8,4},{12,8},{14,12},{10,14},{6,10},{2,6},{0,2},{5,1},{9,5},... | collective-permute-start | bytes 565256 | tf_op jit(solution)/shard_map/ppermute | solution.py:262
  40.0 9.0 %collective-permute-start.9 = (bf16[736,128]{1,0:T(8,128)(2,1)S(1)}, bf16[736,128]{1,0:T(8,128)(2,1)S(1)}, u32[]{:S(2)}, u32[]{:S(2)}) collective-permute-start(bf16[736,128]{1,0:T(8,128)(2,1)S(1)} %collective-permute-done.4.upper), channel_id=1, source_target_pairs={{0,4},{4,8},{8,12},{12,14},{14,10},{10,6},{6,2},{2,0},{1,5},{5,9},... | collective-permute-start | bytes 565256 | tf_op jit(solution)/shard_map/ppermute | solution.py:261
  41.1 7.4 %collective-permute-start.15 = (bf16[720,128]{1,0:T(8,128)(2,1)S(1)}, bf16[720,128]{1,0:T(8,128)(2,1)S(1)}, u32[]{:S(2)}, u32[]{:S(2)}) collective-permute-start(bf16[720,128]{1,0:T(8,128)(2,1)S(1)} %collective-permute-done.12.lower), channel_id=1, source_target_pairs={{4,0},{8,4},{12,8},{14,12},{10,14},{6,10},{2,6},{0,2},{5,1},{9,5},... | collective-permute-start | bytes 552968 | tf_op jit(solution)/shard_map/ppermute | solution.py:267
  44.5 7.0 %collective-permute-start.14 = (bf16[720,128]{1,0:T(8,128)(2,1)S(1)}, bf16[720,128]{1,0:T(8,128)(2,1)S(1)}, u32[]{:S(2)}, u32[]{:S(2)}) collective-permute-start(bf16[720,128]{1,0:T(8,128)(2,1)S(1)} %collective-permute-done.10.lower), channel_id=1, source_target_pairs={{0,4},{4,8},{8,12},{12,14},{14,10},{10,6},{6,2},{2,0},{1,5},{5,9},... | collective-permute-start | bytes 552968 | tf_op jit(solution)/shard_map/ppermute | solution.py:266
  48.4 5.6 %collective-permute-start.18 = (bf16[720,128]{1,0:T(8,128)(2,1)S(1)}, bf16[720,128]{1,0:T(8,128)(2,1)S(1)}, u32[]{:S(2)}, u32[]{:S(2)}) collective-permute-start(bf16[720,128]{1,0:T(8,128)(2,1)S(1)} %collective-permute-done.15.lower), channel_id=1, source_target_pairs={{4,0},{8,4},{12,8},{14,12},{10,14},{6,10},{2,6},{0,2},{5,1},{9,5},... | collective-permute-start | bytes 552968 | tf_op jit(solution)/shard_map/ppermute | solution.py:267
  56.5 6.7 %collective-permute-start.19 = (bf16[720,128]{1,0:T(8,128)(2,1)S(1)}, bf16[720,128]{1,0:T(8,128)(2,1)S(1)}, u32[]{:S(2)}, u32[]{:S(2)}) collective-permute-start(bf16[720,128]{1,0:T(8,128)(2,1)S(1)} %get-tuple-element.84), channel_id=1, source_target_pairs={{0,4},{4,8},{8,12},{12,14},{14,10},{10,6},{6,2},{2,0},{1,5},{5,9},... | collective-permute-start | bytes 552968 | tf_op jit(solution)/shard_map/ppermute | solution.py:274
  58.1 7.0 %collective-permute-start.17 = (bf16[720,128]{1,0:T(8,128)(2,1)S(1)}, bf16[720,128]{1,0:T(8,128)(2,1)S(1)}, u32[]{:S(2)}, u32[]{:S(2)}) collective-permute-start(bf16[720,128]{1,0:T(8,128)(2,1)S(1)} %get-tuple-element.79), channel_id=1, source_target_pairs={{4,0},{8,4},{12,8},{14,12},{10,14},{6,10},{2,6},{0,2},{5,1},{9,5},... | collective-permute-start | bytes 552968 | tf_op jit(solution)/shard_map/ppermute | solution.py:272
  61.1 8.9 %collective-permute-start.25 = (bf16[720,128]{1,0:T(8,128)(2,1)S(1)}, bf16[720,128]{1,0:T(8,128)(2,1)S(1)}, u32[]{:S(2)}, u32[]{:S(2)}) collective-permute-start(bf16[720,128]{1,0:T(8,128)(2,1)S(1)} %collective-permute-done.18.lower), channel_id=1, source_target_pairs={{4,0},{8,4},{12,8},{14,12},{10,14},{6,10},{2,6},{0,2},{5,1},{9,5},... | collective-permute-start | bytes 552968 | tf_op jit(solution)/shard_map/ppermute | solution.py:267
  62.8 7.3 %collective-permute-start.24 = (bf16[736,128]{1,0:T(8,128)(2,1)S(1)}, bf16[736,128]{1,0:T(8,128)(2,1)S(1)}, u32[]{:S(2)}, u32[]{:S(2)}) collective-permute-start(bf16[736,128]{1,0:T(8,128)(2,1)S(1)} %collective-permute-done.9.upper), channel_id=1, source_target_pairs={{0,4},{4,8},{8,12},{12,14},{14,10},{10,6},{6,2},{2,0},{1,5},{5,9},... | collective-permute-start | bytes 565256 | tf_op jit(solution)/shard_map/ppermute | solution.py:261
  65.2 9.5 %collective-permute-start.22 = (bf16[720,128]{1,0:T(8,128)(2,1)S(1)}, bf16[720,128]{1,0:T(8,128)(2,1)S(1)}, u32[]{:S(2)}, u32[]{:S(2)}) collective-permute-start(bf16[720,128]{1,0:T(8,128)(2,1)S(1)} %add_convert_fusion.9), channel_id=1, source_target_pairs={{0,4},{4,8},{8,12},{12,14},{14,10},{10,6},{6,2},{2,0},{1,5},{5,9},... | collective-permute-start | bytes 552968 | tf_op jit(solution)/shard_map/ppermute | solution.py:281
  67.3 14.8 %collective-permute-start.20 = (bf16[720,128]{1,0:T(8,128)(2,1)S(1)}, bf16[720,128]{1,0:T(8,128)(2,1)S(1)}, u32[]{:S(2)}, u32[]{:S(2)}) collective-permute-start(bf16[720,128]{1,0:T(8,128)(2,1)S(1)} %add_convert_fusion.11), channel_id=1, source_target_pairs={{4,0},{8,4},{12,8},{14,12},{10,14},{6,10},{2,6},{0,2},{5,1},{9,5},... | collective-permute-start | bytes 552968 | tf_op jit(solution)/shard_map/ppermute | solution.py:281
  72.6 6.8 %collective-permute-start.27 = (bf16[720,128]{1,0:T(8,128)(2,1)S(1)}, bf16[720,128]{1,0:T(8,128)(2,1)S(1)}, u32[]{:S(2)}, u32[]{:S(2)}) collective-permute-start(bf16[720,128]{1,0:T(8,128)(2,1)S(1)} %get-tuple-element.99), channel_id=1, source_target_pairs={{0,4},{4,8},{8,12},{12,14},{14,10},{10,6},{6,2},{2,0},{1,5},{5,9},... | collective-permute-start | bytes 552968 | tf_op jit(solution)/shard_map/ppermute | solution.py:276
  74.6 7.2 %collective-permute-start.26 = (bf16[720,128]{1,0:T(8,128)(2,1)S(1)}, bf16[720,128]{1,0:T(8,128)(2,1)S(1)}, u32[]{:S(2)}, u32[]{:S(2)}) collective-permute-start(bf16[720,128]{1,0:T(8,128)(2,1)S(1)} %get-tuple-element.98), channel_id=1, source_target_pairs={{4,0},{8,4},{12,8},{14,12},{10,14},{6,10},{2,6},{0,2},{5,1},{9,5},... | collective-permute-start | bytes 552968 | tf_op jit(solution)/shard_map/ppermute | solution.py:276
  74.7 23.9 %collective-permute-start.23 = (bf16[720,128]{1,0:T(8,128)(2,1)S(1)}, bf16[720,128]{1,0:T(8,128)(2,1)S(1)}, u32[]{:S(2)}, u32[]{:S(2)}) collective-permute-start(bf16[720,128]{1,0:T(8,128)(2,1)S(1)} %add_convert_fusion.8), channel_id=1, source_target_pairs={{0,4},{4,8},{8,12},{12,14},{14,10},{10,6},{6,2},{2,0},{1,5},{5,9},... | collective-permute-start | bytes 552968 | tf_op jit(solution)/shard_map/ppermute | solution.py:281
  81.9 5.8 %collective-permute-start.31 = (bf16[720,128]{1,0:T(8,128)(2,1)S(1)}, bf16[720,128]{1,0:T(8,128)(2,1)S(1)}, u32[]{:S(2)}, u32[]{:S(2)}) collective-permute-start(bf16[720,128]{1,0:T(8,128)(2,1)S(1)} %add_convert_fusion.6), channel_id=1, source_target_pairs={{0,4},{4,8},{8,12},{12,14},{14,10},{10,6},{6,2},{2,0},{1,5},{5,9},... | collective-permute-start | bytes 552968 | tf_op jit(solution)/shard_map/ppermute | solution.py:285
  82.1 16.5 %collective-permute-start.21 = (bf16[720,128]{1,0:T(8,128)(2,1)S(1)}, bf16[720,128]{1,0:T(8,128)(2,1)S(1)}, u32[]{:S(2)}, u32[]{:S(2)}) collective-permute-start(bf16[720,128]{1,0:T(8,128)(2,1)S(1)} %add_convert_fusion.10), channel_id=1, source_target_pairs={{4,0},{8,4},{12,8},{14,12},{10,14},{6,10},{2,6},{0,2},{5,1},{9,5},... | collective-permute-start | bytes 552968 | tf_op jit(solution)/shard_map/ppermute | solution.py:281
  84.1 8.3 %collective-permute-start.28 = (bf16[720,128]{1,0:T(8,128)(2,1)S(1)}, bf16[720,128]{1,0:T(8,128)(2,1)S(1)}, u32[]{:S(2)}, u32[]{:S(2)}) collective-permute-start(bf16[720,128]{1,0:T(8,128)(2,1)S(1)} %add_convert_fusion.7), channel_id=1, source_target_pairs={{4,0},{8,4},{12,8},{14,12},{10,14},{6,10},{2,6},{0,2},{5,1},{9,5},... | collective-permute-start | bytes 552968 | tf_op jit(solution)/shard_map/ppermute | solution.py:285
  87.8 5.6 %collective-permute-start.32 = (bf16[720,128]{1,0:T(8,128)(2,1)S(1)}, bf16[720,128]{1,0:T(8,128)(2,1)S(1)}, u32[]{:S(2)}, u32[]{:S(2)}) collective-permute-start(bf16[720,128]{1,0:T(8,128)(2,1)S(1)} %add_convert_fusion.3), channel_id=1, source_target_pairs={{0,4},{4,8},{8,12},{12,14},{14,10},{10,6},{6,2},{2,0},{1,5},{5,9},... | collective-permute-start | bytes 552968 | tf_op jit(solution)/shard_map/ppermute | solution.py:285
  92.4 5.6 %collective-permute-start.29 = (bf16[720,128]{1,0:T(8,128)(2,1)S(1)}, bf16[720,128]{1,0:T(8,128)(2,1)S(1)}, u32[]{:S(2)}, u32[]{:S(2)}) collective-permute-start(bf16[720,128]{1,0:T(8,128)(2,1)S(1)} %add_convert_fusion.5), channel_id=1, source_target_pairs={{4,0},{8,4},{12,8},{14,12},{10,14},{6,10},{2,6},{0,2},{5,1},{9,5},... | collective-permute-start | bytes 552968 | tf_op jit(solution)/shard_map/ppermute | solution.py:285
  93.4 5.6 %collective-permute-start.33 = (bf16[720,128]{1,0:T(8,128)(2,1)S(1)}, bf16[720,128]{1,0:T(8,128)(2,1)S(1)}, u32[]{:S(2)}, u32[]{:S(2)}) collective-permute-start(bf16[720,128]{1,0:T(8,128)(2,1)S(1)} %add_convert_fusion.2), channel_id=1, source_target_pairs={{0,4},{4,8},{8,12},{12,14},{14,10},{10,6},{6,2},{2,0},{1,5},{5,9},... | collective-permute-start | bytes 552968 | tf_op jit(solution)/shard_map/ppermute | solution.py:285
  98.0 5.6 %collective-permute-start.30 = (bf16[720,128]{1,0:T(8,128)(2,1)S(1)}, bf16[720,128]{1,0:T(8,128)(2,1)S(1)}, u32[]{:S(2)}, u32[]{:S(2)}) collective-permute-start(bf16[720,128]{1,0:T(8,128)(2,1)S(1)} %add_convert_fusion.4), channel_id=1, source_target_pairs={{4,0},{8,4},{12,8},{14,12},{10,14},{6,10},{2,6},{0,2},{5,1},{9,5},... | collective-permute-start | bytes 552968 | tf_op jit(solution)/shard_map/ppermute | solution.py:285

commit v3 on v2

--- a/solution.py
+++ b/solution.py
@@ -50,13 +50,11 @@
     return jnp.concatenate(outs, axis=0)
 
 
-def pack_kernel(place, sink, k, v, q, packed, rim, sems):
-    count, last, width = k.shape[0], k.shape[0] - WINDOW, k.shape[1]
+def pack_kernel(place, sink, gain, k, v, q, packed, gains, sems):
+    count, width = k.shape
     base = 2 * count + BF16_ROWS
     rows = pl.ds(pl.multiple_of((1 - place[0]) * WINDOW, WINDOW), WINDOW)
     moves = [
-        (k.at[last:, :], rim.at[:WINDOW, :]),
-        (v.at[last:, :], rim.at[WINDOW:, :]),
         (k, packed.at[:count, :]),
         (v, packed.at[count : 2 * count, :]),
     ]
@@ -77,35 +75,62 @@
         terms = jnp.where(row == i, term, terms)
         left = left - term
     packed[2 * count : base, :] = terms.astype(BF16)
+    gains[...] = jnp.broadcast_to(gain[...], (WINDOW, gain.shape[1])).T
     for copy in copies:
         copy.wait()
 
 
-def pack(place, sink_logit, key_rows, values, queries):
+def rim_kernel(k, v, rim, sems):
+    last = k.shape[0] - WINDOW
+    copies = [
+        pltpu.make_async_copy(k.at[last:, :], rim.at[:WINDOW, :], sems.at[0]),
+        pltpu.make_async_copy(v.at[last:, :], rim.at[WINDOW:, :], sems.at[1]),
+    ]
+    for copy in copies:
+        copy.start()
+    for copy in copies:
+        copy.wait()
+
+
+def pack_rim(key_rows, values):
+    return pl.pallas_call(
+        rim_kernel,
+        out_shape=jax.ShapeDtypeStruct((2 * WINDOW, key_rows.shape[1]), BF16),
+        in_specs=[ANY, ANY],
+        out_specs=VMEM,
+        scratch_shapes=[pltpu.SemaphoreType.DMA((2,))],
+        cost_estimate=pl.CostEstimate(flops=0, bytes_accessed=4 * key_rows.size, transcendentals=0),
+        compiler_params=pltpu.CompilerParams(vmem_limit_bytes=4 * 2**20),
+        name="rim",
+    )(in_hbm(key_rows), in_hbm(values))
+
+
+def pack(place, sink_logit, norm_gain, key_rows, values, queries):
     rows, width = key_rows.shape
     blocks = queries.shape[1] // width
     return pl.pallas_call(
         pack_kernel,
         out_shape=[
-            jax.ShapeDtypeStruct((n, width), BF16) for n in (2 * rows + BF16_ROWS + blocks * WINDOW, 2 * WINDOW)
+            jax.ShapeDtypeStruct((2 * rows + BF16_ROWS + blocks * WINDOW, width), BF16),
+            jax.ShapeDtypeStruct((norm_gain.shape[0], WINDOW), F32),
         ],
-        in_specs=[SMEM, SMEM, ANY, ANY, ANY],
+        in_specs=[SMEM, SMEM, VMEM, ANY, ANY, ANY],
         out_specs=[VMEM, VMEM],
-        scratch_shapes=[pltpu.SemaphoreType.DMA((4 + blocks,))],
+        scratch_shapes=[pltpu.SemaphoreType.DMA((2 + blocks,))],
         cost_estimate=pl.CostEstimate(flops=0, bytes_accessed=4 * key_rows.size, transcendentals=0),
         compiler_params=pltpu.CompilerParams(vmem_limit_bytes=4 * 2**20),
         name="pack",
-    )(place, sink_logit, in_hbm(key_rows), in_hbm(values), in_hbm(queries))
-
-
-def front_kernel(code_rows, place, packed_a, rim_a, packed_b, *refs):
-    hbm, outs, scratch = refs[:6], refs[6 : 9 if code_rows else 7], refs[9 if code_rows else 7 :]
-    q_a, ow_a, ow_b, resid, routes, codes = hbm
+    )(place, in_hbm(sink_logit), norm_gain[None, :], in_hbm(key_rows), in_hbm(values), in_hbm(queries))
+
+
+def front_kernel(code_rows, place, gains, packed_a, rim_a, packed_b, rim_b, ow_b, *refs):
+    hbm, outs, scratch = refs[:5], refs[5 : 8 if code_rows else 6], refs[8 if code_rows else 6 :]
+    q_a, ow_a, resid, routes, codes = hbm
     core, first = place[0], place[1] == 1
     start = pl.multiple_of(core * WINDOW, WINDOW)
     rows = pl.ds(start, WINDOW)
     held, sems = scratch[:-1], scratch[-1]
-    sources = (q_a.at[rows, :], ow_a, ow_b, resid.at[:, rows], routes.at[:, rows], codes.at[:, rows])
+    sources = (q_a.at[rows, :], ow_a, resid.at[:, rows], routes.at[:, rows], codes.at[:, rows])
     copies = [pltpu.make_async_copy(source, held[i], sems.at[i]) for i, source in enumerate(sources)]
     for copy in copies:
         copy.start()
@@ -114,7 +139,6 @@
     blocks = held[0].shape[1] // width
     base = packed_a.shape[0] - blocks * WINDOW
     count = (base - BF16_ROWS) // 2
-    tail = packed_b.at[packed_a.shape[0] :, :]
     later = pl.ds(pl.multiple_of(count + start, WINDOW), WINDOW)
 
     def attend(packed, rim, q_blocks):
@@ -132,64 +156,71 @@
         return heads_of(q_cols, past, present, sinks, first)
 
     theirs = attend(
-        packed_b, tail, [packed_b[base + j * WINDOW : base + (j + 1) * WINDOW, :] for j in range(blocks)]
+        packed_b, rim_b, [packed_b[base + j * WINDOW : base + (j + 1) * WINDOW, :] for j in range(blocks)]
     )
     copies[0].wait()
     ours = attend(packed_a, rim_a, [held[0][:, j * width : (j + 1) * width] for j in range(blocks)])
-    copies[2].wait()
-    projected = jnp.dot(held[2][...], theirs, preferred_element_type=F32)
+    projected = jnp.dot(ow_b[...], theirs, preferred_element_type=F32)
     copies[1].wait()
     projected += jnp.dot(held[1][...], ours, preferred_element_type=F32)
-    for copy in copies[3:]:
+    for copy in copies[2:]:
         copy.wait()
-    attended = (held[3][...].astype(F32) + projected).astype(BF16)
+    attended = (held[2][...].astype(F32) + projected).astype(BF16)
     outs[0][...] = attended
     if code_rows:
         expert = lax.broadcasted_iota(jnp.int32, (code_rows, WINDOW), 0)
         table = jnp.zeros((code_rows, WINDOW), F32)
         for k in range(TOP):
-            named = jnp.broadcast_to(held[4][k : k + 1, :], expert.shape) == expert
-            table += jnp.where(named, jnp.broadcast_to(held[5][k : k + 1, :], expert.shape).astype(F32), 0.0)
-        outs[1][:code_rows, :] = table.astype(BF16)
-        half = half_of(attended.shape[0])
-        outs[1][code_rows:, :] = attended[:half]
-        outs[2][...] = attended[half:]
-
-
-def front(code_rows, queries, key_rows, values, sink_logit, o_weight, residual, routes, gate_codes):
+            named = jnp.broadcast_to(held[3][k : k + 1, :], expert.shape) == expert
+            table += jnp.where(named, jnp.broadcast_to(held[4][k : k + 1, :], expert.shape).astype(F32), 0.0)
+        widened = attended.astype(F32)
+        spread = jnp.mean(widened * widened, axis=0, keepdims=True)
+        normed = (widened * lax.rsqrt(spread + 1e-05) * gains[...]).astype(BF16)
+        body = normed.shape[0] // WINDOW * WINDOW
+        blocks = [normed[j : j + WINDOW].T for j in range(0, body, WINDOW)]
+        parcel = jnp.concatenate([table.astype(BF16), normed[body:], *blocks], axis=0)
+        outs[1][...] = parcel[: outs[1].shape[0]]
+        outs[2][...] = parcel[outs[1].shape[0] :]
+
+
+def front(code_rows, queries, key_rows, values, sink_logit, o_weight, residual, norm_gain, routes, gate_codes, weights):
     seq, core = lax.axis_index("seq"), lax.axis_index("exp")
     place = jnp.stack([core, jnp.where((seq == 0) & (core == 0), 1, 0)]).astype(jnp.int32)
     ow_b = swapped(o_weight.T)
-    packed, rim = pack(place, sink_logit, key_rows, values, queries)
-    rim_a = lax.ppermute(rim, "seq", [(s, s + 1) for s in range(lax.axis_size("seq") - 1)])
-    packed_b = swapped(jnp.concatenate([packed, rim_a], axis=0))
+    steps = [(s, s + 1) for s in range(lax.axis_size("seq") - 1)]
+    rim = pack_rim(key_rows, values)
+    rim_a = lax.ppermute(rim, "seq", steps)
+    packed, gains = pack(place, sink_logit, norm_gain, key_rows, values, queries)
+    packed, rim_a = after(packed, rim_a)
+    packed_b, rim_b = swapped(packed), swapped(rim_a)
+    weights, rim_b = after(weights, rim_b)
     features, block = residual.shape[1], residual.shape[0] // lax.axis_size("exp")
     half = half_of(features)
     shapes = [(features, block)] + ([(code_rows + half, block), (features - half, block)] if code_rows else [])
-    held = [queries[:WINDOW], o_weight.T, o_weight.T]
+    held = [queries[:WINDOW], o_weight.T]
     held += [residual.T[:, :WINDOW], routes.T[:, :WINDOW], gate_codes.T[:, :WINDOW]]
     outs = pl.pallas_call(
         functools.partial(front_kernel, code_rows),
         out_shape=[jax.ShapeDtypeStruct(shape, BF16) for shape in shapes],
-        in_specs=[SMEM] + [VMEM] * 3 + [ANY] * 6,
+        in_specs=[SMEM] + [VMEM] * 6 + [ANY] * 5,
         out_specs=[VMEM] * len(shapes),
         scratch_shapes=[pltpu.VMEM(h.shape, h.dtype) for h in held] + [pltpu.SemaphoreType.DMA((len(held),))],
         cost_estimate=pl.CostEstimate(flops=2 * 10**9, bytes_accessed=10**7, transcendentals=10**6),
         compiler_params=pltpu.CompilerParams(vmem_limit_bytes=20 * 2**20),
         name="front",
     )(
-        place, packed, rim_a, packed_b, in_hbm(queries), in_hbm(o_weight.T), in_hbm(ow_b),
+        place, gains, packed, rim_a, packed_b, rim_b, in_vmem(ow_b), in_hbm(queries), in_hbm(o_weight.T),
         in_hbm(residual.T), in_hbm(routes.T), in_hbm(gate_codes.T),
     )
-    return outs, packed_b[:BF16_ROWS]
+    return outs, weights
 
 
 def swapped(value):
     return lax.ppermute(value, "exp", [(0, 1), (1, 0)])
 
 
-def after(value, *earlier):
-    return lax.optimization_barrier((value, *earlier))[0]
+def after(value, earlier):
+    return lax.optimization_barrier((value, earlier))
 
 
 def rms_norm(stream, norm_gain):
@@ -198,9 +229,14 @@
     return (widened * lax.rsqrt(spread + 1e-05) * norm_gain).astype(BF16)
 
 
-def expert_kernel(code_rows, place, gain, upper, lower, *refs):
+def expert_kernel(code_rows, place, upper, lower, *refs):
     weights, (out_upper, out_lower) = refs[:6], refs[6:]
-    rows = rms_norm(jnp.concatenate([upper[code_rows:, :], lower[...]], axis=0).T, gain[...])
+    parcel = jnp.concatenate([upper[...], lower[...]], axis=0)
+    body = (parcel.shape[0] - code_rows) // WINDOW * WINDOW
+    head = parcel.shape[0] - body
+    blocks = [parcel[j : j + WINDOW] for j in range(head, head + body, WINDOW)]
+    over = parcel[:head].T
+    rows = jnp.concatenate([*blocks, over[:, code_rows:]], axis=1)
     total = None
     for w_gate, w_up, w_down in (weights[:3], weights[3:]):
         gate_val = jnp.dot(rows, w_gate[...], preferred_element_type=F32)
@@ -208,28 +244,53 @@
         hidden = swiglu(gate_val, up_val).astype(BF16)
         term = jnp.dot(hidden, w_down[...], preferred_element_type=F32)
         total = term if total is None else total + term
-    codes = upper[:code_rows, :].astype(F32)
-    mine = lax.broadcasted_iota(jnp.int32, codes.shape, 0) == place[0]
-    code = jnp.sum(jnp.where(mine, codes, 0.0), axis=0, keepdims=True)
-    term = (total.T * (code / jnp.sum(codes, axis=0, keepdims=True))).astype(BF16)
+    codes = over[:, :code_rows].astype(F32)
+    mine = lax.broadcasted_iota(jnp.int32, codes.shape, 1) == place[0]
+    code = jnp.sum(jnp.where(mine, codes, 0.0), axis=1, keepdims=True)
+    terms = (total * (code / jnp.sum(codes, axis=1, keepdims=True))).astype(BF16)
+    blocks = [terms[:, j : j + WINDOW] for j in range(0, body, WINDOW)]
+    terms = jnp.concatenate([terms[:, body:].T, *blocks], axis=0)
     half = out_upper.shape[0]
-    out_upper[...] = term[:half]
-    out_lower[...] = term[half:]
-
-
-def expert_terms(code_rows, expert, gain, weights, parcel):
-    features = gain.shape[1]
-    half = half_of(features)
-    flops = 2 * WINDOW * features * 3 * 2 * weights[0].shape[1]
+    out_upper[...] = terms[:half]
+    out_lower[...] = terms[half:]
+
+
+def expert_terms(code_rows, expert, weights, parcel):
+    half, rest = parcel[0].shape[0] - code_rows, parcel[1].shape[0]
     return pl.pallas_call(
         functools.partial(expert_kernel, code_rows),
-        out_shape=[jax.ShapeDtypeStruct((n, WINDOW), BF16) for n in (half, features - half)],
-        in_specs=[SMEM] + [VMEM] * 9,
+        out_shape=[jax.ShapeDtypeStruct((n, WINDOW), BF16) for n in (half, rest)],
+        in_specs=[SMEM] + [VMEM] * 8,
         out_specs=[VMEM] * 2,
-        cost_estimate=pl.CostEstimate(flops=flops, bytes_accessed=10**6, transcendentals=10**5),
+        cost_estimate=pl.CostEstimate(flops=1, bytes_accessed=1, transcendentals=0),
         compiler_params=pltpu.CompilerParams(vmem_limit_bytes=24 * 2**20),
         name="experts",
-    )(expert, gain, *parcel, *weights)
+    )(expert, *parcel, *weights)
+
+
+def total_kernel(*refs):
+    uppers, lowers, out = refs[:3], refs[3:6], refs[6]
+    summed = [sum(ref[...].astype(F32) for ref in half) for half in (uppers, lowers)]
+    summed = jnp.concatenate(summed, axis=0).astype(BF16)
+    head = summed.shape[0] % WINDOW
+    body = summed.shape[0] - head
+    for j in range(0, body, WINDOW):
+        out[j : j + WINDOW, :] = summed[head + j : head + j + WINDOW].T
+    if head:
+        out[body:, :] = summed[:head]
+
+
+def total_of(uppers, lowers):
+    features = uppers[0].shape[0] + lowers[0].shape[0]
+    return pl.pallas_call(
+        total_kernel,
+        out_shape=jax.ShapeDtypeStruct((features, WINDOW), BF16),
+        in_specs=[VMEM] * 6,
+        out_specs=VMEM,
+        cost_estimate=pl.CostEstimate(flops=1, bytes_accessed=1, transcendentals=0),
+        compiler_params=pltpu.CompilerParams(vmem_limit_bytes=16 * 2**20),
+        name="total",
+    )(*uppers, *lowers)
 
 
 def half_of(features):
@@ -246,47 +307,60 @@
     return (a.astype(F32) + b.astype(F32)).astype(BF16)
 
 
-def mixed_by_ring(parcel, code_rows, gain, weights):
+def mixed_by_ring(parcel, code_rows, weights):
     count = lax.axis_size("seq")
     right, left = ring_of(count)
     far = count // 2
     expert = lax.axis_index("seq").astype(jnp.int32)[None]
     to_right = functools.partial(lax.ppermute, axis_name="seq", perm=right)
     to_left = functools.partial(lax.ppermute, axis_name="seq", perm=left)
-    apply = functools.partial(expert_terms, code_rows, expert, gain, weights)
+    apply = functools.partial(expert_terms, code_rows, expert, weights)
     at = {0: parcel}
     at[-1], at[1] = [to_right(half) for half in parcel], [to_left(half) for half in parcel]
-    terms, waited = {}, ()
+    terms = {}
+
+    def work(k, arrived):
+        at[k], arrived = after(at[k], arrived)
+        terms[k] = apply(at[k])
+        return arrived
+
+    last = None
     for k in range(2, far + 1):
-        upper_left = to_right(after(at[1 - k][0], *waited))
-        upper_right = to_left(after(at[k - 1][0], *waited)) if k < far else None
+        uppers, lowers = (at[1 - k][0], at[k - 1][0]), (at[1 - k][1], at[k - 1][1])
+        if last is not None:
+            uppers, terms[last] = after(uppers, terms[last])
+        upper_left = to_right(uppers[0])
+        upper_right = to_left(uppers[1]) if k < far else None
         if k > 2:
-            terms[k - 2] = apply(after(at[k - 2], *at[1 - k][:1], *at[k - 1][:1]))
-            waited = terms[k - 2]
-        lower_left = to_right(after(at[1 - k][1], *waited)) if k < far else None
-        lower_right = to_left(after(at[k - 1][1], *waited))
-        terms[1 - k] = apply(after(at[1 - k], *waited))
-        waited = terms[1 - k]
-        at[-k], at[k] = [upper_left, lower_left], [upper_right, lower_right]
-    opposite = [at[-far][0], at[far][1]]
+            uppers = work(k - 2, uppers)
+            lowers, terms[k - 2] = after(lowers, terms[k - 2])
+        lower_left = to_right(lowers[0]) if k < far else None
+        lower_right = to_left(lowers[1])
+        at[1 - k], at[k - 1] = (uppers[0], lowers[0]), (uppers[1], lowers[1])
+        if k < far:
+            last = 1 - k
+            terms[last] = apply(at[last])
+        at[-k], at[k] = (upper_left, lower_left), (upper_right, lower_right)
+    opposite = (at[-far][0], at[far][1])
+    terms[far - 1] = apply(at[far - 1])
+    right_low = to_right(terms[far - 1][1])
+    terms[far - 1] = work(1 - far, terms[far - 1])
     left_up = to_left(terms[1 - far][0])
-    terms[far - 1] = apply(after(at[far - 1], *waited))
-    right_low = to_right(terms[far - 1][1])
-    farthest = apply(after(opposite, *terms[far - 1]))
+    opposite, terms[1 - far] = after(opposite, terms[1 - far])
+    farthest = apply(opposite)
+    farthest = work(0, farthest)
     right_up, left_low = to_right(farthest[0]), to_left(farthest[1])
-    terms[0] = apply(after(parcel, left_up, right_low))
+    (left_up, right_low), terms[0] = after((left_up, right_low), terms[0])
     for k in range(far - 1, 0, -1):
         if k > 1:
-            going = add(terms[1 - k][0], left_up), add(terms[k - 1][1], right_low)
-            left_up, right_low = to_left(going[0]), to_right(going[1])
-        going = add(terms[-k][1], left_low), add(terms[k][0], right_up)
-        if k == far - 1:
-            going = after(going, *terms[0])
-        left_low, right_up = to_left(going[0]), to_right(going[1])
-    near, left_up, right_low = after((terms[0], left_up, right_low), left_low, right_up)
-    upper = near[0].astype(F32) + left_up.astype(F32) + right_up.astype(F32)
-    lower = near[1].astype(F32) + left_low.astype(F32) + right_low.astype(F32)
-    return jnp.concatenate([upper, lower], axis=0).astype(BF16)
+            left_up = to_left(add(terms[1 - k][0], left_up))
+            right_low = to_right(add(terms[k - 1][1], right_low))
+        left_low = to_left(add(terms[-k][1], left_low))
+        right_up = to_right(add(terms[k][0], right_up))
+    near, final = after((terms[0], left_up, right_low), (left_low, right_up))
+    (upper, lower), left_up, right_low = near
+    left_low, right_up = final
+    return total_of((upper, left_up, right_up), (lower, left_low, right_low))
 
 
 def pack_rows(normed, expert_ids, gate_codes, expert_count, capacity):
@@ -343,18 +417,19 @@
     expert_count = w_gate.shape[0] * lax.axis_size("seq")
     capacity = max(2, 2 * block_rows * TOP // expert_count)
     weights = (w_gate[0], w_up[0], w_down[0])
-    attention = (queries, key_rows, values, sink_logit, o_weight, residual, routes, gate_codes)
+    attention = (queries, key_rows, values, sink_logit, o_weight, residual, norm_gain, routes, gate_codes)
     if capacity < block_rows:
-        (attended,), _ = front(0, *attention)
+        (attended,), weights = front(0, *attention, weights)
         attended = attended.T
         normed = rms_norm(attended, norm_gain)
         return (attended, mixed_by_packing(normed, routes, gate_codes, weights, expert_count, capacity))
     code_rows = -(-expert_count // BF16_ROWS) * BF16_ROWS
-    (attended, *parcel), arrived = front(code_rows, *attention)
-    gate_b, up_b = (swapped(after(weight, arrived)) for weight in weights[:2])
-    down_b = swapped(after(weights[2], gate_b, up_b, attended))
+    (attended, *parcel), weights = front(code_rows, *attention, weights)
+    gate_b, up_b = swapped(weights[0]), swapped(weights[1])
+    down, parcel = after(weights[2], parcel)
+    down_b = swapped(down)
     weights = [in_vmem(weight) for weight in (*weights, gate_b, up_b, down_b)]
-    return (attended.T, mixed_by_ring(parcel, code_rows, norm_gain[None, :], weights).T)
+    return (attended.T, mixed_by_ring(parcel, code_rows, weights).T)
 
 
 def solution(mesh):

time: 105 us -> 89.9 us (0.86)
  waiting for transfers between devices: 33.4 us -> 22.7 us
  local copies, waits for them, and re-layouts: 2.25 us -> 0.72 us
  Pallas kernels: 28.8 us -> 27.7 us
    ppermute x2, waiting for transfers between devices: 4.98 us -> 0.94 us  [mixed_by_ring(): right_up, left_low = (to_right(farthest[0]), to_left(farthest[1]))]
    ppermute x2, starting transfers between devices: 3.6 us -> 0.01 us  [mixed_by_ring(): to_left(half)]
    ppermute x2, waiting for transfers between devices: 3.22 us -> 0.07 us  [mixed_by_ring(): to_left(half)]
    ppermute x21, waiting for transfers between devices: 19 us -> 15.9 us  [the longest x3 9.41 us: mixed_by_ring(): right_up = to_right(add(terms[k][0], right_up))]
    pallas_call x8, Pallas kernels: 20 us -> 17.7 us  [expert_terms(): pl.pallas_call(functools.partial(expert_kernel, code_rows), out_shape=[ja...]
    unnamed x12 -> x6, local copies, waits for them, and re-layouts: 2.24 us -> 0.01 us
    pallas_call x1 -> x3, Pallas kernels: 1.62 us -> 3.57 us  [the longest x1 1.84 us: pack(): pl.pallas_call(pack_kernel, out_shape=[jax.ShapeDtypeStruct((2 * rows + B...]
    ppermute x2, waiting for transfers between devices: 2.5 us -> 4.45 us  [mixed_by_ring(): to_right(half)]
  transfers between devices with their start and end apart: 34 -> 35, of which waited for: 15 -> 11; matrix products, arithmetic and copies ran while one was open for 1% -> 1% of each run, Pallas kernels for 25% -> 30%
where the time goes in v3:
time: 89.9 us; the launch traced here: 89.6 us
  starting transfers between devices  37.1 us (41%)
  Pallas kernels  27.7 us (31%)
  waiting for transfers between devices  22.7 us (25%)
    pallas_call x8, Pallas kernels, expert_terms(): pl.pallas_call(functools.partial(expert_kernel, code_rows), out_shape=[ja...  17.7 us
    ppermute x3, waiting for transfers between devices, mixed_by_ring(): right_up = to_right(add(terms[k][0], right_up))  9.41 us
    pallas_call x1, Pallas kernels, front(): pl.pallas_call(functools.partial(front_kernel, code_rows), out_shape=[jax...  6.44 us
    ppermute x3, starting transfers between devices, mixed_by_ring(): upper_left = to_right(uppers[0])  5.87 us
    ppermute x3, starting transfers between devices, mixed_by_ring(): right_up = to_right(add(terms[k][0], right_up))  4.99 us
    ppermute x2, starting transfers between devices, mixed_by_ring(): to_right(half)  4.67 us
    ppermute x2, waiting for transfers between devices, mixed_by_ring(): to_right(half)  4.45 us
    ppermute x1, starting transfers between devices, front(): rim_a = lax.ppermute(rim, 'seq', steps)  4.44 us
  transfers between devices with their start and end apart: 35, of which 11 were waited for; matrix products, arithmetic and copies ran while one was open for 1% of the time, Pallas kernels for 30%

profile of v3, /device:TPU:0, one launch (start us, length us, event | category | flops | bytes accessed | tf_op | source)
XLA Modules:
  0.0 89.6 jit_solution(9602669990065399542)
XLA Ops:
  0.6 0.5 collective-permute-start.3
  1.1 0.8 rim.1
  1.9 4.4 %collective-permute-start = (bf16[256,128]{1,0:T(8,128)(2,1)S(1)}, bf16[256,128]{1,0:T(8,128)(2,1)S(1)}, u32[]{:S(2)}, u32[]{:S(2)}) collective-permute-start(bf16[256,128]{1,0:T(8,128)(2,1)S(1)} %rim.1), channel_id=1, source_target_pairs={{0,2},{2,4},{4,6},{6,8},{8,10},{10,12},{12,14},{1,3},{3,5},{5,7},{... | collective-permute-start | bytes 196616 | tf_op jit(solution)/shard_map/ppermute | solution.py:192
  6.4 0.7 broadcast_in_dim.6.gain
  7.2 1.8 %pack.1 = (bf16[1552,128]{1,0:T(8,128)(2,1)S(1)}, f32[1440,128]{1,0:T(8,128)S(1)}) custom-call(s32[2]{0:T(128)S(1)} %pad_add_fusion.place, f32[16]{0:T(128)} %sink.1, f32[1,1440]{1,0:T(1,128)S(1)} %broadcast_in_dim.6.gain, bf16[256,128]{1,0:T(8,128)(2,1)} %k.3, bf16[256,128]{1,0:T(8,128)(2,1)} %v.3, bf16[256,1024]{1,0:T(8,128)(2,1)} %refs_0_.1), custom_call_target="tpu_custom_call" | custom-call | bytes 131072 | tf_op jit(solution)/shard_map/pack/pallas_call | solution.py:111
  9.6 1.3 %collective-permute-done.2.rim_b = bf16[256,128]{1,0:T(8,128)(2,1)S(1)} collective-permute-done((bf16[256,128]{1,0:T(8,128)(2,1)S(1)}, bf16[256,128]{1,0:T(8,128)(2,1)S(1)}, u32[]{:S(2)}, u32[]{:S(2)}) %collective-permute-start.2) | collective-permute-done | bytes 65568 | tf_op jit(solution)/shard_map/ppermute | solution.py:219
  11.5 6.4 %front.1 = (bf16[1440,128]{1,0:T(8,128)(2,1)}, bf16[736,128]{1,0:T(8,128)(2,1)S(1)}, bf16[720,128]{1,0:T(8,128)(2,1)S(1)}) custom-call(s32[2]{0:T(128)S(1)} %pad_add_fusion.place, f32[1440,128]{1,0:T(8,128)S(1)} %get-tuple-element.76.gains, bf16[1552,128]{1,0:T(8,128)(2,1)S(1)} %get-tuple-element.78.packed_a, ...), custom_call_target="tpu_custom_call" | custom-call | flops 2000000000 | bytes 10000000 | tf_op jit(solution)/shard_map/front/pallas_call | solution.py:202
  18.2 2.6 %collective-permute-start.6 = (bf16[736,128]{1,0:T(8,128)(2,1)S(1)}, bf16[736,128]{1,0:T(8,128)(2,1)S(1)}, u32[]{:S(2)}, u32[]{:S(2)}) collective-permute-start(bf16[736,128]{1,0:T(8,128)(2,1)S(1)} %get-tuple-element.124.upper), channel_id=1, source_target_pairs={{0,4},{4,8},{8,12},{12,14},{14,10},{10,6},{6,2},{2,0},{1,5},{5,9},... | collective-permute-start | bytes 565256 | tf_op jit(solution)/shard_map/ppermute | solution.py:319
  20.9 2.0 %collective-permute-start.9 = (bf16[720,128]{1,0:T(8,128)(2,1)S(1)}, bf16[720,128]{1,0:T(8,128)(2,1)S(1)}, u32[]{:S(2)}, u32[]{:S(2)}) collective-permute-start(bf16[720,128]{1,0:T(8,128)(2,1)S(1)} %get-tuple-element.125.lower), channel_id=1, source_target_pairs={{0,4},{4,8},{8,12},{12,14},{14,10},{10,6},{6,2},{2,0},{1,5},{5,9},... | collective-permute-start | bytes 552968 | tf_op jit(solution)/shard_map/ppermute | solution.py:319
  22.9 3.0 %collective-permute-done.6.upper = bf16[736,128]{1,0:T(8,128)(2,1)S(1)} collective-permute-done((bf16[736,128]{1,0:T(8,128)(2,1)S(1)}, bf16[736,128]{1,0:T(8,128)(2,1)S(1)}, u32[]{:S(2)}, u32[]{:S(2)}) %collective-permute-start.6) | collective-permute-done | bytes 188448 | tf_op jit(solution)/shard_map/ppermute | solution.py:319
  25.9 2.5 %collective-permute-start.7 = (bf16[736,128]{1,0:T(8,128)(2,1)S(1)}, bf16[736,128]{1,0:T(8,128)(2,1)S(1)}, u32[]{:S(2)}, u32[]{:S(2)}) collective-permute-start(bf16[736,128]{1,0:T(8,128)(2,1)S(1)} %collective-permute-done.6.upper), channel_id=1, source_target_pairs={{0,4},{4,8},{8,12},{12,14},{14,10},{10,6},{6,2},{2,0},{1,5},{5,9},... | collective-permute-start | bytes 565256 | tf_op jit(solution)/shard_map/ppermute | solution.py:332
  28.4 1.4 %collective-permute-done.9.lower = bf16[720,128]{1,0:T(8,128)(2,1)S(1)} collective-permute-done((bf16[720,128]{1,0:T(8,128)(2,1)S(1)}, bf16[720,128]{1,0:T(8,128)(2,1)S(1)}, u32[]{:S(2)}, u32[]{:S(2)}) %collective-permute-start.9) | collective-permute-done | bytes 184352 | tf_op jit(solution)/shard_map/ppermute | solution.py:319
  29.9 2.5 %collective-permute-start.13 = (bf16[720,128]{1,0:T(8,128)(2,1)S(1)}, bf16[720,128]{1,0:T(8,128)(2,1)S(1)}, u32[]{:S(2)}, u32[]{:S(2)}) collective-permute-start(bf16[720,128]{1,0:T(8,128)(2,1)S(1)} %collective-permute-done.9.lower), channel_id=1, source_target_pairs={{0,4},{4,8},{8,12},{12,14},{14,10},{10,6},{6,2},{2,0},{1,5},{5,9},... | collective-permute-start | bytes 552968 | tf_op jit(solution)/shard_map/ppermute | solution.py:337
  32.4 2.2 %experts.8 = (bf16[720,128]{1,0:T(8,128)(2,1)S(1)}, bf16[720,128]{1,0:T(8,128)(2,1)S(1)}) custom-call(s32[1]{0:T(128)} %bitcast.10.place, bf16[736,128]{1,0:T(8,128)(2,1)S(1)} %collective-permute-done.6.upper, bf16[720,128]{1,0:T(8,128)(2,1)S(1)} %collective-permute-done.9.lower, bf16[1440,720]{1,0:T(8,128)(2,1)S(1)} %bitcast.13, ...), custom_call_target="tpu_custom_call" | custom-call | flops 1 | bytes 1 | tf_op jit(solution)/shard_map/experts/pallas_call | solution.py:260
  34.6 1.8 %collective-permute-done.8.upper = bf16[736,128]{1,0:T(8,128)(2,1)S(1)} collective-permute-done((bf16[736,128]{1,0:T(8,128)(2,1)S(1)}, bf16[736,128]{1,0:T(8,128)(2,1)S(1)}, u32[]{:S(2)}, u32[]{:S(2)}) %collective-permute-start.8) | collective-permute-done | bytes 188448 | tf_op jit(solution)/shard_map/ppermute | solution.py:333
  36.4 1.6 %collective-permute-start.15 = (bf16[736,128]{1,0:T(8,128)(2,1)S(1)}, bf16[736,128]{1,0:T(8,128)(2,1)S(1)}, u32[]{:S(2)}, u32[]{:S(2)}) collective-permute-start(bf16[736,128]{1,0:T(8,128)(2,1)S(1)} %collective-permute-done.7.upper), channel_id=1, source_target_pairs={{0,4},{4,8},{8,12},{12,14},{14,10},{10,6},{6,2},{2,0},{1,5},{5,9},... | collective-permute-start | bytes 565256 | tf_op jit(solution)/shard_map/ppermute | solution.py:332
  38.0 0.4 collective-permute-start.16
  38.5 2.2 %experts.9 = (bf16[720,128]{1,0:T(8,128)(2,1)S(1)}, bf16[720,128]{1,0:T(8,128)(2,1)S(1)}) custom-call(s32[1]{0:T(128)} %bitcast.10.place, bf16[736,128]{1,0:T(8,128)(2,1)S(1)} %collective-permute-done.4.upper, bf16[720,128]{1,0:T(8,128)(2,1)S(1)} %collective-permute-done.5.lower, bf16[1440,720]{1,0:T(8,128)(2,1)S(1)} %bitcast.14, ...), custom_call_target="tpu_custom_call" | custom-call | flops 1 | bytes 1 | tf_op jit(solution)/shard_map/experts/pallas_call | solution.py:260
  40.6 1.6 %collective-permute-start.17 = (bf16[720,128]{1,0:T(8,128)(2,1)S(1)}, bf16[720,128]{1,0:T(8,128)(2,1)S(1)}, u32[]{:S(2)}, u32[]{:S(2)}) collective-permute-start(bf16[720,128]{1,0:T(8,128)(2,1)S(1)} %collective-permute-done.13.lower), channel_id=1, source_target_pairs={{0,4},{4,8},{8,12},{12,14},{14,10},{10,6},{6,2},{2,0},{1,5},{5,9},... | collective-permute-start | bytes 552968 | tf_op jit(solution)/shard_map/ppermute | solution.py:337
  42.3 0.4 collective-permute-start.18
  42.7 2.2 %experts.10 = (bf16[720,128]{1,0:T(8,128)(2,1)S(1)}, bf16[720,128]{1,0:T(8,128)(2,1)S(1)}) custom-call(s32[1]{0:T(128)} %bitcast.10.place, bf16[736,128]{1,0:T(8,128)(2,1)S(1)} %collective-permute-done.7.upper, bf16[720,128]{1,0:T(8,128)(2,1)S(1)} %collective-permute-done.13.lower, bf16[1440,720]{1,0:T(8,128)(2,1)S(1)} %bitcast.15, ...), custom_call_target="tpu_custom_call" | custom-call | flops 1 | bytes 1 | tf_op jit(solution)/shard_map/experts/pallas_call | solution.py:260
  45.0 1.8 %collective-permute-start.21 = (bf16[736,128]{1,0:T(8,128)(2,1)S(1)}, bf16[736,128]{1,0:T(8,128)(2,1)S(1)}, u32[]{:S(2)}, u32[]{:S(2)}) collective-permute-start(bf16[736,128]{1,0:T(8,128)(2,1)S(1)} %collective-permute-done.15.upper), channel_id=1, source_target_pairs={{0,4},{4,8},{8,12},{12,14},{14,10},{10,6},{6,2},{2,0},{1,5},{5,9},... | collective-permute-start | bytes 565256 | tf_op jit(solution)/shard_map/ppermute | solution.py:332
  46.8 2.2 %experts.11 = (bf16[720,128]{1,0:T(8,128)(2,1)S(1)}, bf16[720,128]{1,0:T(8,128)(2,1)S(1)}) custom-call(s32[1]{0:T(128)} %bitcast.10.place, bf16[736,128]{1,0:T(8,128)(2,1)S(1)} %collective-permute-done.8.upper, bf16[720,128]{1,0:T(8,128)(2,1)S(1)} %collective-permute-done.14.lower, bf16[1440,720]{1,0:T(8,128)(2,1)S(1)} %bitcast.16, ...), custom_call_target="tpu_custom_call" | custom-call | flops 1 | bytes 1 | tf_op jit(solution)/shard_map/experts/pallas_call | solution.py:260
  49.0 0.5 collective-permute-start.22
  49.5 2.2 %experts.12 = (bf16[720,128]{1,0:T(8,128)(2,1)S(1)}, bf16[720,128]{1,0:T(8,128)(2,1)S(1)}) custom-call(s32[1]{0:T(128)} %bitcast.10.place, bf16[736,128]{1,0:T(8,128)(2,1)S(1)} %collective-permute-done.16.upper, bf16[720,128]{1,0:T(8,128)(2,1)S(1)} %collective-permute-done.18.lower, bf16[1440,720]{1,0:T(8,128)(2,1)S(1)} %bitcast.17, ...), custom_call_target="tpu_custom_call" | custom-call | flops 1 | bytes 1 | tf_op jit(solution)/shard_map/experts/pallas_call | solution.py:260
  51.7 2.2 %experts.13 = (bf16[720,128]{1,0:T(8,128)(2,1)S(1)}, bf16[720,128]{1,0:T(8,128)(2,1)S(1)}) custom-call(s32[1]{0:T(128)} %bitcast.10.place, bf16[736,128]{1,0:T(8,128)(2,1)S(1)} %collective-permute-done.15.upper, bf16[720,128]{1,0:T(8,128)(2,1)S(1)} %collective-permute-done.17.lower, bf16[1440,720]{1,0:T(8,128)(2,1)S(1)} %bitcast.18, ...), custom_call_target="tpu_custom_call" | custom-call | flops 1 | bytes 1 | tf_op jit(solution)/shard_map/experts/pallas_call | solution.py:260
  53.9 2.0 %collective-permute-start.20 = (bf16[720,128]{1,0:T(8,128)(2,1)S(1)}, bf16[720,128]{1,0:T(8,128)(2,1)S(1)}, u32[]{:S(2)}, u32[]{:S(2)}) collective-permute-start(bf16[720,128]{1,0:T(8,128)(2,1)S(1)} %get-tuple-element.115), channel_id=1, source_target_pairs={{0,4},{4,8},{8,12},{12,14},{14,10},{10,6},{6,2},{2,0},{1,5},{5,9},... | collective-permute-start | bytes 552968 | tf_op jit(solution)/shard_map/ppermute | solution.py:346
  55.9 2.2 %experts.14 = (bf16[720,128]{1,0:T(8,128)(2,1)S(1)}, bf16[720,128]{1,0:T(8,128)(2,1)S(1)}) custom-call(s32[1]{0:T(128)} %bitcast.10.place, bf16[736,128]{1,0:T(8,128)(2,1)S(1)} %collective-permute-done.21.upper, bf16[720,128]{1,0:T(8,128)(2,1)S(1)} %collective-permute-done.22.lower, bf16[1440,720]{1,0:T(8,128)(2,1)S(1)} %bitcast.19, ...), custom_call_target="tpu_custom_call" | custom-call | flops 1 | bytes 1 | tf_op jit(solution)/shard_map/experts/pallas_call | solution.py:260
  58.1 1.6 %collective-permute-start.31 = (bf16[720,128]{1,0:T(8,128)(2,1)S(1)}, bf16[720,128]{1,0:T(8,128)(2,1)S(1)}, u32[]{:S(2)}, u32[]{:S(2)}) collective-permute-start(bf16[720,128]{1,0:T(8,128)(2,1)S(1)} %get-tuple-element.143), channel_id=1, source_target_pairs={{0,4},{4,8},{8,12},{12,14},{14,10},{10,6},{6,2},{2,0},{1,5},{5,9},... | collective-permute-start | bytes 552968 | tf_op jit(solution)/shard_map/ppermute | solution.py:352
  59.7 0.4 collective-permute-start.27
  60.2 2.3 %experts.15 = (bf16[720,128]{1,0:T(8,128)(2,1)S(1)}, bf16[720,128]{1,0:T(8,128)(2,1)S(1)}) custom-call(s32[1]{0:T(128)} %bitcast.10.place, bf16[736,128]{1,0:T(8,128)(2,1)S(1)} %get-tuple-element.124.upper, bf16[720,128]{1,0:T(8,128)(2,1)S(1)} %get-tuple-element.125.lower, bf16[1440,720]{1,0:T(8,128)(2,1)S(1)} %bitcast.20, bf16[1440,720]{1,0:T(8,128)(2,1)S(1)} %bitcast.29, ...), custom_call_target="tpu_custom_call" | custom-call | flops 1 | bytes 1 | tf_op jit(solution)/shard_map/experts/pallas_call | solution.py:260
  62.5 1.6 %collective-permute-start.25 = (bf16[720,128]{1,0:T(8,128)(2,1)S(1)}, bf16[720,128]{1,0:T(8,128)(2,1)S(1)}, u32[]{:S(2)}, u32[]{:S(2)}) collective-permute-start(bf16[720,128]{1,0:T(8,128)(2,1)S(1)} %add_convert_fusion.7), channel_id=1, source_target_pairs={{0,4},{4,8},{8,12},{12,14},{14,10},{10,6},{6,2},{2,0},{1,5},{5,9},... | collective-permute-start | bytes 552968 | tf_op jit(solution)/shard_map/ppermute | solution.py:357
  64.2 0.5 collective-permute-start.23
  64.7 0.9 %collective-permute-done.31 = bf16[720,128]{1,0:T(8,128)(2,1)S(1)} collective-permute-done((bf16[720,128]{1,0:T(8,128)(2,1)S(1)}, bf16[720,128]{1,0:T(8,128)(2,1)S(1)}, u32[]{:S(2)}, u32[]{:S(2)}) %collective-permute-start.31) | collective-permute-done | bytes 184352 | tf_op jit(solution)/shard_map/ppermute | solution.py:352
  65.7 1.6 %collective-permute-start.32 = (bf16[720,128]{1,0:T(8,128)(2,1)S(1)}, bf16[720,128]{1,0:T(8,128)(2,1)S(1)}, u32[]{:S(2)}, u32[]{:S(2)}) collective-permute-start(bf16[720,128]{1,0:T(8,128)(2,1)S(1)} %add_convert_fusion.2), channel_id=1, source_target_pairs={{0,4},{4,8},{8,12},{12,14},{14,10},{10,6},{6,2},{2,0},{1,5},{5,9},... | collective-permute-start | bytes 552968 | tf_op jit(solution)/shard_map/ppermute | solution.py:359
  67.4 0.5 collective-permute-start.28
  67.9 2.3 %collective-permute-done.25 = bf16[720,128]{1,0:T(8,128)(2,1)S(1)} collective-permute-done((bf16[720,128]{1,0:T(8,128)(2,1)S(1)}, bf16[720,128]{1,0:T(8,128)(2,1)S(1)}, u32[]{:S(2)}, u32[]{:S(2)}) %collective-permute-start.25) | collective-permute-done | bytes 184352 | tf_op jit(solution)/shard_map/ppermute | solution.py:357
  70.2 1.6 %collective-permute-start.26 = (bf16[720,128]{1,0:T(8,128)(2,1)S(1)}, bf16[720,128]{1,0:T(8,128)(2,1)S(1)}, u32[]{:S(2)}, u32[]{:S(2)}) collective-permute-start(bf16[720,128]{1,0:T(8,128)(2,1)S(1)} %add_convert_fusion.6), channel_id=1, source_target_pairs={{0,4},{4,8},{8,12},{12,14},{14,10},{10,6},{6,2},{2,0},{1,5},{5,9},... | collective-permute-start | bytes 552968 | tf_op jit(solution)/shard_map/ppermute | solution.py:357
  71.9 0.5 collective-permute-start.24
  72.4 1.7 %collective-permute-done.32 = bf16[720,128]{1,0:T(8,128)(2,1)S(1)} collective-permute-done((bf16[720,128]{1,0:T(8,128)(2,1)S(1)}, bf16[720,128]{1,0:T(8,128)(2,1)S(1)}, u32[]{:S(2)}, u32[]{:S(2)}) %collective-permute-start.32) | collective-permute-done | bytes 184352 | tf_op jit(solution)/shard_map/ppermute | solution.py:359
  74.1 1.6 %collective-permute-start.33 = (bf16[720,128]{1,0:T(8,128)(2,1)S(1)}, bf16[720,128]{1,0:T(8,128)(2,1)S(1)}, u32[]{:S(2)}, u32[]{:S(2)}) collective-permute-start(bf16[720,128]{1,0:T(8,128)(2,1)S(1)} %add_convert_fusion.1), channel_id=1, source_target_pairs={{0,4},{4,8},{8,12},{12,14},{14,10},{10,6},{6,2},{2,0},{1,5},{5,9},... | collective-permute-start | bytes 552968 | tf_op jit(solution)/shard_map/ppermute | solution.py:359
  75.8 0.5 collective-permute-start.29
  76.3 4.6 %collective-permute-done.33 = bf16[720,128]{1,0:T(8,128)(2,1)S(1)} collective-permute-done((bf16[720,128]{1,0:T(8,128)(2,1)S(1)}, bf16[720,128]{1,0:T(8,128)(2,1)S(1)}, u32[]{:S(2)}, u32[]{:S(2)}) %collective-permute-start.33) | collective-permute-done | bytes 184352 | tf_op jit(solution)/shard_map/ppermute | solution.py:359
  81.0 1.7 %collective-permute-start.34 = (bf16[720,128]{1,0:T(8,128)(2,1)S(1)}, bf16[720,128]{1,0:T(8,128)(2,1)S(1)}, u32[]{:S(2)}, u32[]{:S(2)}) collective-permute-start(bf16[720,128]{1,0:T(8,128)(2,1)S(1)} %add_convert_fusion), channel_id=1, source_target_pairs={{0,4},{4,8},{8,12},{12,14},{14,10},{10,6},{6,2},{2,0},{1,5},{5,9},... | collective-permute-start | bytes 552968 | tf_op jit(solution)/shard_map/ppermute | solution.py:359
  83.1 0.4 collective-permute-start.30
  83.5 3.1 %collective-permute-done.34.refs_2_ = bf16[720,128]{1,0:T(8,128)(2,1)S(1)} collective-permute-done((bf16[720,128]{1,0:T(8,128)(2,1)S(1)}, bf16[720,128]{1,0:T(8,128)(2,1)S(1)}, u32[]{:S(2)}, u32[]{:S(2)}) %collective-permute-start.34) | collective-permute-done | bytes 184352 | tf_op jit(solution)/shard_map/ppermute | solution.py:359
  86.6 2.1 %collective-permute-done.30.refs_4_ = bf16[720,128]{1,0:T(8,128)(2,1)S(1)} collective-permute-done((bf16[720,128]{1,0:T(8,128)(2,1)S(1)}, bf16[720,128]{1,0:T(8,128)(2,1)S(1)}, u32[]{:S(2)}, u32[]{:S(2)}) %collective-permute-start.30) | collective-permute-done | bytes 184352 | tf_op jit(solution)/shard_map/ppermute | solution.py:358
  88.7 0.9 %total.1 = bf16[1440,128]{1,0:T(8,128)(2,1)} custom-call(bf16[720,128]{1,0:T(8,128)(2,1)S(1)} %get-tuple-element.144.refs_0_, bf16[720,128]{1,0:T(8,128)(2,1)S(1)} %collective-permute-done.24.refs_1_, bf16[720,128]{1,0:T(8,128)(2,1)S(1)} %collective-permute-done.34.refs_2_, bf16[720,128]{1,0:T(8,128)(2,1)S(1)} %get-tuple-element.147.refs_3_, ...), custom_call_target="tpu_custom_call" | custom-call | flops 1 | bytes 1 | tf_op jit(solution)/shard_map/total/pallas_call | solution.py:285
  (52 shorter events, 2.5 us)
Async XLA Ops:
  0.6 10.8 %collective-permute-start.3 = (bf16[1440,1024]{1,0:T(8,128)(2,1)}, bf16[1440,1024]{1,0:T(8,128)(2,1)S(1)}, u32[]{:S(2)}, u32[]{:S(2)}) collective-permute-start(bf16[1440,1024]{1,0:T(8,128)(2,1)} %bitcast.39), channel_id=1, source_target_pairs={{0,1},{1,0},{2,3},{3,2},{4,5},{5,4},{6,7},{7,6},{8,9},{9,8},{10,11... | collective-permute-start | bytes 8847368 | tf_op jit(solution)/shard_map/ppermute | solution.py:219
  1.9 7.1 %collective-permute-start = (bf16[256,128]{1,0:T(8,128)(2,1)S(1)}, bf16[256,128]{1,0:T(8,128)(2,1)S(1)}, u32[]{:S(2)}, u32[]{:S(2)}) collective-permute-start(bf16[256,128]{1,0:T(8,128)(2,1)S(1)} %rim.1), channel_id=1, source_target_pairs={{0,2},{2,4},{4,6},{6,8},{8,10},{10,12},{12,14},{1,3},{3,5},{5,7},{... | collective-permute-start | bytes 196616 | tf_op jit(solution)/shard_map/ppermute | solution.py:192
  9.0 2.4 %collective-permute-start.1 = (bf16[1552,128]{1,0:T(8,128)(2,1)S(1)}, bf16[1552,128]{1,0:T(8,128)(2,1)S(1)}, u32[]{:S(2)}, u32[]{:S(2)}) collective-permute-start(bf16[1552,128]{1,0:T(8,128)(2,1)S(1)} %get-tuple-element.78.packed_a), channel_id=1, source_target_pairs={{0,1},{1,0},{2,3},{3,2},{4,5},{5,4},{6,7},{7,6},{8,9},{9,8},{10,11... | collective-permute-start | bytes 1191944 | tf_op jit(solution)/shard_map/ppermute | solution.py:219
  9.3 1.6 %collective-permute-start.2 = (bf16[256,128]{1,0:T(8,128)(2,1)S(1)}, bf16[256,128]{1,0:T(8,128)(2,1)S(1)}, u32[]{:S(2)}, u32[]{:S(2)}) collective-permute-start(bf16[256,128]{1,0:T(8,128)(2,1)S(1)} %collective-permute-done.rim_a), channel_id=1, source_target_pairs={{0,1},{1,0},{2,3},{3,2},{4,5},{5,4},{6,7},{7,6},{8,9},{9,8},{10,11... | collective-permute-start | bytes 196616 | tf_op jit(solution)/shard_map/ppermute | solution.py:219
  10.9 9.9 %collective-permute-start.10 = (bf16[1440,720]{1,0:T(8,128)(2,1)}, bf16[1440,720]{1,0:T(8,128)(2,1)S(1)}, u32[]{:S(2)}, u32[]{:S(2)}) collective-permute-start(bf16[1440,720]{1,0:T(8,128)(2,1)} %bitcast.12), channel_id=1, source_target_pairs={{0,1},{1,0},{2,3},{3,2},{4,5},{5,4},{6,7},{7,6},{8,9},{9,8},{10,11... | collective-permute-start | bytes 6220808 | tf_op jit(solution)/shard_map/ppermute | solution.py:219
  11.1 11.7 %collective-permute-start.11 = (bf16[1440,720]{1,0:T(8,128)(2,1)}, bf16[1440,720]{1,0:T(8,128)(2,1)S(1)}, u32[]{:S(2)}, u32[]{:S(2)}) collective-permute-start(bf16[1440,720]{1,0:T(8,128)(2,1)} %bitcast.21), channel_id=1, source_target_pairs={{0,1},{1,0},{2,3},{3,2},{4,5},{5,4},{6,7},{7,6},{8,9},{9,8},{10,11... | collective-permute-start | bytes 6220808 | tf_op jit(solution)/shard_map/ppermute | solution.py:219
  11.5 6.5 %copy-start.2 = (bf16[1,720,1440]{2,1,0:T(8,128)(2,1)S(1)}, bf16[1,720,1440]{2,1,0:T(8,128)(2,1)}, u32[]{:S(2)}) copy-start(bf16[1,720,1440]{2,1,0:T(8,128)(2,1)} %param.23) | copy-start | bytes 6220804
  11.5 20.9 %copy-start = (bf16[1,1440,720]{2,1,0:T(8,128)(2,1)S(1)}, bf16[1,1440,720]{2,1,0:T(8,128)(2,1)}, u32[]{:S(2)}) copy-start(bf16[1,1440,720]{2,1,0:T(8,128)(2,1)} %param.21) | copy-start | bytes 6220804
  11.5 20.9 %copy-start.1 = (bf16[1,1440,720]{2,1,0:T(8,128)(2,1)S(1)}, bf16[1,1440,720]{2,1,0:T(8,128)(2,1)}, u32[]{:S(2)}) copy-start(bf16[1,1440,720]{2,1,0:T(8,128)(2,1)} %param.22) | copy-start | bytes 6220804
  17.9 14.5 %collective-permute-start.12 = (bf16[720,1440]{1,0:T(8,128)(2,1)S(1)}, bf16[720,1440]{1,0:T(8,128)(2,1)S(1)}, u32[]{:S(2)}, u32[]{:S(2)}) collective-permute-start(bf16[720,1440]{1,0:T(8,128)(2,1)S(1)} %bitcast.30), channel_id=1, source_target_pairs={{0,1},{1,0},{2,3},{3,2},{4,5},{5,4},{6,7},{7,6},{8,9},{9,8},{10,11... | collective-permute-start | bytes 6220808 | tf_op jit(solution)/shard_map/ppermute | solution.py:219
  18.2 7.7 %collective-permute-start.6 = (bf16[736,128]{1,0:T(8,128)(2,1)S(1)}, bf16[736,128]{1,0:T(8,128)(2,1)S(1)}, u32[]{:S(2)}, u32[]{:S(2)}) collective-permute-start(bf16[736,128]{1,0:T(8,128)(2,1)S(1)} %get-tuple-element.124.upper), channel_id=1, source_target_pairs={{0,4},{4,8},{8,12},{12,14},{14,10},{10,6},{6,2},{2,0},{1,5},{5,9},... | collective-permute-start | bytes 565256 | tf_op jit(solution)/shard_map/ppermute | solution.py:319
  20.9 7.6 %collective-permute-start.4 = (bf16[736,128]{1,0:T(8,128)(2,1)S(1)}, bf16[736,128]{1,0:T(8,128)(2,1)S(1)}, u32[]{:S(2)}, u32[]{:S(2)}) collective-permute-start(bf16[736,128]{1,0:T(8,128)(2,1)S(1)} %get-tuple-element.124.upper), channel_id=1, source_target_pairs={{4,0},{8,4},{12,8},{14,12},{10,14},{6,10},{2,6},{0,2},{5,1},{9,5},... | collective-permute-start | bytes 565256 | tf_op jit(solution)/shard_map/ppermute | solution.py:319
  20.9 9.0 %collective-permute-start.9 = (bf16[720,128]{1,0:T(8,128)(2,1)S(1)}, bf16[720,128]{1,0:T(8,128)(2,1)S(1)}, u32[]{:S(2)}, u32[]{:S(2)}) collective-permute-start(bf16[720,128]{1,0:T(8,128)(2,1)S(1)} %get-tuple-element.125.lower), channel_id=1, source_target_pairs={{0,4},{4,8},{8,12},{12,14},{14,10},{10,6},{6,2},{2,0},{1,5},{5,9},... | collective-permute-start | bytes 552968 | tf_op jit(solution)/shard_map/ppermute | solution.py:319
  22.9 9.5 %collective-permute-start.5 = (bf16[720,128]{1,0:T(8,128)(2,1)S(1)}, bf16[720,128]{1,0:T(8,128)(2,1)S(1)}, u32[]{:S(2)}, u32[]{:S(2)}) collective-permute-start(bf16[720,128]{1,0:T(8,128)(2,1)S(1)} %get-tuple-element.125.lower), channel_id=1, source_target_pairs={{4,0},{8,4},{12,8},{14,12},{10,14},{6,10},{2,6},{0,2},{5,1},{9,5},... | collective-permute-start | bytes 552968 | tf_op jit(solution)/shard_map/ppermute | solution.py:319
  25.9 8.7 %collective-permute-start.7 = (bf16[736,128]{1,0:T(8,128)(2,1)S(1)}, bf16[736,128]{1,0:T(8,128)(2,1)S(1)}, u32[]{:S(2)}, u32[]{:S(2)}) collective-permute-start(bf16[736,128]{1,0:T(8,128)(2,1)S(1)} %collective-permute-done.6.upper), channel_id=1, source_target_pairs={{0,4},{4,8},{8,12},{12,14},{14,10},{10,6},{6,2},{2,0},{1,5},{5,9},... | collective-permute-start | bytes 565256 | tf_op jit(solution)/shard_map/ppermute | solution.py:332
  28.4 8.0 %collective-permute-start.8 = (bf16[736,128]{1,0:T(8,128)(2,1)S(1)}, bf16[736,128]{1,0:T(8,128)(2,1)S(1)}, u32[]{:S(2)}, u32[]{:S(2)}) collective-permute-start(bf16[736,128]{1,0:T(8,128)(2,1)S(1)} %collective-permute-done.4.upper), channel_id=1, source_target_pairs={{4,0},{8,4},{12,8},{14,12},{10,14},{6,10},{2,6},{0,2},{5,1},{9,5},... | collective-permute-start | bytes 565256 | tf_op jit(solution)/shard_map/ppermute | solution.py:333
  29.9 10.8 %collective-permute-start.13 = (bf16[720,128]{1,0:T(8,128)(2,1)S(1)}, bf16[720,128]{1,0:T(8,128)(2,1)S(1)}, u32[]{:S(2)}, u32[]{:S(2)}) collective-permute-start(bf16[720,128]{1,0:T(8,128)(2,1)S(1)} %collective-permute-done.9.lower), channel_id=1, source_target_pairs={{0,4},{4,8},{8,12},{12,14},{14,10},{10,6},{6,2},{2,0},{1,5},{5,9},... | collective-permute-start | bytes 552968 | tf_op jit(solution)/shard_map/ppermute | solution.py:337
  32.4 8.3 %collective-permute-start.14 = (bf16[720,128]{1,0:T(8,128)(2,1)S(1)}, bf16[720,128]{1,0:T(8,128)(2,1)S(1)}, u32[]{:S(2)}, u32[]{:S(2)}) collective-permute-start(bf16[720,128]{1,0:T(8,128)(2,1)S(1)} %collective-permute-done.5.lower), channel_id=1, source_target_pairs={{4,0},{8,4},{12,8},{14,12},{10,14},{6,10},{2,6},{0,2},{5,1},{9,5},... | collective-permute-start | bytes 552968 | tf_op jit(solution)/shard_map/ppermute | solution.py:338
  36.4 8.6 %collective-permute-start.15 = (bf16[736,128]{1,0:T(8,128)(2,1)S(1)}, bf16[736,128]{1,0:T(8,128)(2,1)S(1)}, u32[]{:S(2)}, u32[]{:S(2)}) collective-permute-start(bf16[736,128]{1,0:T(8,128)(2,1)S(1)} %collective-permute-done.7.upper), channel_id=1, source_target_pairs={{0,4},{4,8},{8,12},{12,14},{14,10},{10,6},{6,2},{2,0},{1,5},{5,9},... | collective-permute-start | bytes 565256 | tf_op jit(solution)/shard_map/ppermute | solution.py:332
  38.0 7.0 %collective-permute-start.16 = (bf16[736,128]{1,0:T(8,128)(2,1)S(1)}, bf16[736,128]{1,0:T(8,128)(2,1)S(1)}, u32[]{:S(2)}, u32[]{:S(2)}) collective-permute-start(bf16[736,128]{1,0:T(8,128)(2,1)S(1)} %collective-permute-done.8.upper), channel_id=1, source_target_pairs={{4,0},{8,4},{12,8},{14,12},{10,14},{6,10},{2,6},{0,2},{5,1},{9,5},... | collective-permute-start | bytes 565256 | tf_op jit(solution)/shard_map/ppermute | solution.py:333
  40.6 8.4 %collective-permute-start.17 = (bf16[720,128]{1,0:T(8,128)(2,1)S(1)}, bf16[720,128]{1,0:T(8,128)(2,1)S(1)}, u32[]{:S(2)}, u32[]{:S(2)}) collective-permute-start(bf16[720,128]{1,0:T(8,128)(2,1)S(1)} %collective-permute-done.13.lower), channel_id=1, source_target_pairs={{0,4},{4,8},{8,12},{12,14},{14,10},{10,6},{6,2},{2,0},{1,5},{5,9},... | collective-permute-start | bytes 552968 | tf_op jit(solution)/shard_map/ppermute | solution.py:337
  42.3 6.7 %collective-permute-start.18 = (bf16[720,128]{1,0:T(8,128)(2,1)S(1)}, bf16[720,128]{1,0:T(8,128)(2,1)S(1)}, u32[]{:S(2)}, u32[]{:S(2)}) collective-permute-start(bf16[720,128]{1,0:T(8,128)(2,1)S(1)} %collective-permute-done.14.lower), channel_id=1, source_target_pairs={{4,0},{8,4},{12,8},{14,12},{10,14},{6,10},{2,6},{0,2},{5,1},{9,5},... | collective-permute-start | bytes 552968 | tf_op jit(solution)/shard_map/ppermute | solution.py:338
  45.0 11.0 %collective-permute-start.21 = (bf16[736,128]{1,0:T(8,128)(2,1)S(1)}, bf16[736,128]{1,0:T(8,128)(2,1)S(1)}, u32[]{:S(2)}, u32[]{:S(2)}) collective-permute-start(bf16[736,128]{1,0:T(8,128)(2,1)S(1)} %collective-permute-done.15.upper), channel_id=1, source_target_pairs={{0,4},{4,8},{8,12},{12,14},{14,10},{10,6},{6,2},{2,0},{1,5},{5,9},... | collective-permute-start | bytes 565256 | tf_op jit(solution)/shard_map/ppermute | solution.py:332
  49.0 6.9 %collective-permute-start.22 = (bf16[720,128]{1,0:T(8,128)(2,1)S(1)}, bf16[720,128]{1,0:T(8,128)(2,1)S(1)}, u32[]{:S(2)}, u32[]{:S(2)}) collective-permute-start(bf16[720,128]{1,0:T(8,128)(2,1)S(1)} %collective-permute-done.18.lower), channel_id=1, source_target_pairs={{4,0},{8,4},{12,8},{14,12},{10,14},{6,10},{2,6},{0,2},{5,1},{9,5},... | collective-permute-start | bytes 552968 | tf_op jit(solution)/shard_map/ppermute | solution.py:338
  53.9 8.6 %collective-permute-start.19 = (bf16[720,128]{1,0:T(8,128)(2,1)S(1)}, bf16[720,128]{1,0:T(8,128)(2,1)S(1)}, u32[]{:S(2)}, u32[]{:S(2)}) collective-permute-start(bf16[720,128]{1,0:T(8,128)(2,1)S(1)} %get-tuple-element.118), channel_id=1, source_target_pairs={{4,0},{8,4},{12,8},{14,12},{10,14},{6,10},{2,6},{0,2},{5,1},{9,5},... | collective-permute-start | bytes 552968 | tf_op jit(solution)/shard_map/ppermute | solution.py:348
  53.9 8.5 %collective-permute-start.20 = (bf16[720,128]{1,0:T(8,128)(2,1)S(1)}, bf16[720,128]{1,0:T(8,128)(2,1)S(1)}, u32[]{:S(2)}, u32[]{:S(2)}) collective-permute-start(bf16[720,128]{1,0:T(8,128)(2,1)S(1)} %get-tuple-element.115), channel_id=1, source_target_pairs={{0,4},{4,8},{8,12},{12,14},{14,10},{10,6},{6,2},{2,0},{1,5},{5,9},... | collective-permute-start | bytes 552968 | tf_op jit(solution)/shard_map/ppermute | solution.py:346
  58.1 7.5 %collective-permute-start.31 = (bf16[720,128]{1,0:T(8,128)(2,1)S(1)}, bf16[720,128]{1,0:T(8,128)(2,1)S(1)}, u32[]{:S(2)}, u32[]{:S(2)}) collective-permute-start(bf16[720,128]{1,0:T(8,128)(2,1)S(1)} %get-tuple-element.143), channel_id=1, source_target_pairs={{0,4},{4,8},{8,12},{12,14},{14,10},{10,6},{6,2},{2,0},{1,5},{5,9},... | collective-permute-start | bytes 552968 | tf_op jit(solution)/shard_map/ppermute | solution.py:352
  59.7 7.6 %collective-permute-start.27 = (bf16[720,128]{1,0:T(8,128)(2,1)S(1)}, bf16[720,128]{1,0:T(8,128)(2,1)S(1)}, u32[]{:S(2)}, u32[]{:S(2)}) collective-permute-start(bf16[720,128]{1,0:T(8,128)(2,1)S(1)} %get-tuple-element.139), channel_id=1, source_target_pairs={{4,0},{8,4},{12,8},{14,12},{10,14},{6,10},{2,6},{0,2},{5,1},{9,5},... | collective-permute-start | bytes 552968 | tf_op jit(solution)/shard_map/ppermute | solution.py:352
  62.5 7.6 %collective-permute-start.25 = (bf16[720,128]{1,0:T(8,128)(2,1)S(1)}, bf16[720,128]{1,0:T(8,128)(2,1)S(1)}, u32[]{:S(2)}, u32[]{:S(2)}) collective-permute-start(bf16[720,128]{1,0:T(8,128)(2,1)S(1)} %add_convert_fusion.7), channel_id=1, source_target_pairs={{0,4},{4,8},{8,12},{12,14},{14,10},{10,6},{6,2},{2,0},{1,5},{5,9},... | collective-permute-start | bytes 552968 | tf_op jit(solution)/shard_map/ppermute | solution.py:357
  64.2 7.6 %collective-permute-start.23 = (bf16[720,128]{1,0:T(8,128)(2,1)S(1)}, bf16[720,128]{1,0:T(8,128)(2,1)S(1)}, u32[]{:S(2)}, u32[]{:S(2)}) collective-permute-start(bf16[720,128]{1,0:T(8,128)(2,1)S(1)} %add_convert_fusion.9), channel_id=1, source_target_pairs={{4,0},{8,4},{12,8},{14,12},{10,14},{6,10},{2,6},{0,2},{5,1},{9,5},... | collective-permute-start | bytes 552968 | tf_op jit(solution)/shard_map/ppermute | solution.py:356
  65.7 8.4 %collective-permute-start.32 = (bf16[720,128]{1,0:T(8,128)(2,1)S(1)}, bf16[720,128]{1,0:T(8,128)(2,1)S(1)}, u32[]{:S(2)}, u32[]{:S(2)}) collective-permute-start(bf16[720,128]{1,0:T(8,128)(2,1)S(1)} %add_convert_fusion.2), channel_id=1, source_target_pairs={{0,4},{4,8},{8,12},{12,14},{14,10},{10,6},{6,2},{2,0},{1,5},{5,9},... | collective-permute-start | bytes 552968 | tf_op jit(solution)/shard_map/ppermute | solution.py:359
  67.4 8.4 %collective-permute-start.28 = (bf16[720,128]{1,0:T(8,128)(2,1)S(1)}, bf16[720,128]{1,0:T(8,128)(2,1)S(1)}, u32[]{:S(2)}, u32[]{:S(2)}) collective-permute-start(bf16[720,128]{1,0:T(8,128)(2,1)S(1)} %add_convert_fusion.5), channel_id=1, source_target_pairs={{4,0},{8,4},{12,8},{14,12},{10,14},{6,10},{2,6},{0,2},{5,1},{9,5},... | collective-permute-start | bytes 552968 | tf_op jit(solution)/shard_map/ppermute | solution.py:358
  70.2 13.3 %collective-permute-start.26 = (bf16[720,128]{1,0:T(8,128)(2,1)S(1)}, bf16[720,128]{1,0:T(8,128)(2,1)S(1)}, u32[]{:S(2)}, u32[]{:S(2)}) collective-permute-start(bf16[720,128]{1,0:T(8,128)(2,1)S(1)} %add_convert_fusion.6), channel_id=1, source_target_pairs={{0,4},{4,8},{8,12},{12,14},{14,10},{10,6},{6,2},{2,0},{1,5},{5,9},... | collective-permute-start | bytes 552968 | tf_op jit(solution)/shard_map/ppermute | solution.py:357
  71.9 11.6 %collective-permute-start.24 = (bf16[720,128]{1,0:T(8,128)(2,1)S(1)}, bf16[720,128]{1,0:T(8,128)(2,1)S(1)}, u32[]{:S(2)}, u32[]{:S(2)}) collective-permute-start(bf16[720,128]{1,0:T(8,128)(2,1)S(1)} %add_convert_fusion.8), channel_id=1, source_target_pairs={{4,0},{8,4},{12,8},{14,12},{10,14},{6,10},{2,6},{0,2},{5,1},{9,5},... | collective-permute-start | bytes 552968 | tf_op jit(solution)/shard_map/ppermute | solution.py:356
  74.1 6.8 %collective-permute-start.33 = (bf16[720,128]{1,0:T(8,128)(2,1)S(1)}, bf16[720,128]{1,0:T(8,128)(2,1)S(1)}, u32[]{:S(2)}, u32[]{:S(2)}) collective-permute-start(bf16[720,128]{1,0:T(8,128)(2,1)S(1)} %add_convert_fusion.1), channel_id=1, source_target_pairs={{0,4},{4,8},{8,12},{12,14},{14,10},{10,6},{6,2},{2,0},{1,5},{5,9},... | collective-permute-start | bytes 552968 | tf_op jit(solution)/shard_map/ppermute | solution.py:359
  75.8 7.2 %collective-permute-start.29 = (bf16[720,128]{1,0:T(8,128)(2,1)S(1)}, bf16[720,128]{1,0:T(8,128)(2,1)S(1)}, u32[]{:S(2)}, u32[]{:S(2)}) collective-permute-start(bf16[720,128]{1,0:T(8,128)(2,1)S(1)} %add_convert_fusion.4), channel_id=1, source_target_pairs={{4,0},{8,4},{12,8},{14,12},{10,14},{6,10},{2,6},{0,2},{5,1},{9,5},... | collective-permute-start | bytes 552968 | tf_op jit(solution)/shard_map/ppermute | solution.py:358
  81.0 5.6 %collective-permute-start.34 = (bf16[720,128]{1,0:T(8,128)(2,1)S(1)}, bf16[720,128]{1,0:T(8,128)(2,1)S(1)}, u32[]{:S(2)}, u32[]{:S(2)}) collective-permute-start(bf16[720,128]{1,0:T(8,128)(2,1)S(1)} %add_convert_fusion), channel_id=1, source_target_pairs={{0,4},{4,8},{8,12},{12,14},{14,10},{10,6},{6,2},{2,0},{1,5},{5,9},... | collective-permute-start | bytes 552968 | tf_op jit(solution)/shard_map/ppermute | solution.py:359
  83.1 5.6 %collective-permute-start.30 = (bf16[720,128]{1,0:T(8,128)(2,1)S(1)}, bf16[720,128]{1,0:T(8,128)(2,1)S(1)}, u32[]{:S(2)}, u32[]{:S(2)}) collective-permute-start(bf16[720,128]{1,0:T(8,128)(2,1)S(1)} %add_convert_fusion.3), channel_id=1, source_target_pairs={{4,0},{8,4},{12,8},{14,12},{10,14},{6,10},{2,6},{0,2},{5,1},{9,5},... | collective-permute-start | bytes 552968 | tf_op jit(solution)/shard_map/ppermute | solution.py:358

commit v4 on v3

--- a/solution.py
+++ b/solution.py
@@ -50,17 +50,16 @@
     return jnp.concatenate(outs, axis=0)
 
 
-def pack_kernel(place, sink, gain, k, v, q, packed, gains, sems):
+def pack_kernel(code_rows, place, sink, gain, routes, codes, k, v, q, packed, *refs):
+    *extra, sems = refs
     count, width = k.shape
     base = 2 * count + BF16_ROWS
-    rows = pl.ds(pl.multiple_of((1 - place[0]) * WINDOW, WINDOW), WINDOW)
-    moves = [
-        (k, packed.at[:count, :]),
-        (v, packed.at[count : 2 * count, :]),
-    ]
+    rows = pl.ds(pl.multiple_of(place[0] * WINDOW, WINDOW), WINDOW)
+    others = pl.ds(pl.multiple_of((1 - place[0]) * WINDOW, WINDOW), WINDOW)
+    moves = [(k, packed.at[:count, :]), (v, packed.at[count : 2 * count, :])]
     for j in range(q.shape[1] // width):
         to = base + j * WINDOW
-        moves.append((q.at[rows, j * width : (j + 1) * width], packed.at[to : to + WINDOW, :]))
+        moves.append((q.at[others, j * width : (j + 1) * width], packed.at[to : to + WINDOW, :]))
     copies = [pltpu.make_async_copy(source, target, sems.at[i]) for i, (source, target) in enumerate(moves)]
     for copy in copies:
         copy.start()
@@ -75,9 +74,39 @@
         terms = jnp.where(row == i, term, terms)
         left = left - term
     packed[2 * count : base, :] = terms.astype(BF16)
-    gains[...] = jnp.broadcast_to(gain[...], (WINDOW, gain.shape[1])).T
+    if code_rows:
+        gains, table_ref = extra
+        gains[...] = jnp.broadcast_to(gain[...], (WINDOW, gain.shape[1])).T
+        expert = lax.broadcasted_iota(jnp.int32, (code_rows, WINDOW), 0)
+        table = jnp.zeros((code_rows, WINDOW), F32)
+        for i in range(TOP):
+            named = jnp.broadcast_to(routes[i : i + 1, rows], expert.shape) == expert
+            table += jnp.where(named, jnp.broadcast_to(codes[i : i + 1, rows], expert.shape).astype(F32), 0.0)
+        table_ref[...] = table.astype(BF16)
     for copy in copies:
         copy.wait()
+
+
+def pack(code_rows, place, sink_logit, norm_gain, routes, gate_codes, key_rows, values, queries):
+    rows, width = key_rows.shape
+    tall = queries.shape[1] // width * WINDOW
+    shapes = [jax.ShapeDtypeStruct((2 * rows + BF16_ROWS + tall, width), BF16)]
+    if code_rows:
+        features = norm_gain.shape[0]
+        shapes += [jax.ShapeDtypeStruct((features, WINDOW), F32), jax.ShapeDtypeStruct((code_rows, WINDOW), BF16)]
+    return pl.pallas_call(
+        functools.partial(pack_kernel, code_rows),
+        out_shape=shapes,
+        in_specs=[SMEM] * 2 + [VMEM] * 3 + [ANY] * 3,
+        out_specs=[VMEM] * len(shapes),
+        scratch_shapes=[pltpu.SemaphoreType.DMA((2 + tall // WINDOW,))],
+        cost_estimate=pl.CostEstimate(flops=1, bytes_accessed=1, transcendentals=0),
+        compiler_params=pltpu.CompilerParams(vmem_limit_bytes=16 * 2**20),
+        name="pack",
+    )(
+        place, in_hbm(sink_logit), norm_gain[None, :], in_hbm(routes.T), in_hbm(gate_codes.T),
+        in_hbm(key_rows), in_hbm(values), in_hbm(queries),
+    )
 
 
 def rim_kernel(k, v, rim, sems):
@@ -105,82 +134,65 @@
     )(in_hbm(key_rows), in_hbm(values))
 
 
-def pack(place, sink_logit, norm_gain, key_rows, values, queries):
-    rows, width = key_rows.shape
-    blocks = queries.shape[1] // width
-    return pl.pallas_call(
-        pack_kernel,
-        out_shape=[
-            jax.ShapeDtypeStruct((2 * rows + BF16_ROWS + blocks * WINDOW, width), BF16),
-            jax.ShapeDtypeStruct((norm_gain.shape[0], WINDOW), F32),
-        ],
-        in_specs=[SMEM, SMEM, VMEM, ANY, ANY, ANY],
-        out_specs=[VMEM, VMEM],
-        scratch_shapes=[pltpu.SemaphoreType.DMA((2 + blocks,))],
-        cost_estimate=pl.CostEstimate(flops=0, bytes_accessed=4 * key_rows.size, transcendentals=0),
-        compiler_params=pltpu.CompilerParams(vmem_limit_bytes=4 * 2**20),
-        name="pack",
-    )(place, in_hbm(sink_logit), norm_gain[None, :], in_hbm(key_rows), in_hbm(values), in_hbm(queries))
-
-
-def front_kernel(code_rows, place, gains, packed_a, rim_a, packed_b, rim_b, ow_b, *refs):
-    hbm, outs, scratch = refs[:5], refs[5 : 8 if code_rows else 6], refs[8 if code_rows else 6 :]
-    q_a, ow_a, resid, routes, codes = hbm
+def attend(place, packed, rim, q_blocks):
     core, first = place[0], place[1] == 1
     start = pl.multiple_of(core * WINDOW, WINDOW)
-    rows = pl.ds(start, WINDOW)
-    held, sems = scratch[:-1], scratch[-1]
-    sources = (q_a.at[rows, :], ow_a, resid.at[:, rows], routes.at[:, rows], codes.at[:, rows])
-    copies = [pltpu.make_async_copy(source, held[i], sems.at[i]) for i, source in enumerate(sources)]
+    lead = core == 0
+    tall = q_blocks.shape[0]
+    base = packed.shape[0] - tall
+    count = (base - BF16_ROWS) // 2
+    past = jnp.concatenate(
+        [
+            jnp.where(lead, rim[:WINDOW, :], packed[:WINDOW, :]),
+            jnp.where(lead, rim[WINDOW:, :], packed[count : count + WINDOW, :]),
+        ],
+        axis=1,
+    )
+    later = pl.ds(pl.multiple_of(count + start, WINDOW), WINDOW)
+    present = jnp.concatenate([packed[pl.ds(start, WINDOW), :], packed[later, :]], axis=1)
+    terms = packed[2 * count : base, :].astype(F32)
+    sinks = terms[0:1] + terms[1:2] + terms[2:3]
+    q_cols = [(q_blocks[j : j + WINDOW] * HEAD_DIM ** (-0.5)).T for j in range(0, tall, WINDOW)]
+    return heads_of(jnp.concatenate(q_cols, axis=0), past, present, sinks, first)
+
+
+def front_own_kernel(place, packed, rim, q, ow, resid, out, q_held, ow_held, resid_held, sems):
+    rows = pl.ds(pl.multiple_of(place[0] * WINDOW, WINDOW), WINDOW)
+    width = packed.shape[1]
+    moves = [
+        (q.at[rows, j * width : (j + 1) * width], q_held.at[j * WINDOW : (j + 1) * WINDOW, :])
+        for j in range(q.shape[1] // width)
+    ]
+    moves += [(ow, ow_held), (resid.at[:, rows], resid_held)]
+    copies = [pltpu.make_async_copy(source, target, sems.at[i]) for i, (source, target) in enumerate(moves)]
     for copy in copies:
         copy.start()
-    lead = core == 0
-    width = rim_a.shape[1]
-    blocks = held[0].shape[1] // width
-    base = packed_a.shape[0] - blocks * WINDOW
-    count = (base - BF16_ROWS) // 2
-    later = pl.ds(pl.multiple_of(count + start, WINDOW), WINDOW)
-
-    def attend(packed, rim, q_blocks):
-        past = jnp.concatenate(
-            [
-                jnp.where(lead, rim[:WINDOW, :], packed[:WINDOW, :]),
-                jnp.where(lead, rim[WINDOW:, :], packed[count : count + WINDOW, :]),
-            ],
-            axis=1,
-        )
-        present = jnp.concatenate([packed[rows, :], packed[later, :]], axis=1)
-        terms = packed[2 * count : base, :].astype(F32)
-        sinks = terms[0:1] + terms[1:2] + terms[2:3]
-        q_cols = jnp.concatenate([(block * HEAD_DIM ** (-0.5)).T for block in q_blocks], axis=0)
-        return heads_of(q_cols, past, present, sinks, first)
-
-    theirs = attend(
-        packed_b, rim_b, [packed_b[base + j * WINDOW : base + (j + 1) * WINDOW, :] for j in range(blocks)]
-    )
-    copies[0].wait()
-    ours = attend(packed_a, rim_a, [held[0][:, j * width : (j + 1) * width] for j in range(blocks)])
-    projected = jnp.dot(ow_b[...], theirs, preferred_element_type=F32)
-    copies[1].wait()
-    projected += jnp.dot(held[1][...], ours, preferred_element_type=F32)
-    for copy in copies[2:]:
+    for copy in copies[:-2]:
         copy.wait()
-    attended = (held[2][...].astype(F32) + projected).astype(BF16)
-    outs[0][...] = attended
-    if code_rows:
-        expert = lax.broadcasted_iota(jnp.int32, (code_rows, WINDOW), 0)
-        table = jnp.zeros((code_rows, WINDOW), F32)
-        for k in range(TOP):
-            named = jnp.broadcast_to(held[3][k : k + 1, :], expert.shape) == expert
-            table += jnp.where(named, jnp.broadcast_to(held[4][k : k + 1, :], expert.shape).astype(F32), 0.0)
-        widened = attended.astype(F32)
-        spread = jnp.mean(widened * widened, axis=0, keepdims=True)
-        normed = (widened * lax.rsqrt(spread + 1e-05) * gains[...]).astype(BF16)
-        body = normed.shape[0] // WINDOW * WINDOW
-        blocks = [normed[j : j + WINDOW].T for j in range(0, body, WINDOW)]
-        parcel = jnp.concatenate([table.astype(BF16), normed[body:], *blocks], axis=0)
-        outs[1][...] = parcel[: outs[1].shape[0]]
-        outs[2][...] = parcel[outs[1].shape[0] :]
+    heads = attend(place, packed, rim, q_held[...])
+    for copy in copies[-2:]:
+        copy.wait()
+    projected = jnp.dot(ow_held[...], heads, preferred_element_type=F32)
+    out[...] = projected + resid_held[...].astype(F32)
+
+
+def front_kernel(code_rows, place, packed, rim, ow, stream, *refs):
+    base = packed.shape[0] - ow.shape[1] // packed.shape[1] * WINDOW
+    heads = attend(place, packed, rim, packed[base:, :])
+    attended = (stream[...] + jnp.dot(ow[...], heads, preferred_element_type=F32)).astype(BF16)
+    if not code_rows:
+        refs[0][...] = attended
+        return
+    gains, table, attended_ref, upper, lower = refs
+    attended_ref[...] = attended
+    widened = attended.astype(F32)
+    spread = jnp.mean(widened * widened, axis=0, keepdims=True)
+    normed = (widened * lax.rsqrt(spread + 1e-05) * gains[...]).astype(BF16)
+    body = normed.shape[0] // WINDOW * WINDOW
+    blocks = [normed[j : j + WINDOW].T for j in range(0, body, WINDOW)]
+    parcel = jnp.concatenate([table[...], normed[body:], *blocks], axis=0)
+    upper[...] = parcel[: upper.shape[0]]
+    lower[...] = parcel[upper.shape[0] :]
 
 
 def front(code_rows, queries, key_rows, values, sink_logit, o_weight, residual, norm_gain, routes, gate_codes, weights):
@@ -188,30 +200,41 @@
     place = jnp.stack([core, jnp.where((seq == 0) & (core == 0), 1, 0)]).astype(jnp.int32)
     ow_b = swapped(o_weight.T)
     steps = [(s, s + 1) for s in range(lax.axis_size("seq") - 1)]
-    rim = pack_rim(key_rows, values)
-    rim_a = lax.ppermute(rim, "seq", steps)
-    packed, gains = pack(place, sink_logit, norm_gain, key_rows, values, queries)
+    rim_a = lax.ppermute(pack_rim(key_rows, values), "seq", steps)
+    packed, *extra = pack(
+        code_rows, place, sink_logit, norm_gain, routes, gate_codes, key_rows, values, queries
+    )
     packed, rim_a = after(packed, rim_a)
     packed_b, rim_b = swapped(packed), swapped(rim_a)
-    weights, rim_b = after(weights, rim_b)
-    features, block = residual.shape[1], residual.shape[0] // lax.axis_size("exp")
+    weights, rim_a = after(weights, rim_a)
+    features = residual.shape[1]
     half = half_of(features)
-    shapes = [(features, block)] + ([(code_rows + half, block), (features - half, block)] if code_rows else [])
-    held = [queries[:WINDOW], o_weight.T]
-    held += [residual.T[:, :WINDOW], routes.T[:, :WINDOW], gate_codes.T[:, :WINDOW]]
+    blocks = queries.shape[1] // packed.shape[1]
+    held = ((blocks * WINDOW, packed.shape[1]), o_weight.T.shape, (features, WINDOW))
+    cost = pl.CostEstimate(flops=1, bytes_accessed=1, transcendentals=0)
+    params = pltpu.CompilerParams(vmem_limit_bytes=20 * 2**20)
+    stream = pl.pallas_call(
+        front_own_kernel,
+        out_shape=jax.ShapeDtypeStruct((features, WINDOW), F32),
+        in_specs=[SMEM] + [VMEM] * 2 + [ANY] * 3,
+        out_specs=VMEM,
+        scratch_shapes=[pltpu.VMEM(shape, BF16) for shape in held] + [pltpu.SemaphoreType.DMA((blocks + 2,))],
+        cost_estimate=cost,
+        compiler_params=params,
+        name="front_own",
+    )(place, packed, rim_a, in_hbm(queries), in_hbm(o_weight.T), in_hbm(residual.T))
+    shapes = [(features, WINDOW)]
+    if code_rows:
+        shapes += [(code_rows + half, WINDOW), (features - half, WINDOW)]
     outs = pl.pallas_call(
         functools.partial(front_kernel, code_rows),
         out_shape=[jax.ShapeDtypeStruct(shape, BF16) for shape in shapes],
-        in_specs=[SMEM] + [VMEM] * 6 + [ANY] * 5,
+        in_specs=[SMEM] + [VMEM] * (4 + len(extra)),
         out_specs=[VMEM] * len(shapes),
-        scratch_shapes=[pltpu.VMEM(h.shape, h.dtype) for h in held] + [pltpu.SemaphoreType.DMA((len(held),))],
-        cost_estimate=pl.CostEstimate(flops=2 * 10**9, bytes_accessed=10**7, transcendentals=10**6),
-        compiler_params=pltpu.CompilerParams(vmem_limit_bytes=20 * 2**20),
+        cost_estimate=cost,
+        compiler_params=params,
         name="front",
-    )(
-        place, gains, packed, rim_a, packed_b, rim_b, in_vmem(ow_b), in_hbm(queries), in_hbm(o_weight.T),
-        in_hbm(residual.T), in_hbm(routes.T), in_hbm(gate_codes.T),
-    )
+    )(place, packed_b, rim_b, in_vmem(ow_b), stream, *extra)
     return outs, weights
 
 
@@ -230,7 +253,7 @@
 
 
 def expert_kernel(code_rows, place, upper, lower, *refs):
-    weights, (out_upper, out_lower) = refs[:6], refs[6:]
+    weights, more, (out_upper, out_lower) = refs[:6], refs[6:-2], refs[-2:]
     parcel = jnp.concatenate([upper[...], lower[...]], axis=0)
     body = (parcel.shape[0] - code_rows) // WINDOW * WINDOW
     head = parcel.shape[0] - body
@@ -252,20 +275,20 @@
     terms = jnp.concatenate([terms[:, body:].T, *blocks], axis=0)
     half = out_upper.shape[0]
     out_upper[...] = terms[:half]
-    out_lower[...] = terms[half:]
-
-
-def expert_terms(code_rows, expert, weights, parcel):
+    out_lower[...] = add(terms[half:], more[0][...]) if more else terms[half:]
+
+
+def expert_terms(code_rows, expert, weights, parcel, *more):
     half, rest = parcel[0].shape[0] - code_rows, parcel[1].shape[0]
     return pl.pallas_call(
         functools.partial(expert_kernel, code_rows),
         out_shape=[jax.ShapeDtypeStruct((n, WINDOW), BF16) for n in (half, rest)],
-        in_specs=[SMEM] + [VMEM] * 8,
+        in_specs=[SMEM] + [VMEM] * (8 + len(more)),
         out_specs=[VMEM] * 2,
-        cost_estimate=pl.CostEstimate(flops=1, bytes_accessed=1, transcendentals=0),
+        cost_estimate=pl.CostEstimate(flops=1000000000, bytes_accessed=1, transcendentals=0),
         compiler_params=pltpu.CompilerParams(vmem_limit_bytes=24 * 2**20),
         name="experts",
-    )(expert, *parcel, *weights)
+    )(expert, *parcel, *weights, *more)
 
 
 def total_kernel(*refs):
@@ -297,10 +320,11 @@
     return features // 2 // BF16_ROWS * BF16_ROWS
 
 
-def ring_of(count):
+def ring_of(count, cores):
     order = list(range(0, count, 2)) + list(range(count - 1, 0, -2))
-    right = [(order[i], order[(i + 1) % count]) for i in range(count)]
-    return right, [(target, source) for source, target in right]
+    right = [(order[i], order[(i + 1) % count], core) for i in range(count) for core in range(cores)]
+    steps = [(s * cores + c, t * cores + c) if c % 2 == 0 else (t * cores + c, s * cores + c) for s, t, c in right]
+    return steps, [(target, source) for source, target in steps]
 
 
 def add(a, b):
@@ -309,29 +333,31 @@
 
 def mixed_by_ring(parcel, code_rows, weights):
     count = lax.axis_size("seq")
-    right, left = ring_of(count)
+    right, left = ring_of(count, lax.axis_size("exp"))
     far = count // 2
     expert = lax.axis_index("seq").astype(jnp.int32)[None]
-    to_right = functools.partial(lax.ppermute, axis_name="seq", perm=right)
-    to_left = functools.partial(lax.ppermute, axis_name="seq", perm=left)
+    to_right = functools.partial(lax.ppermute, axis_name=("seq", "exp"), perm=right)
+    to_left = functools.partial(lax.ppermute, axis_name=("seq", "exp"), perm=left)
     apply = functools.partial(expert_terms, code_rows, expert, weights)
     at = {0: parcel}
     at[-1], at[1] = [to_right(half) for half in parcel], [to_left(half) for half in parcel]
     terms = {}
 
-    def work(k, arrived):
+    def work(k, arrived, *more):
         at[k], arrived = after(at[k], arrived)
-        terms[k] = apply(at[k])
+        terms[k] = apply(at[k], *more)
         return arrived
 
     last = None
+    last = 0
+    terms[0] = apply(parcel)
     for k in range(2, far + 1):
         uppers, lowers = (at[1 - k][0], at[k - 1][0]), (at[1 - k][1], at[k - 1][1])
         if last is not None:
             uppers, terms[last] = after(uppers, terms[last])
         upper_left = to_right(uppers[0])
         upper_right = to_left(uppers[1]) if k < far else None
-        if k > 2:
+        if 2 < k == far:
             uppers = work(k - 2, uppers)
             lowers, terms[k - 2] = after(lowers, terms[k - 2])
         lower_left = to_right(lowers[0]) if k < far else None
@@ -348,15 +374,21 @@
     left_up = to_left(terms[1 - far][0])
     opposite, terms[1 - far] = after(opposite, terms[1 - far])
     farthest = apply(opposite)
-    farthest = work(0, farthest)
     right_up, left_low = to_right(farthest[0]), to_left(farthest[1])
-    (left_up, right_low), terms[0] = after((left_up, right_low), terms[0])
+    fused = False
+    farthest = work(1, farthest)
+    right_low, terms[1] = after(right_low, terms[1])
+    left_up, terms[1] = after(left_up, terms[1])
     for k in range(far - 1, 0, -1):
         if k > 1:
+            going = terms[k - 1][1]
+            if not fused:
+                going = add(going, right_low)
+            fused = False
+            right_low = to_right(going)
             left_up = to_left(add(terms[1 - k][0], left_up))
-            right_low = to_right(add(terms[k - 1][1], right_low))
+        right_up = to_right(add(terms[k][0], right_up))
         left_low = to_left(add(terms[-k][1], left_low))
-        right_up = to_right(add(terms[k][0], right_up))
     near, final = after((terms[0], left_up, right_low), (left_low, right_up))
     (upper, lower), left_up, right_low = near
     left_low, right_up = final

time: 89.9 us -> 86.8 us (0.966)
  waiting for transfers between devices: 22.7 us -> 19.8 us
  starting transfers between devices: 37.1 us -> 36.2 us
    pallas_call x1 -> x2, Pallas kernels: 1.84 us -> 5.6 us  [the longest x1 3.73 us: front(): pl.pallas_call(front_own_kernel, out_shape=jax.ShapeDtypeStruct((features...]
    ppermute x2, waiting for transfers between devices: 4.45 us -> 0.75 us  [mixed_by_ring(): to_right(half)]
    pallas_call x1, Pallas kernels: 6.44 us -> 3.25 us  [front(): pl.pallas_call(functools.partial(front_kernel, code_rows), out_shape=[jax...]
    ppermute x2, waiting for transfers between devices: 0.07 us -> 2.33 us  [mixed_by_ring(): to_left(half)]
    ppermute x3, starting transfers between devices: 1.4 us -> 3.01 us  [mixed_by_ring(): left_low = to_left(add(terms[-k][1], left_low))]
    ppermute x3, starting transfers between devices: 4.99 us -> 3.38 us  [mixed_by_ring(): right_up = to_right(add(terms[k][0], right_up))]
    ppermute x6, waiting for transfers between devices: 1.32 us -> 0.02 us  [swapped(): return lax.ppermute(value, 'exp', [(0, 1), (1, 0)])]
    ppermute x2, waiting for transfers between devices: 0.01 us -> 1.25 us  [mixed_by_ring(): lower_left = to_right(lowers[0]) if k < far else None]
  transfers between devices with their start and end apart: 35 -> 35, of which waited for: 11 -> 11; matrix products, arithmetic and copies ran while one was open for 1% -> 1% of each run, Pallas kernels for 30% -> 32%
where the time goes in v4:
time: 86.8 us; the launch traced here: 86.5 us
  starting transfers between devices  36.2 us (42%)
  Pallas kernels  28.4 us (33%)
  waiting for transfers between devices  19.8 us (23%)
    pallas_call x8, Pallas kernels, expert_terms(): pl.pallas_call(functools.partial(expert_kernel, code_rows), out_shape=[ja...  17.8 us
    ppermute x3, waiting for transfers between devices, mixed_by_ring(): right_up = to_right(add(terms[k][0], right_up))  8.52 us
    ppermute x3, starting transfers between devices, mixed_by_ring(): upper_left = to_right(uppers[0])  4.64 us
    ppermute x2, starting transfers between devices, mixed_by_ring(): lower_left = to_right(lowers[0]) if k < far else None  4.56 us
    ppermute x2, starting transfers between devices, mixed_by_ring(): to_right(half)  4.49 us
    ppermute x1, starting transfers between devices, front(): rim_a = lax.ppermute(pack_rim(key_rows, values), 'seq', steps)  4.44 us
    pallas_call x1, Pallas kernels, front(): pl.pallas_call(front_own_kernel, out_shape=jax.ShapeDtypeStruct((features...  3.73 us
    ppermute x3, starting transfers between devices, mixed_by_ring(): right_up = to_right(add(terms[k][0], right_up))  3.38 us
  transfers between devices with their start and end apart: 35, of which 11 were waited for; matrix products, arithmetic and copies ran while one was open for 1% of the time, Pallas kernels for 32%

profile of v4, /device:TPU:0, one launch (start us, length us, event | category | flops | bytes accessed | tf_op | source)
XLA Modules:
  0.0 86.5 jit_solution(9204670653473764807)
XLA Ops:
  1.1 0.8 rim.1
  1.9 4.4 %collective-permute-start = (bf16[256,128]{1,0:T(8,128)(2,1)S(1)}, bf16[256,128]{1,0:T(8,128)(2,1)S(1)}, u32[]{:S(2)}, u32[]{:S(2)}) collective-permute-start(bf16[256,128]{1,0:T(8,128)(2,1)S(1)} %rim.1), channel_id=1, source_target_pairs={{0,2},{2,4},{4,6},{6,8},{8,10},{10,12},{12,14},{1,3},{3,5},{5,7},{... | collective-permute-start | bytes 196616 | tf_op jit(solution)/shard_map/ppermute | solution.py:203
  6.4 0.7 broadcast_in_dim.6.gain
  7.2 1.9 %pack.1 = (bf16[1552,128]{1,0:T(8,128)(2,1)S(1)}, f32[1440,128]{1,0:T(8,128)S(1)}, bf16[16,128]{1,0:T(8,128)(2,1)S(1)}) custom-call(s32[2]{0:T(128)S(1)} %pad_add_fusion.place, f32[16]{0:T(128)} %sink.1, f32[1,1440]{1,0:T(1,128)S(1)} %broadcast_in_dim.6.gain, s32[4,256]{1,0:T(4,128)} %bitcast.43, s32[4,256]{1,0:T(4,128)} %bitcast.44, bf16[256,128]{1,0:T(8,128)(2,1)} %k.3, ...), custom_call_target="tpu_custom_call" | custom-call | flops 1 | bytes 1 | tf_op jit(solution)/shard_map/pack/pallas_call | solution.py:97
  10.2 3.7 %front_own.1.stream = f32[1440,128]{1,0:T(8,128)S(1)} custom-call(s32[2]{0:T(128)S(1)} %pad_add_fusion.place, bf16[1552,128]{1,0:T(8,128)(2,1)S(1)} %get-tuple-element.74.packed, bf16[256,128]{1,0:T(8,128)(2,1)S(1)} %collective-permute-done.rim, bf16[256,1024]{1,0:T(8,128)(2,1)} %q.3, bf16[1440,1024]{1,0:T(8,128)(2,1)} %bitcast.40, bf16[1440,256]{1,0:T(8,128)(2,1)} %bitcast.41), custom_call_target="tpu_custom_call" | custom-call | flops 1 | bytes 1 | tf_op jit(solution)/shard_map/front_own/pallas_call | solution.py:216
  14.0 3.2 %front.1 = (bf16[1440,128]{1,0:T(8,128)(2,1)}, bf16[736,128]{1,0:T(8,128)(2,1)S(1)}, bf16[720,128]{1,0:T(8,128)(2,1)S(1)}) custom-call(s32[2]{0:T(128)S(1)} %pad_add_fusion.place, bf16[1552,128]{1,0:T(8,128)(2,1)S(1)} %collective-permute-done.1.packed, bf16[256,128]{1,0:T(8,128)(2,1)S(1)} %collective-permute-done.2.rim, ...), custom_call_target="tpu_custom_call" | custom-call | flops 1 | bytes 1 | tf_op jit(solution)/shard_map/front/pallas_call | solution.py:229
  17.4 2.5 %collective-permute-start.4 = (bf16[736,128]{1,0:T(8,128)(2,1)S(1)}, bf16[736,128]{1,0:T(8,128)(2,1)S(1)}, u32[]{:S(2)}, u32[]{:S(2)}) collective-permute-start(bf16[736,128]{1,0:T(8,128)(2,1)S(1)} %get-tuple-element.83.upper), channel_id=1, source_target_pairs={{0,4},{5,1},{4,8},{9,5},{8,12},{13,9},{12,14},{15,13},{14,10},{11,... | collective-permute-start | bytes 565256 | tf_op jit(solution)/shard_map/ppermute | solution.py:343
  19.9 2.0 %collective-permute-start.11 = (bf16[720,128]{1,0:T(8,128)(2,1)S(1)}, bf16[720,128]{1,0:T(8,128)(2,1)S(1)}, u32[]{:S(2)}, u32[]{:S(2)}) collective-permute-start(bf16[720,128]{1,0:T(8,128)(2,1)S(1)} %get-tuple-element.84.lower), channel_id=1, source_target_pairs={{0,4},{5,1},{4,8},{9,5},{8,12},{13,9},{12,14},{15,13},{14,10},{11,... | collective-permute-start | bytes 552968 | tf_op jit(solution)/shard_map/ppermute | solution.py:343
  21.9 2.2 %experts.8 = (bf16[720,128]{1,0:T(8,128)(2,1)S(1)}, bf16[720,128]{1,0:T(8,128)(2,1)S(1)}) custom-call(s32[1]{0:T(128)} %bitcast.10.place, bf16[736,128]{1,0:T(8,128)(2,1)S(1)} %get-tuple-element.83.upper, bf16[720,128]{1,0:T(8,128)(2,1)S(1)} %get-tuple-element.84.lower, bf16[1440,720]{1,0:T(8,128)(2,1)S(1)} %bitcast.13, bf16[1440,720]{1,0:T(8,128)(2,1)S(1)} %bitcast.22, ...), custom_call_target="tpu_custom_call" | custom-call | flops 1000000000 | bytes 1 | tf_op jit(solution)/shard_map/experts/pallas_call | solution.py:283
  24.2 0.8 collective-permute-done.4.upper
  24.9 2.3 %collective-permute-done.5.upper = bf16[736,128]{1,0:T(8,128)(2,1)S(1)} collective-permute-done((bf16[736,128]{1,0:T(8,128)(2,1)S(1)}, bf16[736,128]{1,0:T(8,128)(2,1)S(1)}, u32[]{:S(2)}, u32[]{:S(2)}) %collective-permute-start.5) | collective-permute-done | bytes 188448 | tf_op jit(solution)/shard_map/ppermute | solution.py:343
  27.5 1.7 %collective-permute-start.9 = (bf16[736,128]{1,0:T(8,128)(2,1)S(1)}, bf16[736,128]{1,0:T(8,128)(2,1)S(1)}, u32[]{:S(2)}, u32[]{:S(2)}) collective-permute-start(bf16[736,128]{1,0:T(8,128)(2,1)S(1)} %collective-permute-done.4.upper), channel_id=1, source_target_pairs={{0,4},{5,1},{4,8},{9,5},{8,12},{13,9},{12,14},{15,13},{14,10},{11,... | collective-permute-start | bytes 565256 | tf_op jit(solution)/shard_map/ppermute | solution.py:358
  29.3 2.1 %collective-permute-start.14 = (bf16[720,128]{1,0:T(8,128)(2,1)S(1)}, bf16[720,128]{1,0:T(8,128)(2,1)S(1)}, u32[]{:S(2)}, u32[]{:S(2)}) collective-permute-start(bf16[720,128]{1,0:T(8,128)(2,1)S(1)} %collective-permute-done.11.lower), channel_id=1, source_target_pairs={{0,4},{5,1},{4,8},{9,5},{8,12},{13,9},{12,14},{15,13},{14,10},{11,... | collective-permute-start | bytes 552968 | tf_op jit(solution)/shard_map/ppermute | solution.py:363
  31.4 2.3 %experts.9 = (bf16[720,128]{1,0:T(8,128)(2,1)S(1)}, bf16[720,128]{1,0:T(8,128)(2,1)S(1)}) custom-call(s32[1]{0:T(128)} %bitcast.10.place, bf16[736,128]{1,0:T(8,128)(2,1)S(1)} %collective-permute-done.4.upper, bf16[720,128]{1,0:T(8,128)(2,1)S(1)} %collective-permute-done.11.lower, bf16[1440,720]{1,0:T(8,128)(2,1)S(1)} %bitcast.14, ...), custom_call_target="tpu_custom_call" | custom-call | flops 1000000000 | bytes 1 | tf_op jit(solution)/shard_map/experts/pallas_call | solution.py:283
  33.6 1.3 %collective-permute-done.10.upper = bf16[736,128]{1,0:T(8,128)(2,1)S(1)} collective-permute-done((bf16[736,128]{1,0:T(8,128)(2,1)S(1)}, bf16[736,128]{1,0:T(8,128)(2,1)S(1)}, u32[]{:S(2)}, u32[]{:S(2)}) %collective-permute-start.10) | collective-permute-done | bytes 188448 | tf_op jit(solution)/shard_map/ppermute | solution.py:359
  34.9 1.8 %collective-permute-start.12 = (bf16[736,128]{1,0:T(8,128)(2,1)S(1)}, bf16[736,128]{1,0:T(8,128)(2,1)S(1)}, u32[]{:S(2)}, u32[]{:S(2)}) collective-permute-start(bf16[736,128]{1,0:T(8,128)(2,1)S(1)} %collective-permute-done.9.upper), channel_id=1, source_target_pairs={{0,4},{5,1},{4,8},{9,5},{8,12},{13,9},{12,14},{15,13},{14,10},{11,... | collective-permute-start | bytes 565256 | tf_op jit(solution)/shard_map/ppermute | solution.py:358
  36.9 1.2 %collective-permute-done.14.lower = bf16[720,128]{1,0:T(8,128)(2,1)S(1)} collective-permute-done((bf16[720,128]{1,0:T(8,128)(2,1)S(1)}, bf16[720,128]{1,0:T(8,128)(2,1)S(1)}, u32[]{:S(2)}, u32[]{:S(2)}) %collective-permute-start.14) | collective-permute-done | bytes 184352 | tf_op jit(solution)/shard_map/ppermute | solution.py:363
  38.2 2.5 %collective-permute-start.17 = (bf16[720,128]{1,0:T(8,128)(2,1)S(1)}, bf16[720,128]{1,0:T(8,128)(2,1)S(1)}, u32[]{:S(2)}, u32[]{:S(2)}) collective-permute-start(bf16[720,128]{1,0:T(8,128)(2,1)S(1)} %collective-permute-done.14.lower), channel_id=1, source_target_pairs={{0,4},{5,1},{4,8},{9,5},{8,12},{13,9},{12,14},{15,13},{14,10},{11,... | collective-permute-start | bytes 552968 | tf_op jit(solution)/shard_map/ppermute | solution.py:363
  40.7 2.2 %experts.10 = (bf16[720,128]{1,0:T(8,128)(2,1)S(1)}, bf16[720,128]{1,0:T(8,128)(2,1)S(1)}) custom-call(s32[1]{0:T(128)} %bitcast.10.place, bf16[736,128]{1,0:T(8,128)(2,1)S(1)} %collective-permute-done.9.upper, bf16[720,128]{1,0:T(8,128)(2,1)S(1)} %collective-permute-done.14.lower, bf16[1440,720]{1,0:T(8,128)(2,1)S(1)} %bitcast.15, ...), custom_call_target="tpu_custom_call" | custom-call | flops 1000000000 | bytes 1 | tf_op jit(solution)/shard_map/experts/pallas_call | solution.py:283
  42.9 1.2 %collective-permute-done.13.upper = bf16[736,128]{1,0:T(8,128)(2,1)S(1)} collective-permute-done((bf16[736,128]{1,0:T(8,128)(2,1)S(1)}, bf16[736,128]{1,0:T(8,128)(2,1)S(1)}, u32[]{:S(2)}, u32[]{:S(2)}) %collective-permute-start.13) | collective-permute-done | bytes 188448 | tf_op jit(solution)/shard_map/ppermute | solution.py:359
  44.1 1.1 %collective-permute-start.21 = (bf16[736,128]{1,0:T(8,128)(2,1)S(1)}, bf16[736,128]{1,0:T(8,128)(2,1)S(1)}, u32[]{:S(2)}, u32[]{:S(2)}) collective-permute-start(bf16[736,128]{1,0:T(8,128)(2,1)S(1)} %collective-permute-done.12.upper), channel_id=1, source_target_pairs={{0,4},{5,1},{4,8},{9,5},{8,12},{13,9},{12,14},{15,13},{14,10},{11,... | collective-permute-start | bytes 565256 | tf_op jit(solution)/shard_map/ppermute | solution.py:358
  45.1 2.2 %experts.11 = (bf16[720,128]{1,0:T(8,128)(2,1)S(1)}, bf16[720,128]{1,0:T(8,128)(2,1)S(1)}) custom-call(s32[1]{0:T(128)} %bitcast.10.place, bf16[736,128]{1,0:T(8,128)(2,1)S(1)} %collective-permute-done.10.upper, bf16[720,128]{1,0:T(8,128)(2,1)S(1)} %collective-permute-done.16.lower, bf16[1440,720]{1,0:T(8,128)(2,1)S(1)} %bitcast.16, ...), custom_call_target="tpu_custom_call" | custom-call | flops 1000000000 | bytes 1 | tf_op jit(solution)/shard_map/experts/pallas_call | solution.py:283
  47.4 1.0 %collective-permute-start.22 = (bf16[720,128]{1,0:T(8,128)(2,1)S(1)}, bf16[720,128]{1,0:T(8,128)(2,1)S(1)}, u32[]{:S(2)}, u32[]{:S(2)}) collective-permute-start(bf16[720,128]{1,0:T(8,128)(2,1)S(1)} %collective-permute-done.18.lower), channel_id=1, source_target_pairs={{4,0},{1,5},{8,4},{5,9},{12,8},{9,13},{14,12},{13,15},{10,14},{15,... | collective-permute-start | bytes 552968 | tf_op jit(solution)/shard_map/ppermute | solution.py:364
  48.3 2.2 %experts.12 = (bf16[720,128]{1,0:T(8,128)(2,1)S(1)}, bf16[720,128]{1,0:T(8,128)(2,1)S(1)}) custom-call(s32[1]{0:T(128)} %bitcast.10.place, bf16[736,128]{1,0:T(8,128)(2,1)S(1)} %collective-permute-done.13.upper, bf16[720,128]{1,0:T(8,128)(2,1)S(1)} %collective-permute-done.18.lower, bf16[1440,720]{1,0:T(8,128)(2,1)S(1)} %bitcast.17, ...), custom_call_target="tpu_custom_call" | custom-call | flops 1000000000 | bytes 1 | tf_op jit(solution)/shard_map/experts/pallas_call | solution.py:283
  50.6 1.1 %collective-permute-start.20 = (bf16[720,128]{1,0:T(8,128)(2,1)S(1)}, bf16[720,128]{1,0:T(8,128)(2,1)S(1)}, u32[]{:S(2)}, u32[]{:S(2)}) collective-permute-start(bf16[720,128]{1,0:T(8,128)(2,1)S(1)} %get-tuple-element.113), channel_id=1, source_target_pairs={{0,4},{5,1},{4,8},{9,5},{8,12},{13,9},{12,14},{15,13},{14,10},{11,... | collective-permute-start | bytes 552968 | tf_op jit(solution)/shard_map/ppermute | solution.py:372
  51.7 2.2 %experts.13 = (bf16[720,128]{1,0:T(8,128)(2,1)S(1)}, bf16[720,128]{1,0:T(8,128)(2,1)S(1)}) custom-call(s32[1]{0:T(128)} %bitcast.10.place, bf16[736,128]{1,0:T(8,128)(2,1)S(1)} %collective-permute-done.12.upper, bf16[720,128]{1,0:T(8,128)(2,1)S(1)} %collective-permute-done.17.lower, bf16[1440,720]{1,0:T(8,128)(2,1)S(1)} %bitcast.18, ...), custom_call_target="tpu_custom_call" | custom-call | flops 1000000000 | bytes 1 | tf_op jit(solution)/shard_map/experts/pallas_call | solution.py:283
  53.9 1.0 %collective-permute-start.19 = (bf16[720,128]{1,0:T(8,128)(2,1)S(1)}, bf16[720,128]{1,0:T(8,128)(2,1)S(1)}, u32[]{:S(2)}, u32[]{:S(2)}) collective-permute-start(bf16[720,128]{1,0:T(8,128)(2,1)S(1)} %get-tuple-element.116), channel_id=1, source_target_pairs={{4,0},{1,5},{8,4},{5,9},{12,8},{9,13},{14,12},{13,15},{10,14},{15,... | collective-permute-start | bytes 552968 | tf_op jit(solution)/shard_map/ppermute | solution.py:374
  54.9 2.2 %experts.14 = (bf16[720,128]{1,0:T(8,128)(2,1)S(1)}, bf16[720,128]{1,0:T(8,128)(2,1)S(1)}) custom-call(s32[1]{0:T(128)} %bitcast.10.place, bf16[736,128]{1,0:T(8,128)(2,1)S(1)} %collective-permute-done.21.upper, bf16[720,128]{1,0:T(8,128)(2,1)S(1)} %collective-permute-done.22.lower, bf16[1440,720]{1,0:T(8,128)(2,1)S(1)} %bitcast.19, ...), custom_call_target="tpu_custom_call" | custom-call | flops 1000000000 | bytes 1 | tf_op jit(solution)/shard_map/experts/pallas_call | solution.py:283
  57.1 1.1 %collective-permute-start.31 = (bf16[720,128]{1,0:T(8,128)(2,1)S(1)}, bf16[720,128]{1,0:T(8,128)(2,1)S(1)}, u32[]{:S(2)}, u32[]{:S(2)}) collective-permute-start(bf16[720,128]{1,0:T(8,128)(2,1)S(1)} %get-tuple-element.120), channel_id=1, source_target_pairs={{0,4},{5,1},{4,8},{9,5},{8,12},{13,9},{12,14},{15,13},{14,10},{11,... | collective-permute-start | bytes 552968 | tf_op jit(solution)/shard_map/ppermute | solution.py:377
  58.1 1.0 %collective-permute-start.27 = (bf16[720,128]{1,0:T(8,128)(2,1)S(1)}, bf16[720,128]{1,0:T(8,128)(2,1)S(1)}, u32[]{:S(2)}, u32[]{:S(2)}) collective-permute-start(bf16[720,128]{1,0:T(8,128)(2,1)S(1)} %get-tuple-element.121), channel_id=1, source_target_pairs={{4,0},{1,5},{8,4},{5,9},{12,8},{9,13},{14,12},{13,15},{10,14},{15,... | collective-permute-start | bytes 552968 | tf_op jit(solution)/shard_map/ppermute | solution.py:377
  59.1 2.3 %experts.15 = (bf16[720,128]{1,0:T(8,128)(2,1)S(1)}, bf16[720,128]{1,0:T(8,128)(2,1)S(1)}) custom-call(s32[1]{0:T(128)} %bitcast.10.place, bf16[736,128]{1,0:T(8,128)(2,1)S(1)} %collective-permute-done.5.upper, bf16[720,128]{1,0:T(8,128)(2,1)S(1)} %collective-permute-done.15.lower, bf16[1440,720]{1,0:T(8,128)(2,1)S(1)} %bitcast.20, ...), custom_call_target="tpu_custom_call" | custom-call | flops 1000000000 | bytes 1 | tf_op jit(solution)/shard_map/experts/pallas_call | solution.py:283
  61.4 1.1 %collective-permute-start.25 = (bf16[720,128]{1,0:T(8,128)(2,1)S(1)}, bf16[720,128]{1,0:T(8,128)(2,1)S(1)}, u32[]{:S(2)}, u32[]{:S(2)}) collective-permute-start(bf16[720,128]{1,0:T(8,128)(2,1)S(1)} %add_convert_fusion.7), channel_id=1, source_target_pairs={{0,4},{5,1},{4,8},{9,5},{8,12},{13,9},{12,14},{15,13},{14,10},{11,... | collective-permute-start | bytes 552968 | tf_op jit(solution)/shard_map/ppermute | solution.py:388
  62.6 1.0 %collective-permute-start.23 = (bf16[720,128]{1,0:T(8,128)(2,1)S(1)}, bf16[720,128]{1,0:T(8,128)(2,1)S(1)}, u32[]{:S(2)}, u32[]{:S(2)}) collective-permute-start(bf16[720,128]{1,0:T(8,128)(2,1)S(1)} %add_convert_fusion.9), channel_id=1, source_target_pairs={{4,0},{1,5},{8,4},{5,9},{12,8},{9,13},{14,12},{13,15},{10,14},{15,... | collective-permute-start | bytes 552968 | tf_op jit(solution)/shard_map/ppermute | solution.py:389
  63.6 1.0 %collective-permute-done.31 = bf16[720,128]{1,0:T(8,128)(2,1)S(1)} collective-permute-done((bf16[720,128]{1,0:T(8,128)(2,1)S(1)}, bf16[720,128]{1,0:T(8,128)(2,1)S(1)}, u32[]{:S(2)}, u32[]{:S(2)}) %collective-permute-start.31) | collective-permute-done | bytes 184352 | tf_op jit(solution)/shard_map/ppermute | solution.py:377
  64.6 1.1 %collective-permute-start.32 = (bf16[720,128]{1,0:T(8,128)(2,1)S(1)}, bf16[720,128]{1,0:T(8,128)(2,1)S(1)}, u32[]{:S(2)}, u32[]{:S(2)}) collective-permute-start(bf16[720,128]{1,0:T(8,128)(2,1)S(1)} %add_convert_fusion.2), channel_id=1, source_target_pairs={{0,4},{5,1},{4,8},{9,5},{8,12},{13,9},{12,14},{15,13},{14,10},{11,... | collective-permute-start | bytes 552968 | tf_op jit(solution)/shard_map/ppermute | solution.py:390
  65.8 1.0 %collective-permute-start.28 = (bf16[720,128]{1,0:T(8,128)(2,1)S(1)}, bf16[720,128]{1,0:T(8,128)(2,1)S(1)}, u32[]{:S(2)}, u32[]{:S(2)}) collective-permute-start(bf16[720,128]{1,0:T(8,128)(2,1)S(1)} %add_convert_fusion.5), channel_id=1, source_target_pairs={{4,0},{1,5},{8,4},{5,9},{12,8},{9,13},{14,12},{13,15},{10,14},{15,... | collective-permute-start | bytes 552968 | tf_op jit(solution)/shard_map/ppermute | solution.py:391
  66.8 2.2 %collective-permute-done.25 = bf16[720,128]{1,0:T(8,128)(2,1)S(1)} collective-permute-done((bf16[720,128]{1,0:T(8,128)(2,1)S(1)}, bf16[720,128]{1,0:T(8,128)(2,1)S(1)}, u32[]{:S(2)}, u32[]{:S(2)}) %collective-permute-start.25) | collective-permute-done | bytes 184352 | tf_op jit(solution)/shard_map/ppermute | solution.py:388
  69.1 1.1 %collective-permute-start.26 = (bf16[720,128]{1,0:T(8,128)(2,1)S(1)}, bf16[720,128]{1,0:T(8,128)(2,1)S(1)}, u32[]{:S(2)}, u32[]{:S(2)}) collective-permute-start(bf16[720,128]{1,0:T(8,128)(2,1)S(1)} %add_convert_fusion.6), channel_id=1, source_target_pairs={{0,4},{5,1},{4,8},{9,5},{8,12},{13,9},{12,14},{15,13},{14,10},{11,... | collective-permute-start | bytes 552968 | tf_op jit(solution)/shard_map/ppermute | solution.py:388
  70.3 1.0 %collective-permute-start.24 = (bf16[720,128]{1,0:T(8,128)(2,1)S(1)}, bf16[720,128]{1,0:T(8,128)(2,1)S(1)}, u32[]{:S(2)}, u32[]{:S(2)}) collective-permute-start(bf16[720,128]{1,0:T(8,128)(2,1)S(1)} %add_convert_fusion.8), channel_id=1, source_target_pairs={{4,0},{1,5},{8,4},{5,9},{12,8},{9,13},{14,12},{13,15},{10,14},{15,... | collective-permute-start | bytes 552968 | tf_op jit(solution)/shard_map/ppermute | solution.py:389
  71.3 1.7 %collective-permute-done.32 = bf16[720,128]{1,0:T(8,128)(2,1)S(1)} collective-permute-done((bf16[720,128]{1,0:T(8,128)(2,1)S(1)}, bf16[720,128]{1,0:T(8,128)(2,1)S(1)}, u32[]{:S(2)}, u32[]{:S(2)}) %collective-permute-start.32) | collective-permute-done | bytes 184352 | tf_op jit(solution)/shard_map/ppermute | solution.py:390
  73.1 1.1 %collective-permute-start.33 = (bf16[720,128]{1,0:T(8,128)(2,1)S(1)}, bf16[720,128]{1,0:T(8,128)(2,1)S(1)}, u32[]{:S(2)}, u32[]{:S(2)}) collective-permute-start(bf16[720,128]{1,0:T(8,128)(2,1)S(1)} %add_convert_fusion.1), channel_id=1, source_target_pairs={{0,4},{5,1},{4,8},{9,5},{8,12},{13,9},{12,14},{15,13},{14,10},{11,... | collective-permute-start | bytes 552968 | tf_op jit(solution)/shard_map/ppermute | solution.py:390
  74.2 1.0 %collective-permute-start.29 = (bf16[720,128]{1,0:T(8,128)(2,1)S(1)}, bf16[720,128]{1,0:T(8,128)(2,1)S(1)}, u32[]{:S(2)}, u32[]{:S(2)}) collective-permute-start(bf16[720,128]{1,0:T(8,128)(2,1)S(1)} %add_convert_fusion.4), channel_id=1, source_target_pairs={{4,0},{1,5},{8,4},{5,9},{12,8},{9,13},{14,12},{13,15},{10,14},{15,... | collective-permute-start | bytes 552968 | tf_op jit(solution)/shard_map/ppermute | solution.py:391
  75.3 3.4 %collective-permute-done.33 = bf16[720,128]{1,0:T(8,128)(2,1)S(1)} collective-permute-done((bf16[720,128]{1,0:T(8,128)(2,1)S(1)}, bf16[720,128]{1,0:T(8,128)(2,1)S(1)}, u32[]{:S(2)}, u32[]{:S(2)}) %collective-permute-start.33) | collective-permute-done | bytes 184352 | tf_op jit(solution)/shard_map/ppermute | solution.py:390
  78.7 1.1 %collective-permute-start.34 = (bf16[720,128]{1,0:T(8,128)(2,1)S(1)}, bf16[720,128]{1,0:T(8,128)(2,1)S(1)}, u32[]{:S(2)}, u32[]{:S(2)}) collective-permute-start(bf16[720,128]{1,0:T(8,128)(2,1)S(1)} %add_convert_fusion), channel_id=1, source_target_pairs={{0,4},{5,1},{4,8},{9,5},{8,12},{13,9},{12,14},{15,13},{14,10},{11,... | collective-permute-start | bytes 552968 | tf_op jit(solution)/shard_map/ppermute | solution.py:390
  79.9 1.0 %collective-permute-start.30 = (bf16[720,128]{1,0:T(8,128)(2,1)S(1)}, bf16[720,128]{1,0:T(8,128)(2,1)S(1)}, u32[]{:S(2)}, u32[]{:S(2)}) collective-permute-start(bf16[720,128]{1,0:T(8,128)(2,1)S(1)} %add_convert_fusion.3), channel_id=1, source_target_pairs={{4,0},{1,5},{8,4},{5,9},{12,8},{9,13},{14,12},{13,15},{10,14},{15,... | collective-permute-start | bytes 552968 | tf_op jit(solution)/shard_map/ppermute | solution.py:391
  80.9 3.4 %collective-permute-done.34.refs_2_ = bf16[720,128]{1,0:T(8,128)(2,1)S(1)} collective-permute-done((bf16[720,128]{1,0:T(8,128)(2,1)S(1)}, bf16[720,128]{1,0:T(8,128)(2,1)S(1)}, u32[]{:S(2)}, u32[]{:S(2)}) %collective-permute-start.34) | collective-permute-done | bytes 184352 | tf_op jit(solution)/shard_map/ppermute | solution.py:390
  84.3 1.2 %collective-permute-done.30.refs_4_ = bf16[720,128]{1,0:T(8,128)(2,1)S(1)} collective-permute-done((bf16[720,128]{1,0:T(8,128)(2,1)S(1)}, bf16[720,128]{1,0:T(8,128)(2,1)S(1)}, u32[]{:S(2)}, u32[]{:S(2)}) %collective-permute-start.30) | collective-permute-done | bytes 184352 | tf_op jit(solution)/shard_map/ppermute | solution.py:391
  85.5 0.9 %total.1 = bf16[1440,128]{1,0:T(8,128)(2,1)} custom-call(bf16[720,128]{1,0:T(8,128)(2,1)S(1)} %get-tuple-element.138.refs_0_, bf16[720,128]{1,0:T(8,128)(2,1)S(1)} %collective-permute-done.24.refs_1_, bf16[720,128]{1,0:T(8,128)(2,1)S(1)} %collective-permute-done.34.refs_2_, bf16[720,128]{1,0:T(8,128)(2,1)S(1)} %get-tuple-element.141.refs_3_, ...), custom_call_target="tpu_custom_call" | custom-call | flops 1 | bytes 1 | tf_op jit(solution)/shard_map/total/pallas_call | solution.py:308
  (53 shorter events, 3.0 us)
Async XLA Ops:
  0.6 13.3 %collective-permute-start.3 = (bf16[1440,1024]{1,0:T(8,128)(2,1)}, bf16[1440,1024]{1,0:T(8,128)(2,1)S(1)}, u32[]{:S(2)}, u32[]{:S(2)}) collective-permute-start(bf16[1440,1024]{1,0:T(8,128)(2,1)} %bitcast.39), channel_id=1, source_target_pairs={{0,1},{1,0},{2,3},{3,2},{4,5},{5,4},{6,7},{7,6},{8,9},{9,8},{10,11... | collective-permute-start | bytes 8847368 | tf_op jit(solution)/shard_map/ppermute | solution.py:242
  1.9 7.1 %collective-permute-start = (bf16[256,128]{1,0:T(8,128)(2,1)S(1)}, bf16[256,128]{1,0:T(8,128)(2,1)S(1)}, u32[]{:S(2)}, u32[]{:S(2)}) collective-permute-start(bf16[256,128]{1,0:T(8,128)(2,1)S(1)} %rim.1), channel_id=1, source_target_pairs={{0,2},{2,4},{4,6},{6,8},{8,10},{10,12},{12,14},{1,3},{3,5},{5,7},{... | collective-permute-start | bytes 196616 | tf_op jit(solution)/shard_map/ppermute | solution.py:203
  9.1 4.8 %collective-permute-start.1 = (bf16[1552,128]{1,0:T(8,128)(2,1)S(1)}, bf16[1552,128]{1,0:T(8,128)(2,1)S(1)}, u32[]{:S(2)}, u32[]{:S(2)}) collective-permute-start(bf16[1552,128]{1,0:T(8,128)(2,1)S(1)} %get-tuple-element.74.packed), channel_id=1, source_target_pairs={{0,1},{1,0},{2,3},{3,2},{4,5},{5,4},{6,7},{7,6},{8,9},{9,8},{10,11... | collective-permute-start | bytes 1191944 | tf_op jit(solution)/shard_map/ppermute | solution.py:242
  9.3 4.6 %collective-permute-start.2 = (bf16[256,128]{1,0:T(8,128)(2,1)S(1)}, bf16[256,128]{1,0:T(8,128)(2,1)S(1)}, u32[]{:S(2)}, u32[]{:S(2)}) collective-permute-start(bf16[256,128]{1,0:T(8,128)(2,1)S(1)} %collective-permute-done.rim), channel_id=1, source_target_pairs={{0,1},{1,0},{2,3},{3,2},{4,5},{5,4},{6,7},{7,6},{8,9},{9,8},{10,11... | collective-permute-start | bytes 196616 | tf_op jit(solution)/shard_map/ppermute | solution.py:242
  9.7 10.2 %collective-permute-start.6 = (bf16[1440,720]{1,0:T(8,128)(2,1)}, bf16[1440,720]{1,0:T(8,128)(2,1)S(1)}, u32[]{:S(2)}, u32[]{:S(2)}) collective-permute-start(bf16[1440,720]{1,0:T(8,128)(2,1)} %bitcast.12), channel_id=1, source_target_pairs={{0,1},{1,0},{2,3},{3,2},{4,5},{5,4},{6,7},{7,6},{8,9},{9,8},{10,11... | collective-permute-start | bytes 6220808 | tf_op jit(solution)/shard_map/ppermute | solution.py:242
  9.9 12.1 %collective-permute-start.7 = (bf16[1440,720]{1,0:T(8,128)(2,1)}, bf16[1440,720]{1,0:T(8,128)(2,1)S(1)}, u32[]{:S(2)}, u32[]{:S(2)}) collective-permute-start(bf16[1440,720]{1,0:T(8,128)(2,1)} %bitcast.21), channel_id=1, source_target_pairs={{0,1},{1,0},{2,3},{3,2},{4,5},{5,4},{6,7},{7,6},{8,9},{9,8},{10,11... | collective-permute-start | bytes 6220808 | tf_op jit(solution)/shard_map/ppermute | solution.py:242
  10.2 7.0 %copy-start.2 = (bf16[1,720,1440]{2,1,0:T(8,128)(2,1)S(1)}, bf16[1,720,1440]{2,1,0:T(8,128)(2,1)}, u32[]{:S(2)}) copy-start(bf16[1,720,1440]{2,1,0:T(8,128)(2,1)} %param.23) | copy-start | bytes 6220804
  13.9 8.0 %copy-start = (bf16[1,1440,720]{2,1,0:T(8,128)(2,1)S(1)}, bf16[1,1440,720]{2,1,0:T(8,128)(2,1)}, u32[]{:S(2)}) copy-start(bf16[1,1440,720]{2,1,0:T(8,128)(2,1)} %param.21) | copy-start | bytes 6220804
  13.9 8.0 %copy-start.1 = (bf16[1,1440,720]{2,1,0:T(8,128)(2,1)S(1)}, bf16[1,1440,720]{2,1,0:T(8,128)(2,1)}, u32[]{:S(2)}) copy-start(bf16[1,1440,720]{2,1,0:T(8,128)(2,1)} %param.22) | copy-start | bytes 6220804
  17.2 4.7 %collective-permute-start.8 = (bf16[720,1440]{1,0:T(8,128)(2,1)S(1)}, bf16[720,1440]{1,0:T(8,128)(2,1)S(1)}, u32[]{:S(2)}, u32[]{:S(2)}) collective-permute-start(bf16[720,1440]{1,0:T(8,128)(2,1)S(1)} %bitcast.30), channel_id=1, source_target_pairs={{0,1},{1,0},{2,3},{3,2},{4,5},{5,4},{6,7},{7,6},{8,9},{9,8},{10,11... | collective-permute-start | bytes 6220808 | tf_op jit(solution)/shard_map/ppermute | solution.py:242
  17.4 7.5 %collective-permute-start.4 = (bf16[736,128]{1,0:T(8,128)(2,1)S(1)}, bf16[736,128]{1,0:T(8,128)(2,1)S(1)}, u32[]{:S(2)}, u32[]{:S(2)}) collective-permute-start(bf16[736,128]{1,0:T(8,128)(2,1)S(1)} %get-tuple-element.83.upper), channel_id=1, source_target_pairs={{0,4},{5,1},{4,8},{9,5},{8,12},{13,9},{12,14},{15,13},{14,10},{11,... | collective-permute-start | bytes 565256 | tf_op jit(solution)/shard_map/ppermute | solution.py:343
  19.9 7.4 %collective-permute-start.5 = (bf16[736,128]{1,0:T(8,128)(2,1)S(1)}, bf16[736,128]{1,0:T(8,128)(2,1)S(1)}, u32[]{:S(2)}, u32[]{:S(2)}) collective-permute-start(bf16[736,128]{1,0:T(8,128)(2,1)S(1)} %get-tuple-element.83.upper), channel_id=1, source_target_pairs={{4,0},{1,5},{8,4},{5,9},{12,8},{9,13},{14,12},{13,15},{10,14},{15,... | collective-permute-start | bytes 565256 | tf_op jit(solution)/shard_map/ppermute | solution.py:343
  19.9 9.4 %collective-permute-start.11 = (bf16[720,128]{1,0:T(8,128)(2,1)S(1)}, bf16[720,128]{1,0:T(8,128)(2,1)S(1)}, u32[]{:S(2)}, u32[]{:S(2)}) collective-permute-start(bf16[720,128]{1,0:T(8,128)(2,1)S(1)} %get-tuple-element.84.lower), channel_id=1, source_target_pairs={{0,4},{5,1},{4,8},{9,5},{8,12},{13,9},{12,14},{15,13},{14,10},{11,... | collective-permute-start | bytes 552968 | tf_op jit(solution)/shard_map/ppermute | solution.py:343
  21.9 9.4 %collective-permute-start.15 = (bf16[720,128]{1,0:T(8,128)(2,1)S(1)}, bf16[720,128]{1,0:T(8,128)(2,1)S(1)}, u32[]{:S(2)}, u32[]{:S(2)}) collective-permute-start(bf16[720,128]{1,0:T(8,128)(2,1)S(1)} %get-tuple-element.84.lower), channel_id=1, source_target_pairs={{4,0},{1,5},{8,4},{5,9},{12,8},{9,13},{14,12},{13,15},{10,14},{15,... | collective-permute-start | bytes 552968 | tf_op jit(solution)/shard_map/ppermute | solution.py:343
  27.3 7.7 %collective-permute-start.10 = (bf16[736,128]{1,0:T(8,128)(2,1)S(1)}, bf16[736,128]{1,0:T(8,128)(2,1)S(1)}, u32[]{:S(2)}, u32[]{:S(2)}) collective-permute-start(bf16[736,128]{1,0:T(8,128)(2,1)S(1)} %collective-permute-done.5.upper), channel_id=1, source_target_pairs={{4,0},{1,5},{8,4},{5,9},{12,8},{9,13},{14,12},{13,15},{10,14},{15,... | collective-permute-start | bytes 565256 | tf_op jit(solution)/shard_map/ppermute | solution.py:359
  27.5 7.4 %collective-permute-start.9 = (bf16[736,128]{1,0:T(8,128)(2,1)S(1)}, bf16[736,128]{1,0:T(8,128)(2,1)S(1)}, u32[]{:S(2)}, u32[]{:S(2)}) collective-permute-start(bf16[736,128]{1,0:T(8,128)(2,1)S(1)} %collective-permute-done.4.upper), channel_id=1, source_target_pairs={{0,4},{5,1},{4,8},{9,5},{8,12},{13,9},{12,14},{15,13},{14,10},{11,... | collective-permute-start | bytes 565256 | tf_op jit(solution)/shard_map/ppermute | solution.py:358
  29.3 8.9 %collective-permute-start.14 = (bf16[720,128]{1,0:T(8,128)(2,1)S(1)}, bf16[720,128]{1,0:T(8,128)(2,1)S(1)}, u32[]{:S(2)}, u32[]{:S(2)}) collective-permute-start(bf16[720,128]{1,0:T(8,128)(2,1)S(1)} %collective-permute-done.11.lower), channel_id=1, source_target_pairs={{0,4},{5,1},{4,8},{9,5},{8,12},{13,9},{12,14},{15,13},{14,10},{11,... | collective-permute-start | bytes 552968 | tf_op jit(solution)/shard_map/ppermute | solution.py:363
  31.4 9.3 %collective-permute-start.16 = (bf16[720,128]{1,0:T(8,128)(2,1)S(1)}, bf16[720,128]{1,0:T(8,128)(2,1)S(1)}, u32[]{:S(2)}, u32[]{:S(2)}) collective-permute-start(bf16[720,128]{1,0:T(8,128)(2,1)S(1)} %collective-permute-done.15.lower), channel_id=1, source_target_pairs={{4,0},{1,5},{8,4},{5,9},{12,8},{9,13},{14,12},{13,15},{10,14},{15,... | collective-permute-start | bytes 552968 | tf_op jit(solution)/shard_map/ppermute | solution.py:364
  34.9 8.0 %collective-permute-start.12 = (bf16[736,128]{1,0:T(8,128)(2,1)S(1)}, bf16[736,128]{1,0:T(8,128)(2,1)S(1)}, u32[]{:S(2)}, u32[]{:S(2)}) collective-permute-start(bf16[736,128]{1,0:T(8,128)(2,1)S(1)} %collective-permute-done.9.upper), channel_id=1, source_target_pairs={{0,4},{5,1},{4,8},{9,5},{8,12},{13,9},{12,14},{15,13},{14,10},{11,... | collective-permute-start | bytes 565256 | tf_op jit(solution)/shard_map/ppermute | solution.py:358
  36.7 7.3 %collective-permute-start.13 = (bf16[736,128]{1,0:T(8,128)(2,1)S(1)}, bf16[736,128]{1,0:T(8,128)(2,1)S(1)}, u32[]{:S(2)}, u32[]{:S(2)}) collective-permute-start(bf16[736,128]{1,0:T(8,128)(2,1)S(1)} %collective-permute-done.10.upper), channel_id=1, source_target_pairs={{4,0},{1,5},{8,4},{5,9},{12,8},{9,13},{14,12},{13,15},{10,14},{15,... | collective-permute-start | bytes 565256 | tf_op jit(solution)/shard_map/ppermute | solution.py:359
  38.2 9.2 %collective-permute-start.17 = (bf16[720,128]{1,0:T(8,128)(2,1)S(1)}, bf16[720,128]{1,0:T(8,128)(2,1)S(1)}, u32[]{:S(2)}, u32[]{:S(2)}) collective-permute-start(bf16[720,128]{1,0:T(8,128)(2,1)S(1)} %collective-permute-done.14.lower), channel_id=1, source_target_pairs={{0,4},{5,1},{4,8},{9,5},{8,12},{13,9},{12,14},{15,13},{14,10},{11,... | collective-permute-start | bytes 552968 | tf_op jit(solution)/shard_map/ppermute | solution.py:363
  40.7 6.7 %collective-permute-start.18 = (bf16[720,128]{1,0:T(8,128)(2,1)S(1)}, bf16[720,128]{1,0:T(8,128)(2,1)S(1)}, u32[]{:S(2)}, u32[]{:S(2)}) collective-permute-start(bf16[720,128]{1,0:T(8,128)(2,1)S(1)} %collective-permute-done.16.lower), channel_id=1, source_target_pairs={{4,0},{1,5},{8,4},{5,9},{12,8},{9,13},{14,12},{13,15},{10,14},{15,... | collective-permute-start | bytes 552968 | tf_op jit(solution)/shard_map/ppermute | solution.py:364
  44.1 10.8 %collective-permute-start.21 = (bf16[736,128]{1,0:T(8,128)(2,1)S(1)}, bf16[736,128]{1,0:T(8,128)(2,1)S(1)}, u32[]{:S(2)}, u32[]{:S(2)}) collective-permute-start(bf16[736,128]{1,0:T(8,128)(2,1)S(1)} %collective-permute-done.12.upper), channel_id=1, source_target_pairs={{0,4},{5,1},{4,8},{9,5},{8,12},{13,9},{12,14},{15,13},{14,10},{11,... | collective-permute-start | bytes 565256 | tf_op jit(solution)/shard_map/ppermute | solution.py:358
  47.4 7.5 %collective-permute-start.22 = (bf16[720,128]{1,0:T(8,128)(2,1)S(1)}, bf16[720,128]{1,0:T(8,128)(2,1)S(1)}, u32[]{:S(2)}, u32[]{:S(2)}) collective-permute-start(bf16[720,128]{1,0:T(8,128)(2,1)S(1)} %collective-permute-done.18.lower), channel_id=1, source_target_pairs={{4,0},{1,5},{8,4},{5,9},{12,8},{9,13},{14,12},{13,15},{10,14},{15,... | collective-permute-start | bytes 552968 | tf_op jit(solution)/shard_map/ppermute | solution.py:364
  50.6 10.8 %collective-permute-start.20 = (bf16[720,128]{1,0:T(8,128)(2,1)S(1)}, bf16[720,128]{1,0:T(8,128)(2,1)S(1)}, u32[]{:S(2)}, u32[]{:S(2)}) collective-permute-start(bf16[720,128]{1,0:T(8,128)(2,1)S(1)} %get-tuple-element.113), channel_id=1, source_target_pairs={{0,4},{5,1},{4,8},{9,5},{8,12},{13,9},{12,14},{15,13},{14,10},{11,... | collective-permute-start | bytes 552968 | tf_op jit(solution)/shard_map/ppermute | solution.py:372
  53.9 7.5 %collective-permute-start.19 = (bf16[720,128]{1,0:T(8,128)(2,1)S(1)}, bf16[720,128]{1,0:T(8,128)(2,1)S(1)}, u32[]{:S(2)}, u32[]{:S(2)}) collective-permute-start(bf16[720,128]{1,0:T(8,128)(2,1)S(1)} %get-tuple-element.116), channel_id=1, source_target_pairs={{4,0},{1,5},{8,4},{5,9},{12,8},{9,13},{14,12},{13,15},{10,14},{15,... | collective-permute-start | bytes 552968 | tf_op jit(solution)/shard_map/ppermute | solution.py:374
  57.1 7.5 %collective-permute-start.31 = (bf16[720,128]{1,0:T(8,128)(2,1)S(1)}, bf16[720,128]{1,0:T(8,128)(2,1)S(1)}, u32[]{:S(2)}, u32[]{:S(2)}) collective-permute-start(bf16[720,128]{1,0:T(8,128)(2,1)S(1)} %get-tuple-element.120), channel_id=1, source_target_pairs={{0,4},{5,1},{4,8},{9,5},{8,12},{13,9},{12,14},{15,13},{14,10},{11,... | collective-permute-start | bytes 552968 | tf_op jit(solution)/shard_map/ppermute | solution.py:377
  58.1 7.6 %collective-permute-start.27 = (bf16[720,128]{1,0:T(8,128)(2,1)S(1)}, bf16[720,128]{1,0:T(8,128)(2,1)S(1)}, u32[]{:S(2)}, u32[]{:S(2)}) collective-permute-start(bf16[720,128]{1,0:T(8,128)(2,1)S(1)} %get-tuple-element.121), channel_id=1, source_target_pairs={{4,0},{1,5},{8,4},{5,9},{12,8},{9,13},{14,12},{13,15},{10,14},{15,... | collective-permute-start | bytes 552968 | tf_op jit(solution)/shard_map/ppermute | solution.py:377
  61.4 7.6 %collective-permute-start.25 = (bf16[720,128]{1,0:T(8,128)(2,1)S(1)}, bf16[720,128]{1,0:T(8,128)(2,1)S(1)}, u32[]{:S(2)}, u32[]{:S(2)}) collective-permute-start(bf16[720,128]{1,0:T(8,128)(2,1)S(1)} %add_convert_fusion.7), channel_id=1, source_target_pairs={{0,4},{5,1},{4,8},{9,5},{8,12},{13,9},{12,14},{15,13},{14,10},{11,... | collective-permute-start | bytes 552968 | tf_op jit(solution)/shard_map/ppermute | solution.py:388
  62.6 7.6 %collective-permute-start.23 = (bf16[720,128]{1,0:T(8,128)(2,1)S(1)}, bf16[720,128]{1,0:T(8,128)(2,1)S(1)}, u32[]{:S(2)}, u32[]{:S(2)}) collective-permute-start(bf16[720,128]{1,0:T(8,128)(2,1)S(1)} %add_convert_fusion.9), channel_id=1, source_target_pairs={{4,0},{1,5},{8,4},{5,9},{12,8},{9,13},{14,12},{13,15},{10,14},{15,... | collective-permute-start | bytes 552968 | tf_op jit(solution)/shard_map/ppermute | solution.py:389
  64.6 8.4 %collective-permute-start.32 = (bf16[720,128]{1,0:T(8,128)(2,1)S(1)}, bf16[720,128]{1,0:T(8,128)(2,1)S(1)}, u32[]{:S(2)}, u32[]{:S(2)}) collective-permute-start(bf16[720,128]{1,0:T(8,128)(2,1)S(1)} %add_convert_fusion.2), channel_id=1, source_target_pairs={{0,4},{5,1},{4,8},{9,5},{8,12},{13,9},{12,14},{15,13},{14,10},{11,... | collective-permute-start | bytes 552968 | tf_op jit(solution)/shard_map/ppermute | solution.py:390
  65.8 8.4 %collective-permute-start.28 = (bf16[720,128]{1,0:T(8,128)(2,1)S(1)}, bf16[720,128]{1,0:T(8,128)(2,1)S(1)}, u32[]{:S(2)}, u32[]{:S(2)}) collective-permute-start(bf16[720,128]{1,0:T(8,128)(2,1)S(1)} %add_convert_fusion.5), channel_id=1, source_target_pairs={{4,0},{1,5},{8,4},{5,9},{12,8},{9,13},{14,12},{13,15},{10,14},{15,... | collective-permute-start | bytes 552968 | tf_op jit(solution)/shard_map/ppermute | solution.py:391
  69.1 11.8 %collective-permute-start.26 = (bf16[720,128]{1,0:T(8,128)(2,1)S(1)}, bf16[720,128]{1,0:T(8,128)(2,1)S(1)}, u32[]{:S(2)}, u32[]{:S(2)}) collective-permute-start(bf16[720,128]{1,0:T(8,128)(2,1)S(1)} %add_convert_fusion.6), channel_id=1, source_target_pairs={{0,4},{5,1},{4,8},{9,5},{8,12},{13,9},{12,14},{15,13},{14,10},{11,... | collective-permute-start | bytes 552968 | tf_op jit(solution)/shard_map/ppermute | solution.py:388
  70.3 10.6 %collective-permute-start.24 = (bf16[720,128]{1,0:T(8,128)(2,1)S(1)}, bf16[720,128]{1,0:T(8,128)(2,1)S(1)}, u32[]{:S(2)}, u32[]{:S(2)}) collective-permute-start(bf16[720,128]{1,0:T(8,128)(2,1)S(1)} %add_convert_fusion.8), channel_id=1, source_target_pairs={{4,0},{1,5},{8,4},{5,9},{12,8},{9,13},{14,12},{13,15},{10,14},{15,... | collective-permute-start | bytes 552968 | tf_op jit(solution)/shard_map/ppermute | solution.py:389
  73.1 5.6 %collective-permute-start.33 = (bf16[720,128]{1,0:T(8,128)(2,1)S(1)}, bf16[720,128]{1,0:T(8,128)(2,1)S(1)}, u32[]{:S(2)}, u32[]{:S(2)}) collective-permute-start(bf16[720,128]{1,0:T(8,128)(2,1)S(1)} %add_convert_fusion.1), channel_id=1, source_target_pairs={{0,4},{5,1},{4,8},{9,5},{8,12},{13,9},{12,14},{15,13},{14,10},{11,... | collective-permute-start | bytes 552968 | tf_op jit(solution)/shard_map/ppermute | solution.py:390
  74.2 5.6 %collective-permute-start.29 = (bf16[720,128]{1,0:T(8,128)(2,1)S(1)}, bf16[720,128]{1,0:T(8,128)(2,1)S(1)}, u32[]{:S(2)}, u32[]{:S(2)}) collective-permute-start(bf16[720,128]{1,0:T(8,128)(2,1)S(1)} %add_convert_fusion.4), channel_id=1, source_target_pairs={{4,0},{1,5},{8,4},{5,9},{12,8},{9,13},{14,12},{13,15},{10,14},{15,... | collective-permute-start | bytes 552968 | tf_op jit(solution)/shard_map/ppermute | solution.py:391
  78.7 5.6 %collective-permute-start.34 = (bf16[720,128]{1,0:T(8,128)(2,1)S(1)}, bf16[720,128]{1,0:T(8,128)(2,1)S(1)}, u32[]{:S(2)}, u32[]{:S(2)}) collective-permute-start(bf16[720,128]{1,0:T(8,128)(2,1)S(1)} %add_convert_fusion), channel_id=1, source_target_pairs={{0,4},{5,1},{4,8},{9,5},{8,12},{13,9},{12,14},{15,13},{14,10},{11,... | collective-permute-start | bytes 552968 | tf_op jit(solution)/shard_map/ppermute | solution.py:390
  79.9 5.6 %collective-permute-start.30 = (bf16[720,128]{1,0:T(8,128)(2,1)S(1)}, bf16[720,128]{1,0:T(8,128)(2,1)S(1)}, u32[]{:S(2)}, u32[]{:S(2)}) collective-permute-start(bf16[720,128]{1,0:T(8,128)(2,1)S(1)} %add_convert_fusion.3), channel_id=1, source_target_pairs={{4,0},{1,5},{8,4},{5,9},{12,8},{9,13},{14,12},{13,15},{10,14},{15,... | collective-permute-start | bytes 552968 | tf_op jit(solution)/shard_map/ppermute | solution.py:391

commit v5 on v4

--- a/solution.py
+++ b/solution.py
@@ -253,7 +253,7 @@
 
 
 def expert_kernel(code_rows, place, upper, lower, *refs):
-    weights, more, (out_upper, out_lower) = refs[:6], refs[6:-2], refs[-2:]
+    weights, (out_upper, out_lower) = refs[:6], refs[6:]
     parcel = jnp.concatenate([upper[...], lower[...]], axis=0)
     body = (parcel.shape[0] - code_rows) // WINDOW * WINDOW
     head = parcel.shape[0] - body
@@ -275,20 +275,20 @@
     terms = jnp.concatenate([terms[:, body:].T, *blocks], axis=0)
     half = out_upper.shape[0]
     out_upper[...] = terms[:half]
-    out_lower[...] = add(terms[half:], more[0][...]) if more else terms[half:]
-
-
-def expert_terms(code_rows, expert, weights, parcel, *more):
+    out_lower[...] = terms[half:]
+
+
+def expert_terms(code_rows, expert, weights, parcel):
     half, rest = parcel[0].shape[0] - code_rows, parcel[1].shape[0]
     return pl.pallas_call(
         functools.partial(expert_kernel, code_rows),
         out_shape=[jax.ShapeDtypeStruct((n, WINDOW), BF16) for n in (half, rest)],
-        in_specs=[SMEM] + [VMEM] * (8 + len(more)),
+        in_specs=[SMEM] + [VMEM] * 8,
         out_specs=[VMEM] * 2,
-        cost_estimate=pl.CostEstimate(flops=1000000000, bytes_accessed=1, transcendentals=0),
+        cost_estimate=pl.CostEstimate(flops=10**9, bytes_accessed=1, transcendentals=0),
         compiler_params=pltpu.CompilerParams(vmem_limit_bytes=24 * 2**20),
         name="experts",
-    )(expert, *parcel, *weights, *more)
+    )(expert, *parcel, *weights)
 
 
 def total_kernel(*refs):
@@ -343,18 +343,16 @@
     at[-1], at[1] = [to_right(half) for half in parcel], [to_left(half) for half in parcel]
     terms = {}
 
-    def work(k, arrived, *more):
+    def work(k, arrived):
         at[k], arrived = after(at[k], arrived)
-        terms[k] = apply(at[k], *more)
+        terms[k] = apply(at[k])
         return arrived
 
-    last = None
     last = 0
     terms[0] = apply(parcel)
     for k in range(2, far + 1):
         uppers, lowers = (at[1 - k][0], at[k - 1][0]), (at[1 - k][1], at[k - 1][1])
-        if last is not None:
-            uppers, terms[last] = after(uppers, terms[last])
+        uppers, terms[last] = after(uppers, terms[last])
         upper_left = to_right(uppers[0])
         upper_right = to_left(uppers[1]) if k < far else None
         if 2 < k == far:
@@ -375,20 +373,15 @@
     opposite, terms[1 - far] = after(opposite, terms[1 - far])
     farthest = apply(opposite)
     right_up, left_low = to_right(farthest[0]), to_left(farthest[1])
-    fused = False
-    farthest = work(1, farthest)
-    right_low, terms[1] = after(right_low, terms[1])
-    left_up, terms[1] = after(left_up, terms[1])
+    for k in range(1, far - 2):
+        farthest = work(k, farthest)
+        (left_up, right_low), terms[k] = after((left_up, right_low), terms[k])
     for k in range(far - 1, 0, -1):
-        if k > 1:
-            going = terms[k - 1][1]
-            if not fused:
-                going = add(going, right_low)
-            fused = False
-            right_low = to_right(going)
-            left_up = to_left(add(terms[1 - k][0], left_up))
         right_up = to_right(add(terms[k][0], right_up))
         left_low = to_left(add(terms[-k][1], left_low))
+        if k > 1:
+            right_low = to_right(add(terms[k - 1][1], right_low))
+            left_up = to_left(add(terms[1 - k][0], left_up))
     near, final = after((terms[0], left_up, right_low), (left_low, right_up))
     (upper, lower), left_up, right_low = near
     left_low, right_up = final

time: 86.8 us -> 86.8 us (level)
  no operation moved by 1% of the time
where the time goes in v5:
time: 86.8 us; the launch traced here: 86.5 us
  starting transfers between devices  36.2 us (42%)
  Pallas kernels  28.4 us (33%)
  waiting for transfers between devices  19.8 us (23%)
    pallas_call x8, Pallas kernels, expert_terms(): pl.pallas_call(functools.partial(expert_kernel, code_rows), out_shape=[ja...  17.8 us
    ppermute x3, waiting for transfers between devices, mixed_by_ring(): right_up = to_right(add(terms[k][0], right_up))  8.51 us
    ppermute x3, starting transfers between devices, mixed_by_ring(): upper_left = to_right(uppers[0])  4.64 us
    ppermute x2, starting transfers between devices, mixed_by_ring(): lower_left = to_right(lowers[0]) if k < far else None  4.56 us
    ppermute x2, starting transfers between devices, mixed_by_ring(): to_right(half)  4.49 us
    ppermute x1, starting transfers between devices, front(): rim_a = lax.ppermute(pack_rim(key_rows, values), 'seq', steps)  4.44 us
    pallas_call x1, Pallas kernels, front(): pl.pallas_call(front_own_kernel, out_shape=jax.ShapeDtypeStruct((features...  3.73 us
    ppermute x3, starting transfers between devices, mixed_by_ring(): right_up = to_right(add(terms[k][0], right_up))  3.39 us
  transfers between devices with their start and end apart: 35, of which 11 were waited for; matrix products, arithmetic and copies ran while one was open for 1% of the time, Pallas kernels for 32%

profile of v5, /device:TPU:0, one launch (start us, length us, event | category | flops | bytes accessed | tf_op | source)
XLA Modules:
  0.0 86.5 jit_solution(11036781453860350442)
XLA Ops:
  1.1 0.8 rim.1
  1.9 4.4 %collective-permute-start = (bf16[256,128]{1,0:T(8,128)(2,1)S(1)}, bf16[256,128]{1,0:T(8,128)(2,1)S(1)}, u32[]{:S(2)}, u32[]{:S(2)}) collective-permute-start(bf16[256,128]{1,0:T(8,128)(2,1)S(1)} %rim.1), channel_id=1, source_target_pairs={{0,2},{2,4},{4,6},{6,8},{8,10},{10,12},{12,14},{1,3},{3,5},{5,7},{... | collective-permute-start | bytes 196616 | tf_op jit(solution)/shard_map/ppermute | solution.py:203
  6.4 0.7 broadcast_in_dim.6.gain
  7.2 1.9 %pack.1 = (bf16[1552,128]{1,0:T(8,128)(2,1)S(1)}, f32[1440,128]{1,0:T(8,128)S(1)}, bf16[16,128]{1,0:T(8,128)(2,1)S(1)}) custom-call(s32[2]{0:T(128)S(1)} %pad_add_fusion.place, f32[16]{0:T(128)} %sink.1, f32[1,1440]{1,0:T(1,128)S(1)} %broadcast_in_dim.6.gain, s32[4,256]{1,0:T(4,128)} %bitcast.43, s32[4,256]{1,0:T(4,128)} %bitcast.44, bf16[256,128]{1,0:T(8,128)(2,1)} %k.3, ...), custom_call_target="tpu_custom_call" | custom-call | flops 1 | bytes 1 | tf_op jit(solution)/shard_map/pack/pallas_call | solution.py:97
  10.2 3.7 %front_own.1.stream = f32[1440,128]{1,0:T(8,128)S(1)} custom-call(s32[2]{0:T(128)S(1)} %pad_add_fusion.place, bf16[1552,128]{1,0:T(8,128)(2,1)S(1)} %get-tuple-element.72.packed, bf16[256,128]{1,0:T(8,128)(2,1)S(1)} %collective-permute-done.rim, bf16[256,1024]{1,0:T(8,128)(2,1)} %q.3, bf16[1440,1024]{1,0:T(8,128)(2,1)} %bitcast.40, bf16[1440,256]{1,0:T(8,128)(2,1)} %bitcast.41), custom_call_target="tpu_custom_call" | custom-call | flops 1 | bytes 1 | tf_op jit(solution)/shard_map/front_own/pallas_call | solution.py:216
  14.0 3.2 %front.1 = (bf16[1440,128]{1,0:T(8,128)(2,1)}, bf16[736,128]{1,0:T(8,128)(2,1)S(1)}, bf16[720,128]{1,0:T(8,128)(2,1)S(1)}) custom-call(s32[2]{0:T(128)S(1)} %pad_add_fusion.place, bf16[1552,128]{1,0:T(8,128)(2,1)S(1)} %collective-permute-done.1.packed, bf16[256,128]{1,0:T(8,128)(2,1)S(1)} %collective-permute-done.2.rim, ...), custom_call_target="tpu_custom_call" | custom-call | flops 1 | bytes 1 | tf_op jit(solution)/shard_map/front/pallas_call | solution.py:229
  17.4 2.5 %collective-permute-start.4 = (bf16[736,128]{1,0:T(8,128)(2,1)S(1)}, bf16[736,128]{1,0:T(8,128)(2,1)S(1)}, u32[]{:S(2)}, u32[]{:S(2)}) collective-permute-start(bf16[736,128]{1,0:T(8,128)(2,1)S(1)} %get-tuple-element.81.upper), channel_id=1, source_target_pairs={{0,4},{5,1},{4,8},{9,5},{8,12},{13,9},{12,14},{15,13},{14,10},{11,... | collective-permute-start | bytes 565256 | tf_op jit(solution)/shard_map/ppermute | solution.py:343
  19.9 2.0 %collective-permute-start.11 = (bf16[720,128]{1,0:T(8,128)(2,1)S(1)}, bf16[720,128]{1,0:T(8,128)(2,1)S(1)}, u32[]{:S(2)}, u32[]{:S(2)}) collective-permute-start(bf16[720,128]{1,0:T(8,128)(2,1)S(1)} %get-tuple-element.82.lower), channel_id=1, source_target_pairs={{0,4},{5,1},{4,8},{9,5},{8,12},{13,9},{12,14},{15,13},{14,10},{11,... | collective-permute-start | bytes 552968 | tf_op jit(solution)/shard_map/ppermute | solution.py:343
  21.9 2.2 %experts.8 = (bf16[720,128]{1,0:T(8,128)(2,1)S(1)}, bf16[720,128]{1,0:T(8,128)(2,1)S(1)}) custom-call(s32[1]{0:T(128)} %bitcast.10.place, bf16[736,128]{1,0:T(8,128)(2,1)S(1)} %get-tuple-element.81.upper, bf16[720,128]{1,0:T(8,128)(2,1)S(1)} %get-tuple-element.82.lower, bf16[1440,720]{1,0:T(8,128)(2,1)S(1)} %bitcast.13, bf16[1440,720]{1,0:T(8,128)(2,1)S(1)} %bitcast.22, ...), custom_call_target="tpu_custom_call" | custom-call | flops 1000000000 | bytes 1 | tf_op jit(solution)/shard_map/experts/pallas_call | solution.py:283
  24.2 0.8 collective-permute-done.4.upper
  24.9 2.3 %collective-permute-done.5.upper = bf16[736,128]{1,0:T(8,128)(2,1)S(1)} collective-permute-done((bf16[736,128]{1,0:T(8,128)(2,1)S(1)}, bf16[736,128]{1,0:T(8,128)(2,1)S(1)}, u32[]{:S(2)}, u32[]{:S(2)}) %collective-permute-start.5) | collective-permute-done | bytes 188448 | tf_op jit(solution)/shard_map/ppermute | solution.py:343
  27.5 1.7 %collective-permute-start.9 = (bf16[736,128]{1,0:T(8,128)(2,1)S(1)}, bf16[736,128]{1,0:T(8,128)(2,1)S(1)}, u32[]{:S(2)}, u32[]{:S(2)}) collective-permute-start(bf16[736,128]{1,0:T(8,128)(2,1)S(1)} %collective-permute-done.4.upper), channel_id=1, source_target_pairs={{0,4},{5,1},{4,8},{9,5},{8,12},{13,9},{12,14},{15,13},{14,10},{11,... | collective-permute-start | bytes 565256 | tf_op jit(solution)/shard_map/ppermute | solution.py:356
  29.3 2.1 %collective-permute-start.14 = (bf16[720,128]{1,0:T(8,128)(2,1)S(1)}, bf16[720,128]{1,0:T(8,128)(2,1)S(1)}, u32[]{:S(2)}, u32[]{:S(2)}) collective-permute-start(bf16[720,128]{1,0:T(8,128)(2,1)S(1)} %collective-permute-done.11.lower), channel_id=1, source_target_pairs={{0,4},{5,1},{4,8},{9,5},{8,12},{13,9},{12,14},{15,13},{14,10},{11,... | collective-permute-start | bytes 552968 | tf_op jit(solution)/shard_map/ppermute | solution.py:361
  31.4 2.3 %experts.9 = (bf16[720,128]{1,0:T(8,128)(2,1)S(1)}, bf16[720,128]{1,0:T(8,128)(2,1)S(1)}) custom-call(s32[1]{0:T(128)} %bitcast.10.place, bf16[736,128]{1,0:T(8,128)(2,1)S(1)} %collective-permute-done.4.upper, bf16[720,128]{1,0:T(8,128)(2,1)S(1)} %collective-permute-done.11.lower, bf16[1440,720]{1,0:T(8,128)(2,1)S(1)} %bitcast.14, ...), custom_call_target="tpu_custom_call" | custom-call | flops 1000000000 | bytes 1 | tf_op jit(solution)/shard_map/experts/pallas_call | solution.py:283
  33.6 1.3 %collective-permute-done.10.upper = bf16[736,128]{1,0:T(8,128)(2,1)S(1)} collective-permute-done((bf16[736,128]{1,0:T(8,128)(2,1)S(1)}, bf16[736,128]{1,0:T(8,128)(2,1)S(1)}, u32[]{:S(2)}, u32[]{:S(2)}) %collective-permute-start.10) | collective-permute-done | bytes 188448 | tf_op jit(solution)/shard_map/ppermute | solution.py:357
  34.9 1.8 %collective-permute-start.12 = (bf16[736,128]{1,0:T(8,128)(2,1)S(1)}, bf16[736,128]{1,0:T(8,128)(2,1)S(1)}, u32[]{:S(2)}, u32[]{:S(2)}) collective-permute-start(bf16[736,128]{1,0:T(8,128)(2,1)S(1)} %collective-permute-done.9.upper), channel_id=1, source_target_pairs={{0,4},{5,1},{4,8},{9,5},{8,12},{13,9},{12,14},{15,13},{14,10},{11,... | collective-permute-start | bytes 565256 | tf_op jit(solution)/shard_map/ppermute | solution.py:356
  36.9 1.2 %collective-permute-done.14.lower = bf16[720,128]{1,0:T(8,128)(2,1)S(1)} collective-permute-done((bf16[720,128]{1,0:T(8,128)(2,1)S(1)}, bf16[720,128]{1,0:T(8,128)(2,1)S(1)}, u32[]{:S(2)}, u32[]{:S(2)}) %collective-permute-start.14) | collective-permute-done | bytes 184352 | tf_op jit(solution)/shard_map/ppermute | solution.py:361
  38.2 2.5 %collective-permute-start.17 = (bf16[720,128]{1,0:T(8,128)(2,1)S(1)}, bf16[720,128]{1,0:T(8,128)(2,1)S(1)}, u32[]{:S(2)}, u32[]{:S(2)}) collective-permute-start(bf16[720,128]{1,0:T(8,128)(2,1)S(1)} %collective-permute-done.14.lower), channel_id=1, source_target_pairs={{0,4},{5,1},{4,8},{9,5},{8,12},{13,9},{12,14},{15,13},{14,10},{11,... | collective-permute-start | bytes 552968 | tf_op jit(solution)/shard_map/ppermute | solution.py:361
  40.7 2.2 %experts.10 = (bf16[720,128]{1,0:T(8,128)(2,1)S(1)}, bf16[720,128]{1,0:T(8,128)(2,1)S(1)}) custom-call(s32[1]{0:T(128)} %bitcast.10.place, bf16[736,128]{1,0:T(8,128)(2,1)S(1)} %collective-permute-done.9.upper, bf16[720,128]{1,0:T(8,128)(2,1)S(1)} %collective-permute-done.14.lower, bf16[1440,720]{1,0:T(8,128)(2,1)S(1)} %bitcast.15, ...), custom_call_target="tpu_custom_call" | custom-call | flops 1000000000 | bytes 1 | tf_op jit(solution)/shard_map/experts/pallas_call | solution.py:283
  42.9 1.2 %collective-permute-done.13.upper = bf16[736,128]{1,0:T(8,128)(2,1)S(1)} collective-permute-done((bf16[736,128]{1,0:T(8,128)(2,1)S(1)}, bf16[736,128]{1,0:T(8,128)(2,1)S(1)}, u32[]{:S(2)}, u32[]{:S(2)}) %collective-permute-start.13) | collective-permute-done | bytes 188448 | tf_op jit(solution)/shard_map/ppermute | solution.py:357
  44.1 1.1 %collective-permute-start.21 = (bf16[736,128]{1,0:T(8,128)(2,1)S(1)}, bf16[736,128]{1,0:T(8,128)(2,1)S(1)}, u32[]{:S(2)}, u32[]{:S(2)}) collective-permute-start(bf16[736,128]{1,0:T(8,128)(2,1)S(1)} %collective-permute-done.12.upper), channel_id=1, source_target_pairs={{0,4},{5,1},{4,8},{9,5},{8,12},{13,9},{12,14},{15,13},{14,10},{11,... | collective-permute-start | bytes 565256 | tf_op jit(solution)/shard_map/ppermute | solution.py:356
  45.1 2.2 %experts.11 = (bf16[720,128]{1,0:T(8,128)(2,1)S(1)}, bf16[720,128]{1,0:T(8,128)(2,1)S(1)}) custom-call(s32[1]{0:T(128)} %bitcast.10.place, bf16[736,128]{1,0:T(8,128)(2,1)S(1)} %collective-permute-done.10.upper, bf16[720,128]{1,0:T(8,128)(2,1)S(1)} %collective-permute-done.16.lower, bf16[1440,720]{1,0:T(8,128)(2,1)S(1)} %bitcast.16, ...), custom_call_target="tpu_custom_call" | custom-call | flops 1000000000 | bytes 1 | tf_op jit(solution)/shard_map/experts/pallas_call | solution.py:283
  47.4 1.0 %collective-permute-start.22 = (bf16[720,128]{1,0:T(8,128)(2,1)S(1)}, bf16[720,128]{1,0:T(8,128)(2,1)S(1)}, u32[]{:S(2)}, u32[]{:S(2)}) collective-permute-start(bf16[720,128]{1,0:T(8,128)(2,1)S(1)} %collective-permute-done.18.lower), channel_id=1, source_target_pairs={{4,0},{1,5},{8,4},{5,9},{12,8},{9,13},{14,12},{13,15},{10,14},{15,... | collective-permute-start | bytes 552968 | tf_op jit(solution)/shard_map/ppermute | solution.py:362
  48.3 2.2 %experts.12 = (bf16[720,128]{1,0:T(8,128)(2,1)S(1)}, bf16[720,128]{1,0:T(8,128)(2,1)S(1)}) custom-call(s32[1]{0:T(128)} %bitcast.10.place, bf16[736,128]{1,0:T(8,128)(2,1)S(1)} %collective-permute-done.13.upper, bf16[720,128]{1,0:T(8,128)(2,1)S(1)} %collective-permute-done.18.lower, bf16[1440,720]{1,0:T(8,128)(2,1)S(1)} %bitcast.17, ...), custom_call_target="tpu_custom_call" | custom-call | flops 1000000000 | bytes 1 | tf_op jit(solution)/shard_map/experts/pallas_call | solution.py:283
  50.6 1.1 %collective-permute-start.20 = (bf16[720,128]{1,0:T(8,128)(2,1)S(1)}, bf16[720,128]{1,0:T(8,128)(2,1)S(1)}, u32[]{:S(2)}, u32[]{:S(2)}) collective-permute-start(bf16[720,128]{1,0:T(8,128)(2,1)S(1)} %get-tuple-element.111), channel_id=1, source_target_pairs={{0,4},{5,1},{4,8},{9,5},{8,12},{13,9},{12,14},{15,13},{14,10},{11,... | collective-permute-start | bytes 552968 | tf_op jit(solution)/shard_map/ppermute | solution.py:370
  51.7 2.2 %experts.13 = (bf16[720,128]{1,0:T(8,128)(2,1)S(1)}, bf16[720,128]{1,0:T(8,128)(2,1)S(1)}) custom-call(s32[1]{0:T(128)} %bitcast.10.place, bf16[736,128]{1,0:T(8,128)(2,1)S(1)} %collective-permute-done.12.upper, bf16[720,128]{1,0:T(8,128)(2,1)S(1)} %collective-permute-done.17.lower, bf16[1440,720]{1,0:T(8,128)(2,1)S(1)} %bitcast.18, ...), custom_call_target="tpu_custom_call" | custom-call | flops 1000000000 | bytes 1 | tf_op jit(solution)/shard_map/experts/pallas_call | solution.py:283
  53.9 1.0 %collective-permute-start.19 = (bf16[720,128]{1,0:T(8,128)(2,1)S(1)}, bf16[720,128]{1,0:T(8,128)(2,1)S(1)}, u32[]{:S(2)}, u32[]{:S(2)}) collective-permute-start(bf16[720,128]{1,0:T(8,128)(2,1)S(1)} %get-tuple-element.114), channel_id=1, source_target_pairs={{4,0},{1,5},{8,4},{5,9},{12,8},{9,13},{14,12},{13,15},{10,14},{15,... | collective-permute-start | bytes 552968 | tf_op jit(solution)/shard_map/ppermute | solution.py:372
  54.9 2.2 %experts.14 = (bf16[720,128]{1,0:T(8,128)(2,1)S(1)}, bf16[720,128]{1,0:T(8,128)(2,1)S(1)}) custom-call(s32[1]{0:T(128)} %bitcast.10.place, bf16[736,128]{1,0:T(8,128)(2,1)S(1)} %collective-permute-done.21.upper, bf16[720,128]{1,0:T(8,128)(2,1)S(1)} %collective-permute-done.22.lower, bf16[1440,720]{1,0:T(8,128)(2,1)S(1)} %bitcast.19, ...), custom_call_target="tpu_custom_call" | custom-call | flops 1000000000 | bytes 1 | tf_op jit(solution)/shard_map/experts/pallas_call | solution.py:283
  57.1 1.1 %collective-permute-start.31 = (bf16[720,128]{1,0:T(8,128)(2,1)S(1)}, bf16[720,128]{1,0:T(8,128)(2,1)S(1)}, u32[]{:S(2)}, u32[]{:S(2)}) collective-permute-start(bf16[720,128]{1,0:T(8,128)(2,1)S(1)} %get-tuple-element.118), channel_id=1, source_target_pairs={{0,4},{5,1},{4,8},{9,5},{8,12},{13,9},{12,14},{15,13},{14,10},{11,... | collective-permute-start | bytes 552968 | tf_op jit(solution)/shard_map/ppermute | solution.py:375
  58.1 1.0 %collective-permute-start.27 = (bf16[720,128]{1,0:T(8,128)(2,1)S(1)}, bf16[720,128]{1,0:T(8,128)(2,1)S(1)}, u32[]{:S(2)}, u32[]{:S(2)}) collective-permute-start(bf16[720,128]{1,0:T(8,128)(2,1)S(1)} %get-tuple-element.119), channel_id=1, source_target_pairs={{4,0},{1,5},{8,4},{5,9},{12,8},{9,13},{14,12},{13,15},{10,14},{15,... | collective-permute-start | bytes 552968 | tf_op jit(solution)/shard_map/ppermute | solution.py:375
  59.1 2.3 %experts.15 = (bf16[720,128]{1,0:T(8,128)(2,1)S(1)}, bf16[720,128]{1,0:T(8,128)(2,1)S(1)}) custom-call(s32[1]{0:T(128)} %bitcast.10.place, bf16[736,128]{1,0:T(8,128)(2,1)S(1)} %collective-permute-done.5.upper, bf16[720,128]{1,0:T(8,128)(2,1)S(1)} %collective-permute-done.15.lower, bf16[1440,720]{1,0:T(8,128)(2,1)S(1)} %bitcast.20, ...), custom_call_target="tpu_custom_call" | custom-call | flops 1000000000 | bytes 1 | tf_op jit(solution)/shard_map/experts/pallas_call | solution.py:283
  61.4 1.1 %collective-permute-start.25 = (bf16[720,128]{1,0:T(8,128)(2,1)S(1)}, bf16[720,128]{1,0:T(8,128)(2,1)S(1)}, u32[]{:S(2)}, u32[]{:S(2)}) collective-permute-start(bf16[720,128]{1,0:T(8,128)(2,1)S(1)} %add_convert_fusion.7), channel_id=1, source_target_pairs={{0,4},{5,1},{4,8},{9,5},{8,12},{13,9},{12,14},{15,13},{14,10},{11,... | collective-permute-start | bytes 552968 | tf_op jit(solution)/shard_map/ppermute | solution.py:383
  62.6 1.0 %collective-permute-start.23 = (bf16[720,128]{1,0:T(8,128)(2,1)S(1)}, bf16[720,128]{1,0:T(8,128)(2,1)S(1)}, u32[]{:S(2)}, u32[]{:S(2)}) collective-permute-start(bf16[720,128]{1,0:T(8,128)(2,1)S(1)} %add_convert_fusion.9), channel_id=1, source_target_pairs={{4,0},{1,5},{8,4},{5,9},{12,8},{9,13},{14,12},{13,15},{10,14},{15,... | collective-permute-start | bytes 552968 | tf_op jit(solution)/shard_map/ppermute | solution.py:384
  63.6 1.0 %collective-permute-done.31 = bf16[720,128]{1,0:T(8,128)(2,1)S(1)} collective-permute-done((bf16[720,128]{1,0:T(8,128)(2,1)S(1)}, bf16[720,128]{1,0:T(8,128)(2,1)S(1)}, u32[]{:S(2)}, u32[]{:S(2)}) %collective-permute-start.31) | collective-permute-done | bytes 184352 | tf_op jit(solution)/shard_map/ppermute | solution.py:375
  64.7 1.1 %collective-permute-start.32 = (bf16[720,128]{1,0:T(8,128)(2,1)S(1)}, bf16[720,128]{1,0:T(8,128)(2,1)S(1)}, u32[]{:S(2)}, u32[]{:S(2)}) collective-permute-start(bf16[720,128]{1,0:T(8,128)(2,1)S(1)} %add_convert_fusion.2), channel_id=1, source_target_pairs={{0,4},{5,1},{4,8},{9,5},{8,12},{13,9},{12,14},{15,13},{14,10},{11,... | collective-permute-start | bytes 552968 | tf_op jit(solution)/shard_map/ppermute | solution.py:380
  65.8 1.0 %collective-permute-start.28 = (bf16[720,128]{1,0:T(8,128)(2,1)S(1)}, bf16[720,128]{1,0:T(8,128)(2,1)S(1)}, u32[]{:S(2)}, u32[]{:S(2)}) collective-permute-start(bf16[720,128]{1,0:T(8,128)(2,1)S(1)} %add_convert_fusion.5), channel_id=1, source_target_pairs={{4,0},{1,5},{8,4},{5,9},{12,8},{9,13},{14,12},{13,15},{10,14},{15,... | collective-permute-start | bytes 552968 | tf_op jit(solution)/shard_map/ppermute | solution.py:381
  66.8 2.2 %collective-permute-done.25 = bf16[720,128]{1,0:T(8,128)(2,1)S(1)} collective-permute-done((bf16[720,128]{1,0:T(8,128)(2,1)S(1)}, bf16[720,128]{1,0:T(8,128)(2,1)S(1)}, u32[]{:S(2)}, u32[]{:S(2)}) %collective-permute-start.25) | collective-permute-done | bytes 184352 | tf_op jit(solution)/shard_map/ppermute | solution.py:383
  69.1 1.1 %collective-permute-start.26 = (bf16[720,128]{1,0:T(8,128)(2,1)S(1)}, bf16[720,128]{1,0:T(8,128)(2,1)S(1)}, u32[]{:S(2)}, u32[]{:S(2)}) collective-permute-start(bf16[720,128]{1,0:T(8,128)(2,1)S(1)} %add_convert_fusion.6), channel_id=1, source_target_pairs={{0,4},{5,1},{4,8},{9,5},{8,12},{13,9},{12,14},{15,13},{14,10},{11,... | collective-permute-start | bytes 552968 | tf_op jit(solution)/shard_map/ppermute | solution.py:383
  70.3 1.0 %collective-permute-start.24 = (bf16[720,128]{1,0:T(8,128)(2,1)S(1)}, bf16[720,128]{1,0:T(8,128)(2,1)S(1)}, u32[]{:S(2)}, u32[]{:S(2)}) collective-permute-start(bf16[720,128]{1,0:T(8,128)(2,1)S(1)} %add_convert_fusion.8), channel_id=1, source_target_pairs={{4,0},{1,5},{8,4},{5,9},{12,8},{9,13},{14,12},{13,15},{10,14},{15,... | collective-permute-start | bytes 552968 | tf_op jit(solution)/shard_map/ppermute | solution.py:384
  71.3 1.7 %collective-permute-done.32 = bf16[720,128]{1,0:T(8,128)(2,1)S(1)} collective-permute-done((bf16[720,128]{1,0:T(8,128)(2,1)S(1)}, bf16[720,128]{1,0:T(8,128)(2,1)S(1)}, u32[]{:S(2)}, u32[]{:S(2)}) %collective-permute-start.32) | collective-permute-done | bytes 184352 | tf_op jit(solution)/shard_map/ppermute | solution.py:380
  73.1 1.1 %collective-permute-start.33 = (bf16[720,128]{1,0:T(8,128)(2,1)S(1)}, bf16[720,128]{1,0:T(8,128)(2,1)S(1)}, u32[]{:S(2)}, u32[]{:S(2)}) collective-permute-start(bf16[720,128]{1,0:T(8,128)(2,1)S(1)} %add_convert_fusion.1), channel_id=1, source_target_pairs={{0,4},{5,1},{4,8},{9,5},{8,12},{13,9},{12,14},{15,13},{14,10},{11,... | collective-permute-start | bytes 552968 | tf_op jit(solution)/shard_map/ppermute | solution.py:380
  74.2 1.0 %collective-permute-start.29 = (bf16[720,128]{1,0:T(8,128)(2,1)S(1)}, bf16[720,128]{1,0:T(8,128)(2,1)S(1)}, u32[]{:S(2)}, u32[]{:S(2)}) collective-permute-start(bf16[720,128]{1,0:T(8,128)(2,1)S(1)} %add_convert_fusion.4), channel_id=1, source_target_pairs={{4,0},{1,5},{8,4},{5,9},{12,8},{9,13},{14,12},{13,15},{10,14},{15,... | collective-permute-start | bytes 552968 | tf_op jit(solution)/shard_map/ppermute | solution.py:381
  75.3 3.4 %collective-permute-done.33 = bf16[720,128]{1,0:T(8,128)(2,1)S(1)} collective-permute-done((bf16[720,128]{1,0:T(8,128)(2,1)S(1)}, bf16[720,128]{1,0:T(8,128)(2,1)S(1)}, u32[]{:S(2)}, u32[]{:S(2)}) %collective-permute-start.33) | collective-permute-done | bytes 184352 | tf_op jit(solution)/shard_map/ppermute | solution.py:380
  78.7 1.2 %collective-permute-start.34 = (bf16[720,128]{1,0:T(8,128)(2,1)S(1)}, bf16[720,128]{1,0:T(8,128)(2,1)S(1)}, u32[]{:S(2)}, u32[]{:S(2)}) collective-permute-start(bf16[720,128]{1,0:T(8,128)(2,1)S(1)} %add_convert_fusion), channel_id=1, source_target_pairs={{0,4},{5,1},{4,8},{9,5},{8,12},{13,9},{12,14},{15,13},{14,10},{11,... | collective-permute-start | bytes 552968 | tf_op jit(solution)/shard_map/ppermute | solution.py:380
  79.9 1.0 %collective-permute-start.30 = (bf16[720,128]{1,0:T(8,128)(2,1)S(1)}, bf16[720,128]{1,0:T(8,128)(2,1)S(1)}, u32[]{:S(2)}, u32[]{:S(2)}) collective-permute-start(bf16[720,128]{1,0:T(8,128)(2,1)S(1)} %add_convert_fusion.3), channel_id=1, source_target_pairs={{4,0},{1,5},{8,4},{5,9},{12,8},{9,13},{14,12},{13,15},{10,14},{15,... | collective-permute-start | bytes 552968 | tf_op jit(solution)/shard_map/ppermute | solution.py:381
  80.9 3.4 %collective-permute-done.34.refs_2_ = bf16[720,128]{1,0:T(8,128)(2,1)S(1)} collective-permute-done((bf16[720,128]{1,0:T(8,128)(2,1)S(1)}, bf16[720,128]{1,0:T(8,128)(2,1)S(1)}, u32[]{:S(2)}, u32[]{:S(2)}) %collective-permute-start.34) | collective-permute-done | bytes 184352 | tf_op jit(solution)/shard_map/ppermute | solution.py:380
  84.3 1.2 %collective-permute-done.30.refs_4_ = bf16[720,128]{1,0:T(8,128)(2,1)S(1)} collective-permute-done((bf16[720,128]{1,0:T(8,128)(2,1)S(1)}, bf16[720,128]{1,0:T(8,128)(2,1)S(1)}, u32[]{:S(2)}, u32[]{:S(2)}) %collective-permute-start.30) | collective-permute-done | bytes 184352 | tf_op jit(solution)/shard_map/ppermute | solution.py:381
  85.5 0.9 %total.1 = bf16[1440,128]{1,0:T(8,128)(2,1)} custom-call(bf16[720,128]{1,0:T(8,128)(2,1)S(1)} %get-tuple-element.134.refs_0_, bf16[720,128]{1,0:T(8,128)(2,1)S(1)} %collective-permute-done.24.refs_1_, bf16[720,128]{1,0:T(8,128)(2,1)S(1)} %collective-permute-done.34.refs_2_, bf16[720,128]{1,0:T(8,128)(2,1)S(1)} %get-tuple-element.137.refs_3_, ...), custom_call_target="tpu_custom_call" | custom-call | flops 1 | bytes 1 | tf_op jit(solution)/shard_map/total/pallas_call | solution.py:308
  (53 shorter events, 3.0 us)
Async XLA Ops:
  0.6 13.3 %collective-permute-start.3 = (bf16[1440,1024]{1,0:T(8,128)(2,1)}, bf16[1440,1024]{1,0:T(8,128)(2,1)S(1)}, u32[]{:S(2)}, u32[]{:S(2)}) collective-permute-start(bf16[1440,1024]{1,0:T(8,128)(2,1)} %bitcast.39), channel_id=1, source_target_pairs={{0,1},{1,0},{2,3},{3,2},{4,5},{5,4},{6,7},{7,6},{8,9},{9,8},{10,11... | collective-permute-start | bytes 8847368 | tf_op jit(solution)/shard_map/ppermute | solution.py:242
  1.9 7.1 %collective-permute-start = (bf16[256,128]{1,0:T(8,128)(2,1)S(1)}, bf16[256,128]{1,0:T(8,128)(2,1)S(1)}, u32[]{:S(2)}, u32[]{:S(2)}) collective-permute-start(bf16[256,128]{1,0:T(8,128)(2,1)S(1)} %rim.1), channel_id=1, source_target_pairs={{0,2},{2,4},{4,6},{6,8},{8,10},{10,12},{12,14},{1,3},{3,5},{5,7},{... | collective-permute-start | bytes 196616 | tf_op jit(solution)/shard_map/ppermute | solution.py:203
  9.1 4.8 %collective-permute-start.1 = (bf16[1552,128]{1,0:T(8,128)(2,1)S(1)}, bf16[1552,128]{1,0:T(8,128)(2,1)S(1)}, u32[]{:S(2)}, u32[]{:S(2)}) collective-permute-start(bf16[1552,128]{1,0:T(8,128)(2,1)S(1)} %get-tuple-element.72.packed), channel_id=1, source_target_pairs={{0,1},{1,0},{2,3},{3,2},{4,5},{5,4},{6,7},{7,6},{8,9},{9,8},{10,11... | collective-permute-start | bytes 1191944 | tf_op jit(solution)/shard_map/ppermute | solution.py:242
  9.3 4.6 %collective-permute-start.2 = (bf16[256,128]{1,0:T(8,128)(2,1)S(1)}, bf16[256,128]{1,0:T(8,128)(2,1)S(1)}, u32[]{:S(2)}, u32[]{:S(2)}) collective-permute-start(bf16[256,128]{1,0:T(8,128)(2,1)S(1)} %collective-permute-done.rim), channel_id=1, source_target_pairs={{0,1},{1,0},{2,3},{3,2},{4,5},{5,4},{6,7},{7,6},{8,9},{9,8},{10,11... | collective-permute-start | bytes 196616 | tf_op jit(solution)/shard_map/ppermute | solution.py:242
  9.7 10.2 %collective-permute-start.6 = (bf16[1440,720]{1,0:T(8,128)(2,1)}, bf16[1440,720]{1,0:T(8,128)(2,1)S(1)}, u32[]{:S(2)}, u32[]{:S(2)}) collective-permute-start(bf16[1440,720]{1,0:T(8,128)(2,1)} %bitcast.12), channel_id=1, source_target_pairs={{0,1},{1,0},{2,3},{3,2},{4,5},{5,4},{6,7},{7,6},{8,9},{9,8},{10,11... | collective-permute-start | bytes 6220808 | tf_op jit(solution)/shard_map/ppermute | solution.py:242
  9.9 12.1 %collective-permute-start.7 = (bf16[1440,720]{1,0:T(8,128)(2,1)}, bf16[1440,720]{1,0:T(8,128)(2,1)S(1)}, u32[]{:S(2)}, u32[]{:S(2)}) collective-permute-start(bf16[1440,720]{1,0:T(8,128)(2,1)} %bitcast.21), channel_id=1, source_target_pairs={{0,1},{1,0},{2,3},{3,2},{4,5},{5,4},{6,7},{7,6},{8,9},{9,8},{10,11... | collective-permute-start | bytes 6220808 | tf_op jit(solution)/shard_map/ppermute | solution.py:242
  10.2 7.0 %copy-start.2 = (bf16[1,720,1440]{2,1,0:T(8,128)(2,1)S(1)}, bf16[1,720,1440]{2,1,0:T(8,128)(2,1)}, u32[]{:S(2)}) copy-start(bf16[1,720,1440]{2,1,0:T(8,128)(2,1)} %param.23) | copy-start | bytes 6220804
  13.9 8.0 %copy-start = (bf16[1,1440,720]{2,1,0:T(8,128)(2,1)S(1)}, bf16[1,1440,720]{2,1,0:T(8,128)(2,1)}, u32[]{:S(2)}) copy-start(bf16[1,1440,720]{2,1,0:T(8,128)(2,1)} %param.21) | copy-start | bytes 6220804
  13.9 8.0 %copy-start.1 = (bf16[1,1440,720]{2,1,0:T(8,128)(2,1)S(1)}, bf16[1,1440,720]{2,1,0:T(8,128)(2,1)}, u32[]{:S(2)}) copy-start(bf16[1,1440,720]{2,1,0:T(8,128)(2,1)} %param.22) | copy-start | bytes 6220804
  17.2 4.7 %collective-permute-start.8 = (bf16[720,1440]{1,0:T(8,128)(2,1)S(1)}, bf16[720,1440]{1,0:T(8,128)(2,1)S(1)}, u32[]{:S(2)}, u32[]{:S(2)}) collective-permute-start(bf16[720,1440]{1,0:T(8,128)(2,1)S(1)} %bitcast.30), channel_id=1, source_target_pairs={{0,1},{1,0},{2,3},{3,2},{4,5},{5,4},{6,7},{7,6},{8,9},{9,8},{10,11... | collective-permute-start | bytes 6220808 | tf_op jit(solution)/shard_map/ppermute | solution.py:242
  17.4 7.5 %collective-permute-start.4 = (bf16[736,128]{1,0:T(8,128)(2,1)S(1)}, bf16[736,128]{1,0:T(8,128)(2,1)S(1)}, u32[]{:S(2)}, u32[]{:S(2)}) collective-permute-start(bf16[736,128]{1,0:T(8,128)(2,1)S(1)} %get-tuple-element.81.upper), channel_id=1, source_target_pairs={{0,4},{5,1},{4,8},{9,5},{8,12},{13,9},{12,14},{15,13},{14,10},{11,... | collective-permute-start | bytes 565256 | tf_op jit(solution)/shard_map/ppermute | solution.py:343
  19.9 7.4 %collective-permute-start.5 = (bf16[736,128]{1,0:T(8,128)(2,1)S(1)}, bf16[736,128]{1,0:T(8,128)(2,1)S(1)}, u32[]{:S(2)}, u32[]{:S(2)}) collective-permute-start(bf16[736,128]{1,0:T(8,128)(2,1)S(1)} %get-tuple-element.81.upper), channel_id=1, source_target_pairs={{4,0},{1,5},{8,4},{5,9},{12,8},{9,13},{14,12},{13,15},{10,14},{15,... | collective-permute-start | bytes 565256 | tf_op jit(solution)/shard_map/ppermute | solution.py:343
  19.9 9.4 %collective-permute-start.11 = (bf16[720,128]{1,0:T(8,128)(2,1)S(1)}, bf16[720,128]{1,0:T(8,128)(2,1)S(1)}, u32[]{:S(2)}, u32[]{:S(2)}) collective-permute-start(bf16[720,128]{1,0:T(8,128)(2,1)S(1)} %get-tuple-element.82.lower), channel_id=1, source_target_pairs={{0,4},{5,1},{4,8},{9,5},{8,12},{13,9},{12,14},{15,13},{14,10},{11,... | collective-permute-start | bytes 552968 | tf_op jit(solution)/shard_map/ppermute | solution.py:343
  21.9 9.4 %collective-permute-start.15 = (bf16[720,128]{1,0:T(8,128)(2,1)S(1)}, bf16[720,128]{1,0:T(8,128)(2,1)S(1)}, u32[]{:S(2)}, u32[]{:S(2)}) collective-permute-start(bf16[720,128]{1,0:T(8,128)(2,1)S(1)} %get-tuple-element.82.lower), channel_id=1, source_target_pairs={{4,0},{1,5},{8,4},{5,9},{12,8},{9,13},{14,12},{13,15},{10,14},{15,... | collective-permute-start | bytes 552968 | tf_op jit(solution)/shard_map/ppermute | solution.py:343
  27.3 7.7 %collective-permute-start.10 = (bf16[736,128]{1,0:T(8,128)(2,1)S(1)}, bf16[736,128]{1,0:T(8,128)(2,1)S(1)}, u32[]{:S(2)}, u32[]{:S(2)}) collective-permute-start(bf16[736,128]{1,0:T(8,128)(2,1)S(1)} %collective-permute-done.5.upper), channel_id=1, source_target_pairs={{4,0},{1,5},{8,4},{5,9},{12,8},{9,13},{14,12},{13,15},{10,14},{15,... | collective-permute-start | bytes 565256 | tf_op jit(solution)/shard_map/ppermute | solution.py:357
  27.5 7.4 %collective-permute-start.9 = (bf16[736,128]{1,0:T(8,128)(2,1)S(1)}, bf16[736,128]{1,0:T(8,128)(2,1)S(1)}, u32[]{:S(2)}, u32[]{:S(2)}) collective-permute-start(bf16[736,128]{1,0:T(8,128)(2,1)S(1)} %collective-permute-done.4.upper), channel_id=1, source_target_pairs={{0,4},{5,1},{4,8},{9,5},{8,12},{13,9},{12,14},{15,13},{14,10},{11,... | collective-permute-start | bytes 565256 | tf_op jit(solution)/shard_map/ppermute | solution.py:356
  29.3 8.9 %collective-permute-start.14 = (bf16[720,128]{1,0:T(8,128)(2,1)S(1)}, bf16[720,128]{1,0:T(8,128)(2,1)S(1)}, u32[]{:S(2)}, u32[]{:S(2)}) collective-permute-start(bf16[720,128]{1,0:T(8,128)(2,1)S(1)} %collective-permute-done.11.lower), channel_id=1, source_target_pairs={{0,4},{5,1},{4,8},{9,5},{8,12},{13,9},{12,14},{15,13},{14,10},{11,... | collective-permute-start | bytes 552968 | tf_op jit(solution)/shard_map/ppermute | solution.py:361
  31.4 9.3 %collective-permute-start.16 = (bf16[720,128]{1,0:T(8,128)(2,1)S(1)}, bf16[720,128]{1,0:T(8,128)(2,1)S(1)}, u32[]{:S(2)}, u32[]{:S(2)}) collective-permute-start(bf16[720,128]{1,0:T(8,128)(2,1)S(1)} %collective-permute-done.15.lower), channel_id=1, source_target_pairs={{4,0},{1,5},{8,4},{5,9},{12,8},{9,13},{14,12},{13,15},{10,14},{15,... | collective-permute-start | bytes 552968 | tf_op jit(solution)/shard_map/ppermute | solution.py:362
  34.9 8.0 %collective-permute-start.12 = (bf16[736,128]{1,0:T(8,128)(2,1)S(1)}, bf16[736,128]{1,0:T(8,128)(2,1)S(1)}, u32[]{:S(2)}, u32[]{:S(2)}) collective-permute-start(bf16[736,128]{1,0:T(8,128)(2,1)S(1)} %collective-permute-done.9.upper), channel_id=1, source_target_pairs={{0,4},{5,1},{4,8},{9,5},{8,12},{13,9},{12,14},{15,13},{14,10},{11,... | collective-permute-start | bytes 565256 | tf_op jit(solution)/shard_map/ppermute | solution.py:356
  36.7 7.3 %collective-permute-start.13 = (bf16[736,128]{1,0:T(8,128)(2,1)S(1)}, bf16[736,128]{1,0:T(8,128)(2,1)S(1)}, u32[]{:S(2)}, u32[]{:S(2)}) collective-permute-start(bf16[736,128]{1,0:T(8,128)(2,1)S(1)} %collective-permute-done.10.upper), channel_id=1, source_target_pairs={{4,0},{1,5},{8,4},{5,9},{12,8},{9,13},{14,12},{13,15},{10,14},{15,... | collective-permute-start | bytes 565256 | tf_op jit(solution)/shard_map/ppermute | solution.py:357
  38.2 9.2 %collective-permute-start.17 = (bf16[720,128]{1,0:T(8,128)(2,1)S(1)}, bf16[720,128]{1,0:T(8,128)(2,1)S(1)}, u32[]{:S(2)}, u32[]{:S(2)}) collective-permute-start(bf16[720,128]{1,0:T(8,128)(2,1)S(1)} %collective-permute-done.14.lower), channel_id=1, source_target_pairs={{0,4},{5,1},{4,8},{9,5},{8,12},{13,9},{12,14},{15,13},{14,10},{11,... | collective-permute-start | bytes 552968 | tf_op jit(solution)/shard_map/ppermute | solution.py:361
  40.7 6.7 %collective-permute-start.18 = (bf16[720,128]{1,0:T(8,128)(2,1)S(1)}, bf16[720,128]{1,0:T(8,128)(2,1)S(1)}, u32[]{:S(2)}, u32[]{:S(2)}) collective-permute-start(bf16[720,128]{1,0:T(8,128)(2,1)S(1)} %collective-permute-done.16.lower), channel_id=1, source_target_pairs={{4,0},{1,5},{8,4},{5,9},{12,8},{9,13},{14,12},{13,15},{10,14},{15,... | collective-permute-start | bytes 552968 | tf_op jit(solution)/shard_map/ppermute | solution.py:362
  44.1 10.8 %collective-permute-start.21 = (bf16[736,128]{1,0:T(8,128)(2,1)S(1)}, bf16[736,128]{1,0:T(8,128)(2,1)S(1)}, u32[]{:S(2)}, u32[]{:S(2)}) collective-permute-start(bf16[736,128]{1,0:T(8,128)(2,1)S(1)} %collective-permute-done.12.upper), channel_id=1, source_target_pairs={{0,4},{5,1},{4,8},{9,5},{8,12},{13,9},{12,14},{15,13},{14,10},{11,... | collective-permute-start | bytes 565256 | tf_op jit(solution)/shard_map/ppermute | solution.py:356
  47.4 7.5 %collective-permute-start.22 = (bf16[720,128]{1,0:T(8,128)(2,1)S(1)}, bf16[720,128]{1,0:T(8,128)(2,1)S(1)}, u32[]{:S(2)}, u32[]{:S(2)}) collective-permute-start(bf16[720,128]{1,0:T(8,128)(2,1)S(1)} %collective-permute-done.18.lower), channel_id=1, source_target_pairs={{4,0},{1,5},{8,4},{5,9},{12,8},{9,13},{14,12},{13,15},{10,14},{15,... | collective-permute-start | bytes 552968 | tf_op jit(solution)/shard_map/ppermute | solution.py:362
  50.6 10.8 %collective-permute-start.20 = (bf16[720,128]{1,0:T(8,128)(2,1)S(1)}, bf16[720,128]{1,0:T(8,128)(2,1)S(1)}, u32[]{:S(2)}, u32[]{:S(2)}) collective-permute-start(bf16[720,128]{1,0:T(8,128)(2,1)S(1)} %get-tuple-element.111), channel_id=1, source_target_pairs={{0,4},{5,1},{4,8},{9,5},{8,12},{13,9},{12,14},{15,13},{14,10},{11,... | collective-permute-start | bytes 552968 | tf_op jit(solution)/shard_map/ppermute | solution.py:370
  53.9 7.5 %collective-permute-start.19 = (bf16[720,128]{1,0:T(8,128)(2,1)S(1)}, bf16[720,128]{1,0:T(8,128)(2,1)S(1)}, u32[]{:S(2)}, u32[]{:S(2)}) collective-permute-start(bf16[720,128]{1,0:T(8,128)(2,1)S(1)} %get-tuple-element.114), channel_id=1, source_target_pairs={{4,0},{1,5},{8,4},{5,9},{12,8},{9,13},{14,12},{13,15},{10,14},{15,... | collective-permute-start | bytes 552968 | tf_op jit(solution)/shard_map/ppermute | solution.py:372
  57.1 7.5 %collective-permute-start.31 = (bf16[720,128]{1,0:T(8,128)(2,1)S(1)}, bf16[720,128]{1,0:T(8,128)(2,1)S(1)}, u32[]{:S(2)}, u32[]{:S(2)}) collective-permute-start(bf16[720,128]{1,0:T(8,128)(2,1)S(1)} %get-tuple-element.118), channel_id=1, source_target_pairs={{0,4},{5,1},{4,8},{9,5},{8,12},{13,9},{12,14},{15,13},{14,10},{11,... | collective-permute-start | bytes 552968 | tf_op jit(solution)/shard_map/ppermute | solution.py:375
  58.1 7.6 %collective-permute-start.27 = (bf16[720,128]{1,0:T(8,128)(2,1)S(1)}, bf16[720,128]{1,0:T(8,128)(2,1)S(1)}, u32[]{:S(2)}, u32[]{:S(2)}) collective-permute-start(bf16[720,128]{1,0:T(8,128)(2,1)S(1)} %get-tuple-element.119), channel_id=1, source_target_pairs={{4,0},{1,5},{8,4},{5,9},{12,8},{9,13},{14,12},{13,15},{10,14},{15,... | collective-permute-start | bytes 552968 | tf_op jit(solution)/shard_map/ppermute | solution.py:375
  61.4 7.6 %collective-permute-start.25 = (bf16[720,128]{1,0:T(8,128)(2,1)S(1)}, bf16[720,128]{1,0:T(8,128)(2,1)S(1)}, u32[]{:S(2)}, u32[]{:S(2)}) collective-permute-start(bf16[720,128]{1,0:T(8,128)(2,1)S(1)} %add_convert_fusion.7), channel_id=1, source_target_pairs={{0,4},{5,1},{4,8},{9,5},{8,12},{13,9},{12,14},{15,13},{14,10},{11,... | collective-permute-start | bytes 552968 | tf_op jit(solution)/shard_map/ppermute | solution.py:383
  62.6 7.6 %collective-permute-start.23 = (bf16[720,128]{1,0:T(8,128)(2,1)S(1)}, bf16[720,128]{1,0:T(8,128)(2,1)S(1)}, u32[]{:S(2)}, u32[]{:S(2)}) collective-permute-start(bf16[720,128]{1,0:T(8,128)(2,1)S(1)} %add_convert_fusion.9), channel_id=1, source_target_pairs={{4,0},{1,5},{8,4},{5,9},{12,8},{9,13},{14,12},{13,15},{10,14},{15,... | collective-permute-start | bytes 552968 | tf_op jit(solution)/shard_map/ppermute | solution.py:384
  64.7 8.4 %collective-permute-start.32 = (bf16[720,128]{1,0:T(8,128)(2,1)S(1)}, bf16[720,128]{1,0:T(8,128)(2,1)S(1)}, u32[]{:S(2)}, u32[]{:S(2)}) collective-permute-start(bf16[720,128]{1,0:T(8,128)(2,1)S(1)} %add_convert_fusion.2), channel_id=1, source_target_pairs={{0,4},{5,1},{4,8},{9,5},{8,12},{13,9},{12,14},{15,13},{14,10},{11,... | collective-permute-start | bytes 552968 | tf_op jit(solution)/shard_map/ppermute | solution.py:380
  65.8 8.4 %collective-permute-start.28 = (bf16[720,128]{1,0:T(8,128)(2,1)S(1)}, bf16[720,128]{1,0:T(8,128)(2,1)S(1)}, u32[]{:S(2)}, u32[]{:S(2)}) collective-permute-start(bf16[720,128]{1,0:T(8,128)(2,1)S(1)} %add_convert_fusion.5), channel_id=1, source_target_pairs={{4,0},{1,5},{8,4},{5,9},{12,8},{9,13},{14,12},{13,15},{10,14},{15,... | collective-permute-start | bytes 552968 | tf_op jit(solution)/shard_map/ppermute | solution.py:381
  69.1 11.8 %collective-permute-start.26 = (bf16[720,128]{1,0:T(8,128)(2,1)S(1)}, bf16[720,128]{1,0:T(8,128)(2,1)S(1)}, u32[]{:S(2)}, u32[]{:S(2)}) collective-permute-start(bf16[720,128]{1,0:T(8,128)(2,1)S(1)} %add_convert_fusion.6), channel_id=1, source_target_pairs={{0,4},{5,1},{4,8},{9,5},{8,12},{13,9},{12,14},{15,13},{14,10},{11,... | collective-permute-start | bytes 552968 | tf_op jit(solution)/shard_map/ppermute | solution.py:383
  70.3 10.6 %collective-permute-start.24 = (bf16[720,128]{1,0:T(8,128)(2,1)S(1)}, bf16[720,128]{1,0:T(8,128)(2,1)S(1)}, u32[]{:S(2)}, u32[]{:S(2)}) collective-permute-start(bf16[720,128]{1,0:T(8,128)(2,1)S(1)} %add_convert_fusion.8), channel_id=1, source_target_pairs={{4,0},{1,5},{8,4},{5,9},{12,8},{9,13},{14,12},{13,15},{10,14},{15,... | collective-permute-start | bytes 552968 | tf_op jit(solution)/shard_map/ppermute | solution.py:384
  73.1 5.6 %collective-permute-start.33 = (bf16[720,128]{1,0:T(8,128)(2,1)S(1)}, bf16[720,128]{1,0:T(8,128)(2,1)S(1)}, u32[]{:S(2)}, u32[]{:S(2)}) collective-permute-start(bf16[720,128]{1,0:T(8,128)(2,1)S(1)} %add_convert_fusion.1), channel_id=1, source_target_pairs={{0,4},{5,1},{4,8},{9,5},{8,12},{13,9},{12,14},{15,13},{14,10},{11,... | collective-permute-start | bytes 552968 | tf_op jit(solution)/shard_map/ppermute | solution.py:380
  74.2 5.6 %collective-permute-start.29 = (bf16[720,128]{1,0:T(8,128)(2,1)S(1)}, bf16[720,128]{1,0:T(8,128)(2,1)S(1)}, u32[]{:S(2)}, u32[]{:S(2)}) collective-permute-start(bf16[720,128]{1,0:T(8,128)(2,1)S(1)} %add_convert_fusion.4), channel_id=1, source_target_pairs={{4,0},{1,5},{8,4},{5,9},{12,8},{9,13},{14,12},{13,15},{10,14},{15,... | collective-permute-start | bytes 552968 | tf_op jit(solution)/shard_map/ppermute | solution.py:381
  78.7 5.6 %collective-permute-start.34 = (bf16[720,128]{1,0:T(8,128)(2,1)S(1)}, bf16[720,128]{1,0:T(8,128)(2,1)S(1)}, u32[]{:S(2)}, u32[]{:S(2)}) collective-permute-start(bf16[720,128]{1,0:T(8,128)(2,1)S(1)} %add_convert_fusion), channel_id=1, source_target_pairs={{0,4},{5,1},{4,8},{9,5},{8,12},{13,9},{12,14},{15,13},{14,10},{11,... | collective-permute-start | bytes 552968 | tf_op jit(solution)/shard_map/ppermute | solution.py:380
  79.9 5.6 %collective-permute-start.30 = (bf16[720,128]{1,0:T(8,128)(2,1)S(1)}, bf16[720,128]{1,0:T(8,128)(2,1)S(1)}, u32[]{:S(2)}, u32[]{:S(2)}) collective-permute-start(bf16[720,128]{1,0:T(8,128)(2,1)S(1)} %add_convert_fusion.3), channel_id=1, source_target_pairs={{4,0},{1,5},{8,4},{5,9},{12,8},{9,13},{14,12},{13,15},{10,14},{15,... | collective-permute-start | bytes 552968 | tf_op jit(solution)/shard_map/ppermute | solution.py:381

commit v6 on v5

--- a/solution.py
+++ b/solution.py
@@ -204,9 +204,9 @@
     packed, *extra = pack(
         code_rows, place, sink_logit, norm_gain, routes, gate_codes, key_rows, values, queries
     )
+    weights, packed = after(weights, packed)
     packed, rim_a = after(packed, rim_a)
     packed_b, rim_b = swapped(packed), swapped(rim_a)
-    weights, rim_a = after(weights, rim_a)
     features = residual.shape[1]
     half = half_of(features)
     blocks = queries.shape[1] // packed.shape[1]

time: 86.8 us -> 86.8 us (level)
  no operation moved by 1% of the time
where the time goes in v6:
time: 86.8 us; the launch traced here: 86.5 us
  starting transfers between devices  36.2 us (42%)
  Pallas kernels  28.4 us (33%)
  waiting for transfers between devices  19.8 us (23%)
    pallas_call x8, Pallas kernels, expert_terms(): pl.pallas_call(functools.partial(expert_kernel, code_rows), out_shape=[ja...  17.8 us
    ppermute x3, waiting for transfers between devices, mixed_by_ring(): right_up = to_right(add(terms[k][0], right_up))  8.51 us
    ppermute x3, starting transfers between devices, mixed_by_ring(): upper_left = to_right(uppers[0])  4.64 us
    ppermute x2, starting transfers between devices, mixed_by_ring(): lower_left = to_right(lowers[0]) if k < far else None  4.56 us
    ppermute x2, starting transfers between devices, mixed_by_ring(): to_right(half)  4.49 us
    ppermute x1, starting transfers between devices, front(): rim_a = lax.ppermute(pack_rim(key_rows, values), 'seq', steps)  4.44 us
    pallas_call x1, Pallas kernels, front(): pl.pallas_call(front_own_kernel, out_shape=jax.ShapeDtypeStruct((features...  3.73 us
    ppermute x3, starting transfers between devices, mixed_by_ring(): right_up = to_right(add(terms[k][0], right_up))  3.39 us
  transfers between devices with their start and end apart: 35, of which 11 were waited for; matrix products, arithmetic and copies ran while one was open for 1% of the time, Pallas kernels for 32%

profile of v6, /device:TPU:0, one launch (start us, length us, event | category | flops | bytes accessed | tf_op | source)
XLA Modules:
  0.0 86.5 jit_solution(11036781453860350442)
XLA Ops:
  1.1 0.8 rim.1
  1.9 4.4 %collective-permute-start = (bf16[256,128]{1,0:T(8,128)(2,1)S(1)}, bf16[256,128]{1,0:T(8,128)(2,1)S(1)}, u32[]{:S(2)}, u32[]{:S(2)}) collective-permute-start(bf16[256,128]{1,0:T(8,128)(2,1)S(1)} %rim.1), channel_id=1, source_target_pairs={{0,2},{2,4},{4,6},{6,8},{8,10},{10,12},{12,14},{1,3},{3,5},{5,7},{... | collective-permute-start | bytes 196616 | tf_op jit(solution)/shard_map/ppermute | solution.py:203
  6.4 0.7 broadcast_in_dim.6.gain
  7.2 1.9 %pack.1 = (bf16[1552,128]{1,0:T(8,128)(2,1)S(1)}, f32[1440,128]{1,0:T(8,128)S(1)}, bf16[16,128]{1,0:T(8,128)(2,1)S(1)}) custom-call(s32[2]{0:T(128)S(1)} %pad_add_fusion.place, f32[16]{0:T(128)} %sink.1, f32[1,1440]{1,0:T(1,128)S(1)} %broadcast_in_dim.6.gain, s32[4,256]{1,0:T(4,128)} %bitcast.43, s32[4,256]{1,0:T(4,128)} %bitcast.44, bf16[256,128]{1,0:T(8,128)(2,1)} %k.3, ...), custom_call_target="tpu_custom_call" | custom-call | flops 1 | bytes 1 | tf_op jit(solution)/shard_map/pack/pallas_call | solution.py:97
  10.2 3.7 %front_own.1.stream = f32[1440,128]{1,0:T(8,128)S(1)} custom-call(s32[2]{0:T(128)S(1)} %pad_add_fusion.place, bf16[1552,128]{1,0:T(8,128)(2,1)S(1)} %get-tuple-element.73.packed, bf16[256,128]{1,0:T(8,128)(2,1)S(1)} %collective-permute-done.rim, bf16[256,1024]{1,0:T(8,128)(2,1)} %q.3, bf16[1440,1024]{1,0:T(8,128)(2,1)} %bitcast.40, bf16[1440,256]{1,0:T(8,128)(2,1)} %bitcast.41), custom_call_target="tpu_custom_call" | custom-call | flops 1 | bytes 1 | tf_op jit(solution)/shard_map/front_own/pallas_call | solution.py:216
  14.0 3.2 %front.1 = (bf16[1440,128]{1,0:T(8,128)(2,1)}, bf16[736,128]{1,0:T(8,128)(2,1)S(1)}, bf16[720,128]{1,0:T(8,128)(2,1)S(1)}) custom-call(s32[2]{0:T(128)S(1)} %pad_add_fusion.place, bf16[1552,128]{1,0:T(8,128)(2,1)S(1)} %collective-permute-done.1.packed, bf16[256,128]{1,0:T(8,128)(2,1)S(1)} %collective-permute-done.2.rim, ...), custom_call_target="tpu_custom_call" | custom-call | flops 1 | bytes 1 | tf_op jit(solution)/shard_map/front/pallas_call | solution.py:229
  17.4 2.5 %collective-permute-start.4 = (bf16[736,128]{1,0:T(8,128)(2,1)S(1)}, bf16[736,128]{1,0:T(8,128)(2,1)S(1)}, u32[]{:S(2)}, u32[]{:S(2)}) collective-permute-start(bf16[736,128]{1,0:T(8,128)(2,1)S(1)} %get-tuple-element.81.upper), channel_id=1, source_target_pairs={{0,4},{5,1},{4,8},{9,5},{8,12},{13,9},{12,14},{15,13},{14,10},{11,... | collective-permute-start | bytes 565256 | tf_op jit(solution)/shard_map/ppermute | solution.py:343
  19.9 2.0 %collective-permute-start.11 = (bf16[720,128]{1,0:T(8,128)(2,1)S(1)}, bf16[720,128]{1,0:T(8,128)(2,1)S(1)}, u32[]{:S(2)}, u32[]{:S(2)}) collective-permute-start(bf16[720,128]{1,0:T(8,128)(2,1)S(1)} %get-tuple-element.82.lower), channel_id=1, source_target_pairs={{0,4},{5,1},{4,8},{9,5},{8,12},{13,9},{12,14},{15,13},{14,10},{11,... | collective-permute-start | bytes 552968 | tf_op jit(solution)/shard_map/ppermute | solution.py:343
  21.9 2.2 %experts.8 = (bf16[720,128]{1,0:T(8,128)(2,1)S(1)}, bf16[720,128]{1,0:T(8,128)(2,1)S(1)}) custom-call(s32[1]{0:T(128)} %bitcast.10.place, bf16[736,128]{1,0:T(8,128)(2,1)S(1)} %get-tuple-element.81.upper, bf16[720,128]{1,0:T(8,128)(2,1)S(1)} %get-tuple-element.82.lower, bf16[1440,720]{1,0:T(8,128)(2,1)S(1)} %bitcast.13, bf16[1440,720]{1,0:T(8,128)(2,1)S(1)} %bitcast.22, ...), custom_call_target="tpu_custom_call" | custom-call | flops 1000000000 | bytes 1 | tf_op jit(solution)/shard_map/experts/pallas_call | solution.py:283
  24.2 0.8 collective-permute-done.4.upper
  24.9 2.3 %collective-permute-done.5.upper = bf16[736,128]{1,0:T(8,128)(2,1)S(1)} collective-permute-done((bf16[736,128]{1,0:T(8,128)(2,1)S(1)}, bf16[736,128]{1,0:T(8,128)(2,1)S(1)}, u32[]{:S(2)}, u32[]{:S(2)}) %collective-permute-start.5) | collective-permute-done | bytes 188448 | tf_op jit(solution)/shard_map/ppermute | solution.py:343
  27.5 1.7 %collective-permute-start.9 = (bf16[736,128]{1,0:T(8,128)(2,1)S(1)}, bf16[736,128]{1,0:T(8,128)(2,1)S(1)}, u32[]{:S(2)}, u32[]{:S(2)}) collective-permute-start(bf16[736,128]{1,0:T(8,128)(2,1)S(1)} %collective-permute-done.4.upper), channel_id=1, source_target_pairs={{0,4},{5,1},{4,8},{9,5},{8,12},{13,9},{12,14},{15,13},{14,10},{11,... | collective-permute-start | bytes 565256 | tf_op jit(solution)/shard_map/ppermute | solution.py:356
  29.3 2.1 %collective-permute-start.14 = (bf16[720,128]{1,0:T(8,128)(2,1)S(1)}, bf16[720,128]{1,0:T(8,128)(2,1)S(1)}, u32[]{:S(2)}, u32[]{:S(2)}) collective-permute-start(bf16[720,128]{1,0:T(8,128)(2,1)S(1)} %collective-permute-done.11.lower), channel_id=1, source_target_pairs={{0,4},{5,1},{4,8},{9,5},{8,12},{13,9},{12,14},{15,13},{14,10},{11,... | collective-permute-start | bytes 552968 | tf_op jit(solution)/shard_map/ppermute | solution.py:361
  31.4 2.3 %experts.9 = (bf16[720,128]{1,0:T(8,128)(2,1)S(1)}, bf16[720,128]{1,0:T(8,128)(2,1)S(1)}) custom-call(s32[1]{0:T(128)} %bitcast.10.place, bf16[736,128]{1,0:T(8,128)(2,1)S(1)} %collective-permute-done.4.upper, bf16[720,128]{1,0:T(8,128)(2,1)S(1)} %collective-permute-done.11.lower, bf16[1440,720]{1,0:T(8,128)(2,1)S(1)} %bitcast.14, ...), custom_call_target="tpu_custom_call" | custom-call | flops 1000000000 | bytes 1 | tf_op jit(solution)/shard_map/experts/pallas_call | solution.py:283
  33.6 1.3 %collective-permute-done.10.upper = bf16[736,128]{1,0:T(8,128)(2,1)S(1)} collective-permute-done((bf16[736,128]{1,0:T(8,128)(2,1)S(1)}, bf16[736,128]{1,0:T(8,128)(2,1)S(1)}, u32[]{:S(2)}, u32[]{:S(2)}) %collective-permute-start.10) | collective-permute-done | bytes 188448 | tf_op jit(solution)/shard_map/ppermute | solution.py:357
  34.9 1.8 %collective-permute-start.12 = (bf16[736,128]{1,0:T(8,128)(2,1)S(1)}, bf16[736,128]{1,0:T(8,128)(2,1)S(1)}, u32[]{:S(2)}, u32[]{:S(2)}) collective-permute-start(bf16[736,128]{1,0:T(8,128)(2,1)S(1)} %collective-permute-done.9.upper), channel_id=1, source_target_pairs={{0,4},{5,1},{4,8},{9,5},{8,12},{13,9},{12,14},{15,13},{14,10},{11,... | collective-permute-start | bytes 565256 | tf_op jit(solution)/shard_map/ppermute | solution.py:356
  36.9 1.2 %collective-permute-done.14.lower = bf16[720,128]{1,0:T(8,128)(2,1)S(1)} collective-permute-done((bf16[720,128]{1,0:T(8,128)(2,1)S(1)}, bf16[720,128]{1,0:T(8,128)(2,1)S(1)}, u32[]{:S(2)}, u32[]{:S(2)}) %collective-permute-start.14) | collective-permute-done | bytes 184352 | tf_op jit(solution)/shard_map/ppermute | solution.py:361
  38.2 2.5 %collective-permute-start.17 = (bf16[720,128]{1,0:T(8,128)(2,1)S(1)}, bf16[720,128]{1,0:T(8,128)(2,1)S(1)}, u32[]{:S(2)}, u32[]{:S(2)}) collective-permute-start(bf16[720,128]{1,0:T(8,128)(2,1)S(1)} %collective-permute-done.14.lower), channel_id=1, source_target_pairs={{0,4},{5,1},{4,8},{9,5},{8,12},{13,9},{12,14},{15,13},{14,10},{11,... | collective-permute-start | bytes 552968 | tf_op jit(solution)/shard_map/ppermute | solution.py:361
  40.7 2.2 %experts.10 = (bf16[720,128]{1,0:T(8,128)(2,1)S(1)}, bf16[720,128]{1,0:T(8,128)(2,1)S(1)}) custom-call(s32[1]{0:T(128)} %bitcast.10.place, bf16[736,128]{1,0:T(8,128)(2,1)S(1)} %collective-permute-done.9.upper, bf16[720,128]{1,0:T(8,128)(2,1)S(1)} %collective-permute-done.14.lower, bf16[1440,720]{1,0:T(8,128)(2,1)S(1)} %bitcast.15, ...), custom_call_target="tpu_custom_call" | custom-call | flops 1000000000 | bytes 1 | tf_op jit(solution)/shard_map/experts/pallas_call | solution.py:283
  42.9 1.2 %collective-permute-done.13.upper = bf16[736,128]{1,0:T(8,128)(2,1)S(1)} collective-permute-done((bf16[736,128]{1,0:T(8,128)(2,1)S(1)}, bf16[736,128]{1,0:T(8,128)(2,1)S(1)}, u32[]{:S(2)}, u32[]{:S(2)}) %collective-permute-start.13) | collective-permute-done | bytes 188448 | tf_op jit(solution)/shard_map/ppermute | solution.py:357
  44.1 1.1 %collective-permute-start.21 = (bf16[736,128]{1,0:T(8,128)(2,1)S(1)}, bf16[736,128]{1,0:T(8,128)(2,1)S(1)}, u32[]{:S(2)}, u32[]{:S(2)}) collective-permute-start(bf16[736,128]{1,0:T(8,128)(2,1)S(1)} %collective-permute-done.12.upper), channel_id=1, source_target_pairs={{0,4},{5,1},{4,8},{9,5},{8,12},{13,9},{12,14},{15,13},{14,10},{11,... | collective-permute-start | bytes 565256 | tf_op jit(solution)/shard_map/ppermute | solution.py:356
  45.1 2.2 %experts.11 = (bf16[720,128]{1,0:T(8,128)(2,1)S(1)}, bf16[720,128]{1,0:T(8,128)(2,1)S(1)}) custom-call(s32[1]{0:T(128)} %bitcast.10.place, bf16[736,128]{1,0:T(8,128)(2,1)S(1)} %collective-permute-done.10.upper, bf16[720,128]{1,0:T(8,128)(2,1)S(1)} %collective-permute-done.16.lower, bf16[1440,720]{1,0:T(8,128)(2,1)S(1)} %bitcast.16, ...), custom_call_target="tpu_custom_call" | custom-call | flops 1000000000 | bytes 1 | tf_op jit(solution)/shard_map/experts/pallas_call | solution.py:283
  47.4 1.0 %collective-permute-start.22 = (bf16[720,128]{1,0:T(8,128)(2,1)S(1)}, bf16[720,128]{1,0:T(8,128)(2,1)S(1)}, u32[]{:S(2)}, u32[]{:S(2)}) collective-permute-start(bf16[720,128]{1,0:T(8,128)(2,1)S(1)} %collective-permute-done.18.lower), channel_id=1, source_target_pairs={{4,0},{1,5},{8,4},{5,9},{12,8},{9,13},{14,12},{13,15},{10,14},{15,... | collective-permute-start | bytes 552968 | tf_op jit(solution)/shard_map/ppermute | solution.py:362
  48.3 2.2 %experts.12 = (bf16[720,128]{1,0:T(8,128)(2,1)S(1)}, bf16[720,128]{1,0:T(8,128)(2,1)S(1)}) custom-call(s32[1]{0:T(128)} %bitcast.10.place, bf16[736,128]{1,0:T(8,128)(2,1)S(1)} %collective-permute-done.13.upper, bf16[720,128]{1,0:T(8,128)(2,1)S(1)} %collective-permute-done.18.lower, bf16[1440,720]{1,0:T(8,128)(2,1)S(1)} %bitcast.17, ...), custom_call_target="tpu_custom_call" | custom-call | flops 1000000000 | bytes 1 | tf_op jit(solution)/shard_map/experts/pallas_call | solution.py:283
  50.6 1.1 %collective-permute-start.20 = (bf16[720,128]{1,0:T(8,128)(2,1)S(1)}, bf16[720,128]{1,0:T(8,128)(2,1)S(1)}, u32[]{:S(2)}, u32[]{:S(2)}) collective-permute-start(bf16[720,128]{1,0:T(8,128)(2,1)S(1)} %get-tuple-element.111), channel_id=1, source_target_pairs={{0,4},{5,1},{4,8},{9,5},{8,12},{13,9},{12,14},{15,13},{14,10},{11,... | collective-permute-start | bytes 552968 | tf_op jit(solution)/shard_map/ppermute | solution.py:370
  51.7 2.2 %experts.13 = (bf16[720,128]{1,0:T(8,128)(2,1)S(1)}, bf16[720,128]{1,0:T(8,128)(2,1)S(1)}) custom-call(s32[1]{0:T(128)} %bitcast.10.place, bf16[736,128]{1,0:T(8,128)(2,1)S(1)} %collective-permute-done.12.upper, bf16[720,128]{1,0:T(8,128)(2,1)S(1)} %collective-permute-done.17.lower, bf16[1440,720]{1,0:T(8,128)(2,1)S(1)} %bitcast.18, ...), custom_call_target="tpu_custom_call" | custom-call | flops 1000000000 | bytes 1 | tf_op jit(solution)/shard_map/experts/pallas_call | solution.py:283
  53.9 1.0 %collective-permute-start.19 = (bf16[720,128]{1,0:T(8,128)(2,1)S(1)}, bf16[720,128]{1,0:T(8,128)(2,1)S(1)}, u32[]{:S(2)}, u32[]{:S(2)}) collective-permute-start(bf16[720,128]{1,0:T(8,128)(2,1)S(1)} %get-tuple-element.114), channel_id=1, source_target_pairs={{4,0},{1,5},{8,4},{5,9},{12,8},{9,13},{14,12},{13,15},{10,14},{15,... | collective-permute-start | bytes 552968 | tf_op jit(solution)/shard_map/ppermute | solution.py:372
  54.9 2.2 %experts.14 = (bf16[720,128]{1,0:T(8,128)(2,1)S(1)}, bf16[720,128]{1,0:T(8,128)(2,1)S(1)}) custom-call(s32[1]{0:T(128)} %bitcast.10.place, bf16[736,128]{1,0:T(8,128)(2,1)S(1)} %collective-permute-done.21.upper, bf16[720,128]{1,0:T(8,128)(2,1)S(1)} %collective-permute-done.22.lower, bf16[1440,720]{1,0:T(8,128)(2,1)S(1)} %bitcast.19, ...), custom_call_target="tpu_custom_call" | custom-call | flops 1000000000 | bytes 1 | tf_op jit(solution)/shard_map/experts/pallas_call | solution.py:283
  57.1 1.1 %collective-permute-start.31 = (bf16[720,128]{1,0:T(8,128)(2,1)S(1)}, bf16[720,128]{1,0:T(8,128)(2,1)S(1)}, u32[]{:S(2)}, u32[]{:S(2)}) collective-permute-start(bf16[720,128]{1,0:T(8,128)(2,1)S(1)} %get-tuple-element.118), channel_id=1, source_target_pairs={{0,4},{5,1},{4,8},{9,5},{8,12},{13,9},{12,14},{15,13},{14,10},{11,... | collective-permute-start | bytes 552968 | tf_op jit(solution)/shard_map/ppermute | solution.py:375
  58.1 1.0 %collective-permute-start.27 = (bf16[720,128]{1,0:T(8,128)(2,1)S(1)}, bf16[720,128]{1,0:T(8,128)(2,1)S(1)}, u32[]{:S(2)}, u32[]{:S(2)}) collective-permute-start(bf16[720,128]{1,0:T(8,128)(2,1)S(1)} %get-tuple-element.119), channel_id=1, source_target_pairs={{4,0},{1,5},{8,4},{5,9},{12,8},{9,13},{14,12},{13,15},{10,14},{15,... | collective-permute-start | bytes 552968 | tf_op jit(solution)/shard_map/ppermute | solution.py:375
  59.1 2.3 %experts.15 = (bf16[720,128]{1,0:T(8,128)(2,1)S(1)}, bf16[720,128]{1,0:T(8,128)(2,1)S(1)}) custom-call(s32[1]{0:T(128)} %bitcast.10.place, bf16[736,128]{1,0:T(8,128)(2,1)S(1)} %collective-permute-done.5.upper, bf16[720,128]{1,0:T(8,128)(2,1)S(1)} %collective-permute-done.15.lower, bf16[1440,720]{1,0:T(8,128)(2,1)S(1)} %bitcast.20, ...), custom_call_target="tpu_custom_call" | custom-call | flops 1000000000 | bytes 1 | tf_op jit(solution)/shard_map/experts/pallas_call | solution.py:283
  61.4 1.1 %collective-permute-start.25 = (bf16[720,128]{1,0:T(8,128)(2,1)S(1)}, bf16[720,128]{1,0:T(8,128)(2,1)S(1)}, u32[]{:S(2)}, u32[]{:S(2)}) collective-permute-start(bf16[720,128]{1,0:T(8,128)(2,1)S(1)} %add_convert_fusion.7), channel_id=1, source_target_pairs={{0,4},{5,1},{4,8},{9,5},{8,12},{13,9},{12,14},{15,13},{14,10},{11,... | collective-permute-start | bytes 552968 | tf_op jit(solution)/shard_map/ppermute | solution.py:383
  62.6 1.0 %collective-permute-start.23 = (bf16[720,128]{1,0:T(8,128)(2,1)S(1)}, bf16[720,128]{1,0:T(8,128)(2,1)S(1)}, u32[]{:S(2)}, u32[]{:S(2)}) collective-permute-start(bf16[720,128]{1,0:T(8,128)(2,1)S(1)} %add_convert_fusion.9), channel_id=1, source_target_pairs={{4,0},{1,5},{8,4},{5,9},{12,8},{9,13},{14,12},{13,15},{10,14},{15,... | collective-permute-start | bytes 552968 | tf_op jit(solution)/shard_map/ppermute | solution.py:384
  63.6 1.0 %collective-permute-done.31 = bf16[720,128]{1,0:T(8,128)(2,1)S(1)} collective-permute-done((bf16[720,128]{1,0:T(8,128)(2,1)S(1)}, bf16[720,128]{1,0:T(8,128)(2,1)S(1)}, u32[]{:S(2)}, u32[]{:S(2)}) %collective-permute-start.31) | collective-permute-done | bytes 184352 | tf_op jit(solution)/shard_map/ppermute | solution.py:375
  64.7 1.1 %collective-permute-start.32 = (bf16[720,128]{1,0:T(8,128)(2,1)S(1)}, bf16[720,128]{1,0:T(8,128)(2,1)S(1)}, u32[]{:S(2)}, u32[]{:S(2)}) collective-permute-start(bf16[720,128]{1,0:T(8,128)(2,1)S(1)} %add_convert_fusion.2), channel_id=1, source_target_pairs={{0,4},{5,1},{4,8},{9,5},{8,12},{13,9},{12,14},{15,13},{14,10},{11,... | collective-permute-start | bytes 552968 | tf_op jit(solution)/shard_map/ppermute | solution.py:380
  65.8 1.0 %collective-permute-start.28 = (bf16[720,128]{1,0:T(8,128)(2,1)S(1)}, bf16[720,128]{1,0:T(8,128)(2,1)S(1)}, u32[]{:S(2)}, u32[]{:S(2)}) collective-permute-start(bf16[720,128]{1,0:T(8,128)(2,1)S(1)} %add_convert_fusion.5), channel_id=1, source_target_pairs={{4,0},{1,5},{8,4},{5,9},{12,8},{9,13},{14,12},{13,15},{10,14},{15,... | collective-permute-start | bytes 552968 | tf_op jit(solution)/shard_map/ppermute | solution.py:381
  66.8 2.2 %collective-permute-done.25 = bf16[720,128]{1,0:T(8,128)(2,1)S(1)} collective-permute-done((bf16[720,128]{1,0:T(8,128)(2,1)S(1)}, bf16[720,128]{1,0:T(8,128)(2,1)S(1)}, u32[]{:S(2)}, u32[]{:S(2)}) %collective-permute-start.25) | collective-permute-done | bytes 184352 | tf_op jit(solution)/shard_map/ppermute | solution.py:383
  69.1 1.1 %collective-permute-start.26 = (bf16[720,128]{1,0:T(8,128)(2,1)S(1)}, bf16[720,128]{1,0:T(8,128)(2,1)S(1)}, u32[]{:S(2)}, u32[]{:S(2)}) collective-permute-start(bf16[720,128]{1,0:T(8,128)(2,1)S(1)} %add_convert_fusion.6), channel_id=1, source_target_pairs={{0,4},{5,1},{4,8},{9,5},{8,12},{13,9},{12,14},{15,13},{14,10},{11,... | collective-permute-start | bytes 552968 | tf_op jit(solution)/shard_map/ppermute | solution.py:383
  70.3 1.0 %collective-permute-start.24 = (bf16[720,128]{1,0:T(8,128)(2,1)S(1)}, bf16[720,128]{1,0:T(8,128)(2,1)S(1)}, u32[]{:S(2)}, u32[]{:S(2)}) collective-permute-start(bf16[720,128]{1,0:T(8,128)(2,1)S(1)} %add_convert_fusion.8), channel_id=1, source_target_pairs={{4,0},{1,5},{8,4},{5,9},{12,8},{9,13},{14,12},{13,15},{10,14},{15,... | collective-permute-start | bytes 552968 | tf_op jit(solution)/shard_map/ppermute | solution.py:384
  71.3 1.7 %collective-permute-done.32 = bf16[720,128]{1,0:T(8,128)(2,1)S(1)} collective-permute-done((bf16[720,128]{1,0:T(8,128)(2,1)S(1)}, bf16[720,128]{1,0:T(8,128)(2,1)S(1)}, u32[]{:S(2)}, u32[]{:S(2)}) %collective-permute-start.32) | collective-permute-done | bytes 184352 | tf_op jit(solution)/shard_map/ppermute | solution.py:380
  73.1 1.1 %collective-permute-start.33 = (bf16[720,128]{1,0:T(8,128)(2,1)S(1)}, bf16[720,128]{1,0:T(8,128)(2,1)S(1)}, u32[]{:S(2)}, u32[]{:S(2)}) collective-permute-start(bf16[720,128]{1,0:T(8,128)(2,1)S(1)} %add_convert_fusion.1), channel_id=1, source_target_pairs={{0,4},{5,1},{4,8},{9,5},{8,12},{13,9},{12,14},{15,13},{14,10},{11,... | collective-permute-start | bytes 552968 | tf_op jit(solution)/shard_map/ppermute | solution.py:380
  74.2 1.0 %collective-permute-start.29 = (bf16[720,128]{1,0:T(8,128)(2,1)S(1)}, bf16[720,128]{1,0:T(8,128)(2,1)S(1)}, u32[]{:S(2)}, u32[]{:S(2)}) collective-permute-start(bf16[720,128]{1,0:T(8,128)(2,1)S(1)} %add_convert_fusion.4), channel_id=1, source_target_pairs={{4,0},{1,5},{8,4},{5,9},{12,8},{9,13},{14,12},{13,15},{10,14},{15,... | collective-permute-start | bytes 552968 | tf_op jit(solution)/shard_map/ppermute | solution.py:381
  75.3 3.4 %collective-permute-done.33 = bf16[720,128]{1,0:T(8,128)(2,1)S(1)} collective-permute-done((bf16[720,128]{1,0:T(8,128)(2,1)S(1)}, bf16[720,128]{1,0:T(8,128)(2,1)S(1)}, u32[]{:S(2)}, u32[]{:S(2)}) %collective-permute-start.33) | collective-permute-done | bytes 184352 | tf_op jit(solution)/shard_map/ppermute | solution.py:380
  78.7 1.2 %collective-permute-start.34 = (bf16[720,128]{1,0:T(8,128)(2,1)S(1)}, bf16[720,128]{1,0:T(8,128)(2,1)S(1)}, u32[]{:S(2)}, u32[]{:S(2)}) collective-permute-start(bf16[720,128]{1,0:T(8,128)(2,1)S(1)} %add_convert_fusion), channel_id=1, source_target_pairs={{0,4},{5,1},{4,8},{9,5},{8,12},{13,9},{12,14},{15,13},{14,10},{11,... | collective-permute-start | bytes 552968 | tf_op jit(solution)/shard_map/ppermute | solution.py:380
  79.9 1.0 %collective-permute-start.30 = (bf16[720,128]{1,0:T(8,128)(2,1)S(1)}, bf16[720,128]{1,0:T(8,128)(2,1)S(1)}, u32[]{:S(2)}, u32[]{:S(2)}) collective-permute-start(bf16[720,128]{1,0:T(8,128)(2,1)S(1)} %add_convert_fusion.3), channel_id=1, source_target_pairs={{4,0},{1,5},{8,4},{5,9},{12,8},{9,13},{14,12},{13,15},{10,14},{15,... | collective-permute-start | bytes 552968 | tf_op jit(solution)/shard_map/ppermute | solution.py:381
  80.9 3.4 %collective-permute-done.34.refs_2_ = bf16[720,128]{1,0:T(8,128)(2,1)S(1)} collective-permute-done((bf16[720,128]{1,0:T(8,128)(2,1)S(1)}, bf16[720,128]{1,0:T(8,128)(2,1)S(1)}, u32[]{:S(2)}, u32[]{:S(2)}) %collective-permute-start.34) | collective-permute-done | bytes 184352 | tf_op jit(solution)/shard_map/ppermute | solution.py:380
  84.3 1.2 %collective-permute-done.30.refs_4_ = bf16[720,128]{1,0:T(8,128)(2,1)S(1)} collective-permute-done((bf16[720,128]{1,0:T(8,128)(2,1)S(1)}, bf16[720,128]{1,0:T(8,128)(2,1)S(1)}, u32[]{:S(2)}, u32[]{:S(2)}) %collective-permute-start.30) | collective-permute-done | bytes 184352 | tf_op jit(solution)/shard_map/ppermute | solution.py:381
  85.5 0.9 %total.1 = bf16[1440,128]{1,0:T(8,128)(2,1)} custom-call(bf16[720,128]{1,0:T(8,128)(2,1)S(1)} %get-tuple-element.134.refs_0_, bf16[720,128]{1,0:T(8,128)(2,1)S(1)} %collective-permute-done.24.refs_1_, bf16[720,128]{1,0:T(8,128)(2,1)S(1)} %collective-permute-done.34.refs_2_, bf16[720,128]{1,0:T(8,128)(2,1)S(1)} %get-tuple-element.137.refs_3_, ...), custom_call_target="tpu_custom_call" | custom-call | flops 1 | bytes 1 | tf_op jit(solution)/shard_map/total/pallas_call | solution.py:308
  (53 shorter events, 3.0 us)
Async XLA Ops:
  0.6 13.3 %collective-permute-start.3 = (bf16[1440,1024]{1,0:T(8,128)(2,1)}, bf16[1440,1024]{1,0:T(8,128)(2,1)S(1)}, u32[]{:S(2)}, u32[]{:S(2)}) collective-permute-start(bf16[1440,1024]{1,0:T(8,128)(2,1)} %bitcast.39), channel_id=1, source_target_pairs={{0,1},{1,0},{2,3},{3,2},{4,5},{5,4},{6,7},{7,6},{8,9},{9,8},{10,11... | collective-permute-start | bytes 8847368 | tf_op jit(solution)/shard_map/ppermute | solution.py:242
  1.9 7.1 %collective-permute-start = (bf16[256,128]{1,0:T(8,128)(2,1)S(1)}, bf16[256,128]{1,0:T(8,128)(2,1)S(1)}, u32[]{:S(2)}, u32[]{:S(2)}) collective-permute-start(bf16[256,128]{1,0:T(8,128)(2,1)S(1)} %rim.1), channel_id=1, source_target_pairs={{0,2},{2,4},{4,6},{6,8},{8,10},{10,12},{12,14},{1,3},{3,5},{5,7},{... | collective-permute-start | bytes 196616 | tf_op jit(solution)/shard_map/ppermute | solution.py:203
  9.1 4.8 %collective-permute-start.1 = (bf16[1552,128]{1,0:T(8,128)(2,1)S(1)}, bf16[1552,128]{1,0:T(8,128)(2,1)S(1)}, u32[]{:S(2)}, u32[]{:S(2)}) collective-permute-start(bf16[1552,128]{1,0:T(8,128)(2,1)S(1)} %get-tuple-element.73.packed), channel_id=1, source_target_pairs={{0,1},{1,0},{2,3},{3,2},{4,5},{5,4},{6,7},{7,6},{8,9},{9,8},{10,11... | collective-permute-start | bytes 1191944 | tf_op jit(solution)/shard_map/ppermute | solution.py:242
  9.3 4.6 %collective-permute-start.2 = (bf16[256,128]{1,0:T(8,128)(2,1)S(1)}, bf16[256,128]{1,0:T(8,128)(2,1)S(1)}, u32[]{:S(2)}, u32[]{:S(2)}) collective-permute-start(bf16[256,128]{1,0:T(8,128)(2,1)S(1)} %collective-permute-done.rim), channel_id=1, source_target_pairs={{0,1},{1,0},{2,3},{3,2},{4,5},{5,4},{6,7},{7,6},{8,9},{9,8},{10,11... | collective-permute-start | bytes 196616 | tf_op jit(solution)/shard_map/ppermute | solution.py:242
  9.7 10.2 %collective-permute-start.6 = (bf16[1440,720]{1,0:T(8,128)(2,1)}, bf16[1440,720]{1,0:T(8,128)(2,1)S(1)}, u32[]{:S(2)}, u32[]{:S(2)}) collective-permute-start(bf16[1440,720]{1,0:T(8,128)(2,1)} %bitcast.12), channel_id=1, source_target_pairs={{0,1},{1,0},{2,3},{3,2},{4,5},{5,4},{6,7},{7,6},{8,9},{9,8},{10,11... | collective-permute-start | bytes 6220808 | tf_op jit(solution)/shard_map/ppermute | solution.py:242
  9.9 12.1 %collective-permute-start.7 = (bf16[1440,720]{1,0:T(8,128)(2,1)}, bf16[1440,720]{1,0:T(8,128)(2,1)S(1)}, u32[]{:S(2)}, u32[]{:S(2)}) collective-permute-start(bf16[1440,720]{1,0:T(8,128)(2,1)} %bitcast.21), channel_id=1, source_target_pairs={{0,1},{1,0},{2,3},{3,2},{4,5},{5,4},{6,7},{7,6},{8,9},{9,8},{10,11... | collective-permute-start | bytes 6220808 | tf_op jit(solution)/shard_map/ppermute | solution.py:242
  10.2 7.0 %copy-start.2 = (bf16[1,720,1440]{2,1,0:T(8,128)(2,1)S(1)}, bf16[1,720,1440]{2,1,0:T(8,128)(2,1)}, u32[]{:S(2)}) copy-start(bf16[1,720,1440]{2,1,0:T(8,128)(2,1)} %param.23) | copy-start | bytes 6220804
  13.9 8.0 %copy-start = (bf16[1,1440,720]{2,1,0:T(8,128)(2,1)S(1)}, bf16[1,1440,720]{2,1,0:T(8,128)(2,1)}, u32[]{:S(2)}) copy-start(bf16[1,1440,720]{2,1,0:T(8,128)(2,1)} %param.21) | copy-start | bytes 6220804
  13.9 8.0 %copy-start.1 = (bf16[1,1440,720]{2,1,0:T(8,128)(2,1)S(1)}, bf16[1,1440,720]{2,1,0:T(8,128)(2,1)}, u32[]{:S(2)}) copy-start(bf16[1,1440,720]{2,1,0:T(8,128)(2,1)} %param.22) | copy-start | bytes 6220804
  17.2 4.7 %collective-permute-start.8 = (bf16[720,1440]{1,0:T(8,128)(2,1)S(1)}, bf16[720,1440]{1,0:T(8,128)(2,1)S(1)}, u32[]{:S(2)}, u32[]{:S(2)}) collective-permute-start(bf16[720,1440]{1,0:T(8,128)(2,1)S(1)} %bitcast.30), channel_id=1, source_target_pairs={{0,1},{1,0},{2,3},{3,2},{4,5},{5,4},{6,7},{7,6},{8,9},{9,8},{10,11... | collective-permute-start | bytes 6220808 | tf_op jit(solution)/shard_map/ppermute | solution.py:242
  17.4 7.5 %collective-permute-start.4 = (bf16[736,128]{1,0:T(8,128)(2,1)S(1)}, bf16[736,128]{1,0:T(8,128)(2,1)S(1)}, u32[]{:S(2)}, u32[]{:S(2)}) collective-permute-start(bf16[736,128]{1,0:T(8,128)(2,1)S(1)} %get-tuple-element.81.upper), channel_id=1, source_target_pairs={{0,4},{5,1},{4,8},{9,5},{8,12},{13,9},{12,14},{15,13},{14,10},{11,... | collective-permute-start | bytes 565256 | tf_op jit(solution)/shard_map/ppermute | solution.py:343
  19.9 7.4 %collective-permute-start.5 = (bf16[736,128]{1,0:T(8,128)(2,1)S(1)}, bf16[736,128]{1,0:T(8,128)(2,1)S(1)}, u32[]{:S(2)}, u32[]{:S(2)}) collective-permute-start(bf16[736,128]{1,0:T(8,128)(2,1)S(1)} %get-tuple-element.81.upper), channel_id=1, source_target_pairs={{4,0},{1,5},{8,4},{5,9},{12,8},{9,13},{14,12},{13,15},{10,14},{15,... | collective-permute-start | bytes 565256 | tf_op jit(solution)/shard_map/ppermute | solution.py:343
  19.9 9.4 %collective-permute-start.11 = (bf16[720,128]{1,0:T(8,128)(2,1)S(1)}, bf16[720,128]{1,0:T(8,128)(2,1)S(1)}, u32[]{:S(2)}, u32[]{:S(2)}) collective-permute-start(bf16[720,128]{1,0:T(8,128)(2,1)S(1)} %get-tuple-element.82.lower), channel_id=1, source_target_pairs={{0,4},{5,1},{4,8},{9,5},{8,12},{13,9},{12,14},{15,13},{14,10},{11,... | collective-permute-start | bytes 552968 | tf_op jit(solution)/shard_map/ppermute | solution.py:343
  21.9 9.4 %collective-permute-start.15 = (bf16[720,128]{1,0:T(8,128)(2,1)S(1)}, bf16[720,128]{1,0:T(8,128)(2,1)S(1)}, u32[]{:S(2)}, u32[]{:S(2)}) collective-permute-start(bf16[720,128]{1,0:T(8,128)(2,1)S(1)} %get-tuple-element.82.lower), channel_id=1, source_target_pairs={{4,0},{1,5},{8,4},{5,9},{12,8},{9,13},{14,12},{13,15},{10,14},{15,... | collective-permute-start | bytes 552968 | tf_op jit(solution)/shard_map/ppermute | solution.py:343
  27.3 7.7 %collective-permute-start.10 = (bf16[736,128]{1,0:T(8,128)(2,1)S(1)}, bf16[736,128]{1,0:T(8,128)(2,1)S(1)}, u32[]{:S(2)}, u32[]{:S(2)}) collective-permute-start(bf16[736,128]{1,0:T(8,128)(2,1)S(1)} %collective-permute-done.5.upper), channel_id=1, source_target_pairs={{4,0},{1,5},{8,4},{5,9},{12,8},{9,13},{14,12},{13,15},{10,14},{15,... | collective-permute-start | bytes 565256 | tf_op jit(solution)/shard_map/ppermute | solution.py:357
  27.5 7.4 %collective-permute-start.9 = (bf16[736,128]{1,0:T(8,128)(2,1)S(1)}, bf16[736,128]{1,0:T(8,128)(2,1)S(1)}, u32[]{:S(2)}, u32[]{:S(2)}) collective-permute-start(bf16[736,128]{1,0:T(8,128)(2,1)S(1)} %collective-permute-done.4.upper), channel_id=1, source_target_pairs={{0,4},{5,1},{4,8},{9,5},{8,12},{13,9},{12,14},{15,13},{14,10},{11,... | collective-permute-start | bytes 565256 | tf_op jit(solution)/shard_map/ppermute | solution.py:356
  29.3 8.9 %collective-permute-start.14 = (bf16[720,128]{1,0:T(8,128)(2,1)S(1)}, bf16[720,128]{1,0:T(8,128)(2,1)S(1)}, u32[]{:S(2)}, u32[]{:S(2)}) collective-permute-start(bf16[720,128]{1,0:T(8,128)(2,1)S(1)} %collective-permute-done.11.lower), channel_id=1, source_target_pairs={{0,4},{5,1},{4,8},{9,5},{8,12},{13,9},{12,14},{15,13},{14,10},{11,... | collective-permute-start | bytes 552968 | tf_op jit(solution)/shard_map/ppermute | solution.py:361
  31.4 9.3 %collective-permute-start.16 = (bf16[720,128]{1,0:T(8,128)(2,1)S(1)}, bf16[720,128]{1,0:T(8,128)(2,1)S(1)}, u32[]{:S(2)}, u32[]{:S(2)}) collective-permute-start(bf16[720,128]{1,0:T(8,128)(2,1)S(1)} %collective-permute-done.15.lower), channel_id=1, source_target_pairs={{4,0},{1,5},{8,4},{5,9},{12,8},{9,13},{14,12},{13,15},{10,14},{15,... | collective-permute-start | bytes 552968 | tf_op jit(solution)/shard_map/ppermute | solution.py:362
  34.9 8.0 %collective-permute-start.12 = (bf16[736,128]{1,0:T(8,128)(2,1)S(1)}, bf16[736,128]{1,0:T(8,128)(2,1)S(1)}, u32[]{:S(2)}, u32[]{:S(2)}) collective-permute-start(bf16[736,128]{1,0:T(8,128)(2,1)S(1)} %collective-permute-done.9.upper), channel_id=1, source_target_pairs={{0,4},{5,1},{4,8},{9,5},{8,12},{13,9},{12,14},{15,13},{14,10},{11,... | collective-permute-start | bytes 565256 | tf_op jit(solution)/shard_map/ppermute | solution.py:356
  36.7 7.3 %collective-permute-start.13 = (bf16[736,128]{1,0:T(8,128)(2,1)S(1)}, bf16[736,128]{1,0:T(8,128)(2,1)S(1)}, u32[]{:S(2)}, u32[]{:S(2)}) collective-permute-start(bf16[736,128]{1,0:T(8,128)(2,1)S(1)} %collective-permute-done.10.upper), channel_id=1, source_target_pairs={{4,0},{1,5},{8,4},{5,9},{12,8},{9,13},{14,12},{13,15},{10,14},{15,... | collective-permute-start | bytes 565256 | tf_op jit(solution)/shard_map/ppermute | solution.py:357
  38.2 9.2 %collective-permute-start.17 = (bf16[720,128]{1,0:T(8,128)(2,1)S(1)}, bf16[720,128]{1,0:T(8,128)(2,1)S(1)}, u32[]{:S(2)}, u32[]{:S(2)}) collective-permute-start(bf16[720,128]{1,0:T(8,128)(2,1)S(1)} %collective-permute-done.14.lower), channel_id=1, source_target_pairs={{0,4},{5,1},{4,8},{9,5},{8,12},{13,9},{12,14},{15,13},{14,10},{11,... | collective-permute-start | bytes 552968 | tf_op jit(solution)/shard_map/ppermute | solution.py:361
  40.7 6.7 %collective-permute-start.18 = (bf16[720,128]{1,0:T(8,128)(2,1)S(1)}, bf16[720,128]{1,0:T(8,128)(2,1)S(1)}, u32[]{:S(2)}, u32[]{:S(2)}) collective-permute-start(bf16[720,128]{1,0:T(8,128)(2,1)S(1)} %collective-permute-done.16.lower), channel_id=1, source_target_pairs={{4,0},{1,5},{8,4},{5,9},{12,8},{9,13},{14,12},{13,15},{10,14},{15,... | collective-permute-start | bytes 552968 | tf_op jit(solution)/shard_map/ppermute | solution.py:362
  44.1 10.8 %collective-permute-start.21 = (bf16[736,128]{1,0:T(8,128)(2,1)S(1)}, bf16[736,128]{1,0:T(8,128)(2,1)S(1)}, u32[]{:S(2)}, u32[]{:S(2)}) collective-permute-start(bf16[736,128]{1,0:T(8,128)(2,1)S(1)} %collective-permute-done.12.upper), channel_id=1, source_target_pairs={{0,4},{5,1},{4,8},{9,5},{8,12},{13,9},{12,14},{15,13},{14,10},{11,... | collective-permute-start | bytes 565256 | tf_op jit(solution)/shard_map/ppermute | solution.py:356
  47.4 7.5 %collective-permute-start.22 = (bf16[720,128]{1,0:T(8,128)(2,1)S(1)}, bf16[720,128]{1,0:T(8,128)(2,1)S(1)}, u32[]{:S(2)}, u32[]{:S(2)}) collective-permute-start(bf16[720,128]{1,0:T(8,128)(2,1)S(1)} %collective-permute-done.18.lower), channel_id=1, source_target_pairs={{4,0},{1,5},{8,4},{5,9},{12,8},{9,13},{14,12},{13,15},{10,14},{15,... | collective-permute-start | bytes 552968 | tf_op jit(solution)/shard_map/ppermute | solution.py:362
  50.6 10.8 %collective-permute-start.20 = (bf16[720,128]{1,0:T(8,128)(2,1)S(1)}, bf16[720,128]{1,0:T(8,128)(2,1)S(1)}, u32[]{:S(2)}, u32[]{:S(2)}) collective-permute-start(bf16[720,128]{1,0:T(8,128)(2,1)S(1)} %get-tuple-element.111), channel_id=1, source_target_pairs={{0,4},{5,1},{4,8},{9,5},{8,12},{13,9},{12,14},{15,13},{14,10},{11,... | collective-permute-start | bytes 552968 | tf_op jit(solution)/shard_map/ppermute | solution.py:370
  53.9 7.5 %collective-permute-start.19 = (bf16[720,128]{1,0:T(8,128)(2,1)S(1)}, bf16[720,128]{1,0:T(8,128)(2,1)S(1)}, u32[]{:S(2)}, u32[]{:S(2)}) collective-permute-start(bf16[720,128]{1,0:T(8,128)(2,1)S(1)} %get-tuple-element.114), channel_id=1, source_target_pairs={{4,0},{1,5},{8,4},{5,9},{12,8},{9,13},{14,12},{13,15},{10,14},{15,... | collective-permute-start | bytes 552968 | tf_op jit(solution)/shard_map/ppermute | solution.py:372
  57.1 7.5 %collective-permute-start.31 = (bf16[720,128]{1,0:T(8,128)(2,1)S(1)}, bf16[720,128]{1,0:T(8,128)(2,1)S(1)}, u32[]{:S(2)}, u32[]{:S(2)}) collective-permute-start(bf16[720,128]{1,0:T(8,128)(2,1)S(1)} %get-tuple-element.118), channel_id=1, source_target_pairs={{0,4},{5,1},{4,8},{9,5},{8,12},{13,9},{12,14},{15,13},{14,10},{11,... | collective-permute-start | bytes 552968 | tf_op jit(solution)/shard_map/ppermute | solution.py:375
  58.1 7.6 %collective-permute-start.27 = (bf16[720,128]{1,0:T(8,128)(2,1)S(1)}, bf16[720,128]{1,0:T(8,128)(2,1)S(1)}, u32[]{:S(2)}, u32[]{:S(2)}) collective-permute-start(bf16[720,128]{1,0:T(8,128)(2,1)S(1)} %get-tuple-element.119), channel_id=1, source_target_pairs={{4,0},{1,5},{8,4},{5,9},{12,8},{9,13},{14,12},{13,15},{10,14},{15,... | collective-permute-start | bytes 552968 | tf_op jit(solution)/shard_map/ppermute | solution.py:375
  61.4 7.6 %collective-permute-start.25 = (bf16[720,128]{1,0:T(8,128)(2,1)S(1)}, bf16[720,128]{1,0:T(8,128)(2,1)S(1)}, u32[]{:S(2)}, u32[]{:S(2)}) collective-permute-start(bf16[720,128]{1,0:T(8,128)(2,1)S(1)} %add_convert_fusion.7), channel_id=1, source_target_pairs={{0,4},{5,1},{4,8},{9,5},{8,12},{13,9},{12,14},{15,13},{14,10},{11,... | collective-permute-start | bytes 552968 | tf_op jit(solution)/shard_map/ppermute | solution.py:383
  62.6 7.6 %collective-permute-start.23 = (bf16[720,128]{1,0:T(8,128)(2,1)S(1)}, bf16[720,128]{1,0:T(8,128)(2,1)S(1)}, u32[]{:S(2)}, u32[]{:S(2)}) collective-permute-start(bf16[720,128]{1,0:T(8,128)(2,1)S(1)} %add_convert_fusion.9), channel_id=1, source_target_pairs={{4,0},{1,5},{8,4},{5,9},{12,8},{9,13},{14,12},{13,15},{10,14},{15,... | collective-permute-start | bytes 552968 | tf_op jit(solution)/shard_map/ppermute | solution.py:384
  64.7 8.4 %collective-permute-start.32 = (bf16[720,128]{1,0:T(8,128)(2,1)S(1)}, bf16[720,128]{1,0:T(8,128)(2,1)S(1)}, u32[]{:S(2)}, u32[]{:S(2)}) collective-permute-start(bf16[720,128]{1,0:T(8,128)(2,1)S(1)} %add_convert_fusion.2), channel_id=1, source_target_pairs={{0,4},{5,1},{4,8},{9,5},{8,12},{13,9},{12,14},{15,13},{14,10},{11,... | collective-permute-start | bytes 552968 | tf_op jit(solution)/shard_map/ppermute | solution.py:380
  65.8 8.4 %collective-permute-start.28 = (bf16[720,128]{1,0:T(8,128)(2,1)S(1)}, bf16[720,128]{1,0:T(8,128)(2,1)S(1)}, u32[]{:S(2)}, u32[]{:S(2)}) collective-permute-start(bf16[720,128]{1,0:T(8,128)(2,1)S(1)} %add_convert_fusion.5), channel_id=1, source_target_pairs={{4,0},{1,5},{8,4},{5,9},{12,8},{9,13},{14,12},{13,15},{10,14},{15,... | collective-permute-start | bytes 552968 | tf_op jit(solution)/shard_map/ppermute | solution.py:381
  69.1 11.8 %collective-permute-start.26 = (bf16[720,128]{1,0:T(8,128)(2,1)S(1)}, bf16[720,128]{1,0:T(8,128)(2,1)S(1)}, u32[]{:S(2)}, u32[]{:S(2)}) collective-permute-start(bf16[720,128]{1,0:T(8,128)(2,1)S(1)} %add_convert_fusion.6), channel_id=1, source_target_pairs={{0,4},{5,1},{4,8},{9,5},{8,12},{13,9},{12,14},{15,13},{14,10},{11,... | collective-permute-start | bytes 552968 | tf_op jit(solution)/shard_map/ppermute | solution.py:383
  70.3 10.6 %collective-permute-start.24 = (bf16[720,128]{1,0:T(8,128)(2,1)S(1)}, bf16[720,128]{1,0:T(8,128)(2,1)S(1)}, u32[]{:S(2)}, u32[]{:S(2)}) collective-permute-start(bf16[720,128]{1,0:T(8,128)(2,1)S(1)} %add_convert_fusion.8), channel_id=1, source_target_pairs={{4,0},{1,5},{8,4},{5,9},{12,8},{9,13},{14,12},{13,15},{10,14},{15,... | collective-permute-start | bytes 552968 | tf_op jit(solution)/shard_map/ppermute | solution.py:384
  73.1 5.6 %collective-permute-start.33 = (bf16[720,128]{1,0:T(8,128)(2,1)S(1)}, bf16[720,128]{1,0:T(8,128)(2,1)S(1)}, u32[]{:S(2)}, u32[]{:S(2)}) collective-permute-start(bf16[720,128]{1,0:T(8,128)(2,1)S(1)} %add_convert_fusion.1), channel_id=1, source_target_pairs={{0,4},{5,1},{4,8},{9,5},{8,12},{13,9},{12,14},{15,13},{14,10},{11,... | collective-permute-start | bytes 552968 | tf_op jit(solution)/shard_map/ppermute | solution.py:380
  74.2 5.6 %collective-permute-start.29 = (bf16[720,128]{1,0:T(8,128)(2,1)S(1)}, bf16[720,128]{1,0:T(8,128)(2,1)S(1)}, u32[]{:S(2)}, u32[]{:S(2)}) collective-permute-start(bf16[720,128]{1,0:T(8,128)(2,1)S(1)} %add_convert_fusion.4), channel_id=1, source_target_pairs={{4,0},{1,5},{8,4},{5,9},{12,8},{9,13},{14,12},{13,15},{10,14},{15,... | collective-permute-start | bytes 552968 | tf_op jit(solution)/shard_map/ppermute | solution.py:381
  78.7 5.6 %collective-permute-start.34 = (bf16[720,128]{1,0:T(8,128)(2,1)S(1)}, bf16[720,128]{1,0:T(8,128)(2,1)S(1)}, u32[]{:S(2)}, u32[]{:S(2)}) collective-permute-start(bf16[720,128]{1,0:T(8,128)(2,1)S(1)} %add_convert_fusion), channel_id=1, source_target_pairs={{0,4},{5,1},{4,8},{9,5},{8,12},{13,9},{12,14},{15,13},{14,10},{11,... | collective-permute-start | bytes 552968 | tf_op jit(solution)/shard_map/ppermute | solution.py:380
  79.9 5.6 %collective-permute-start.30 = (bf16[720,128]{1,0:T(8,128)(2,1)S(1)}, bf16[720,128]{1,0:T(8,128)(2,1)S(1)}, u32[]{:S(2)}, u32[]{:S(2)}) collective-permute-start(bf16[720,128]{1,0:T(8,128)(2,1)S(1)} %add_convert_fusion.3), channel_id=1, source_target_pairs={{4,0},{1,5},{8,4},{5,9},{12,8},{9,13},{14,12},{13,15},{10,14},{15,... | collective-permute-start | bytes 552968 | tf_op jit(solution)/shard_map/ppermute | solution.py:381
